TPU v7x, 32 devices: a whole 2x2x4 slice. The times are simulated.
32 devices in a mesh: dp: 8 (over z, x), head: 4 (over y, core).
Axes of the slice: x: 2, y: 2, z: 4, core: 2. Of those that a mesh axis runs over, the one named last changes fastest.
Arguments:
- block_in: bfloat16 [65536, 512], P('dp', 'head'), may hold values from -6 to 6
- crop_ids: int32 [256, 16, 16], P('dp'), may hold values from 0 to 3, as said below
- cotangent: bfloat16 [65536, 512], P('dp', 'head'), may hold values from -6 to 6
- cpe_kernel: bfloat16 [9, 512], P(None, 'head'), may hold values from -2 to 2
- cpe_bias: bfloat16 [512], P('head'), may hold values from -1.75 to 1.75
- norm1_gain: bfloat16 [512], P('head'), may hold values from 0.5 to 1.5
- norm1_shift: bfloat16 [512], P('head'), may hold values from -1.75 to 1.75
- qkv_weight: bfloat16 [512, 3, 512], P(None, None, 'head'), may hold values from -0.25 to 0.25
- qv_bias: bfloat16 [2, 512], P(None, 'head'), may hold values from -3 to 3
- crpe_kernel: bfloat16 [49, 512], P(None, 'head'), may hold values from -1.25 to 1.25
- proj_weight: bfloat16 [512, 512], P('head'), may hold values from -0.25 to 0.25
- proj_bias: bfloat16 [512], P('head'), may hold values from -1.75 to 1.75
- norm2_gain: bfloat16 [512], P('head'), may hold values from 0.5 to 1.5
- norm2_shift: bfloat16 [512], P('head'), may hold values from -1.75 to 1.75
- fc1_weight: bfloat16 [512, 2048], P(None, 'head'), may hold values from -0.25 to 0.25
- fc1_bias: bfloat16 [2048], P('head'), may hold values from -3 to 3
- fc2_weight: bfloat16 [2048, 512], P('head'), may hold values from -0.125 to 0.125
- fc2_bias: bfloat16 [512], P('head'), may hold values from -1.75 to 1.75
Outputs:
- block_out: float32 [65536, 512], P('dp', 'head')
- input_grad: float32 [65536, 512], P('dp', 'head')
- cpe_kernel_grad: float32 [9, 512], P(None, 'head')
- cpe_bias_grad: float32 [512], P('head')
- norm1_gain_grad: float32 [512], P('head')
- norm1_shift_grad: float32 [512], P('head')
- qkv_weight_grad: float32 [512, 3, 512], P(None, None, 'head')
- qv_bias_grad: float32 [2, 512], P(None, 'head')
- crpe_kernel_grad: float32 [49, 512], P(None, 'head')
- proj_weight_grad: float32 [512, 512], P('head')
- proj_bias_grad: float32 [512], P('head')
- norm2_gain_grad: float32 [512], P('head')
- norm2_shift_grad: float32 [512], P('head')
- fc1_weight_grad: float32 [512, 2048], P(None, 'head')
- fc1_bias_grad: float32 [2048], P('head')
- fc2_weight_grad: float32 [2048, 512], P('head')
- fc2_bias_grad: float32 [512], P('head')
Inputs may be any that keep to these rules, and one draw needn't show every extreme that they name: `crop_ids`: every canvas is cut by one row cut into an upper and a lower band, and each band by one column cut; ids are 0 upper left, 1 upper right, 2 lower left, 3 lower right; every rectangle is 3 or more tokens along each side, so all 4 ids occur in every canvas.
All inputs are finite; a program needn't handle non-finite values.
Results may differ from a plain program's by a relative error of at most 0.015.
Values may be sent and summed in bfloat16 or wider, within the bound.
A program may use at most 320 MiB of HBM per device.

v0:
```python
import jax
import jax.numpy as jnp
from jax import lax
from jax.sharding import PartitionSpec as P

D = 512
HEADS = 8
HEAD_DIM = 64
SIDE = 16
CROPS = 4


EPSILON = 1e-06
PRECISE = lax.Precision.HIGHEST
ROOT_HALF = 0.7071067811865476
ROOT_TWO_PI = 2.5066282746310002


def matmul(left, right):
    return jnp.dot(left, right, preferred_element_type=jnp.float32)


def inner_rows(left, right):
    return lax.dot_general(
        left, right, (((0,), (0,)), ((), ())), preferred_element_type=jnp.float32
    )


def outer_rows(left, right):
    return lax.dot_general(
        left, right, (((1,), (1,)), ((), ())), preferred_element_type=jnp.float32
    )


def round_trip(values_f):
    return lax.optimization_barrier(values_f.astype(jnp.bfloat16)).astype(jnp.float32)


def shift_grid(values_grid, row_step, col_step):
    padded = jnp.pad(values_grid, ((0, 0), (3, 3), (3, 3), (0, 0)))
    return padded[:, 3 + row_step : 3 + row_step + SIDE, 3 + col_step : 3 + col_step + SIDE, :]


def same_crop(crop_map, row_step, col_step):
    padded = jnp.pad(crop_map, ((0, 0), (3, 3), (3, 3)), constant_values=-1)
    return (
        padded[:, 3 + row_step : 3 + row_step + SIDE, 3 + col_step : 3 + col_step + SIDE]
        == crop_map
    )[..., None]


def crop_conv(values_grid, crop_map, kernel, reach_size):
    tap_width = 2 * reach_size + 1
    accumulated = jnp.zeros_like(values_grid)
    for row_step in range(-reach_size, reach_size + 1):
        for col_step in range(-reach_size, reach_size + 1):
            tap_index = (row_step + reach_size) * tap_width + col_step + reach_size
            moved = jnp.where(
                same_crop(crop_map, row_step, col_step),
                shift_grid(values_grid, row_step, col_step),
                0.0,
            )
            accumulated = accumulated + kernel[tap_index] * moved
    return accumulated


def conv_weight_grad(grad_grid, values_grid, crop_map, reach_size):
    tap_rows = []
    for row_step in range(-reach_size, reach_size + 1):
        for col_step in range(-reach_size, reach_size + 1):
            moved = jnp.where(
                same_crop(crop_map, row_step, col_step),
                shift_grid(values_grid, row_step, col_step),
                0.0,
            )
            tap_rows.append(jnp.sum(grad_grid * moved, axis=(0, 1, 2)))
    return jnp.stack(tap_rows)


def reach_mask(channel_start, channel_count):
    channel_ids = channel_start + jnp.arange(channel_count, dtype=jnp.int32)
    head_ids = channel_ids // HEAD_DIM
    reach_size = (
        1
        + (head_ids >= HEADS // 4).astype(jnp.int32)
        + (head_ids >= 5 * HEADS // 8).astype(jnp.int32)
    )
    tap_ids = jnp.arange(49, dtype=jnp.int32)
    cycle_size = jnp.maximum(jnp.abs(tap_ids // 7 - 3), jnp.abs(tap_ids % 7 - 3))
    return (cycle_size[:, None] <= reach_size[None, :]).astype(jnp.float32)


def norm_rows(full_rows, gain_vec, shift_vec):
    center = jnp.mean(full_rows, axis=-1, keepdims=True)
    square = jnp.mean(full_rows * full_rows, axis=-1, keepdims=True)
    inv_std = lax.rsqrt(square - center * center + EPSILON)
    return ((full_rows - center) * inv_std * gain_vec + shift_vec, center, inv_std)


def norm_sums(part_grad, full_rows, center, inv_std, gain_full):
    weighted = part_grad * gain_full
    hat_rows = (full_rows - center) * inv_std
    return (jnp.sum(weighted, axis=1), jnp.sum(weighted * hat_rows, axis=1))


def norm_back(norm_grad, local_rows, center, inv_std, gain_local, sum_first, sum_second):
    hat_local = (local_rows - center) * inv_std
    input_part = inv_std * (
        norm_grad * gain_local - sum_first[:, None] / D - hat_local * sum_second[:, None] / D
    )
    return (input_part, jnp.sum(norm_grad * hat_local, axis=0), jnp.sum(norm_grad, axis=0))


def gelu_slope(pre_act):
    return (
        0.5 * (1.0 + lax.erf(pre_act * ROOT_HALF))
        + pre_act * jnp.exp(-0.5 * pre_act * pre_act) / ROOT_TWO_PI
    )


def attend_forward(query_b, keys_b, values_b, crop_map, kernel_eff):
    canvas_count = crop_map.shape[0]
    places = SIDE * SIDE
    channels = query_b.shape[1]
    head_count = channels // HEAD_DIM
    onehot = (
        crop_map.reshape(canvas_count, places)[:, :, None]
        == jnp.arange(CROPS, dtype=jnp.int32)[None, None, :]
    ).astype(jnp.float32)
    keys_f = keys_b.astype(jnp.float32).reshape(canvas_count, places, channels)
    highest = jnp.max(jnp.where(onehot[..., None] > 0, keys_f[:, :, None, :], -1e30), axis=1)
    lifted = jnp.einsum("btc,bcd->btd", onehot, highest, precision=PRECISE)
    exp_keys = jnp.exp(keys_f - lifted)
    totals = jnp.einsum("btc,btd->bcd", onehot, exp_keys, precision=PRECISE)
    key_soft = exp_keys / jnp.einsum("btc,bcd->btd", onehot, totals, precision=PRECISE)
    head_shape = (canvas_count, places, head_count, HEAD_DIM)
    soft_heads = key_soft.astype(jnp.bfloat16).reshape(head_shape)
    value_heads = values_b.reshape(head_shape)
    query_heads = query_b.reshape(head_shape)
    onehot_b = onehot.astype(jnp.bfloat16)
    context_list = [
        jnp.einsum(
            "bthd,bthe->bhde",
            soft_heads * onehot_b[:, :, crop_index, None, None],
            value_heads,
            preferred_element_type=jnp.float32,
        )
        for crop_index in range(CROPS)
    ]
    context_b = jnp.stack(context_list, axis=1).astype(jnp.bfloat16)
    all_crops = jnp.einsum(
        "bthd,bchde->btche", query_heads, context_b, preferred_element_type=jnp.float32
    )
    factor = jnp.sum(all_crops * onehot[:, :, :, None, None], axis=2).reshape(
        canvas_count * places, channels
    )
    value_grid = values_b.astype(jnp.float32).reshape(canvas_count, SIDE, SIDE, channels)
    conv_value = crop_conv(value_grid, crop_map, kernel_eff, 3).reshape(
        canvas_count * places, channels
    )
    attended = factor * HEAD_DIM ** (-0.5) + query_b.astype(jnp.float32) * conv_value
    return (attended, (onehot, key_soft, soft_heads, context_b, conv_value))


def attend_backward(grad_b, query_b, values_b, crop_map, kernel_eff, attn_kept):
    onehot, key_soft, soft_heads, context_b, conv_value = attn_kept
    canvas_count = crop_map.shape[0]
    places = SIDE * SIDE
    row_count, channels = grad_b.shape
    head_count = channels // HEAD_DIM
    head_shape = (canvas_count, places, head_count, HEAD_DIM)
    grad_heads = grad_b.reshape(head_shape)
    query_heads = query_b.reshape(head_shape)
    value_heads = values_b.reshape(head_shape)
    onehot_b = onehot.astype(jnp.bfloat16)
    pick_crop = onehot[:, :, :, None, None]
    query_part = jnp.einsum(
        "bthe,bchde->btchd", grad_heads, context_b, preferred_element_type=jnp.float32
    )
    query_part = jnp.sum(query_part * pick_crop, axis=2).reshape(
        row_count, channels
    ) * HEAD_DIM ** (-0.5)
    context_list = [
        jnp.einsum(
            "bthd,bthe->bhde",
            query_heads * onehot_b[:, :, crop_index, None, None],
            grad_heads,
            preferred_element_type=jnp.float32,
        )
        for crop_index in range(CROPS)
    ]
    context_grad = (jnp.stack(context_list, axis=1) * HEAD_DIM ** (-0.5)).astype(jnp.bfloat16)
    value_part = jnp.einsum(
        "bthd,bchde->btche", soft_heads, context_grad, preferred_element_type=jnp.float32
    )
    value_part = jnp.sum(value_part * pick_crop, axis=2).reshape(row_count, channels)
    soft_grad = jnp.einsum(
        "bthe,bchde->btchd", value_heads, context_grad, preferred_element_type=jnp.float32
    )
    soft_grad = round_trip(
        jnp.sum(soft_grad * pick_crop, axis=2).reshape(canvas_count, places, channels)
    )
    inner_sum = jnp.einsum("btc,btd->bcd", onehot, key_soft * soft_grad, precision=PRECISE)
    keys_grad = key_soft * (
        soft_grad - jnp.einsum("btc,bcd->btd", onehot, inner_sum, precision=PRECISE)
    )
    grad_f = grad_b.astype(jnp.float32)
    query_f = query_b.astype(jnp.float32)
    query_grad = query_part + grad_f * conv_value
    grid_shape = (canvas_count, SIDE, SIDE, channels)
    conv_grad = (grad_f * query_f).reshape(grid_shape)
    value_grid = values_b.astype(jnp.float32).reshape(grid_shape)
    values_grad = value_part + crop_conv(conv_grad, crop_map, kernel_eff[::-1], 3).reshape(
        row_count, channels
    )
    kernel_grad = conv_weight_grad(conv_grad, value_grid, crop_map, 3)
    return (query_grad, keys_grad.reshape(row_count, channels), values_grad, kernel_grad)


def run_block(inputs_f, grads_f, crop_map, weight_set, channel_start):
    (
        cpe_kernel,
        cpe_bias,
        gain_one,
        shift_one,
        qkv_weight,
        qv_bias,
        crpe_kernel,
        proj_weight,
        proj_bias,
        gain_two,
        shift_two,
        fc1_weight,
        fc1_bias,
        fc2_weight,
        fc2_bias,
    ) = weight_set
    row_count, channels = inputs_f.shape
    canvas_count = crop_map.shape[0]
    grid_shape = (canvas_count, SIDE, SIDE, channels)
    cpe_taps = cpe_kernel.astype(jnp.float32)
    gain_one_f = gain_one.astype(jnp.float32)
    gain_two_f = gain_two.astype(jnp.float32)
    input_grid = inputs_f.reshape(grid_shape)
    first_sum = (
        inputs_f
        + crop_conv(input_grid, crop_map, cpe_taps, 1).reshape(row_count, channels)
        + cpe_bias.astype(jnp.float32)
    )
    first_full, gain_one_full, shift_one_full = (
        lax.all_gather(first_sum, "head", axis=1, tiled=True),
        lax.all_gather(gain_one_f, "head", axis=0, tiled=True),
        lax.all_gather(shift_one.astype(jnp.float32), "head", axis=0, tiled=True),
    )
    normed_one, center_one, inv_one = norm_rows(first_full, gain_one_full, shift_one_full)
    hidden_one = normed_one.astype(jnp.bfloat16)
    qkv_flat = qkv_weight.reshape(D, 3 * channels)
    projected = matmul(hidden_one, qkv_flat)
    qv_float = qv_bias.astype(jnp.float32)
    query_b = (projected[:, :channels] + qv_float[0]).astype(jnp.bfloat16)
    keys_b = projected[:, channels : 2 * channels].astype(jnp.bfloat16)
    values_b = (projected[:, 2 * channels :] + qv_float[1]).astype(jnp.bfloat16)
    crpe_mask = reach_mask(channel_start, channels)
    kernel_eff = crpe_kernel.astype(jnp.float32) * crpe_mask
    attended, attn_kept = attend_forward(query_b, keys_b, values_b, crop_map, kernel_eff)
    attended_b = attended.astype(jnp.bfloat16)
    proj_part = matmul(attended_b, proj_weight)
    proj_out = lax.psum_scatter(proj_part, "head", scatter_dimension=1, tiled=True)
    second = first_sum + proj_out + proj_bias.astype(jnp.float32)
    second_full, gain_two_full, shift_two_full = (
        lax.all_gather(second, "head", axis=1, tiled=True),
        lax.all_gather(gain_two_f, "head", axis=0, tiled=True),
        lax.all_gather(shift_two.astype(jnp.float32), "head", axis=0, tiled=True),
    )
    normed_two, center_two, inv_two = norm_rows(second_full, gain_two_full, shift_two_full)
    hidden_two = normed_two.astype(jnp.bfloat16)
    pre_act = matmul(hidden_two, fc1_weight) + fc1_bias.astype(jnp.float32)
    active_b = jax.nn.gelu(pre_act, approximate=False).astype(jnp.bfloat16)
    mlp_part = matmul(active_b, fc2_weight)
    mlp_out = lax.psum_scatter(
        mlp_part.astype(jnp.bfloat16), "head", scatter_dimension=1, tiled=True
    ).astype(jnp.float32)
    output = second + mlp_out + fc2_bias.astype(jnp.float32)
    grad_b = grads_f.astype(jnp.bfloat16)
    grad_full = lax.all_gather(grad_b, "head", axis=1, tiled=True)
    fc2_grad = inner_rows(active_b, grad_full)
    fc2_bias_grad = jnp.sum(grad_b.astype(jnp.float32), axis=0)
    act_grad = outer_rows(grad_full, fc2_weight)
    pre_grad_b = (act_grad * gelu_slope(pre_act)).astype(jnp.bfloat16)
    fc1_grad = inner_rows(hidden_two, pre_grad_b)
    fc1_bias_grad = jnp.sum(pre_grad_b.astype(jnp.float32), axis=0)
    norm_part_two = outer_rows(pre_grad_b, fc1_weight)
    sum_first, sum_second = norm_sums(
        norm_part_two, second_full, center_two, inv_two, gain_two_full
    )
    head_count = lax.axis_size("head")
    norm_grad_two, first_cols, second_cols = (
        lax.psum_scatter(
            norm_part_two.astype(jnp.bfloat16), "head", scatter_dimension=1, tiled=True
        ).astype(jnp.float32),
        lax.psum_scatter(
            jnp.broadcast_to(sum_first[:, None], (row_count, head_count)).astype(jnp.bfloat16),
            "head",
            scatter_dimension=1,
            tiled=True,
        ).astype(jnp.float32),
        lax.psum_scatter(
            jnp.broadcast_to(sum_second[:, None], (row_count, head_count)).astype(jnp.bfloat16),
            "head",
            scatter_dimension=1,
            tiled=True,
        ).astype(jnp.float32),
    )
    sum_first, sum_second = (first_cols[:, 0], second_cols[:, 0])
    input_part, gain_two_grad, shift_two_grad = norm_back(
        norm_grad_two, second, center_two, inv_two, gain_two_f, sum_first, sum_second
    )
    second_grad = grads_f + input_part
    second_low = second_grad.astype(jnp.bfloat16)
    proj_bias_grad = jnp.sum(second_low.astype(jnp.float32), axis=0)
    second_low_full = lax.all_gather(second_low, "head", axis=1, tiled=True)
    proj_grad = inner_rows(attended_b, second_low_full)
    attended_grad = outer_rows(second_low_full, proj_weight).astype(jnp.bfloat16)
    query_grad, keys_grad, values_grad, crpe_raw = attend_backward(
        attended_grad, query_b, values_b, crop_map, kernel_eff, attn_kept
    )
    crpe_grad = crpe_raw * crpe_mask
    query_gb = query_grad.astype(jnp.bfloat16)
    keys_gb = keys_grad.astype(jnp.bfloat16)
    values_gb = values_grad.astype(jnp.bfloat16)
    qkv_grad_b = jnp.concatenate([query_gb, keys_gb, values_gb], axis=1)
    qkv_grad = inner_rows(hidden_one, qkv_grad_b).reshape(D, 3, channels)
    qv_bias_grad = jnp.stack(
        [
            jnp.sum(query_gb.astype(jnp.float32), axis=0),
            jnp.sum(values_gb.astype(jnp.float32), axis=0),
        ]
    )
    norm_part_one = outer_rows(qkv_grad_b, qkv_flat)
    sum_first, sum_second = norm_sums(norm_part_one, first_full, center_one, inv_one, gain_one_full)
    head_count = lax.axis_size("head")
    norm_grad_one, first_cols, second_cols = (
        lax.psum_scatter(
            norm_part_one.astype(jnp.bfloat16), "head", scatter_dimension=1, tiled=True
        ).astype(jnp.float32),
        lax.psum_scatter(
            jnp.broadcast_to(sum_first[:, None], (row_count, head_count)).astype(jnp.bfloat16),
            "head",
            scatter_dimension=1,
            tiled=True,
        ).astype(jnp.float32),
        lax.psum_scatter(
            jnp.broadcast_to(sum_second[:, None], (row_count, head_count)).astype(jnp.bfloat16),
            "head",
            scatter_dimension=1,
            tiled=True,
        ).astype(jnp.float32),
    )
    sum_first, sum_second = (first_cols[:, 0], second_cols[:, 0])
    input_part, gain_one_grad, shift_one_grad = norm_back(
        norm_grad_one, first_sum, center_one, inv_one, gain_one_f, sum_first, sum_second
    )
    first_grad = second_grad + input_part
    first_grid = first_grad.reshape(grid_shape)
    input_grad = first_grad + crop_conv(first_grid, crop_map, cpe_taps[::-1], 1).reshape(
        row_count, channels
    )
    cpe_grad = conv_weight_grad(first_grid, input_grid, crop_map, 1)
    cpe_bias_grad = jnp.sum(first_grad, axis=0)
    gradients = (
        cpe_grad,
        cpe_bias_grad,
        gain_one_grad,
        shift_one_grad,
        qkv_grad,
        qv_bias_grad,
        crpe_grad,
        proj_grad,
        proj_bias_grad,
        gain_two_grad,
        shift_two_grad,
        fc1_grad,
        fc1_bias_grad,
        fc2_grad,
        fc2_bias_grad,
    )
    return (output, input_grad, gradients)


def body(
    block_in,
    crop_ids,
    cotangent,
    cpe_kernel,
    cpe_bias,
    norm1_gain,
    norm1_shift,
    qkv_weight,
    qv_bias,
    crpe_kernel,
    proj_weight,
    proj_bias,
    norm2_gain,
    norm2_shift,
    fc1_weight,
    fc1_bias,
    fc2_weight,
    fc2_bias,
):
    weight_set = (
        cpe_kernel,
        cpe_bias,
        norm1_gain,
        norm1_shift,
        qkv_weight,
        qv_bias,
        crpe_kernel,
        proj_weight,
        proj_bias,
        norm2_gain,
        norm2_shift,
        fc1_weight,
        fc1_bias,
        fc2_weight,
        fc2_bias,
    )
    channels = block_in.shape[1]
    output, input_grad, gradients = run_block(
        block_in.astype(jnp.float32),
        cotangent.astype(jnp.float32),
        crop_ids,
        weight_set,
        lax.axis_index("head") * channels,
    )
    summed = lax.psum(
        (
            gradients[0],
            gradients[1],
            gradients[2],
            gradients[3],
            gradients[4],
            gradients[5],
            gradients[6],
            gradients[7],
            gradients[8],
            gradients[9],
            gradients[10],
            gradients[11],
            gradients[12],
            gradients[13],
            gradients[14],
        ),
        "dp",
    )
    return (
        output,
        input_grad,
        summed[0],
        summed[1],
        summed[2],
        summed[3],
        summed[4],
        summed[5],
        summed[6],
        summed[7],
        summed[8],
        summed[9],
        summed[10],
        summed[11],
        summed[12],
        summed[13],
        summed[14],
    )


def solution(mesh):
    return jax.shard_map(
        body,
        mesh=mesh,
        in_specs=(
            P("dp", "head"),
            P("dp", None, None),
            P("dp", "head"),
            P(None, "head"),
            P("head"),
            P("head"),
            P("head"),
            P(None, None, "head"),
            P(None, "head"),
            P(None, "head"),
            P("head", None),
            P("head"),
            P("head"),
            P("head"),
            P(None, "head"),
            P("head"),
            P("head", None),
            P("head"),
        ),
        out_specs=(
            P("dp", "head"),
            P("dp", "head"),
            P(None, "head"),
            P("head"),
            P("head"),
            P("head"),
            P(None, None, "head"),
            P(None, "head"),
            P(None, "head"),
            P("head", None),
            P("head"),
            P("head"),
            P("head"),
            P(None, "head"),
            P("head"),
            P("head", None),
            P("head"),
        ),
        check_vma=False,
    )
```

profile of v0, /device:TPU:0, one launch (start us, length us, event | category | flops | bytes accessed | tf_op | source)
XLA Modules:
  0.0 1582.0 jit_solution(226262940935419624)
XLA Ops:
  17.3 10.0 multiply_add_fusion.1
  62.3 6.0 all-gather.1
  68.8 5.5 all-gather
  77.5 63.4 %all-gather.9.cloned.1.call-done = f32[8192,512]{1,0:T(8,128)} async-done(((f32[8192,128]{1,0:T(8,128)}), f32[8192,512]{1,0:T(8,128)}) %all-gather.9.cloned.1.call-update) | async-done | bytes 16777232 | tf_op jit(solution)/shard_map/all_gather | solution.py:251
  140.9 8.0 fusion.413
  149.0 7.4 add_convert_fusion.1
  175.3 6.9 select_reduce_fusion
  187.5 5.7 fusion.420
  221.2 8.4 fusion.12
  229.6 4.8 broadcast_multiply_fusion.1
  234.4 11.3 copy.397
  245.8 8.8 reshape.416
  254.7 123.5 %multiply_add_fusion = f32[32,16,16,128]{3,2,1,0:T(8,128)} fusion(f32[32,16,16,128]{3,2,1,0:T(8,128)} %bitcast_convert_fusion.3, f32[128]{0:T(128)} %get-tuple-element.191, f32[128]{0:T(128)} %get-tuple-element.192, f32[128]{0:T(128)} %get-tuple-element.193, f32[128]{0:T(128)} %get-tuple-element.194, f32[128]{0:T(128)} %get-tuple-element.195, ...), kind=kLoop, calls=%fused_computation.495 | loop fusion | flops 152043520 | bytes 8806912 | tf_op jit(solution)/shard_map/add | solution.py:63
  383.7 8.1 fusion.422
  392.4 125.6 %reduce-scatter.11.cloned.1.call-done = f32[8192,128]{1,0:T(8,128)} async-done(((f32[8192,512]{1,0:T(8,128)}), f32[8192,128]{1,0:T(8,128)}) %reduce-scatter.11.cloned.1.call-update) | async-done | bytes 4194320 | tf_op jit(solution)/shard_map/reduce_scatter | solution.py:268
  518.0 5.9 add_add_fusion.1
  525.1 5.0 all-gather.3
  530.2 5.2 all-gather.2
  535.4 96.9 %all-gather.11.cloned.1.call-done = f32[8192,512]{1,0:T(8,128)} async-done(((f32[8192,128]{1,0:T(8,128)}), f32[8192,512]{1,0:T(8,128)}) %all-gather.11.cloned.1.call-update) | async-done | bytes 16777232 | tf_op jit(solution)/shard_map/all_gather | solution.py:271
  632.3 8.0 fusion.412
  640.4 8.9 add_convert_fusion
  652.6 43.6 %fusion.2 = (bf16[8192,512]{1,0:T(8,128)(2,1)}, f32[8192,512]{1,0:T(8,128)}) fusion(f32[512]{0:T(512)S(1)} %convert_element_type.396, bf16[8192,512]{1,0:T(8,128)(2,1)S(1)} %add_convert_fusion, bf16[512,512]{1,0:T(8,128)(2,1)S(1)} %copy-done), kind=kOutput, calls=%fused_computation.116 | convolution fusion | flops 4571791360 | bytes 34080768 | tf_op jit(solution)/shard_map/dot_general | solution.py:20
  696.2 14.4 convert_reduce_fusion
  713.9 8.1 fusion.423
  722.0 17.5 %copy.362 = f32[8192,512]{1,0:T(8,128)} copy(f32[8192,512]{0,1:T(8,128)} %fusion.423) | data formatting | bytes 33554432 | tf_op jit(solution)/shard_map/dot_general | solution.py:30
  739.5 12.8 multiply_reduce_fusion.5
  753.7 10.2 convolution_convert_fusion
  763.9 11.8 copy.405
  775.8 9.0 convert_bitcast_fusion.1
  789.0 70.5 %reduce-scatter.13.cloned.1.call-done = bf16[128,8192]{1,0:T(8,128)(2,1)} async-done(((bf16[512,8192]{1,0:T(8,128)(2,1)}), bf16[128,8192]{1,0:T(8,128)(2,1)}) %reduce-scatter.13.cloned.1.call-update) | async-done | bytes 2097168
  863.6 70.4 %reduce-scatter.15.cloned.1.call-done = bf16[128,8192]{1,0:T(8,128)(2,1)} async-done(((bf16[512,8192]{1,0:T(8,128)(2,1)}), bf16[128,8192]{1,0:T(8,128)(2,1)}) %reduce-scatter.15.cloned.1.call-update) | async-done | bytes 2097168
  938.3 9.8 convert_reduce_fusion.2
  948.2 59.5 %all-gather.15.cloned.1.call-done = bf16[8192,512]{1,0:T(8,128)(2,1)} async-done(((bf16[8192,128]{1,0:T(8,128)(2,1)}), bf16[8192,512]{1,0:T(8,128)(2,1)}) %all-gather.15.cloned.1.call-update) | async-done | bytes 8388624 | tf_op jit(solution)/shard_map/all_gather | solution.py:321
  1007.7 16.0 %multiply_reduce_fusion.11 = (f32[128]{0:T(128)}, f32[128]{0:T(128)}, f32[128]{0:T(128)}, f32[128]{0:T(128)}, f32[128]{0:T(128)}, /*index=5*/f32[128]{0:T(128)},...) fusion(f32[32,16,16,128]{3,2,1,0:T(8,128)} %bitcast_convert_fusion.3, pred[32,16,16]{2,1,0:T(8,128)(4,1)S(1)} %copy-done.86, ...), kind=kOutput, calls=%fused_computation.435 | convolution fusion | flops 1103100928 | bytes 16977920 | tf_op jit(solution)/shard_map/dot_general | solution.py:30
  1030.7 4.6 fusion.296
  1039.9 4.8 fusion.290
  1056.9 11.3 copy.404
  1068.2 9.1 reduce_sum.747
  1077.3 8.8 reshape.418
  1086.1 7.2 fusion.11
  1097.0 10.4 fusion.10
  1111.9 4.7 fusion.25
  1116.6 5.1 fusion.27
  1121.8 11.3 copy.400
  1133.1 8.8 reshape.417
  1142.1 9.3 multiply_reduce_fusion.30
  1151.7 125.9 %convert_reduce_fusion.5 = (f32[128]{0:T(128)}, f32[32,16,16,128]{3,2,1,0:T(8,128)}) fusion(f32[32,16,16,128]{3,2,1,0:T(8,128)} %reduce_sum.747, pred[32,16,16]{2,1,0:T(8,128)(4,1)S(1)} %copy-done.59, f32[128]{0:T(128)} %get-tuple-element.190, pred[32,16,16]{2,1,0:T(8,128)(4,1)S(1)} %copy-done.65, f32[128]{0:T(128)} %get-tuple-element.209, ...), kind=kLoop, calls=%fused_computation.479 | loop fusion | flops 156237696 | bytes 13001728 | tf_op jit(solution)/shard_map/reduce_sum | solution.py:336
  1283.0 8.3 fusion.270
  1291.3 17.4 %copy.385 = f32[8192,512]{1,0:T(8,128)} copy(f32[8192,512]{0,1:T(8,128)} %fusion.270) | data formatting | bytes 33554432 | tf_op jit(solution)/shard_map/dot_general | solution.py:30
  1308.7 12.9 multiply_reduce_fusion.4
  1322.9 9.0 convert_bitcast_fusion
  1332.0 11.4 fusion.425
  1343.4 11.5 fusion.426
  1361.5 20.9 %multiply_reduce_fusion.7 = (f32[128]{0:T(128)S(1)}, f32[128]{0:T(128)S(1)}, f32[128]{0:T(128)S(1)}, f32[128]{0:T(128)S(1)}, f32[128]{0:T(128)}, /*index=5*/f32[128]{0:T(128)}, f32[128]{0:T(128)}, f32[128]{0:T(128)}) fusion(f32[32,16,16,128]{3,2,1,0:T(8,128)} %bitcast_convert_fusion.3, pred[32,16,16]{2,1,0:T(8,128)(4,1)S(1)} %copy-done.65, ...), kind=kLoop, calls=%fused_computation.431 | loop fusion | flops 28310528 | bytes 8458240 | tf_op jit(solution)/shard_map/reduce_sum | solution.py:76
  1382.4 11.9 multiply_reduce_fusion.8
  1394.3 11.8 multiply_reduce_fusion.6
  1406.2 10.7 multiply_reduce_fusion.10
  1417.2 11.1 multiply_reduce_fusion.9
  1430.2 6.0 fusion.424
  1443.6 8.0 convert_reduce_fusion.1
  1451.8 11.5 multiply_reduce_fusion.55
  1463.4 39.9 %all-reduce.9 = (f32[9,128]{1,0:T(8,128)}, f32[128]{0:T(128)}, f32[128]{0:T(128)}, f32[128]{0:T(128)}, f32[2,128]{1,0:T(2,128)}, /*index=5*/f32[49,128]{1,0:T(8,...) all-reduce(f32[9,128]{1,0:T(8,128)S(1)} %stack.243, ...), channel_id=1, replica_groups=mesh['dp'=8,'head'=4] {'dp'}, use_global_device_ids=true, to_apply=%region_30.31 | all-reduce | flops 9088 | bytes 72704 | tf_op jit(solution)/shard_map/psum | solution.py:435
  1503.4 21.0 %fusion.54 = f32[32,16,16,128]{3,2,1,0:T(8,128)S(1)} fusion(f32[32,16,16,128]{3,2,1,0:T(8,128)} %bitcast.386, f32[128]{0:T(128)S(1)} %copy-done.128, f32[128]{0:T(128)S(1)} %copy-done.130, f32[128]{0:T(128)S(1)} %copy-done.132, f32[128]{0:T(128)S(1)} %copy-done.134, f32[128]{0:T(128)S(1)} %copy-done.136, f32[128]{0:T(128)S(1)} %copy-done.138, ...), kind=kLoop, calls=%fused_computation.211 | loop fusion | flops 26214400 | bytes 8458752 | tf_op jit(solution)/shard_map/add | solution.py:63
  1526.8 41.3 %all-reduce.17.cloned.1.call-done = (f32[512,3,128]{2,0,1:T(8,128)}, f32[128,512]{1,0:T(8,128)}, f32[512,512]{1,0:T(8,128)}, f32[512,512]{1,0:T(8,128)}) async-done(((f32[512,3,128]{2,0,1:T(8,128)}, f32[128,512]{1,0:T(8,128)}, f32[512,512]{1,0:T(8,128)}, f32[512,512]{1,0:T(8,128)}), (f32[512,3,128]{2,0,1:T(8,128)}, f32[128,512]{1,0:T(8,128)}, f32[512,512]{1,0:T(8,128)}, ...) | async-done | bytes 3145744 | tf_op jit(solution)/shard_map/psum | solution.py:435
  (563 shorter events, 192.2 us)
Async XLA Ops:
  7.2 645.4 %copy-start = (bf16[512,512]{1,0:T(8,128)(2,1)S(1)}, bf16[512,512]{1,0:T(8,128)(2,1)}, u32[]{:S(2)}) copy-start(bf16[512,512]{1,0:T(8,128)(2,1)} %param.32) | copy-start | bytes 1572868
  7.2 133.7 %all-gather.9.cloned.1.call-start = ((), (), s32[]{:S(2)}) async-start(), calls=%async_computation.4 | async-start | bytes 20971520 | tf_op jit(solution)/shard_map/all_gather | solution.py:251
  8.7 18.7 %copy-start.129 = (f32[128]{0:T(128)}, f32[128]{0:T(128)S(1)}, u32[]{:S(2)}) copy-start(f32[128]{0:T(128)S(1)} %get-tuple-element.241) | copy-start | bytes 1540
  8.7 18.7 %copy-start.131 = (f32[128]{0:T(128)}, f32[128]{0:T(128)S(1)}, u32[]{:S(2)}) copy-start(f32[128]{0:T(128)S(1)} %get-tuple-element.242) | copy-start | bytes 1540
  11.7 242.9 %copy-start.23 = (pred[32,16,16]{2,1,0:T(8,128)(4,1)}, pred[32,16,16]{2,1,0:T(8,128)(4,1)S(1)}, u32[]{:S(2)}) copy-start(pred[32,16,16]{2,1,0:T(8,128)(4,1)S(1)} %copy.302) | copy-start | bytes 24580
  11.9 242.7 %copy-start.25 = (pred[32,16,16]{2,1,0:T(8,128)(4,1)}, pred[32,16,16]{2,1,0:T(8,128)(4,1)S(1)}, u32[]{:S(2)}) copy-start(pred[32,16,16]{2,1,0:T(8,128)(4,1)S(1)} %copy.301) | copy-start | bytes 24580
  12.1 242.5 %copy-start.27 = (pred[32,16,16]{2,1,0:T(8,128)(4,1)}, pred[32,16,16]{2,1,0:T(8,128)(4,1)S(1)}, u32[]{:S(2)}) copy-start(pred[32,16,16]{2,1,0:T(8,128)(4,1)S(1)} %copy.300) | copy-start | bytes 24580
  12.3 242.3 %copy-start.29 = (pred[32,16,16]{2,1,0:T(8,128)(4,1)}, pred[32,16,16]{2,1,0:T(8,128)(4,1)S(1)}, u32[]{:S(2)}) copy-start(pred[32,16,16]{2,1,0:T(8,128)(4,1)S(1)} %copy.299) | copy-start | bytes 24580
  12.6 242.1 %copy-start.31 = (pred[32,16,16]{2,1,0:T(8,128)(4,1)}, pred[32,16,16]{2,1,0:T(8,128)(4,1)S(1)}, u32[]{:S(2)}) copy-start(pred[32,16,16]{2,1,0:T(8,128)(4,1)S(1)} %copy.298) | copy-start | bytes 24580
  12.8 241.9 %copy-start.33 = (pred[32,16,16]{2,1,0:T(8,128)(4,1)}, pred[32,16,16]{2,1,0:T(8,128)(4,1)S(1)}, u32[]{:S(2)}) copy-start(pred[32,16,16]{2,1,0:T(8,128)(4,1)S(1)} %copy.297) | copy-start | bytes 24580
  13.0 241.7 %copy-start.35 = (pred[32,16,16]{2,1,0:T(8,128)(4,1)}, pred[32,16,16]{2,1,0:T(8,128)(4,1)S(1)}, u32[]{:S(2)}) copy-start(pred[32,16,16]{2,1,0:T(8,128)(4,1)S(1)} %copy.296) | copy-start | bytes 24580
  13.2 241.4 %copy-start.37 = (pred[32,16,16]{2,1,0:T(8,128)(4,1)}, pred[32,16,16]{2,1,0:T(8,128)(4,1)S(1)}, u32[]{:S(2)}) copy-start(pred[32,16,16]{2,1,0:T(8,128)(4,1)S(1)} %copy.295) | copy-start | bytes 24580
  29.9 32.4 %copy-start.195 = (bf16[128]{0:T(256)(128)(2,1)S(1)}, bf16[128]{0:T(256)(128)(2,1)}, u32[]{:S(2)}) copy-start(bf16[128]{0:T(256)(128)(2,1)} %param.24) | copy-start | bytes 772
  29.9 38.4 %copy-start.196 = (bf16[128]{0:T(256)(128)(2,1)S(1)}, bf16[128]{0:T(256)(128)(2,1)}, u32[]{:S(2)}) copy-start(bf16[128]{0:T(256)(128)(2,1)} %param.23) | copy-start | bytes 772
  29.9 45.0 %copy-start.124 = (bf16[49,128]{1,0:T(8,128)(2,1)S(1)}, bf16[49,128]{1,0:T(8,128)(2,1)}, u32[]{:S(2)}) copy-start(bf16[49,128]{1,0:T(8,128)(2,1)} %param.27) | copy-start | bytes 37636
  29.9 488.1 %reduce-scatter.11.cloned.1.call-start = ((), (), s32[]{:S(2)}) async-start(), calls=%async_computation.5 | async-start | bytes 20971520 | tf_op jit(solution)/shard_map/reduce_scatter | solution.py:268
  33.1 123.3 %copy-start.52 = (bf16[512,3,128]{0,2,1:T(8,128)(2,1)}, bf16[512,3,128]{0,2,1:T(8,128)(2,1)S(1)}, u32[]{:S(2)}) copy-start(bf16[512,3,128]{0,2,1:T(8,128)(2,1)S(1)} %copy.303) | copy-start | bytes 1179652
  33.3 221.4 %copy-start.56 = (pred[32,16,16]{2,1,0:T(8,128)(4,1)}, pred[32,16,16]{2,1,0:T(8,128)(4,1)S(1)}, u32[]{:S(2)}) copy-start(pred[32,16,16]{2,1,0:T(8,128)(4,1)S(1)} %copy.322) | copy-start | bytes 24580
  33.5 221.2 %copy-start.60 = (pred[32,16,16]{2,1,0:T(8,128)(4,1)}, pred[32,16,16]{2,1,0:T(8,128)(4,1)S(1)}, u32[]{:S(2)}) copy-start(pred[32,16,16]{2,1,0:T(8,128)(4,1)S(1)} %copy.357) | copy-start | bytes 24580
  33.7 221.0 %copy-start.58 = (pred[32,16,16]{2,1,0:T(8,128)(4,1)}, pred[32,16,16]{2,1,0:T(8,128)(4,1)S(1)}, u32[]{:S(2)}) copy-start(pred[32,16,16]{2,1,0:T(8,128)(4,1)S(1)} %copy.359) | copy-start | bytes 24580
  33.9 220.8 %copy-start.64 = (pred[32,16,16]{2,1,0:T(8,128)(4,1)}, pred[32,16,16]{2,1,0:T(8,128)(4,1)S(1)}, u32[]{:S(2)}) copy-start(pred[32,16,16]{2,1,0:T(8,128)(4,1)S(1)} %copy.358) | copy-start | bytes 24580
  34.6 220.1 %copy-start.62 = (pred[32,16,16]{2,1,0:T(8,128)(4,1)}, pred[32,16,16]{2,1,0:T(8,128)(4,1)S(1)}, u32[]{:S(2)}) copy-start(pred[32,16,16]{2,1,0:T(8,128)(4,1)S(1)} %copy.321) | copy-start | bytes 24580
  34.8 219.9 %copy-start.54 = (pred[32,16,16]{2,1,0:T(8,128)(4,1)}, pred[32,16,16]{2,1,0:T(8,128)(4,1)S(1)}, u32[]{:S(2)}) copy-start(pred[32,16,16]{2,1,0:T(8,128)(4,1)S(1)} %copy.339) | copy-start | bytes 24580
  74.3 74.7 %copy-start.112 = (f32[4,1,128]{2,1,0:T(1,128)}, f32[4,1,128]{2,1,0:T(1,128)S(1)}, u32[]{:S(2)}) copy-start(f32[4,1,128]{2,1,0:T(1,128)S(1)} %all-gather) | copy-start | bytes 6148
  74.3 74.6 %copy-start.159 = (s32[49]{0:T(128)}, s32[49]{0:T(128)S(1)}, u32[]{:S(2)}) copy-start(s32[49]{0:T(128)S(1)} %fusion.399) | copy-start | bytes 592
  74.4 74.6 %copy-start.161 = (s32[128]{0:T(128)}, s32[128]{0:T(128)S(1)}, u32[]{:S(2)}) copy-start(s32[128]{0:T(128)S(1)} %fusion.403) | copy-start | bytes 1540
  77.5 129.3 %copy-start.116 = (bf16[32,256]{1,0:T(8,128)(2,1)}, bf16[32,256]{1,0:T(8,128)(2,1)S(1)}, u32[]{:S(2)}) copy-start(bf16[32,256]{1,0:T(8,128)(2,1)S(1)} %get-tuple-element.181) | copy-start | bytes 49156
  166.6 211.7 %copy-start.3 = (bf16[8192,128]{1,0:T(8,128)(2,1)}, bf16[8192,128]{1,0:T(8,128)(2,1)S(1)}, u32[]{:S(2)}) copy-start(bf16[8192,128]{1,0:T(8,128)(2,1)S(1)} %get-tuple-element.116) | copy-start | bytes 6291460
  391.8 240.5 %all-gather.11.cloned.1.call-start = ((), (), s32[]{:S(2)}) async-start(), calls=%async_computation.6 | async-start | bytes 20971520 | tf_op jit(solution)/shard_map/all_gather | solution.py:271
  524.0 172.2 %all-gather.13.cloned.1.call-start = ((), (), s32[]{:S(2)}) async-start(), calls=%async_computation.7 | async-start | bytes 10485760 | tf_op jit(solution)/shard_map/all_gather | solution.py:285
  524.5 261.4 %all-reduce.21.cloned.1.call-start = ((), (), s32[]{:S(2)}) async-start(), calls=%async_computation.14 | async-start | bytes 262144
  535.4 105.0 %copy-start.114 = (f32[4,1,128]{2,1,0:T(1,128)}, f32[4,1,128]{2,1,0:T(1,128)S(1)}, u32[]{:S(2)}) copy-start(f32[4,1,128]{2,1,0:T(1,128)S(1)} %all-gather.2) | copy-start | bytes 6148
  652.6 43.6 %copy-start.193 = (bf16[512,512]{1,0:T(8,128)(2,1)S(1)}, bf16[512,512]{1,0:T(8,128)(2,1)}, u32[]{:S(2)}) copy-start(bf16[512,512]{1,0:T(8,128)(2,1)} %param.34) | copy-start | bytes 1572868
  753.7 105.9 %reduce-scatter.13.cloned.1.call-start = ((), (), s32[]{:S(2)}) async-start(), calls=%async_computation.9 | async-start | bytes 10485760
  775.7 158.4 %reduce-scatter.15.cloned.1.call-start = ((), (), s32[]{:S(2)}) async-start(), calls=%async_computation.10 | async-start | bytes 10485760
  784.8 222.9 %all-gather.15.cloned.1.call-start = ((), (), s32[]{:S(2)}) async-start(), calls=%async_computation.8 | async-start | bytes 10485760 | tf_op jit(solution)/shard_map/all_gather | solution.py:321
  859.6 78.6 %copy-start.192 = (f32[128]{0:T(128)S(1)}, f32[128]{0:T(128)}, u32[]{:S(2)}) copy-start(f32[128]{0:T(128)} %get-tuple-element.252) | copy-start | bytes 1540
  938.2 69.5 %copy-start.4 = (bf16[8192,128]{1,0:T(8,128)(2,1)S(1)}, bf16[8192,128]{1,0:T(8,128)(2,1)}, u32[]{:S(2)}) copy-start(bf16[8192,128]{1,0:T(8,128)(2,1)} %copy-done.3) | copy-start | bytes 6291460
  938.2 69.5 %copy-start.85 = (pred[32,16,16]{2,1,0:T(8,128)(4,1)S(1)}, pred[32,16,16]{2,1,0:T(8,128)(4,1)}, u32[]{:S(2)}) copy-start(pred[32,16,16]{2,1,0:T(8,128)(4,1)} %copy.320) | copy-start | bytes 24580
  938.2 69.5 %copy-start.86 = (pred[32,16,16]{2,1,0:T(8,128)(4,1)S(1)}, pred[32,16,16]{2,1,0:T(8,128)(4,1)}, u32[]{:S(2)}) copy-start(pred[32,16,16]{2,1,0:T(8,128)(4,1)} %copy.354) | copy-start | bytes 24580
  938.2 69.5 %copy-start.87 = (pred[32,16,16]{2,1,0:T(8,128)(4,1)S(1)}, pred[32,16,16]{2,1,0:T(8,128)(4,1)}, u32[]{:S(2)}) copy-start(pred[32,16,16]{2,1,0:T(8,128)(4,1)} %copy.353) | copy-start | bytes 24580
  938.2 69.5 %copy-start.88 = (pred[32,16,16]{2,1,0:T(8,128)(4,1)S(1)}, pred[32,16,16]{2,1,0:T(8,128)(4,1)}, u32[]{:S(2)}) copy-start(pred[32,16,16]{2,1,0:T(8,128)(4,1)} %copy.352) | copy-start | bytes 24580
  938.2 69.5 %copy-start.89 = (pred[32,16,16]{2,1,0:T(8,128)(4,1)S(1)}, pred[32,16,16]{2,1,0:T(8,128)(4,1)}, u32[]{:S(2)}) copy-start(pred[32,16,16]{2,1,0:T(8,128)(4,1)} %copy.351) | copy-start | bytes 24580
  938.2 69.5 %copy-start.90 = (pred[32,16,16]{2,1,0:T(8,128)(4,1)S(1)}, pred[32,16,16]{2,1,0:T(8,128)(4,1)}, u32[]{:S(2)}) copy-start(pred[32,16,16]{2,1,0:T(8,128)(4,1)} %copy.350) | copy-start | bytes 24580
  938.2 69.5 %copy-start.91 = (pred[32,16,16]{2,1,0:T(8,128)(4,1)S(1)}, pred[32,16,16]{2,1,0:T(8,128)(4,1)}, u32[]{:S(2)}) copy-start(pred[32,16,16]{2,1,0:T(8,128)(4,1)} %copy.349) | copy-start | bytes 24580
  938.3 69.5 %copy-start.92 = (pred[32,16,16]{2,1,0:T(8,128)(4,1)S(1)}, pred[32,16,16]{2,1,0:T(8,128)(4,1)}, u32[]{:S(2)}) copy-start(pred[32,16,16]{2,1,0:T(8,128)(4,1)} %copy.348) | copy-start | bytes 24580
  938.3 69.5 %copy-start.101 = (bf16[128,512]{1,0:T(8,128)(2,1)S(1)}, bf16[128,512]{1,0:T(8,128)(2,1)}, u32[]{:S(2)}) copy-start(bf16[128,512]{1,0:T(8,128)(2,1)} %param.28) | copy-start | bytes 393220
  948.1 488.2 %all-reduce.19.cloned.1.call-start = ((), (), s32[]{:S(2)}) async-start(), calls=%async_computation.13 | async-start | bytes 262144
  1322.9 116.6 %reduce-scatter.17.cloned.1.call-start = ((), (), s32[]{:S(2)}) async-start(), calls=%async_computation.11 | async-start | bytes 10485760
  1331.9 236.2 %all-reduce.17.cloned.1.call-start = ((), (), s32[]{:S(2)}) async-start(), calls=%async_computation.12 | async-start | bytes 6291456 | tf_op jit(solution)/shard_map/psum | solution.py:435
  1332.0 22.9 %slice-start = ((s8[8388608]{0:T(1024)(128)(4,1)}), s8[4194304]{0:T(1024)(128)(4,1)S(1)}, s32[]{:S(2)}) async-start(s8[8388608]{0:T(1024)(128)(4,1)} %bitcast.387), calls=%async_computation.15 | async-start | bytes 8388608
  1361.5 20.9 %copy-start.2 = (f32[32,16,16,128]{3,2,1,0:T(8,128)S(1)}, f32[32,16,16,128]{3,2,1,0:T(8,128)}, u32[]{:S(2)}) copy-start(f32[32,16,16,128]{3,2,1,0:T(8,128)} %bitcast_convert_fusion.3) | copy-start | bytes 12582916
  1361.5 20.9 %copy-start.5 = (bf16[8192,128]{1,0:T(8,128)(2,1)S(1)}, bf16[8192,128]{1,0:T(8,128)(2,1)}, u32[]{:S(2)}) copy-start(bf16[8192,128]{1,0:T(8,128)(2,1)} %get-tuple-element.258) | copy-start | bytes 6291460
  1451.7 51.6 %copy-start.126 = (f32[128]{0:T(128)S(1)}, f32[128]{0:T(128)}, u32[]{:S(2)}) copy-start(f32[128]{0:T(128)} %copy-done.125) | copy-start | bytes 1540
  1451.7 51.6 %copy-start.128 = (f32[128]{0:T(128)S(1)}, f32[128]{0:T(128)}, u32[]{:S(2)}) copy-start(f32[128]{0:T(128)} %copy-done.127) | copy-start | bytes 1540
  1451.7 51.6 %copy-start.130 = (f32[128]{0:T(128)S(1)}, f32[128]{0:T(128)}, u32[]{:S(2)}) copy-start(f32[128]{0:T(128)} %copy-done.129) | copy-start | bytes 1540
  1451.7 51.6 %copy-start.132 = (f32[128]{0:T(128)S(1)}, f32[128]{0:T(128)}, u32[]{:S(2)}) copy-start(f32[128]{0:T(128)} %copy-done.131) | copy-start | bytes 1540
  1451.7 51.6 %copy-start.134 = (f32[128]{0:T(128)S(1)}, f32[128]{0:T(128)}, u32[]{:S(2)}) copy-start(f32[128]{0:T(128)} %copy-done.133) | copy-start | bytes 1540
  1451.8 51.6 %copy-start.136 = (f32[128]{0:T(128)S(1)}, f32[128]{0:T(128)}, u32[]{:S(2)}) copy-start(f32[128]{0:T(128)} %copy-done.135) | copy-start | bytes 1540
  1451.8 51.6 %copy-start.138 = (f32[128]{0:T(128)S(1)}, f32[128]{0:T(128)}, u32[]{:S(2)}) copy-start(f32[128]{0:T(128)} %copy-done.137) | copy-start | bytes 1540
  1451.8 51.6 %copy-start.140 = (f32[128]{0:T(128)S(1)}, f32[128]{0:T(128)}, u32[]{:S(2)}) copy-start(f32[128]{0:T(128)} %copy-done.139) | copy-start | bytes 1540
  1451.8 51.6 %copy-start.142 = (f32[128]{0:T(128)S(1)}, f32[128]{0:T(128)}, u32[]{:S(2)}) copy-start(f32[128]{0:T(128)} %copy-done.141) | copy-start | bytes 1540
  1503.4 21.0 %copy-start.7 = (f32[8192,128]{1,0:T(8,128)S(1)}, f32[8192,128]{1,0:T(8,128)}, u32[]{:S(2)}) copy-start(f32[8192,128]{1,0:T(8,128)} %copy-done.6) | copy-start | bytes 12582916
  1524.4 50.8 %copy-start.1 = (bf16[512,512]{1,0:T(8,128)(2,1)S(1)}, bf16[512,512]{1,0:T(8,128)(2,1)}, u32[]{:S(2)}) copy-start(bf16[512,512]{1,0:T(8,128)(2,1)} %param.32) | copy-start | bytes 1572868
  (151 other events, 1353.0 us)
Sparse Core Ops, SparseCore 0:
  30.0 110.8 all-gather.8
  391.9 126.1 reduce-scatter.10
  524.1 108.1 all-gather.10
  633.8 59.4 all-gather.12
  753.8 31.5 all-reduce.20
  787.8 71.7 reduce-scatter.12
  862.3 71.7 reduce-scatter.14
  948.2 59.3 all-gather.14
  1323.0 31.5 all-reduce.18
  1357.2 71.7 reduce-scatter.16
  1436.4 131.7 all-reduce.16
where the time goes:
time: 1590 us; the launch traced here: 1580 us
  waiting for transfers between devices  528 us (33%)
  other arithmetic  523 us (33%)
  matrix products  230 us (14%)
  local copies, waits for them, and re-layouts  221 us (14%)
  blocking collectives  61.6 us (4%)
  between operations  16.8 us (1%)
    add x3, other arithmetic, crop_conv(): accumulated = accumulated + kernel[tap_index] * moved  155 us
    unnamed x16, waiting for transfers between devices  142 us
    reduce_sum x1, other arithmetic, run_block(): jnp.sum(values_gb.astype(jnp.float32), axis=0)  126 us
    reduce_scatter x1, waiting for transfers between devices, run_block(): lax.psum_scatter(proj_part, 'head', scatter_dimension=1, tiled=True)  126 us
    all_gather x1, waiting for transfers between devices, run_block(): lax.all_gather(second, 'head', axis=1, tiled=True)  96.9 us
    reduce_sum x7, other arithmetic, conv_weight_grad(): tap_rows.append(jnp.sum(grad_grid * moved, axis=(0, 1, 2)))  87.2 us
    dot_general x4, matrix products, matmul(): return jnp.dot(left, right, preferred_element_type=jnp.float32)  66.4 us
    all_gather x1, waiting for transfers between devices, run_block(): lax.all_gather(first_sum, 'head', axis=1, tiled=True)  63.4 us
  transfers between devices with their start and end apart: 11, of which 7 were waited for; matrix products, arithmetic and copies ran while one was open for 19% of the time, Pallas kernels for 0%

commit v1 on v0

v1 whole, which is shorter than its diff:
```python
import jax
import jax.numpy as jnp
from jax import lax
from jax.experimental import pallas as pl
from jax.experimental.pallas import tpu as pltpu
from jax.sharding import PartitionSpec as P

D = 512
HEADS = 8
HEAD_DIM = 64
HIDDEN = 2048
SIDE = 16
PLACES = 256
LANES = 128
TILES = 4
REACH = (1, 2, 3, 3)
GAP = 3
GRID_ROWS = SIDE + 3 * GAP + 1
EPSILON = 1e-06
SCALE = HEAD_DIM ** (-0.5)
F32 = jnp.float32
BF16 = jnp.bfloat16


def dot(left, right, dims):
    return lax.dot_general(left, right, (dims, ((), ())), preferred_element_type=F32)


def nn(left, right):
    return dot(left, right, ((1,), (0,)))


def nt(left, right):
    return dot(left, right, ((1,), (1,)))


def tn(left, right):
    return dot(left, right, ((0,), (0,)))


def lane(tile):
    return pl.ds(LANES * tile, LANES)


def fill_masks(cut, col_cuts, mask_ref):
    col = lax.broadcasted_iota(jnp.int32, (SIDE, LANES), 0)
    for band in range(2):
        here = (col >= col_cuts[band]).astype(jnp.int32)
        for step in range(-3, 4):
            if step == 0:
                continue
            there = (col + step >= col_cuts[band]).astype(jnp.int32)
            good = (col + step >= 0) & (col + step < SIDE) & (here == there)
            mask_ref[band, step + 3] = jnp.where(good, 1.0, 0.0).astype(F32)


def place_ids(cut, col_cuts):
    place = lax.broadcasted_iota(jnp.int32, (PLACES, LANES), 0)
    row = lax.shift_right_logical(place, 4)
    col = lax.bitwise_and(place, 15)
    band = (row >= cut).astype(jnp.int32)
    col_cut = jnp.where(band > 0, col_cuts[1], col_cuts[0])
    side = (col >= col_cut).astype(jnp.int32)
    return band, side


def spread(read_row, reach, cut, mask_ref, grid_ref):
    zero = jnp.zeros((GAP * SIDE, LANES), F32)
    for step in range(-reach, reach + 1):
        start = pl.multiple_of(SIDE * (GAP + cut), SIDE)
        grid_ref[step + 3, pl.ds(start, GAP * SIDE), :] = zero
    for row in range(SIDE):
        lower = (row >= cut).astype(jnp.int32)
        start = pl.multiple_of(SIDE * (row + GAP + GAP * lower), SIDE)
        values = read_row(row)
        for step in range(-reach, reach + 1):
            moved = values
            if step != 0:
                moved = pltpu.roll(values, (-step) % SIDE, 0) * mask_ref[lower, step + 3]
            grid_ref[step + 3, pl.ds(start, SIDE), :] = moved


def pair_place(index, cut, upper_pairs, reach):
    lower = (index >= upper_pairs).astype(jnp.int32)
    row = 2 * index + lower * (cut - 2 * upper_pairs)
    base = row + GAP * lower + (GAP - reach)
    return lower, row, base


def conv_tile(reach, cut, grid_ref, taps_ref, tap_reach, tile, out_ref):
    upper_pairs = (cut + 1) // 2
    pairs = upper_pairs + (SIDE - cut + 1) // 2
    width = 2 * tap_reach + 1

    def body(index, carry):
        lower, row, base = pair_place(index, cut, upper_pairs, reach)
        total = [[None, None], [None, None]]
        for step in range(-reach, reach + 1):
            taps = [
                taps_ref[(dr + tap_reach) * width + step + tap_reach, :, lane(tile)]
                for dr in range(-reach, reach + 1)
            ]
            for place in range(2 * reach + 2):
                for half in range(2):
                    start = pl.multiple_of(SIDE * (base + place) + 8 * half, 8)
                    field = grid_ref[step + 3, pl.ds(start, 8), :]
                    for out in range(2):
                        tap = place - out
                        if 0 <= tap <= 2 * reach:
                            term = taps[tap] * field
                            old = total[out][half]
                            total[out][half] = term if old is None else old + term
        for out in range(2):
            for half in range(2):
                start = pl.multiple_of(SIDE * (row + out) + 8 * half, 8)
                out_ref[pl.ds(start, 8), :] = total[out][half]
        return carry

    lax.fori_loop(0, pairs, body, 0)


def conv_back_tile(reach, cut, grid_ref, taps_ref, tap_reach, tile, other_ref, out_ref, sum_ref):
    upper_pairs = (cut + 1) // 2
    pairs = upper_pairs + (SIDE - cut + 1) // 2
    width = 2 * tap_reach + 1

    def body(index, carry):
        lower, row, base = pair_place(index, cut, upper_pairs, reach)
        keep = jnp.where((lower == 0) & (row + 1 >= cut), 0.0, 1.0).astype(F32)
        other = []
        for out in range(2):
            halves = []
            for half in range(2):
                start = pl.multiple_of(SIDE * (row + out) + 8 * half, 8)
                value = other_ref[pl.ds(start, 8), :]
                halves.append(value * keep if out else value)
            other.append(halves)
        total = [[None, None], [None, None]]
        for step in range(-reach, reach + 1):
            sums = [None] * (2 * reach + 1)
            ids = [
                (tap_reach - dr) * width + tap_reach - step for dr in range(-reach, reach + 1)
            ]
            taps = [taps_ref[item, :, lane(tile)] for item in ids]
            for place in range(2 * reach + 2):
                for half in range(2):
                    start = pl.multiple_of(SIDE * (base + place) + 8 * half, 8)
                    field = grid_ref[step + 3, pl.ds(start, 8), :]
                    for out in range(2):
                        tap = place - out
                        if 0 <= tap <= 2 * reach:
                            term = taps[tap] * field
                            old = total[out][half]
                            total[out][half] = term if old is None else old + term
                            part = other[out][half] * field
                            old = sums[tap]
                            sums[tap] = part if old is None else old + part
            for tap in range(2 * reach + 1):
                sum_ref[ids[tap], :, lane(tile)] += sums[tap]
        for out in range(2):
            for half in range(2):
                start = pl.multiple_of(SIDE * (row + out) + 8 * half, 8)
                out_ref[pl.ds(start, 8), :] = total[out][half]
        return carry

    lax.fori_loop(0, pairs, body, 0)


def row_mean(values):
    return jnp.sum(values, axis=1, keepdims=True) * (1.0 / D)


def pick(ids, rows):
    out = rows[0]
    for crop in range(1, 4):
        out = jnp.where(ids >= crop, rows[crop], out)
    return out


def crop_reduce(ids, values, op, empty):
    return [op(jnp.where(ids == crop, values, empty), axis=0, keepdims=True) for crop in range(4)]


def head_block():
    row = lax.broadcasted_iota(jnp.int32, (2 * LANES, 2 * LANES), 0)
    col = lax.broadcasted_iota(jnp.int32, (2 * LANES, 2 * LANES), 1)
    same = lax.bitwise_and(row, HEAD_DIM) == lax.bitwise_and(col, HEAD_DIM)
    return jnp.where(same, 1.0, 0.0).astype(F32)


def both(values, masks):
    return jnp.concatenate([values * masks[0], values * masks[1]], axis=1)


def read_cuts(cuts_ref, base):
    step = pl.program_id(0) + base
    return cuts_ref[step, 0], (cuts_ref[step, 1], cuts_ref[step, 2])


def whole(shape):
    return pl.BlockSpec(shape, lambda *_: (0,) * len(shape))


def once(shape):
    return pl.BlockSpec(shape, lambda *_: (0,) * len(shape), pipeline_mode=pl.Buffered(1))


def rows_spec(width, base=0):
    return pl.BlockSpec((PLACES, width), lambda i, *_: (i + base, 0))


def context_spec(base):
    return pl.BlockSpec((1, TILES, 2 * LANES, 2 * LANES), lambda i, *_: (i + base, 0, 0, 0))


def like(shape, dtype):
    return jax.ShapeDtypeStruct(shape, dtype)


def params(**given):
    return pltpu.CompilerParams(vmem_limit_bytes=58 * 2**20, **given)


def front_kernel(base, kept, *refs):
    (cuts_ref, me_ref, x0_ref, x1_ref, x2_ref, x3_ref, cpe_ref, vec_ref, qkv_ref, crpe_ref) = refs[:10]
    (first_ref, hidden_ref, query_ref, value_ref, soft_ref, context_ref, conv_ref, attended_ref,
     mask_ref, grid_ref, out_ref, x_ref) = refs[10 + kept :]
    cut, col_cuts = read_cuts(cuts_ref, base)
    me = me_ref[0]

    @pl.when(pl.program_id(0) == 0)
    def _():
        grid_ref[...] = jnp.zeros_like(grid_ref)

    for move, piece_ref in enumerate((x0_ref, x1_ref, x2_ref, x3_ref)):
        start = pl.multiple_of(LANES * lax.bitwise_xor(me, move), LANES)
        x_ref[:, pl.ds(start, LANES)] = piece_ref[...].astype(F32)
    fill_masks(cut, col_cuts, mask_ref)
    for tile in range(TILES):
        spread(
            lambda row: x_ref[SIDE * row : SIDE * row + SIDE, lane(tile)],
            1, cut, mask_ref, grid_ref,
        )
        conv_tile(1, cut, grid_ref, cpe_ref, 1, tile, out_ref)
        first_ref[:, lane(tile)] = (
            x_ref[:, lane(tile)] + out_ref[:PLACES, :] + vec_ref[0:1, lane(tile)]
        )
    first = first_ref[...]
    center = row_mean(first)
    square = row_mean(first * first)
    inverse = lax.rsqrt(square - center * center + EPSILON)
    hidden = ((first - center) * inverse * vec_ref[1:2, :] + vec_ref[2:3, :]).astype(BF16)
    hidden_ref[...] = hidden
    band, side = place_ids(cut, col_cuts)
    ids = 2 * band + side
    sides = [(side == item).astype(F32).astype(BF16) for item in range(2)]
    bands = [(band == item).astype(F32).astype(BF16) for item in range(2)]
    blocks = head_block()
    for tile in range(TILES):
        reach = REACH[tile]
        three = nn(hidden, qkv_ref[lax.bitwise_xor(me, tile)])
        query = (three[:, :LANES] + vec_ref[3:4, lane(tile)]).astype(BF16)
        keys = three[:, LANES : 2 * LANES].astype(BF16).astype(F32)
        value = (three[:, 2 * LANES :] + vec_ref[4:5, lane(tile)]).astype(BF16)
        query_ref[:, lane(tile)] = query
        value_ref[:, lane(tile)] = value
        highest = crop_reduce(ids, keys, jnp.max, -1e30)
        powers = jnp.exp(keys - pick(ids, highest))
        totals = crop_reduce(ids, powers, jnp.sum, 0.0)
        soft = (powers * pick(ids, [1.0 / item for item in totals])).astype(BF16)
        soft_ref[:, lane(tile)] = soft
        context = (tn(both(soft, sides), both(value, bands)) * blocks).astype(BF16)
        context_ref[0, tile] = context
        factor = nn(both(query, sides), context)
        factor = jnp.where(band > 0, factor[:, LANES:], factor[:, :LANES])
        spread(
            lambda row: value_ref[SIDE * row : SIDE * row + SIDE, lane(tile)].astype(F32),
            reach, cut, mask_ref, grid_ref,
        )
        conv_tile(reach, cut, grid_ref, crpe_ref, 3, tile, out_ref)
        conv = out_ref[:PLACES, :]
        conv_ref[:, lane(tile)] = conv.astype(BF16)
        attended_ref[:, lane(tile)] = (factor * SCALE + query.astype(F32) * conv).astype(BF16)


def front(cuts, me, x_parts, base, kept, cpe, vec, qkv, crpe):
    count = x_parts[0].shape[0] // PLACES
    total = cuts.shape[0]
    rows = total * PLACES
    wide = rows_spec(D, base)
    flops = 2 * count * PLACES * D * D * 4
    return pl.pallas_call(
        lambda *refs: front_kernel(base, len(kept), *refs),
        grid_spec=pltpu.PrefetchScalarGridSpec(
            num_scalar_prefetch=2,
            grid=(count,),
            in_specs=[rows_spec(LANES)] * 4
            + [whole(cpe.shape), whole(vec.shape), whole(qkv.shape), whole(crpe.shape)]
            + [pl.BlockSpec(memory_space=pl.ANY)] * len(kept),
            out_specs=[wide, wide, wide, wide, wide, context_spec(base), wide, wide],
            scratch_shapes=[
                pltpu.VMEM((2, 7, SIDE, LANES), F32),
                pltpu.VMEM((7, GRID_ROWS * SIDE, LANES), F32),
                pltpu.VMEM((PLACES + SIDE, LANES), F32),
                pltpu.VMEM((PLACES, D), F32),
            ],
        ),
        out_shape=[
            like((rows, D), F32), like((rows, D), BF16), like((rows, D), BF16),
            like((rows, D), BF16), like((rows, D), BF16),
            like((total, TILES, 2 * LANES, 2 * LANES), BF16),
            like((rows, D), BF16), like((rows, D), BF16),
        ],
        input_output_aliases={10 + item: item for item in range(len(kept))},
        compiler_params=params(),
        cost_estimate=pl.CostEstimate(flops=flops * 6, bytes_accessed=count * 10**7, transcendentals=0),
        name="front",
    )(cuts, me, *x_parts, cpe, vec, qkv, crpe, *kept)


def gelu_both(pre):
    power = jnp.exp(pre * pre * -0.5)
    t = 1.0 / (1.0 + jnp.abs(pre) * (0.3275911 * 0.7071067811865476))
    poly = 0.5 * 1.061405429
    for item in (-1.453152027, 1.421413741, -0.284496736, 0.254829592):
        poly = poly * t + 0.5 * item
    tail = poly * t * power
    cdf = jnp.where(pre >= 0.0, 1.0 - tail, tail)
    return pre * cdf, cdf + pre * power * 0.3989422804014327


CHUNK = 256
BLOCK = 512


def middle_kernel(
    me_ref, attended_ref, first_ref, cot0_ref, cot1_ref, cot2_ref, cot3_ref, vec_ref, bias_ref,
    proj_ref, fc1_ref, fc2_ref,
    out0_ref, out1_ref, out2_ref, out3_ref, second_grad_ref, att_grad_ref, fc1_grad_ref,
    fc2_grad_ref, proj_grad_ref, sum_ref, bias_grad_ref,
    cot_ref, hat_ref, inverse_ref, hidden_ref, total_ref, back_ref, active_ref, pre_grad_ref,
):
    me = me_ref[0]
    step = pl.program_id(0)
    rows = attended_ref.shape[0]
    blocks = rows // BLOCK

    def part(index):
        return pl.ds(pl.multiple_of(BLOCK * index, BLOCK), BLOCK)

    @pl.when(step == 0)
    def _():
        sum_ref[...] = jnp.zeros_like(sum_ref)
        for move, piece_ref in enumerate((cot0_ref, cot1_ref, cot2_ref, cot3_ref)):
            start = pl.multiple_of(LANES * lax.bitwise_xor(me, move), LANES)
            cot_ref[:, pl.ds(start, LANES)] = piece_ref[...]

        def enter(index, carry):
            now = part(index)
            second = first_ref[now, :] + vec_ref[0:1, :]
            for tile in range(TILES):
                second += nn(attended_ref[now, lane(tile)], proj_ref[lax.bitwise_xor(me, tile)])
            center = row_mean(second)
            square = row_mean(second * second)
            inverse = lax.rsqrt(square - center * center + EPSILON)
            hat = (second - center) * inverse
            hidden_ref[now, :] = (hat * vec_ref[1:2, :] + vec_ref[2:3, :]).astype(BF16)
            hat_ref[now, :] = hat
            inverse_ref[now, :] = jnp.broadcast_to(inverse, (BLOCK, LANES))
            total_ref[now, :] = second + vec_ref[3:4, :]
            back_ref[now, :] = jnp.zeros((BLOCK, D), F32)
            sum_ref[0:1, :] += jnp.sum(cot_ref[now, :].astype(F32), axis=0, keepdims=True)
            return carry

        lax.fori_loop(0, blocks, enter, 0)

    bias_grad_ref[0] = jnp.zeros((1, CHUNK), F32)

    def chunk(index, carry):
        now = part(index)
        pre = nn(hidden_ref[now, :], fc1_ref[0]) + bias_ref[0]
        active, slope = gelu_both(pre)
        active = active.astype(BF16)
        active_ref[now, :] = active
        total_ref[now, :] += nn(active, fc2_ref[0])
        pre_grad_f = nt(cot_ref[now, :], fc2_ref[0]) * slope
        pre_grad = pre_grad_f.astype(BF16)
        pre_grad_ref[now, :] = pre_grad
        back_ref[now, :] += nt(pre_grad, fc1_ref[0])
        bias_grad_ref[0] += jnp.sum(pre_grad_f, axis=0, keepdims=True)
        return carry

    lax.fori_loop(0, blocks, chunk, 0)
    fc2_grad_ref[0] = tn(active_ref[...], cot_ref[...]).astype(fc2_grad_ref.dtype)
    fc1_grad_ref[0] = tn(hidden_ref[...], pre_grad_ref[...]).astype(fc1_grad_ref.dtype)

    @pl.when(step == pl.num_programs(0) - 1)
    def _():
        def leave(index, carry):
            now = part(index)
            for move, piece_ref in enumerate((out0_ref, out1_ref, out2_ref, out3_ref)):
                start = pl.multiple_of(LANES * lax.bitwise_xor(me, move), LANES)
                piece_ref[now, :] = total_ref[now, pl.ds(start, LANES)].astype(BF16)
            hat = hat_ref[now, :]
            norm_grad = back_ref[now, :]
            weighted = norm_grad * vec_ref[1:2, :]
            second_grad = cot_ref[now, :].astype(F32) + inverse_ref[now, 0:1] * (
                weighted - row_mean(weighted) - hat * row_mean(weighted * hat)
            )
            second_grad_ref[now, :] = second_grad
            low = second_grad.astype(BF16)
            hidden_ref[now, :] = low
            for tile in range(TILES):
                att_grad_ref[now, lane(tile)] = nt(low, proj_ref[lax.bitwise_xor(me, tile)]).astype(BF16)
            sum_ref[1:2, :] += jnp.sum(norm_grad * hat, axis=0, keepdims=True)
            sum_ref[2:3, :] += jnp.sum(norm_grad, axis=0, keepdims=True)
            sum_ref[3:4, :] += jnp.sum(low.astype(F32), axis=0, keepdims=True)
            return carry

        lax.fori_loop(0, blocks, leave, 0)
        for tile in range(TILES):
            proj_grad_ref[lax.bitwise_xor(me, tile)] = tn(
                attended_ref[:, lane(tile)], hidden_ref[...]
            ).astype(proj_grad_ref.dtype)


def middle(me, attended, first, cot_parts, vec, bias, proj, fc1, fc2):
    rows = attended.shape[0]
    split = fc1.shape[2] // CHUNK
    steps = 4 * split
    left = pl.BlockSpec((1, D, CHUNK), lambda i, *_: (i // split, 0, i % split))
    right = pl.BlockSpec((1, CHUNK, D), lambda i, *_: (i // split, i % split, 0))
    piece = once((rows, LANES))
    wide = once((rows, D))
    line = pl.BlockSpec((1, 1, CHUNK), lambda i, *_: (i // split, 0, i % split))
    return pl.pallas_call(
        middle_kernel,
        grid_spec=pltpu.PrefetchScalarGridSpec(
            num_scalar_prefetch=1,
            grid=(steps,),
            in_specs=[
                wide, wide, piece, piece, piece, piece, whole(vec.shape), line, once(proj.shape),
                left, right,
            ],
            out_specs=[
                piece, piece, piece, piece, wide, wide, left, right, once(proj.shape),
                whole((8, D)), line,
            ],
            scratch_shapes=[
                pltpu.VMEM((rows, D), BF16), pltpu.VMEM((rows, D), F32),
                pltpu.VMEM((rows, LANES), F32),
                pltpu.VMEM((rows, D), BF16), pltpu.VMEM((rows, D), F32),
                pltpu.VMEM((rows, D), F32), pltpu.VMEM((rows, CHUNK), BF16),
                pltpu.VMEM((rows, CHUNK), BF16),
            ],
        ),
        out_shape=[like((rows, LANES), BF16)] * 4 + [
            like((rows, D), F32), like((rows, D), BF16),
            like(fc1.shape, BF16), like(fc2.shape, BF16), like(proj.shape, BF16),
            like((8, D), F32), like(bias.shape, F32),
        ],
        compiler_params=params(),
        cost_estimate=pl.CostEstimate(flops=rows * D * D * 60, bytes_accessed=3 * 10**7, transcendentals=0),
        name="middle",
    )(me, attended, first, *cot_parts, vec, bias, proj, fc1, fc2)


def back_kernel(
    base,
    cuts_ref, me_ref, x0_ref, x1_ref, x2_ref, x3_ref,
    grad_ref, query_ref, value_ref, soft_ref, context_ref, conv_ref,
    first_ref, hidden_ref, second_grad_ref, vec_ref, qkv_ref, crpe_ref, cpe_ref,
    out0_ref, out1_ref, out2_ref, out3_ref, qkv_grad_ref, crpe_sum_ref, cpe_sum_ref, sum_ref,
    mask_ref, grid_ref, out_ref, other_ref, three_ref, first_grad_ref, norm_grad_ref,
):
    cut, col_cuts = read_cuts(cuts_ref, base)
    me = me_ref[0]

    @pl.when(pl.program_id(0) == 0)
    def _():
        grid_ref[...] = jnp.zeros_like(grid_ref)
        other_ref[...] = jnp.zeros_like(other_ref)
        qkv_grad_ref[...] = jnp.zeros_like(qkv_grad_ref)
        crpe_sum_ref[...] = jnp.zeros_like(crpe_sum_ref)
        cpe_sum_ref[...] = jnp.zeros_like(cpe_sum_ref)
        sum_ref[...] = jnp.zeros_like(sum_ref)

    fill_masks(cut, col_cuts, mask_ref)
    band, side = place_ids(cut, col_cuts)
    ids = 2 * band + side
    sides = [(side == item).astype(F32).astype(BF16) for item in range(2)]
    bands = [(band == item).astype(F32).astype(BF16) for item in range(2)]
    blocks = head_block() * SCALE
    hidden = hidden_ref[...]
    for tile in range(TILES):
        reach = REACH[tile]
        shard = lax.bitwise_xor(me, tile)
        grad = grad_ref[:, lane(tile)]
        query = query_ref[:, lane(tile)]
        value = value_ref[:, lane(tile)]
        soft = soft_ref[:, lane(tile)]
        context = context_ref[0, tile]
        grad_f = grad.astype(F32)
        grad_bands = both(grad, bands)
        context_grad = (tn(both(query, sides), grad_bands) * blocks).astype(BF16)
        part = nt(grad_bands, context)
        part = jnp.where(side > 0, part[:, LANES:], part[:, :LANES])
        query_grad = (
            part * SCALE + grad_f * conv_ref[:, lane(tile)].astype(F32)
        ).astype(BF16)
        soft_grad = nt(both(value, bands), context_grad)
        soft_grad = jnp.where(side > 0, soft_grad[:, LANES:], soft_grad[:, :LANES])
        soft_f = soft.astype(F32)
        inner = crop_reduce(ids, soft_f * soft_grad, jnp.sum, 0.0)
        keys_grad = (soft_f * (soft_grad - pick(ids, inner))).astype(BF16)
        value_part = nn(both(soft, sides), context_grad)
        value_part = jnp.where(band > 0, value_part[:, LANES:], value_part[:, :LANES])

        def read_row(row):
            part = pl.ds(SIDE * row, SIDE)
            return grad_ref[part, lane(tile)].astype(F32) * query_ref[part, lane(tile)].astype(F32)

        spread(read_row, reach, cut, mask_ref, grid_ref)
        other_ref[:PLACES, :] = value.astype(F32)
        conv_back_tile(reach, cut, grid_ref, crpe_ref, 3, tile, other_ref, out_ref, crpe_sum_ref)
        value_grad = (value_part + out_ref[:PLACES, :]).astype(BF16)
        three_ref[:, :LANES] = query_grad
        three_ref[:, LANES : 2 * LANES] = keys_grad
        three_ref[:, 2 * LANES :] = value_grad
        sum_ref[0:1, lane(tile)] += jnp.sum(query_grad.astype(F32), axis=0, keepdims=True)
        sum_ref[1:2, lane(tile)] += jnp.sum(value_grad.astype(F32), axis=0, keepdims=True)
        three = three_ref[...]
        qkv_grad_ref[shard] += tn(hidden, three)
        back = nt(three, qkv_ref[shard])
        if tile:
            norm_grad_ref[...] += back
        else:
            norm_grad_ref[...] = back
    norm_grad = norm_grad_ref[...]
    first = first_ref[...]
    center = row_mean(first)
    square = row_mean(first * first)
    inverse = lax.rsqrt(square - center * center + EPSILON)
    hat = (first - center) * inverse
    weighted = norm_grad * vec_ref[1:2, :]
    first_grad = second_grad_ref[...] + inverse * (
        weighted - row_mean(weighted) - hat * row_mean(weighted * hat)
    )
    first_grad_ref[...] = first_grad
    sum_ref[2:3, :] += jnp.sum(norm_grad * hat, axis=0, keepdims=True)
    sum_ref[3:4, :] += jnp.sum(norm_grad, axis=0, keepdims=True)
    sum_ref[4:5, :] += jnp.sum(first_grad, axis=0, keepdims=True)
    for move, piece_ref in enumerate((x0_ref, x1_ref, x2_ref, x3_ref)):
        start = pl.multiple_of(LANES * lax.bitwise_xor(me, move), LANES)
        norm_grad_ref[:, pl.ds(start, LANES)] = piece_ref[...].astype(F32)
    for tile in range(TILES):
        spread(
            lambda row: first_grad_ref[SIDE * row : SIDE * row + SIDE, lane(tile)],
            1, cut, mask_ref, grid_ref,
        )
        other_ref[:PLACES, :] = norm_grad_ref[:, lane(tile)]
        conv_back_tile(1, cut, grid_ref, cpe_ref, 1, tile, other_ref, out_ref, cpe_sum_ref)
        first_grad_ref[:, lane(tile)] += out_ref[:PLACES, :]
    for move, piece_ref in enumerate((out0_ref, out1_ref, out2_ref, out3_ref)):
        start = pl.multiple_of(LANES * lax.bitwise_xor(me, move), LANES)
        piece_ref[...] = first_grad_ref[:, pl.ds(start, LANES)].astype(BF16)


def back(cuts, me, x_parts, base, grad, query, value, soft, context, conv, first, hidden,
         second_grad, vec, qkv, crpe, cpe):
    rows = x_parts[0].shape[0]
    count = rows // PLACES
    wide = rows_spec(D, base)
    piece = rows_spec(LANES)
    return pl.pallas_call(
        lambda *refs: back_kernel(base, *refs),
        grid_spec=pltpu.PrefetchScalarGridSpec(
            num_scalar_prefetch=2,
            grid=(count,),
            in_specs=[piece] * 4 + [
                wide, wide, wide, wide, context_spec(base), wide, wide, wide, wide,
                whole(vec.shape), whole(qkv.shape), whole(crpe.shape), whole(cpe.shape),
            ],
            out_specs=[piece] * 4 + [
                whole(qkv.shape), whole((49, 8, D)), whole((9, 8, D)), whole((8, D)),
            ],
            scratch_shapes=[
                pltpu.VMEM((2, 7, SIDE, LANES), F32),
                pltpu.VMEM((7, GRID_ROWS * SIDE, LANES), F32),
                pltpu.VMEM((PLACES + SIDE, LANES), F32),
                pltpu.VMEM((PLACES + SIDE, LANES), F32),
                pltpu.VMEM((PLACES, 3 * LANES), BF16),
                pltpu.VMEM((PLACES, D), F32),
                pltpu.VMEM((PLACES, D), F32),
            ],
        ),
        out_shape=[like((rows, LANES), BF16)] * 4 + [
            like(qkv.shape, F32), like((49, 8, D), F32), like((9, 8, D), F32), like((8, D), F32),
        ],
        compiler_params=params(),
        cost_estimate=pl.CostEstimate(
            flops=rows * D * D * 64, bytes_accessed=count * 10**7, transcendentals=0
        ),
        name="back",
    )(cuts, me, *x_parts, grad, query, value, soft, context, conv, first, hidden, second_grad,
      vec, qkv, crpe, cpe)


def collect_kernel(me_ref, *refs):
    out_ref = refs[-1]
    for item, piece_ref in enumerate(refs[:-1]):

        @pl.when(pl.program_id(0) == item)
        def _():
            out_ref[...] = piece_ref[...].astype(F32)


def collect(me, pieces):
    parts = len(pieces[0])
    rows = pieces[0][0].shape[0]
    return pl.pallas_call(
        collect_kernel,
        grid_spec=pltpu.PrefetchScalarGridSpec(
            num_scalar_prefetch=1,
            grid=(4 * parts,),
            in_specs=[once((rows, LANES))] * (4 * parts),
            out_specs=pl.BlockSpec(
                (rows, LANES),
                lambda i, me: (lax.bitwise_xor(me[0], i // parts) * parts + i % parts, 0),
            ),
        ),
        out_shape=like((4 * parts * rows, LANES), F32),
        compiler_params=params(),
        name="collect",
    )(me, *[piece for move in pieces for piece in move])


HALVES = 2


def find_cuts(crop_ids):
    cut = jnp.sum((crop_ids[:, :, 0] < 2).astype(jnp.int32), axis=1)
    upper = jnp.sum((crop_ids[:, 0, :] == 0).astype(jnp.int32), axis=1)
    lower = jnp.sum((crop_ids[:, SIDE - 1, :] == 2).astype(jnp.int32), axis=1)
    return jnp.stack([cut, upper, lower], axis=1)


def reach_mask():
    head = jnp.arange(D, dtype=jnp.int32) // HEAD_DIM
    reach = 1 + (head >= 2).astype(jnp.int32) + (head >= 5).astype(jnp.int32)
    taps = jnp.arange(49, dtype=jnp.int32)
    ring = jnp.maximum(jnp.abs(taps // 7 - 3), jnp.abs(taps % 7 - 3))
    return (ring[:, None] <= reach[None, :]).astype(F32)


def forward_parts(me, cuts, x_halves, small, qkv):
    zero = jnp.zeros((D,), F32)
    vec = jnp.stack([small[58], small[59], small[60], small[61], small[62], zero, zero, zero])
    crpe = jnp.broadcast_to((small[9:58] * reach_mask())[:, None, :], (49, 8, D))
    cpe = jnp.broadcast_to(small[:9][:, None, :], (9, 8, D))
    kept = ()
    base = 0
    for x_parts in x_halves:
        kept = front(cuts, me, x_parts, base, kept, cpe, vec, qkv, crpe)
        base += x_parts[0].shape[0] // PLACES
    return kept, vec, crpe, cpe


def middle_parts(me, kept, cot_parts, small, bias, proj, fc1, fc2):
    zero = jnp.zeros((D,), F32)
    vec = jnp.stack([small[63], small[64], small[65], small[66], zero, zero, zero, zero])
    return middle(me, kept[7], kept[0], cot_parts, vec, bias, proj, fc1, fc2)


def body(
    block_in, crop_ids, cotangent, cpe_kernel, cpe_bias, norm1_gain, norm1_shift, qkv_weight,
    qv_bias, crpe_kernel, proj_weight, proj_bias, norm2_gain, norm2_shift, fc1_weight, fc1_bias,
    fc2_weight, fc2_bias,
):
    head = lax.axis_index("head")
    me = head.reshape(1).astype(jnp.int32)
    canvases = crop_ids.shape[0] // 4
    rows = canvases * PLACES
    cuts = find_cuts(lax.dynamic_slice_in_dim(crop_ids, head * canvases, canvases, 0))

    def swap(values, move):
        return lax.ppermute(values, "head", [(item, item ^ move) for item in range(4)])

    def take(values, move, part, parts):
        size = rows // parts
        start = lax.bitwise_xor(head, move) * rows + part * size
        return lax.dynamic_slice_in_dim(values, start, size, 0)

    def bring(values, part, parts):
        pieces = [take(values, move, part, parts) for move in range(4)]
        return [pieces[0]] + [swap(pieces[move], move) for move in (1, 2, 3)]

    def gather(shard):
        far = swap(shard, 2)
        near = swap(jnp.stack([shard, far]), 1)
        return jnp.stack([shard, near[0], far, near[1]])

    packed = jnp.concatenate([
        cpe_kernel, crpe_kernel, cpe_bias[None], norm1_gain[None], norm1_shift[None], qv_bias,
        proj_bias[None], norm2_gain[None], norm2_shift[None], fc2_bias[None],
    ]).astype(F32)
    small = lax.all_gather(packed, "head", axis=1, tiled=True)
    x_halves = [bring(block_in, 0, HALVES)]
    qkv = gather(qkv_weight.reshape(D, 3 * LANES))
    x_halves += [bring(block_in, part, HALVES) for part in range(1, HALVES)]
    proj = gather(proj_weight)
    cot_parts = bring(cotangent, 0, 1)
    fc1 = gather(fc1_weight)
    fc2 = gather(fc2_weight)
    bias = gather(fc1_bias.astype(F32).reshape(1, -1))

    kept, vec, crpe, cpe = forward_parts(me, cuts, x_halves, small, qkv)
    first, hidden, query, value, soft, context, conv, attended = kept
    results = middle_parts(me, kept, cot_parts, small, bias, proj, fc1, fc2)
    second_grad, att_grad, fc1_grad, fc2_grad, proj_grad, sums2, bias_grad = results[4:]
    out_parts = [[results[move] if move == 0 else swap(results[move], move)] for move in range(4)]

    def reduce_head(grads):
        near = swap(jnp.stack([grads[1], grads[3]]).astype(BF16), 1).astype(F32)
        far = swap((grads[2].astype(F32) + near[1]).astype(BF16), 2).astype(F32)
        return grads[0].astype(F32) + near[0] + far

    early = jnp.concatenate(
        [fc1_grad, fc2_grad, proj_grad], axis=1
    )
    early = lax.psum(reduce_head(early).astype(BF16), "dp")

    grad_parts = [[] for _ in range(4)]
    sums = []
    base = 0
    for x_parts in x_halves:
        back_results = back(
            cuts, me, x_parts, base, att_grad, query, value, soft, context, conv, first, hidden,
            second_grad, vec, qkv, crpe, cpe,
        )
        for move in range(4):
            piece = back_results[move]
            grad_parts[move].append(piece if move == 0 else swap(piece, move))
        sums.append(back_results[4:])
        base += x_parts[0].shape[0] // PLACES
    qkv_grad, crpe_sum, cpe_sum, sums1 = [sum(items[1:], items[0]) for items in zip(*sums)]
    small_grad = jnp.concatenate([
        jnp.sum(cpe_sum, axis=1), jnp.sum(crpe_sum, axis=1) * reach_mask(), sums1[4:5], sums1[2:4],
        sums1[0:2], sums2[3:4], sums2[1:3], sums2[0:1],
    ]).reshape(-1, 4, LANES).transpose(1, 0, 2)
    order = lax.bitwise_xor(head, jnp.arange(4, dtype=jnp.int32))
    small_grad = jnp.take(small_grad, order, axis=0)
    late = jnp.concatenate([
        qkv_grad.reshape(4, D * 3, LANES), small_grad, bias_grad.reshape(4, 4, LANES),
        jnp.zeros((4, 1, LANES), F32),
    ], axis=1)
    late = lax.psum(reduce_head(late), "dp")
    small_g = late[D * 3 : D * 3 + 67]
    early = early.astype(F32)
    return (
        collect(me, out_parts), collect(me, grad_parts),
        small_g[:9], small_g[58], small_g[59], small_g[60],
        late[: D * 3].reshape(D, 3, LANES), small_g[61:63], small_g[9:58],
        early[2 * D :], small_g[63], small_g[64], small_g[65],
        early[:D], late[D * 3 + 67 : D * 3 + 71].reshape(D), early[D : 2 * D], small_g[66],
    )


def solution(mesh):
    return jax.shard_map(
        body,
        mesh=mesh,
        in_specs=(
            P("dp", "head"), P("dp", None, None), P("dp", "head"), P(None, "head"), P("head"),
            P("head"), P("head"), P(None, None, "head"), P(None, "head"), P(None, "head"),
            P("head", None), P("head"), P("head"), P("head"), P(None, "head"), P("head"),
            P("head", None), P("head"),
        ),
        out_specs=(
            P("dp", "head"), P("dp", "head"), P(None, "head"), P("head"), P("head"), P("head"),
            P(None, None, "head"), P(None, "head"), P(None, "head"), P("head", None), P("head"),
            P("head"), P("head"), P(None, "head"), P("head"), P("head", None), P("head"),
        ),
        check_vma=False,
    )
```

time: 1590 us -> 540 us (0.34)
  other arithmetic: 523 us -> 38.2 us
  waiting for transfers between devices: 528 us -> 178 us
  matrix products: 230 us -> 0 us
  Pallas kernels: 0 us -> 225 us
  local copies, waits for them, and re-layouts: 221 us -> 39.1 us
  blocking collectives: 61.6 us -> 20.7 us
  starting transfers between devices: 0.45 us -> 22.5 us
    reduce_sum x14 -> x4, other arithmetic: 273 us -> 4.17 us  [the longest x1 1.46 us: body(): jnp.sum(crpe_sum, axis=1) * reach_mask()]
    dot_general x29 -> x0, matrix products: 230 us -> none  [the longest x4 66.4 us: matmul(): return jnp.dot(left, right, preferred_element_type=jnp.float32)]
    pallas_call x0 -> x7, Pallas kernels: none -> 225 us  [the longest x2 80.4 us: back(): pl.pallas_call(lambda *refs: back_kernel(base, *refs), grid_spec=pltpu.Pr...]
    all_gather x4 -> x0, waiting for transfers between devices: 220 us -> none  [the longest x1 96.9 us: run_block(): lax.all_gather(second, 'head', axis=1, tiled=True)]
    add x7 -> x4, other arithmetic: 165 us -> 4.93 us  [the longest x2 3.88 us: body(): sum(items[1:], items[0])]
    unnamed x16 -> x2, waiting for transfers between devices: 142 us -> 0.03 us
    reduce_scatter x1 -> x0, waiting for transfers between devices: 126 us -> none  [run_block(): lax.psum_scatter(proj_part, 'head', scatter_dimension=1, tiled=True)]
    ppermute x0 -> x32, waiting for transfers between devices: none -> 83.8 us  [swap(): lax.ppermute(values, 'head', [(item, item ^ move) for item in range(4)])]
  transfers between devices with their start and end apart: 11 -> 34, of which waited for: 7 -> 11; matrix products, arithmetic and copies ran while one was open for 19% -> 10% of each run, Pallas kernels for 0% -> 29%
where the time goes in v1:
time: 540 us; the launch traced here: 539 us
  Pallas kernels  225 us (42%)
  waiting for transfers between devices  178 us (33%)
  local copies, waits for them, and re-layouts  39.1 us (7%)
  other arithmetic  38.2 us (7%)
  starting transfers between devices  22.5 us (4%)
  blocking collectives  20.7 us (4%)
  between operations  14.9 us (3%)
    ppermute x32, waiting for transfers between devices, swap(): lax.ppermute(values, 'head', [(item, item ^ move) for item in range(4)])  83.8 us
    pallas_call x2, Pallas kernels, back(): pl.pallas_call(lambda *refs: back_kernel(base, *refs), grid_spec=pltpu.Pr...  80.4 us
    psum x1, waiting for transfers between devices, body(): early = lax.psum(reduce_head(early).astype(BF16), 'dp')  77.6 us
    pallas_call x1, Pallas kernels, middle(): pl.pallas_call(middle_kernel, grid_spec=pltpu.PrefetchScalarGridSpec(num_...  69.6 us
    pallas_call x2, Pallas kernels, front(): pl.pallas_call(lambda *refs: front_kernel(base, len(kept), *refs), grid_s...  65.9 us
    ppermute x32, starting transfers between devices, swap(): lax.ppermute(values, 'head', [(item, item ^ move) for item in range(4)])  22.5 us
    all_gather x1, blocking collectives, body(): small = lax.all_gather(packed, 'head', axis=1, tiled=True)  20.7 us
    psum x1, waiting for transfers between devices, body(): late = lax.psum(reduce_head(late), 'dp')  16.9 us
  transfers between devices with their start and end apart: 34, of which 11 were waited for; matrix products, arithmetic and copies ran while one was open for 10% of the time, Pallas kernels for 29%

profile of v1, /device:TPU:0, one launch (start us, length us, event | category | flops | bytes accessed | tf_op | source)
XLA Modules:
  0.0 538.6 jit_solution(8608934917152304596)
XLA Ops:
  7.4 3.0 constant_dynamic-slice_fusion.4
  11.1 0.9 copy.53
  12.0 2.5 collective-permute-start.3
  15.1 2.0 collective-permute-start.15
  17.2 0.9 fusion.9
  18.2 0.8 convert_reduce_fusion.1
  19.5 20.7 %all_gather.3 = f32[67,512]{1,0:T(8,128)S(1)} all-gather(f32[67,128]{1,0:T(8,128)S(1)} %convert_element_type.82), channel_id=1, replica_groups=mesh['dp'=8,'head'=4] {'head'}, dimensions={1}, use_global_device_ids=true | all-gather | bytes 171520 | tf_op jit(solution)/shard_map/all_gather | solution.py:707
  40.4 1.4 constant_dynamic-slice_fusion
  45.1 1.7 collective-permute-start.17
  47.7 1.0 pad_maximum_fusion.9
  49.2 1.1 pad_maximum_fusion.7
  50.5 1.3 pad_maximum_fusion.10.bias_ref
  52.1 1.8 pad_maximum_fusion.8.proj_ref
  53.9 1.5 collective-permute-start.7
  55.4 1.2 pad_maximum_fusion.4
  56.6 3.5 collective-permute-done.17
  60.2 1.8 collective-permute-start.1
  62.1 2.4 pad_maximum_fusion.3.refs_8_.refs_16_
  64.7 1.0 collective-permute-done.6.refs_4_
  66.3 4.4 collective-permute-done.7.refs_5_
  71.2 1.0 broadcast_in_dim.58.refs_9_.refs_17_
  72.8 33.0 %front.2 = (f32[2048,512]{1,0:T(8,128)}, bf16[2048,512]{1,0:T(8,128)(2,1)}, bf16[2048,512]{1,0:T(8,128)(2,1)}, bf16[2048,512]{1,0:T(8,128)(2,1)}, bf16[2048,512]...) custom-call(s32[8,3]{1,0:T(8,128)} %pad_add_fusion.refs_0_, ...), custom_call_target="tpu_custom_call" | custom-call | flops 12884901888 | bytes 40000000 | tf_op jit(solution)/shard_map/front/pallas_call | solution.py:292
  105.8 1.4 collective-permute-start.9
  108.0 32.9 %front.3 = (f32[2048,512]{1,0:T(8,128)}, bf16[2048,512]{1,0:T(8,128)(2,1)}, bf16[2048,512]{1,0:T(8,128)(2,1)}, bf16[2048,512]{1,0:T(8,128)(2,1)}, bf16[2048,512]...) custom-call(s32[8,3]{1,0:T(8,128)} %pad_add_fusion.refs_0_, ...), custom_call_target="tpu_custom_call", output_to_operand_aliasing={{0}: (10, {}), {1}: (11, {}), {2}: (12, {}), {3}: (13, {}),... | custom-call | flops 12884901888 | bytes 40000000 | tf_op jit(solution)/shard_map/front/pallas_call | solution.py:292
  141.0 1.3 fusion.25
  142.2 2.6 pad_maximum_fusion.1.fc1_ref
  144.8 1.3 fusion.24
  146.1 1.6 pad_maximum_fusion.2.fc2_ref
  147.8 69.6 %middle.1 = (bf16[2048,128]{1,0:T(8,128)(2,1)}, bf16[2048,128]{1,0:T(8,128)(2,1)}, bf16[2048,128]{1,0:T(8,128)(2,1)}, bf16[2048,128]{1,0:T(8,128)(2,1)}, f32[204...) custom-call(s32[1]{0:T(128)} %bitcast.refs_1_.me_ref, ...), custom_call_target="tpu_custom_call" | custom-call | flops 32212254720 | bytes 30000000 | tf_op jit(solution)/shard_map/middle/pallas_call | solution.py:436
  218.9 1.9 constant_dynamic-update-slice_fusion.2
  221.2 0.9 copy-done.12
  222.3 2.0 copy-done.1
  224.3 1.6 pad_maximum_fusion
  226.0 40.1 %back.3 = (bf16[1024,128]{1,0:T(8,128)(2,1)}, bf16[1024,128]{1,0:T(8,128)(2,1)}, bf16[1024,128]{1,0:T(8,128)(2,1)}, bf16[1024,128]{1,0:T(8,128)(2,1)}, f32[4,512...) custom-call(s32[8,3]{1,0:T(8,128)} %pad_add_fusion.refs_0_, ...), custom_call_target="tpu_custom_call" | custom-call | flops 17179869184 | bytes 40000000 | tf_op jit(solution)/shard_map/back/pallas_call | solution.py:575
  266.1 40.3 %back.2 = (bf16[1024,128]{1,0:T(8,128)(2,1)}, bf16[1024,128]{1,0:T(8,128)(2,1)}, bf16[1024,128]{1,0:T(8,128)(2,1)}, bf16[1024,128]{1,0:T(8,128)(2,1)}, f32[4,512...) custom-call(s32[8,3]{1,0:T(8,128)} %pad_add_fusion.refs_0_, ...), custom_call_target="tpu_custom_call" | custom-call | flops 17179869184 | bytes 40000000 | tf_op jit(solution)/shard_map/back/pallas_call | solution.py:575
  307.2 1.5 add_reduce_fusion
  308.6 1.0 add_reduce_fusion.1
  310.0 3.2 add.180
  313.2 1.8 reshape.142
  315.8 6.1 %concatenate.14 = f32[4,1608,128]{2,1,0:T(8,128)S(1)} concatenate(f32[4,1536,128]{2,1,0:T(8,128)} %reshape.142, f32[4,67,128]{2,1,0:T(8,128)S(1)} %broadcast_select_fusion, f32[4,4,128]{2,1,0:T(4,128)S(1)} %bitcast.69, f32[4,1,128]{2,1,0:T(1,128)S(1)} %broadcast_in_dim.61), dimensions={1} | concatenate | bytes 6586368 | tf_op jit(solution)/shard_map/concatenate | solution.py:753
  322.3 2.3 collective-permute-done.28
  324.7 2.3 convert_element_type.91
  327.1 3.6 fusion.4
  331.5 1.4 collective-permute-start.29
  333.0 34.8 %collective-permute-done.29 = bf16[1608,128]{1,0:T(8,128)(2,1)S(1)} collective-permute-done((bf16[1608,128]{1,0:T(8,128)(2,1)S(1)}, bf16[1608,128]{1,0:T(8,128)(2,1)S(1)}, u32[]{:S(2)}, u32[]{:S(2)}) %collective-permute-start.29) | collective-permute-done | bytes 411680 | tf_op jit(solution)/shard_map/ppermute | solution.py:687
  367.8 1.0 fusion.7
  369.0 0.9 collective-permute-start.25
  370.0 3.8 fusion.3
  373.8 1.0 collective-permute-start.27
  375.4 1.0 collective-permute-start.20
  376.4 1.8 collective-permute-done.25.refs_5_
  378.2 4.7 collective-permute-done.27.refs_7_
  383.0 0.9 collective-permute-start.24
  383.8 1.6 collective-permute-start.26
  385.5 26.4 %collective-permute-done.24.refs_4_ = bf16[1024,128]{1,0:T(8,128)(2,1)S(1)} collective-permute-done((bf16[1024,128]{1,0:T(8,128)(2,1)S(1)}, bf16[1024,128]{1,0:T(8,128)(2,1)S(1)}, u32[]{:S(2)}, u32[]{:S(2)}) %collective-permute-start.24) | collective-permute-done | bytes 262176 | tf_op jit(solution)/shard_map/ppermute | solution.py:687
  411.9 4.8 collective-permute-done.26.refs_6_
  417.4 5.1 collect.3
  423.6 4.0 collect.2
  427.6 16.9 %all-reduce.4.cloned.1.call-done = f32[1608,128]{1,0:T(8,128)} async-done(((f32[1608,128]{1,0:T(8,128)}), f32[1608,128]{1,0:T(8,128)}) %all-reduce.4.cloned.1.call-update) | async-done | bytes 823312 | tf_op jit(solution)/shard_map/psum | solution.py:757
  444.4 1.1 slice-done
  445.9 0.9 copy.57
  449.7 77.6 %all-reduce.6.cloned.1.call-done = bf16[1152,512]{1,0:T(8,128)(2,1)} async-done(((bf16[1152,512]{1,0:T(8,128)(2,1)}), bf16[1152,512]{1,0:T(8,128)(2,1)}) %all-reduce.6.cloned.1.call-update) | async-done | bytes 1179664 | tf_op jit(solution)/shard_map/psum | solution.py:731
  527.3 2.8 fusion.23
  530.1 1.6 slice.260
  (208 shorter events, 21.2 us)
Async XLA Ops:
  7.2 437.2 %all-reduce.4.cloned.1.call-start = ((), (), s32[]{:S(2)}) async-start(), calls=%async_computation | async-start | bytes 1646592 | tf_op jit(solution)/shard_map/psum | solution.py:757
  7.3 7.2 %copy-start.32 = (bf16[512]{0:T(512)(128)(2,1)S(1)}, bf16[512]{0:T(512)(128)(2,1)}, u32[]{:S(2)}) copy-start(bf16[512]{0:T(512)(128)(2,1)} %param.33) | copy-start | bytes 3076
  7.3 7.8 %copy-start.5 = (bf16[512,512]{1,0:T(8,128)(2,1)S(1)}, bf16[512,512]{1,0:T(8,128)(2,1)}, u32[]{:S(2)}) copy-start(bf16[512,512]{1,0:T(8,128)(2,1)} %param.32) | copy-start | bytes 1572868
  7.3 11.9 %copy-start.27 = (bf16[49,128]{1,0:T(8,128)(2,1)S(1)}, bf16[49,128]{1,0:T(8,128)(2,1)}, u32[]{:S(2)}) copy-start(bf16[49,128]{1,0:T(8,128)(2,1)} %param.27) | copy-start | bytes 37636
  7.3 11.9 %copy-start.29 = (bf16[9,128]{1,0:T(8,128)(2,1)S(1)}, bf16[9,128]{1,0:T(8,128)(2,1)}, u32[]{:S(2)}) copy-start(bf16[9,128]{1,0:T(8,128)(2,1)} %param.21) | copy-start | bytes 6916
  7.3 11.9 %copy-start.33 = (bf16[128]{0:T(256)(128)(2,1)S(1)}, bf16[128]{0:T(256)(128)(2,1)}, u32[]{:S(2)}) copy-start(bf16[128]{0:T(256)(128)(2,1)} %param.22) | copy-start | bytes 772
  7.3 11.9 %copy-start.34 = (bf16[128]{0:T(256)(128)(2,1)S(1)}, bf16[128]{0:T(256)(128)(2,1)}, u32[]{:S(2)}) copy-start(bf16[128]{0:T(256)(128)(2,1)} %param.23) | copy-start | bytes 772
  7.3 11.9 %copy-start.35 = (bf16[128]{0:T(256)(128)(2,1)S(1)}, bf16[128]{0:T(256)(128)(2,1)}, u32[]{:S(2)}) copy-start(bf16[128]{0:T(256)(128)(2,1)} %param.24) | copy-start | bytes 772
  7.4 11.9 %copy-start.36 = (bf16[2,128]{1,0:T(2,128)(2,1)S(1)}, bf16[2,128]{1,0:T(2,128)(2,1)}, u32[]{:S(2)}) copy-start(bf16[2,128]{1,0:T(2,128)(2,1)} %param.26) | copy-start | bytes 1540
  7.4 11.9 %copy-start.37 = (bf16[128]{0:T(256)(128)(2,1)S(1)}, bf16[128]{0:T(256)(128)(2,1)}, u32[]{:S(2)}) copy-start(bf16[128]{0:T(256)(128)(2,1)} %param.29) | copy-start | bytes 772
  7.4 11.9 %copy-start.38 = (bf16[128]{0:T(256)(128)(2,1)S(1)}, bf16[128]{0:T(256)(128)(2,1)}, u32[]{:S(2)}) copy-start(bf16[128]{0:T(256)(128)(2,1)} %param.30) | copy-start | bytes 772
  7.4 11.9 %copy-start.39 = (bf16[128]{0:T(256)(128)(2,1)S(1)}, bf16[128]{0:T(256)(128)(2,1)}, u32[]{:S(2)}) copy-start(bf16[128]{0:T(256)(128)(2,1)} %param.31) | copy-start | bytes 772
  7.4 11.9 %copy-start.40 = (bf16[128]{0:T(256)(128)(2,1)S(1)}, bf16[128]{0:T(256)(128)(2,1)}, u32[]{:S(2)}) copy-start(bf16[128]{0:T(256)(128)(2,1)} %param.35) | copy-start | bytes 772
  7.4 32.9 %copy-start.4 = (bf16[8192,128]{1,0:T(8,128)(2,1)S(1)}, bf16[8192,128]{1,0:T(8,128)(2,1)}, u32[]{:S(2)}) copy-start(bf16[8192,128]{1,0:T(8,128)(2,1)} %param.20) | copy-start | bytes 6291460
  10.4 54.1 %collective-permute-start.5 = (bf16[1024,128]{1,0:T(8,128)(2,1)}, bf16[1024,128]{1,0:T(8,128)(2,1)}, u32[]{:S(2)}, u32[]{:S(2)}) collective-permute-start(bf16[1024,128]{1,0:T(8,128)(2,1)} %get-tuple-element.129), channel_id=1, source_target_pairs={{0,1},{1,0},{2,3},{3,2},{4,5},{5,4},{6,7},{7,6},{8,9},{9,8},{10,11... | collective-permute-start | bytes 786440 | tf_op jit(solution)/shard_map/ppermute | solution.py:687
  12.0 36.7 %collective-permute-start.3 = (bf16[512,384]{1,0:T(8,128)(2,1)}, bf16[512,384]{1,0:T(8,128)(2,1)}, u32[]{:S(2)}, u32[]{:S(2)}) collective-permute-start(bf16[512,384]{1,0:T(8,128)(2,1)} %copy.53), channel_id=1, source_target_pairs={{0,2},{1,3},{2,0},{3,1},{4,6},{5,7},{6,4},{7,5},{8,10},{9,11},{10,... | collective-permute-start | bytes 1179656 | tf_op jit(solution)/shard_map/ppermute | solution.py:687
  15.1 30.1 %collective-permute-start.11 = (f32[1,512]{1,0:T(1,128)}, f32[1,512]{1,0:T(1,128)}, u32[]{:S(2)}, u32[]{:S(2)}) collective-permute-start(f32[1,512]{1,0:T(1,128)} %bitcast.15), channel_id=1, source_target_pairs={{0,2},{1,3},{2,0},{3,1},{4,6},{5,7},{6,4},{7,5},{8,10},{9,11},{10,... | collective-permute-start | bytes 6152 | tf_op jit(solution)/shard_map/ppermute | solution.py:687
  15.1 38.9 %collective-permute-start.15 = (bf16[512,512]{1,0:T(8,128)(2,1)S(1)}, bf16[512,512]{1,0:T(8,128)(2,1)}, u32[]{:S(2)}, u32[]{:S(2)}) collective-permute-start(bf16[512,512]{1,0:T(8,128)(2,1)S(1)} %copy-done.5), channel_id=1, source_target_pairs={{0,2},{1,3},{2,0},{3,1},{4,6},{5,7},{6,4},{7,5},{8,10},{9,11},{10,... | collective-permute-start | bytes 1572872 | tf_op jit(solution)/shard_map/ppermute | solution.py:687
  17.1 30.5 %collective-permute-start.13 = (bf16[128,512]{1,0:T(8,128)(2,1)}, bf16[128,512]{1,0:T(8,128)(2,1)}, u32[]{:S(2)}, u32[]{:S(2)}) collective-permute-start(bf16[128,512]{1,0:T(8,128)(2,1)} %param.28), channel_id=1, source_target_pairs={{0,2},{1,3},{2,0},{3,1},{4,6},{5,7},{6,4},{7,5},{8,10},{9,11},{10,... | collective-permute-start | bytes 393224 | tf_op jit(solution)/shard_map/ppermute | solution.py:687
  17.2 25.2 %copy-start.24 = (s32[512]{0:T(512)}, s32[512]{0:T(512)S(1)}, u32[]{:S(2)}) copy-start(s32[512]{0:T(512)S(1)} %convert_add_fusion) | copy-start | bytes 6148
  17.2 25.2 %copy-start.30 = (s32[49]{0:T(128)}, s32[49]{0:T(128)S(1)}, u32[]{:S(2)}) copy-start(s32[49]{0:T(128)S(1)} %fusion.17) | copy-start | bytes 592
  45.1 15.0 %collective-permute-start.17 = (bf16[512,512]{1,0:T(8,128)(2,1)}, bf16[512,512]{1,0:T(8,128)(2,1)S(1)}, u32[]{:S(2)}, u32[]{:S(2)}) collective-permute-start(bf16[512,512]{1,0:T(8,128)(2,1)} %param.34), channel_id=1, source_target_pairs={{0,2},{1,3},{2,0},{3,1},{4,6},{5,7},{6,4},{7,5},{8,10},{9,11},{10,... | collective-permute-start | bytes 1572872 | tf_op jit(solution)/shard_map/ppermute | solution.py:687
  47.6 2.7 collective-permute-start.12
  48.7 3.1 collective-permute-start.14
  50.3 9.8 %copy-start.6 = (bf16[512,512]{1,0:T(8,128)(2,1)S(1)}, bf16[512,512]{1,0:T(8,128)(2,1)}, u32[]{:S(2)}) copy-start(bf16[512,512]{1,0:T(8,128)(2,1)} %param.34) | copy-start | bytes 1572868
  50.3 9.9 %collective-permute-start.4 = (bf16[2,512,384]{2,1,0:T(8,128)(2,1)S(1)}, bf16[2,512,384]{2,1,0:T(8,128)(2,1)S(1)}, u32[]{:S(2)}, u32[]{:S(2)}) collective-permute-start(bf16[2,512,384]{2,1,0:T(8,128)(2,1)S(1)} %pad_maximum_fusion.7), channel_id=1, source_target_pairs={{0,1},{1,0},{2,3},{3,2},{4,5},{5,4},{6,7},{7,6},{8,9},{9,8},{10,11... | collective-permute-start | bytes 2359304 | tf_op jit(solution)/shard_map/ppermute | solution.py:687
  51.8 13.9 %collective-permute-start.6 = (bf16[1024,128]{1,0:T(8,128)(2,1)}, bf16[1024,128]{1,0:T(8,128)(2,1)S(1)}, u32[]{:S(2)}, u32[]{:S(2)}) collective-permute-start(bf16[1024,128]{1,0:T(8,128)(2,1)} %get-tuple-element.135), channel_id=1, source_target_pairs={{0,2},{1,3},{2,0},{3,1},{4,6},{5,7},{6,4},{7,5},{8,10},{9,11},{10,... | collective-permute-start | bytes 786440 | tf_op jit(solution)/shard_map/ppermute | solution.py:687
  53.9 16.7 %collective-permute-start.7 = (bf16[1024,128]{1,0:T(8,128)(2,1)}, bf16[1024,128]{1,0:T(8,128)(2,1)S(1)}, u32[]{:S(2)}, u32[]{:S(2)}) collective-permute-start(bf16[1024,128]{1,0:T(8,128)(2,1)} %get-tuple-element.128), channel_id=1, source_target_pairs={{0,3},{1,2},{2,1},{3,0},{4,7},{5,6},{6,5},{7,4},{8,11},{9,10},{10,... | collective-permute-start | bytes 786440 | tf_op jit(solution)/shard_map/ppermute | solution.py:687
  60.1 45.7 %collective-permute-start = (bf16[1024,128]{1,0:T(8,128)(2,1)}, bf16[1024,128]{1,0:T(8,128)(2,1)}, u32[]{:S(2)}, u32[]{:S(2)}) collective-permute-start(bf16[1024,128]{1,0:T(8,128)(2,1)} %get-tuple-element.133), channel_id=1, source_target_pairs={{0,1},{1,0},{2,3},{3,2},{4,5},{5,4},{6,7},{7,6},{8,9},{9,8},{10,11... | collective-permute-start | bytes 786440 | tf_op jit(solution)/shard_map/ppermute | solution.py:687
  60.2 47.0 %collective-permute-start.1 = (bf16[1024,128]{1,0:T(8,128)(2,1)S(1)}, bf16[1024,128]{1,0:T(8,128)(2,1)}, u32[]{:S(2)}, u32[]{:S(2)}) collective-permute-start(bf16[1024,128]{1,0:T(8,128)(2,1)S(1)} %copy-done.16), channel_id=1, source_target_pairs={{0,2},{1,3},{2,0},{3,1},{4,6},{5,7},{6,4},{7,5},{8,10},{9,11},{10,... | collective-permute-start | bytes 786440 | tf_op jit(solution)/shard_map/ppermute | solution.py:687
  62.1 10.0 %slice-start.1 = ((f32[67,512]{1,0:T(8,128)}), f32[9,512]{1,0:T(8,128)S(1)}, s32[]{:S(2)}) async-start(f32[67,512]{1,0:T(8,128)} %copy-done.8), calls=%async_computation.3 | async-start | bytes 65536 | tf_op jit(solution)/shard_map/slice | solution.py:660
  64.5 42.8 %collective-permute-start.2 = (bf16[1024,128]{1,0:T(8,128)(2,1)S(1)}, bf16[1024,128]{1,0:T(8,128)(2,1)S(1)}, u32[]{:S(2)}, u32[]{:S(2)}) collective-permute-start(bf16[1024,128]{1,0:T(8,128)(2,1)S(1)} %copy-done.15), channel_id=1, source_target_pairs={{0,3},{1,2},{2,1},{3,0},{4,7},{5,6},{6,5},{7,4},{8,11},{9,10},{10,... | collective-permute-start | bytes 786440 | tf_op jit(solution)/shard_map/ppermute | solution.py:687
  65.7 6.4 %copy-start.45 = (bf16[1024,128]{1,0:T(8,128)(2,1)}, bf16[1024,128]{1,0:T(8,128)(2,1)S(1)}, u32[]{:S(2)}) copy-start(bf16[1024,128]{1,0:T(8,128)(2,1)S(1)} %collective-permute-done.6.refs_4_) | copy-start | bytes 786436
  65.7 82.0 %collective-permute-start.10 = (bf16[2048,128]{1,0:T(8,128)(2,1)}, bf16[2048,128]{1,0:T(8,128)(2,1)}, u32[]{:S(2)}, u32[]{:S(2)}) collective-permute-start(bf16[2048,128]{1,0:T(8,128)(2,1)} %get-tuple-element.124), channel_id=1, source_target_pairs={{0,3},{1,2},{2,1},{3,0},{4,7},{5,6},{6,5},{7,4},{8,11},{9,10},{10,... | collective-permute-start | bytes 1572872 | tf_op jit(solution)/shard_map/ppermute | solution.py:687
  70.7 77.1 %collective-permute-start.8 = (bf16[2048,128]{1,0:T(8,128)(2,1)}, bf16[2048,128]{1,0:T(8,128)(2,1)}, u32[]{:S(2)}, u32[]{:S(2)}) collective-permute-start(bf16[2048,128]{1,0:T(8,128)(2,1)} %get-tuple-element.125), channel_id=1, source_target_pairs={{0,1},{1,0},{2,3},{3,2},{4,5},{5,4},{6,7},{7,6},{8,9},{9,8},{10,11... | collective-permute-start | bytes 1572872 | tf_op jit(solution)/shard_map/ppermute | solution.py:687
  72.8 33.0 %copy-start.13 = (bf16[2048,128]{1,0:T(8,128)(2,1)S(1)}, bf16[2048,128]{1,0:T(8,128)(2,1)}, u32[]{:S(2)}) copy-start(bf16[2048,128]{1,0:T(8,128)(2,1)} %get-tuple-element.127) | copy-start | bytes 1572868
  105.8 41.9 %collective-permute-start.9 = (bf16[2048,128]{1,0:T(8,128)(2,1)S(1)}, bf16[2048,128]{1,0:T(8,128)(2,1)}, u32[]{:S(2)}, u32[]{:S(2)}) collective-permute-start(bf16[2048,128]{1,0:T(8,128)(2,1)S(1)} %copy-done.13), channel_id=1, source_target_pairs={{0,2},{1,3},{2,0},{3,1},{4,6},{5,7},{6,4},{7,5},{8,10},{9,11},{10,... | collective-permute-start | bytes 1572872 | tf_op jit(solution)/shard_map/ppermute | solution.py:687
  107.3 33.7 %collective-permute-start.16 = (bf16[2,512,512]{2,1,0:T(8,128)(2,1)S(1)}, bf16[2,512,512]{2,1,0:T(8,128)(2,1)}, u32[]{:S(2)}, u32[]{:S(2)}) collective-permute-start(bf16[2,512,512]{2,1,0:T(8,128)(2,1)S(1)} %pad_maximum_fusion.4), channel_id=1, source_target_pairs={{0,1},{1,0},{2,3},{3,2},{4,5},{5,4},{6,7},{7,6},{8,9},{9,8},{10,11... | collective-permute-start | bytes 3145736 | tf_op jit(solution)/shard_map/ppermute | solution.py:687
  107.3 37.5 %collective-permute-start.18 = (bf16[2,512,512]{2,1,0:T(8,128)(2,1)S(1)}, bf16[2,512,512]{2,1,0:T(8,128)(2,1)}, u32[]{:S(2)}, u32[]{:S(2)}) collective-permute-start(bf16[2,512,512]{2,1,0:T(8,128)(2,1)S(1)} %pad_maximum_fusion.5), channel_id=1, source_target_pairs={{0,1},{1,0},{2,3},{3,2},{4,5},{5,4},{6,7},{7,6},{8,9},{9,8},{10,11... | collective-permute-start | bytes 3145736 | tf_op jit(solution)/shard_map/ppermute | solution.py:687
  226.0 98.8 %collective-permute-start.30 = (bf16[2,1152,512]{2,1,0:T(8,128)(2,1)}, bf16[2,1152,512]{2,1,0:T(8,128)(2,1)}, u32[]{:S(2)}, u32[]{:S(2)}) collective-permute-start(bf16[2,1152,512]{2,1,0:T(8,128)(2,1)} %pad_maximum_fusion), channel_id=1, source_target_pairs={{0,1},{1,0},{2,3},{3,2},{4,5},{5,4},{6,7},{7,6},{8,9},{9,8},{10,11... | collective-permute-start | bytes 7077896 | tf_op jit(solution)/shard_map/ppermute | solution.py:687
  266.1 40.4 %copy-start.26 = (f32[8,512]{1,0:T(8,128)S(1)}, f32[8,512]{1,0:T(8,128)}, u32[]{:S(2)}) copy-start(f32[8,512]{1,0:T(8,128)} %get-tuple-element.97) | copy-start | bytes 49156
  266.1 41.1 %copy-start.7 = (f32[49,8,512]{2,1,0:T(8,128)S(1)}, f32[49,8,512]{2,1,0:T(8,128)}, u32[]{:S(2)}) copy-start(f32[49,8,512]{2,1,0:T(8,128)} %get-tuple-element.95) | copy-start | bytes 2408452
  266.1 42.6 %copy-start.23 = (f32[9,8,512]{2,1,0:T(8,128)S(1)}, f32[9,8,512]{2,1,0:T(8,128)}, u32[]{:S(2)}) copy-start(f32[9,8,512]{2,1,0:T(8,128)} %get-tuple-element.93) | copy-start | bytes 442372
  322.2 2.4 collective-permute-start.28
  330.7 39.2 %collective-permute-start.31 = (bf16[1152,512]{1,0:T(8,128)(2,1)}, bf16[1152,512]{1,0:T(8,128)(2,1)}, u32[]{:S(2)}, u32[]{:S(2)}) collective-permute-start(bf16[1152,512]{1,0:T(8,128)(2,1)} %fusion.4), channel_id=1, source_target_pairs={{0,2},{1,3},{2,0},{3,1},{4,6},{5,7},{6,4},{7,5},{8,10},{9,11},{10,... | collective-permute-start | bytes 3538952 | tf_op jit(solution)/shard_map/ppermute | solution.py:687
  331.5 37.4 %copy-start.51 = (bf16[1024,128]{1,0:T(8,128)(2,1)S(1)}, bf16[1024,128]{1,0:T(8,128)(2,1)}, u32[]{:S(2)}) copy-start(bf16[1024,128]{1,0:T(8,128)(2,1)} %get-tuple-element.87) | copy-start | bytes 786436
  331.5 36.2 %collective-permute-start.29 = (bf16[1608,128]{1,0:T(8,128)(2,1)S(1)}, bf16[1608,128]{1,0:T(8,128)(2,1)S(1)}, u32[]{:S(2)}, u32[]{:S(2)}) collective-permute-start(bf16[1608,128]{1,0:T(8,128)(2,1)S(1)} %fusion.8), channel_id=1, source_target_pairs={{0,2},{1,3},{2,0},{3,1},{4,6},{5,7},{6,4},{7,5},{8,10},{9,11},{10,... | collective-permute-start | bytes 1234952 | tf_op jit(solution)/shard_map/ppermute | solution.py:687
  368.8 158.5 %all-reduce.6.cloned.1.call-start = ((), (), s32[]{:S(2)}) async-start(), calls=%async_computation.1 | async-start | bytes 2359296 | tf_op jit(solution)/shard_map/psum | solution.py:731
  368.9 6.5 %collective-permute-start.23 = (bf16[1024,128]{1,0:T(8,128)(2,1)}, bf16[1024,128]{1,0:T(8,128)(2,1)S(1)}, u32[]{:S(2)}, u32[]{:S(2)}) collective-permute-start(bf16[1024,128]{1,0:T(8,128)(2,1)} %get-tuple-element.85), channel_id=1, source_target_pairs={{0,1},{1,0},{2,3},{3,2},{4,5},{5,4},{6,7},{7,6},{8,9},{9,8},{10,11... | collective-permute-start | bytes 786440 | tf_op jit(solution)/shard_map/ppermute | solution.py:687
  369.0 9.2 %copy-start.42 = (bf16[2048,128]{1,0:T(8,128)(2,1)S(1)}, bf16[2048,128]{1,0:T(8,128)(2,1)}, u32[]{:S(2)}) copy-start(bf16[2048,128]{1,0:T(8,128)(2,1)} %get-tuple-element.73) | copy-start | bytes 1572868
  369.0 14.0 %copy-start.48 = (bf16[1024,128]{1,0:T(8,128)(2,1)S(1)}, bf16[1024,128]{1,0:T(8,128)(2,1)}, u32[]{:S(2)}) copy-start(bf16[1024,128]{1,0:T(8,128)(2,1)} %get-tuple-element.86) | copy-start | bytes 786436
  369.0 14.8 %copy-start.47 = (bf16[1024,128]{1,0:T(8,128)(2,1)S(1)}, bf16[1024,128]{1,0:T(8,128)(2,1)}, u32[]{:S(2)}) copy-start(bf16[1024,128]{1,0:T(8,128)(2,1)} %get-tuple-element.88) | copy-start | bytes 786436
  369.0 9.2 %collective-permute-start.25 = (bf16[1024,128]{1,0:T(8,128)(2,1)S(1)}, bf16[1024,128]{1,0:T(8,128)(2,1)S(1)}, u32[]{:S(2)}, u32[]{:S(2)}) collective-permute-start(bf16[1024,128]{1,0:T(8,128)(2,1)S(1)} %copy-done.51), channel_id=1, source_target_pairs={{0,2},{1,3},{2,0},{3,1},{4,6},{5,7},{6,4},{7,5},{8,10},{9,11},{10,... | collective-permute-start | bytes 786440 | tf_op jit(solution)/shard_map/ppermute | solution.py:687
  373.8 9.1 %collective-permute-start.27 = (bf16[1024,128]{1,0:T(8,128)(2,1)S(1)}, bf16[1024,128]{1,0:T(8,128)(2,1)S(1)}, u32[]{:S(2)}, u32[]{:S(2)}) collective-permute-start(bf16[1024,128]{1,0:T(8,128)(2,1)S(1)} %copy-done.49), channel_id=1, source_target_pairs={{0,3},{1,2},{2,1},{3,0},{4,7},{5,6},{6,5},{7,4},{8,11},{9,10},{10,... | collective-permute-start | bytes 786440 | tf_op jit(solution)/shard_map/ppermute | solution.py:687
  374.9 9.0 %collective-permute-start.22 = (bf16[1024,128]{1,0:T(8,128)(2,1)S(1)}, bf16[1024,128]{1,0:T(8,128)(2,1)S(1)}, u32[]{:S(2)}, u32[]{:S(2)}) collective-permute-start(bf16[1024,128]{1,0:T(8,128)(2,1)S(1)} %copy-done.50), channel_id=1, source_target_pairs={{0,1},{1,0},{2,3},{3,2},{4,5},{5,4},{6,7},{7,6},{8,9},{9,8},{10,11... | collective-permute-start | bytes 786440 | tf_op jit(solution)/shard_map/ppermute | solution.py:687
  375.2 47.2 %collective-permute-start.19 = (bf16[2048,128]{1,0:T(8,128)(2,1)S(1)}, bf16[2048,128]{1,0:T(8,128)(2,1)S(1)}, u32[]{:S(2)}, u32[]{:S(2)}) collective-permute-start(bf16[2048,128]{1,0:T(8,128)(2,1)S(1)} %copy-done.44), channel_id=1, source_target_pairs={{0,1},{1,0},{2,3},{3,2},{4,5},{5,4},{6,7},{7,6},{8,9},{9,8},{10,11... | collective-permute-start | bytes 1572872 | tf_op jit(solution)/shard_map/ppermute | solution.py:687
  375.4 41.3 %copy-start.17 = (bf16[1024,128]{1,0:T(8,128)(2,1)}, bf16[1024,128]{1,0:T(8,128)(2,1)S(1)}, u32[]{:S(2)}) copy-start(bf16[1024,128]{1,0:T(8,128)(2,1)S(1)} %collective-permute-done.23.refs_3_) | copy-start | bytes 786436
  375.4 47.1 %collective-permute-start.20 = (bf16[2048,128]{1,0:T(8,128)(2,1)S(1)}, bf16[2048,128]{1,0:T(8,128)(2,1)S(1)}, u32[]{:S(2)}, u32[]{:S(2)}) collective-permute-start(bf16[2048,128]{1,0:T(8,128)(2,1)S(1)} %copy-done.43), channel_id=1, source_target_pairs={{0,2},{1,3},{2,0},{3,1},{4,6},{5,7},{6,4},{7,5},{8,10},{9,11},{10,... | collective-permute-start | bytes 1572872 | tf_op jit(solution)/shard_map/ppermute | solution.py:687
  378.2 38.5 %copy-start.18 = (bf16[1024,128]{1,0:T(8,128)(2,1)}, bf16[1024,128]{1,0:T(8,128)(2,1)S(1)}, u32[]{:S(2)}) copy-start(bf16[1024,128]{1,0:T(8,128)(2,1)S(1)} %collective-permute-done.25.refs_5_) | copy-start | bytes 786436
  378.2 44.3 %collective-permute-start.21 = (bf16[2048,128]{1,0:T(8,128)(2,1)S(1)}, bf16[2048,128]{1,0:T(8,128)(2,1)S(1)}, u32[]{:S(2)}, u32[]{:S(2)}) collective-permute-start(bf16[2048,128]{1,0:T(8,128)(2,1)S(1)} %copy-done.42), channel_id=1, source_target_pairs={{0,3},{1,2},{2,1},{3,0},{4,7},{5,6},{6,5},{7,4},{8,11},{9,10},{10,... | collective-permute-start | bytes 1572872 | tf_op jit(solution)/shard_map/ppermute | solution.py:687
  383.0 33.7 %copy-start.19 = (bf16[1024,128]{1,0:T(8,128)(2,1)}, bf16[1024,128]{1,0:T(8,128)(2,1)S(1)}, u32[]{:S(2)}) copy-start(bf16[1024,128]{1,0:T(8,128)(2,1)S(1)} %collective-permute-done.27.refs_7_) | copy-start | bytes 786436
  383.0 28.9 %collective-permute-start.24 = (bf16[1024,128]{1,0:T(8,128)(2,1)S(1)}, bf16[1024,128]{1,0:T(8,128)(2,1)S(1)}, u32[]{:S(2)}, u32[]{:S(2)}) collective-permute-start(bf16[1024,128]{1,0:T(8,128)(2,1)S(1)} %copy-done.48), channel_id=1, source_target_pairs={{0,2},{1,3},{2,0},{3,1},{4,6},{5,7},{6,4},{7,5},{8,10},{9,11},{10,... | collective-permute-start | bytes 786440 | tf_op jit(solution)/shard_map/ppermute | solution.py:687
  383.8 32.8 %copy-start.20 = (bf16[1024,128]{1,0:T(8,128)(2,1)}, bf16[1024,128]{1,0:T(8,128)(2,1)S(1)}, u32[]{:S(2)}) copy-start(bf16[1024,128]{1,0:T(8,128)(2,1)S(1)} %collective-permute-done.22.refs_2_) | copy-start | bytes 786436
  383.8 32.8 %collective-permute-start.26 = (bf16[1024,128]{1,0:T(8,128)(2,1)S(1)}, bf16[1024,128]{1,0:T(8,128)(2,1)S(1)}, u32[]{:S(2)}, u32[]{:S(2)}) collective-permute-start(bf16[1024,128]{1,0:T(8,128)(2,1)S(1)} %copy-done.47), channel_id=1, source_target_pairs={{0,3},{1,2},{2,1},{3,0},{4,7},{5,6},{6,5},{7,4},{8,11},{9,10},{10,... | collective-permute-start | bytes 786440 | tf_op jit(solution)/shard_map/ppermute | solution.py:687
  (25 other events, 73.7 us)
Sparse Core Ops, SparseCore 0:
  368.9 75.4 all-reduce.3
  447.9 79.3 all-reduce.5

commit v2 on v1

--- a/solution.py
+++ b/solution.py
@@ -635,6 +635,268 @@
     )(me, *[piece for move in pieces for piece in move])
 
 
+MESH = pl.DeviceIdType.MESH
+PIECE_ROWS = 128
+
+
+def peer(move):
+    return (lax.axis_index("dp"), lax.bitwise_xor(lax.axis_index("head"), move))
+
+
+def meet(peers):
+    barrier = pltpu.get_barrier_semaphore()
+    for item in peers:
+        pl.semaphore_signal(barrier, inc=1, device_id=item, device_id_type=MESH)
+    pl.semaphore_wait(barrier, len(peers))
+
+
+def remote(source, target, send, receive, device):
+    return pltpu.make_async_remote_copy(
+        src_ref=source, dst_ref=target, send_sem=send, recv_sem=receive,
+        device_id=device, device_id_type=MESH,
+    )
+
+
+def entry_kernel(
+    rows, size, x_ref, qkv_ref, small_ref,
+    x1_ref, x2_ref, x3_ref, all_qkv_ref, all_small_ref,
+    send, receive, local,
+):
+    head = lax.axis_index("head")
+    meet([peer(move) for move in (1, 2, 3)])
+    copies = []
+    far = remote(qkv_ref, all_qkv_ref.at[2], send.at[0], receive.at[0], peer(2))
+    far.start()
+    near = remote(qkv_ref, all_qkv_ref.at[1], send.at[1], receive.at[1], peer(1))
+    near.start()
+    for move in (1, 2, 3):
+        copies.append(
+            remote(small_ref, all_small_ref.at[move], send.at[1 + move], receive.at[1 + move], peer(move))
+        )
+        copies[-1].start()
+    for move, target in ((2, x2_ref), (3, x3_ref), (1, x1_ref)):
+        start = pl.multiple_of(lax.bitwise_xor(head, move) * rows, PLACES)
+        copies.append(
+            remote(x_ref.at[pl.ds(start, size)], target, send.at[4 + move], receive.at[4 + move], peer(move))
+        )
+        copies[-1].start()
+    mine = pltpu.make_async_copy(qkv_ref, all_qkv_ref.at[0], local.at[0])
+    mine.start()
+    mine_small = pltpu.make_async_copy(small_ref, all_small_ref.at[0], local.at[1])
+    mine_small.start()
+    far.wait_recv()
+    relay = remote(all_qkv_ref.at[2], all_qkv_ref.at[3], send.at[8], receive.at[8], peer(1))
+    relay.start()
+    far.wait_send()
+    near.wait()
+    for copy in copies:
+        copy.wait()
+    relay.wait()
+    mine.wait()
+    mine_small.wait()
+
+
+def entry(block_in, size, qkv, small):
+    rows = block_in.shape[0] // 4
+    hbm = pl.BlockSpec(memory_space=pl.ANY)
+    return pl.pallas_call(
+        lambda *refs: entry_kernel(rows, size, *refs),
+        in_specs=[hbm] * 3,
+        out_specs=[hbm] * 5,
+        out_shape=[like((size, LANES), BF16)] * 3 + [
+            like((4,) + qkv.shape, BF16), like((4,) + small.shape, F32),
+        ],
+        scratch_shapes=[
+            pltpu.SemaphoreType.DMA((9,)), pltpu.SemaphoreType.DMA((9,)),
+            pltpu.SemaphoreType.DMA((2,)),
+        ],
+        compiler_params=params(collective_id=1, has_side_effects=True),
+        name="entry",
+    )(block_in, qkv, small)
+
+
+def plan_pieces(shapes, count):
+    pieces = []
+    for item, (rows, lanes) in enumerate(shapes):
+        height = min(PIECE_ROWS, rows)
+        unit = 16 * count
+        padded = -(-height // unit) * unit
+        for start in range(0, rows, height):
+            pieces.append((item, start, height, padded, lanes))
+    return pieces
+
+
+def sum_steps(pieces, count, grad_refs, out_refs, near_refs, far_refs, own_refs, mid_refs, part_refs, send, receive):
+    group = count // 2
+    dp = lax.axis_index("dp")
+    head = lax.axis_index("head")
+    low, high = lax.rem(dp, 2), dp // 2
+    made = {}
+
+    def sems(piece, slot):
+        return send.at[piece, slot], receive.at[piece, slot]
+
+    def copy(key, source, target, slot, device):
+        made[key] = remote(source, target, *sems(key[0], slot), device)
+        made[key].start()
+
+    def widths(piece):
+        item, start, height, padded, lanes = pieces[piece]
+        return grad_refs[item], pl.ds(start, height), height, padded, padded // 2, padded // count
+
+    def to_core(piece):
+        grad, span, *_ = widths(piece)
+        copy((piece, "n1"), grad.at[1, span], near_refs[piece].at[0], 0, peer(1))
+        copy((piece, "n3"), grad.at[3, span], near_refs[piece].at[1], 1, peer(1))
+
+    def to_far(piece):
+        grad, span, height, *_ = widths(piece)
+        made[piece, "n3"].wait_recv()
+        own_refs[piece][:height, :] = (
+            grad[2, span, :].astype(F32) + near_refs[piece][1].astype(F32)
+        ).astype(BF16)
+        copy((piece, "far"), own_refs[piece].at[:height], far_refs[piece], 2, peer(2))
+
+    def to_low(piece):
+        grad, span, height, padded, half, _ = widths(piece)
+        made[piece, "n1"].wait()
+        made[piece, "n3"].wait_send()
+        made[piece, "far"].wait()
+        own_refs[piece][:height, :] = (
+            grad[0, span, :].astype(F32) + near_refs[piece][0].astype(F32)
+            + far_refs[piece][...].astype(F32)
+        ).astype(BF16)
+        if padded > height:
+            own_refs[piece][height:, :] = jnp.zeros((padded - height, own_refs[piece].shape[1]), BF16)
+        away = pl.multiple_of((1 - low) * half, half)
+        copy(
+            (piece, "low"), own_refs[piece].at[pl.ds(away, half)], mid_refs[piece].at[1], 3,
+            (dp + 1 - 2 * low, head),
+        )
+
+    def to_high(piece):
+        _, _, _, _, half, part = widths(piece)
+        made[piece, "low"].wait()
+        here = pl.multiple_of(low * half, half)
+        mid_refs[piece][0] = (
+            own_refs[piece][pl.ds(here, half), :].astype(F32) + mid_refs[piece][1].astype(F32)
+        ).astype(BF16)
+        for step in range(1, group):
+            other = lax.rem(high + step, group)
+            start = pl.multiple_of(other * part, part)
+            copy(
+                (piece, "high", step), mid_refs[piece].at[0, pl.ds(start, part)],
+                part_refs[piece].at[step - 1], 3 + step, (other * 2 + low, head),
+            )
+
+    def share_high(piece):
+        _, _, _, _, half, part = widths(piece)
+        mine = pl.multiple_of(high * part, part)
+        total = mid_refs[piece][0, pl.ds(mine, part), :].astype(F32)
+        for step in range(1, group):
+            made[piece, "high", step].wait()
+            total += part_refs[piece][step - 1].astype(F32)
+        spot = own_refs[piece].at[pl.ds(pl.multiple_of(low * half + high * part, part), part)]
+        spot[...] = total.astype(BF16)
+        for step in range(1, group):
+            other = lax.rem(high + step, group)
+            copy((piece, "share", step), spot, spot, 2 + group + step, (other * 2 + low, head))
+
+    def share_low(piece):
+        _, _, _, _, half, _ = widths(piece)
+        for step in range(1, group):
+            made[piece, "share", step].wait()
+        here = own_refs[piece].at[pl.ds(pl.multiple_of(low * half, half), half)]
+        copy((piece, "last"), here, here, 2 + 2 * group, (dp + 1 - 2 * low, head))
+
+    def leave(piece):
+        item, start, height, *_ = pieces[piece]
+        made[piece, "last"].wait()
+        out_refs[item][start : start + height, :] = own_refs[piece][:height, :].astype(F32)
+
+    return [to_core, to_far, to_low, to_high, share_high, share_low, leave]
+
+
+def sum_peers(count):
+    dp, head = lax.axis_index("dp"), lax.axis_index("head")
+    low, high = lax.rem(dp, 2), dp // 2
+    group = count // 2
+    return [peer(1), peer(2), (dp + 1 - 2 * low, head)] + [
+        (lax.rem(high + step, group) * 2 + low, head) for step in range(1, group)
+    ]
+
+
+def sum_scratch(pieces, count):
+    group = count // 2
+    scratch = []
+    for _, _, height, padded, lanes in pieces:
+        scratch.append(pltpu.VMEM((2, height, lanes), BF16))
+    for _, _, height, padded, lanes in pieces:
+        scratch.append(pltpu.VMEM((height, lanes), BF16))
+    for _, _, height, padded, lanes in pieces:
+        scratch.append(pltpu.VMEM((padded, lanes), BF16))
+    for _, _, height, padded, lanes in pieces:
+        scratch.append(pltpu.VMEM((2, padded // 2, lanes), BF16))
+    for _, _, height, padded, lanes in pieces:
+        scratch.append(pltpu.VMEM((group - 1, padded // count, lanes), BF16))
+    sems = pltpu.SemaphoreType.DMA((len(pieces), 3 + 2 * group))
+    return scratch + [sems, sems]
+
+
+def sum_kernel(pieces, count, segments, moves, *refs):
+    refs = list(refs)
+
+    def grab(number):
+        taken = refs[:number]
+        del refs[:number]
+        return taken
+
+    grads, sources = grab(segments), grab(moves)
+    outs, targets = grab(segments), grab(moves)
+    number = len(pieces)
+    near, far, own, mid, part = (grab(number) for _ in range(5))
+    send, receive = grab(2)
+    meet(sum_peers(count) + ([peer(3)] if moves else []))
+    copies = []
+    if moves:
+        extra_send, extra_receive = grab(2)
+        for item, move in enumerate((2, 3, 1)):
+            copies.append(
+                remote(sources[move - 1], targets[move - 1], extra_send.at[item], extra_receive.at[item], peer(move))
+            )
+    steps = sum_steps(pieces, count, grads, outs, near, far, own, mid, part, send, receive)
+    for time in range(number + len(steps) - 1):
+        for stage in reversed(range(len(steps))):
+            if 0 <= time - stage < number:
+                steps[stage](time - stage)
+        if time == 1:
+            for copy in copies:
+                copy.start()
+    for copy in copies:
+        copy.wait()
+
+
+def sum_over_devices(grads, sources, identity):
+    count = lax.axis_size("dp")
+    shapes = [item.shape[1:] for item in grads]
+    pieces = plan_pieces(shapes, count)
+    vmem = pl.BlockSpec(memory_space=pltpu.VMEM)
+    hbm = pl.BlockSpec(memory_space=pl.ANY)
+    scratch = sum_scratch(pieces, count)
+    if sources:
+        scratch += [pltpu.SemaphoreType.DMA((3,)), pltpu.SemaphoreType.DMA((3,))]
+    results = pl.pallas_call(
+        lambda *refs: sum_kernel(pieces, count, len(grads), len(sources), *refs),
+        in_specs=[vmem] * len(grads) + [hbm] * len(sources),
+        out_specs=[vmem] * len(grads) + [hbm] * len(sources),
+        out_shape=[like(shape, F32) for shape in shapes] + [like(item.shape, BF16) for item in sources],
+        scratch_shapes=scratch,
+        compiler_params=params(collective_id=identity, has_side_effects=True),
+        name=f"sum{identity}",
+    )(*grads, *sources)
+    return results[: len(grads)], results[len(grads) :]
+
+
 HALVES = 2
 
 
@@ -703,44 +965,47 @@
     packed = jnp.concatenate([
         cpe_kernel, crpe_kernel, cpe_bias[None], norm1_gain[None], norm1_shift[None], qv_bias,
         proj_bias[None], norm2_gain[None], norm2_shift[None], fc2_bias[None],
+        fc1_bias.reshape(4, LANES), jnp.zeros((1, LANES), BF16),
     ]).astype(F32)
-    small = lax.all_gather(packed, "head", axis=1, tiled=True)
-    x_halves = [bring(block_in, 0, HALVES)]
-    qkv = gather(qkv_weight.reshape(D, 3 * LANES))
+    part_rows = rows // HALVES
+    order = lax.bitwise_xor(head, jnp.arange(4, dtype=jnp.int32))
+    x1, x2, x3, qkv, small_all = entry(
+        block_in, part_rows, qkv_weight.reshape(D, 3 * LANES), packed
+    )
+    x_halves = [[take(block_in, 0, 0, HALVES), x1, x2, x3]]
+    block_in, proj_weight, cotangent, fc1_weight, fc2_weight, x_halves = lax.optimization_barrier(
+        (block_in, proj_weight, cotangent, fc1_weight, fc2_weight, x_halves)
+    )
     x_halves += [bring(block_in, part, HALVES) for part in range(1, HALVES)]
+    cot_parts = bring(cotangent, 0, 1)
     proj = gather(proj_weight)
-    cot_parts = bring(cotangent, 0, 1)
     fc1 = gather(fc1_weight)
     fc2 = gather(fc2_weight)
-    bias = gather(fc1_bias.astype(F32).reshape(1, -1))
+    small = jnp.take(small_all[:, :67], order, axis=0).transpose(1, 0, 2).reshape(67, D)
+    bias = small_all[:, 67:71].reshape(4, 1, D)
 
     kept, vec, crpe, cpe = forward_parts(me, cuts, x_halves, small, qkv)
     first, hidden, query, value, soft, context, conv, attended = kept
     results = middle_parts(me, kept, cot_parts, small, bias, proj, fc1, fc2)
     second_grad, att_grad, fc1_grad, fc2_grad, proj_grad, sums2, bias_grad = results[4:]
-    out_parts = [[results[move] if move == 0 else swap(results[move], move)] for move in range(4)]
-
-    def reduce_head(grads):
-        near = swap(jnp.stack([grads[1], grads[3]]).astype(BF16), 1).astype(F32)
-        far = swap((grads[2].astype(F32) + near[1]).astype(BF16), 2).astype(F32)
-        return grads[0].astype(F32) + near[0] + far
-
-    early = jnp.concatenate(
-        [fc1_grad, fc2_grad, proj_grad], axis=1
+    (fc1_own, fc2_own, proj_own), _ = sum_over_devices([fc1_grad, fc2_grad, proj_grad], [], 2)
+    fc1_own, fc2_own, proj_own, att_grad, out_sent = lax.optimization_barrier(
+        (fc1_own, fc2_own, proj_own, att_grad, list(results[:4]))
     )
-    early = lax.psum(reduce_head(early).astype(BF16), "dp")
+    out_parts = [[out_sent[0]]] + [[swap(out_sent[move], move)] for move in (1, 2, 3)]
 
     grad_parts = [[] for _ in range(4)]
     sums = []
     base = 0
-    for x_parts in x_halves:
+    for index, x_parts in enumerate(x_halves):
         back_results = back(
             cuts, me, x_parts, base, att_grad, query, value, soft, context, conv, first, hidden,
             second_grad, vec, qkv, crpe, cpe,
         )
+        last = index == HALVES - 1
         for move in range(4):
             piece = back_results[move]
-            grad_parts[move].append(piece if move == 0 else swap(piece, move))
+            grad_parts[move].append(piece if move == 0 or last else swap(piece, move))
         sums.append(back_results[4:])
         base += x_parts[0].shape[0] // PLACES
     qkv_grad, crpe_sum, cpe_sum, sums1 = [sum(items[1:], items[0]) for items in zip(*sums)]
@@ -748,21 +1013,21 @@
         jnp.sum(cpe_sum, axis=1), jnp.sum(crpe_sum, axis=1) * reach_mask(), sums1[4:5], sums1[2:4],
         sums1[0:2], sums2[3:4], sums2[1:3], sums2[0:1],
     ]).reshape(-1, 4, LANES).transpose(1, 0, 2)
-    order = lax.bitwise_xor(head, jnp.arange(4, dtype=jnp.int32))
-    small_grad = jnp.take(small_grad, order, axis=0)
-    late = jnp.concatenate([
-        qkv_grad.reshape(4, D * 3, LANES), small_grad, bias_grad.reshape(4, 4, LANES),
-        jnp.zeros((4, 1, LANES), F32),
-    ], axis=1)
-    late = lax.psum(reduce_head(late), "dp")
-    small_g = late[D * 3 : D * 3 + 67]
-    early = early.astype(F32)
+    small_grad = jnp.concatenate([
+        jnp.take(small_grad, order, axis=0), bias_grad.reshape(4, 4, LANES),
+        jnp.zeros((4, PIECE_ROWS - 71, LANES), F32),
+    ], axis=1).astype(BF16)
+    (qkv_own, small_own), last_parts = sum_over_devices(
+        [qkv_grad.astype(BF16), small_grad], [grad_parts[move][-1] for move in (1, 2, 3)], 3
+    )
+    for move in (1, 2, 3):
+        grad_parts[move][-1] = last_parts[move - 1]
     return (
         collect(me, out_parts), collect(me, grad_parts),
-        small_g[:9], small_g[58], small_g[59], small_g[60],
-        late[: D * 3].reshape(D, 3, LANES), small_g[61:63], small_g[9:58],
-        early[2 * D :], small_g[63], small_g[64], small_g[65],
-        early[:D], late[D * 3 + 67 : D * 3 + 71].reshape(D), early[D : 2 * D], small_g[66],
+        small_own[:9], small_own[58], small_own[59], small_own[60],
+        qkv_own.reshape(D, 3, LANES), small_own[61:63], small_own[9:58],
+        proj_own, small_own[63], small_own[64], small_own[65],
+        fc1_own, small_own[67:71].reshape(D), fc2_own, small_own[66],
     )
 
 

time: 540 us -> 461 us (0.85)
  waiting for transfers between devices: 178 us -> 8.86 us
  Pallas kernels: 225 us -> 383 us
  blocking collectives: 20.7 us -> 0 us
  other arithmetic: 38.2 us -> 19.3 us
  between operations: 14.9 us -> 1.26 us
  local copies, waits for them, and re-layouts: 39.1 us -> 30.4 us
  starting transfers between devices: 22.5 us -> 16.2 us
    pallas_call x0 -> x3, Pallas kernels: none -> 160 us  [the longest x2 134 us: sum_over_devices(): pl.pallas_call(lambda *refs: sum_kernel(pieces, count, len(grads), len(so...]
    psum x2 -> x0, waiting for transfers between devices: 94.5 us -> none  [the longest x1 77.6 us: body(): early = lax.psum(reduce_head(early).astype(BF16), 'dp')]
    ppermute x32 -> x18, waiting for transfers between devices: 83.8 us -> 8.86 us  [swap(): lax.ppermute(values, 'head', [(item, item ^ move) for item in range(4)])]
    all_gather x1 -> x0, blocking collectives: 20.7 us -> none  [body(): small = lax.all_gather(packed, 'head', axis=1, tiled=True)]
    convert_element_type x6 -> x1, other arithmetic: 10.6 us -> 3.36 us  [body(): qkv_grad.astype(BF16)]
    ppermute x32 -> x18, starting transfers between devices: 22.5 us -> 16.2 us  [swap(): lax.ppermute(values, 'head', [(item, item ^ move) for item in range(4)])]
    concatenate x2 -> x1, local copies, waits for them, and re-layouts: 6.11 us -> 0.08 us  [body(): jnp.concatenate([jnp.take(small_grad, order, axis=0), bias_grad.reshape(4...]
  transfers between devices with their start and end apart: 34 -> 18, of which waited for: 11 -> 2; matrix products, arithmetic and copies ran while one was open for 10% -> 7% of each run, Pallas kernels for 29% -> 30%
where the time goes in v2:
time: 461 us; the launch traced here: 459 us
  Pallas kernels  383 us (83%)
  local copies, waits for them, and re-layouts  30.4 us (7%)
  other arithmetic  19.3 us (4%)
  starting transfers between devices  16.2 us (4%)
  waiting for transfers between devices  8.86 us (2%)
    pallas_call x2, Pallas kernels, sum_over_devices(): pl.pallas_call(lambda *refs: sum_kernel(pieces, count, len(grads), len(so...  134 us
    pallas_call x2, Pallas kernels, back(): pl.pallas_call(lambda *refs: back_kernel(base, *refs), grid_spec=pltpu.Pr...  79.4 us
    pallas_call x1, Pallas kernels, middle(): pl.pallas_call(middle_kernel, grid_spec=pltpu.PrefetchScalarGridSpec(num_...  69.6 us
    pallas_call x2, Pallas kernels, front(): pl.pallas_call(lambda *refs: front_kernel(base, len(kept), *refs), grid_s...  65.1 us
    pallas_call x1, Pallas kernels, entry(): pl.pallas_call(lambda *refs: entry_kernel(rows, size, *refs), in_specs=[h...  25.9 us
    ppermute x18, starting transfers between devices, swap(): lax.ppermute(values, 'head', [(item, item ^ move) for item in range(4)])  16.2 us
  transfers between devices with their start and end apart: 18, of which 2 were waited for; matrix products, arithmetic and copies ran while one was open for 7% of the time, Pallas kernels for 30%

profile of v2, /device:TPU:0, one launch (start us, length us, event | category | flops | bytes accessed | tf_op | source)
XLA Modules:
  0.0 458.8 jit_solution(5800082044417404543)
XLA Ops:
  0.7 1.2 copy.60
  1.9 0.9 copy.61.refs_1_
  2.8 3.0 concatenate.10
  5.8 0.6 convert_element_type.44.refs_2_
  6.4 1.7 constant_dynamic-slice_fusion.8.refs_2_
  8.1 25.9 %entry.1 = (bf16[1024,128]{1,0:T(8,128)(2,1)}, bf16[1024,128]{1,0:T(8,128)(2,1)}, bf16[1024,128]{1,0:T(8,128)(2,1)}, bf16[4,512,384]{2,1,0:T(8,128)(2,1)}, f32[4,72,128]{2,1,0:T(8,128)}) custom-call(bf16[8192,128]{1,0:T(8,128)(2,1)} %refs_0_.1, bf16[512,384]{1,0:T(8,128)(2,1)} %copy.61.refs_1_, f32[72,128]{1,0:T(8,128)} %convert_element_type.44.refs_2_), custom_call_target="tpu_custom_call" | custom-call | tf_op jit(solution)/shard_map/entry/pallas_call | solution.py:702
  34.0 1.0 constant_dynamic-slice_fusion.4
  35.1 1.6 collective-permute-start.1
  36.7 0.5 collective-permute-start.8
  37.2 1.5 collective-permute-start.10
  38.7 0.5 collective-permute-start.6
  39.3 0.6 gather_fusion
  39.9 0.6 slice_bitcast_fusion
  40.6 0.9 fusion
  41.6 0.8 convert_reduce_fusion.2
  42.7 0.7 pad_add_fusion.refs_0_
  43.5 0.6 stack.71.refs_7_.refs_15_
  44.1 1.0 broadcast_in_dim.64.refs_9_.refs_17_
  45.1 0.7 broadcast_in_dim.63.refs_6_.refs_18_
  45.8 32.5 %front.2 = (f32[2048,512]{1,0:T(8,128)}, bf16[2048,512]{1,0:T(8,128)(2,1)}, bf16[2048,512]{1,0:T(8,128)(2,1)}, bf16[2048,512]{1,0:T(8,128)(2,1)}, bf16[2048,512]...) custom-call(s32[8,3]{1,0:T(8,128)} %pad_add_fusion.refs_0_, ...), custom_call_target="tpu_custom_call" | custom-call | flops 12884901888 | bytes 40000000 | tf_op jit(solution)/shard_map/front/pallas_call | solution.py:292
  78.3 1.4 constant_dynamic-slice_fusion
  79.7 0.6 slice.173
  80.4 1.3 stack.73.vec_ref
  81.7 0.5 collective-permute-start.2
  82.3 1.9 collective-permute-start.3
  84.2 1.1 pad_maximum_fusion.2
  85.4 1.1 pad_maximum_fusion.3
  87.1 2.7 collective-permute-done.2.refs_5_
  89.8 1.4 collective-permute-start.11
  91.2 32.6 %front.3 = (f32[2048,512]{1,0:T(8,128)}, bf16[2048,512]{1,0:T(8,128)(2,1)}, bf16[2048,512]{1,0:T(8,128)(2,1)}, bf16[2048,512]{1,0:T(8,128)(2,1)}, bf16[2048,512]...) custom-call(s32[8,3]{1,0:T(8,128)} %pad_add_fusion.refs_0_, ...), custom_call_target="tpu_custom_call", output_to_operand_aliasing={{0}: (10, {}), {1}: (11, {}), {2}: (12, {}), {3}: (13, {}),... | custom-call | flops 12884901888 | bytes 40000000 | tf_op jit(solution)/shard_map/front/pallas_call | solution.py:292
  123.8 2.1 collective-permute-start.5
  126.0 0.9 pad_maximum_fusion.4.proj_ref
  126.9 2.7 pad_maximum_fusion.fc1_ref
  129.7 2.7 pad_maximum_fusion.1.fc2_ref
  132.4 6.2 %collective-permute-done.5.cot3_ref = bf16[2048,128]{1,0:T(8,128)(2,1)} collective-permute-done((bf16[2048,128]{1,0:T(8,128)(2,1)}, bf16[2048,128]{1,0:T(8,128)(2,1)}, u32[]{:S(2)}, u32[]{:S(2)}) %collective-permute-start.5) | collective-permute-done | bytes 524320 | tf_op jit(solution)/shard_map/ppermute | solution.py:949
  138.5 69.6 %middle.1 = (bf16[2048,128]{1,0:T(8,128)(2,1)}, bf16[2048,128]{1,0:T(8,128)(2,1)}, bf16[2048,128]{1,0:T(8,128)(2,1)}, bf16[2048,128]{1,0:T(8,128)(2,1)}, f32[204...) custom-call(s32[1]{0:T(128)} %bitcast.refs_1_.me_ref, ...), custom_call_target="tpu_custom_call" | custom-call | flops 32212254720 | bytes 30000000 | tf_op jit(solution)/shard_map/middle/pallas_call | solution.py:436
  208.1 66.7 %sum2.1 = (f32[512,512]{1,0:T(8,128)}, f32[512,512]{1,0:T(8,128)}, f32[128,512]{1,0:T(8,128)}) custom-call(bf16[4,512,512]{2,1,0:T(8,128)(2,1)} %get-tuple-element.115.refs_0_, bf16[4,512,512]{2,1,0:T(8,128)(2,1)} %get-tuple-element.116.refs_1_, bf16[4,128,512]{2,1,0:T(8,128)(2,1)} %get-tuple-element.117.refs_2_), custom_call_target="tpu_custom_call" | custom-call | tf_op jit(solution)/shard_map/sum2/pallas_call | solution.py:888
  274.9 39.3 %back.2 = (bf16[1024,128]{1,0:T(8,128)(2,1)}, bf16[1024,128]{1,0:T(8,128)(2,1)}, bf16[1024,128]{1,0:T(8,128)(2,1)}, bf16[1024,128]{1,0:T(8,128)(2,1)}, f32[4,512...) custom-call(s32[8,3]{1,0:T(8,128)} %pad_add_fusion.refs_0_, ...), custom_call_target="tpu_custom_call" | custom-call | flops 17179869184 | bytes 40000000 | tf_op jit(solution)/shard_map/back/pallas_call | solution.py:575
  314.3 40.1 %back.3 = (bf16[1024,128]{1,0:T(8,128)(2,1)}, bf16[1024,128]{1,0:T(8,128)(2,1)}, bf16[1024,128]{1,0:T(8,128)(2,1)}, bf16[1024,128]{1,0:T(8,128)(2,1)}, f32[4,512...) custom-call(s32[8,3]{1,0:T(8,128)} %pad_add_fusion.refs_0_, ...), custom_call_target="tpu_custom_call" | custom-call | flops 17179869184 | bytes 40000000 | tf_op jit(solution)/shard_map/back/pallas_call | solution.py:575
  354.4 0.7 add.136
  355.1 0.8 fusion.14
  355.9 0.7 slice.184
  356.7 1.5 add_reduce_fusion
  358.2 1.0 add_reduce_fusion.1
  359.2 0.5 concatenate.11
  359.8 0.7 gather_fusion.1
  360.7 3.4 collective-permute-start.16
  364.5 1.4 collective-permute-start.14
  365.9 3.4 add_convert_fusion.refs_0_
  369.3 0.7 maximum_maximum_fusion.refs_1_
  370.0 67.0 %sum3.1 = (f32[512,384]{1,0:T(8,128)}, f32[128,128]{1,0:T(8,128)}, bf16[1024,128]{1,0:T(8,128)(2,1)}, bf16[1024,128]{1,0:T(8,128)(2,1)}, bf16[1024,128]{1,0:T(8,128)(2,1)}) custom-call(bf16[4,512,384]{2,1,0:T(8,128)(2,1)} %add_convert_fusion.refs_0_, bf16[4,128,128]{2,1,0:T(8,128)(2,1)} %maximum_maximum_fusion.refs_1_, ...), custom_call_target="tpu_custom_call" | custom-call | tf_op jit(solution)/shard_map/sum3/pallas_call | solution.py:888
  437.2 1.3 slice_bitcast_fusion.9
  438.4 1.4 slice.191
  439.8 1.3 slice.186
  441.1 1.2 slice.190
  442.4 1.4 copy.65
  443.8 1.1 copy.66
  444.9 1.4 slice_bitcast_fusion.10
  446.3 0.7 copy-done.10
  447.0 5.1 %collect.3 = f32[8192,128]{1,0:T(8,128)} custom-call(s32[1]{0:T(128)} %bitcast.refs_1_.me_ref, bf16[1024,128]{1,0:T(8,128)(2,1)} %get-tuple-element.138.refs_0_, bf16[1024,128]{1,0:T(8,128)(2,1)} %get-tuple-element.139.refs_1_, bf16[1024,128]{1,0:T(8,128)(2,1)} %copy-done.9, bf16[1024,128]{1,0:T(8,128)(2,1)} %get-tuple-element.154.refs_3_, ...), custom_call_target="tpu_custom_call" | custom-call | tf_op jit(solution)/shard_map/collect/pallas_call | solution.py:621
  452.1 4.1 collect.2
  456.2 0.7 copy.82
  456.9 1.0 copy.83
  457.9 1.0 copy.84
  (107 shorter events, 2.6 us)
Async XLA Ops:
  1.8 32.1 %copy-start = (bf16[8192,128]{1,0:T(8,128)(2,1)S(1)}, bf16[8192,128]{1,0:T(8,128)(2,1)}, u32[]{:S(2)}) copy-start(bf16[8192,128]{1,0:T(8,128)(2,1)} %refs_0_.1) | copy-start | bytes 6291460
  8.1 28.6 %copy-start.3 = (bf16[512,512]{1,0:T(8,128)(2,1)S(1)}, bf16[512,512]{1,0:T(8,128)(2,1)}, u32[]{:S(2)}) copy-start(bf16[512,512]{1,0:T(8,128)(2,1)} %param.34) | copy-start | bytes 1572868
  8.1 29.1 %copy-start.4 = (bf16[512,512]{1,0:T(8,128)(2,1)S(1)}, bf16[512,512]{1,0:T(8,128)(2,1)}, u32[]{:S(2)}) copy-start(bf16[512,512]{1,0:T(8,128)(2,1)} %param.36) | copy-start | bytes 1572868
  8.1 30.6 %copy-start.8 = (bf16[128,512]{1,0:T(8,128)(2,1)S(1)}, bf16[128,512]{1,0:T(8,128)(2,1)}, u32[]{:S(2)}) copy-start(bf16[128,512]{1,0:T(8,128)(2,1)} %param.30) | copy-start | bytes 393220
  33.9 5.3 %copy-start.12 = (f32[4,72,128]{2,1,0:T(8,128)S(1)}, f32[4,72,128]{2,1,0:T(8,128)}, u32[]{:S(2)}) copy-start(f32[4,72,128]{2,1,0:T(8,128)} %get-tuple-element.95) | copy-start | bytes 442372
  35.0 51.6 %collective-permute-start = (bf16[1024,128]{1,0:T(8,128)(2,1)}, bf16[1024,128]{1,0:T(8,128)(2,1)}, u32[]{:S(2)}, u32[]{:S(2)}) collective-permute-start(bf16[1024,128]{1,0:T(8,128)(2,1)} %get-tuple-element.223), channel_id=1, source_target_pairs={{0,1},{1,0},{2,3},{3,2},{4,5},{5,4},{6,7},{7,6},{8,9},{9,8},{10,11... | collective-permute-start | bytes 786440 | tf_op jit(solution)/shard_map/ppermute | solution.py:949
  35.1 51.6 %collective-permute-start.1 = (bf16[1024,128]{1,0:T(8,128)(2,1)}, bf16[1024,128]{1,0:T(8,128)(2,1)}, u32[]{:S(2)}, u32[]{:S(2)}) collective-permute-start(bf16[1024,128]{1,0:T(8,128)(2,1)} %get-tuple-element.222), channel_id=1, source_target_pairs={{0,2},{1,3},{2,0},{3,1},{4,6},{5,7},{6,4},{7,5},{8,10},{9,11},{10,... | collective-permute-start | bytes 786440 | tf_op jit(solution)/shard_map/ppermute | solution.py:949
  36.7 45.6 %collective-permute-start.8 = (bf16[512,512]{1,0:T(8,128)(2,1)S(1)}, bf16[512,512]{1,0:T(8,128)(2,1)}, u32[]{:S(2)}, u32[]{:S(2)}) collective-permute-start(bf16[512,512]{1,0:T(8,128)(2,1)S(1)} %copy-done.3), channel_id=1, source_target_pairs={{0,2},{1,3},{2,0},{3,1},{4,6},{5,7},{6,4},{7,5},{8,10},{9,11},{10,... | collective-permute-start | bytes 1572872 | tf_op jit(solution)/shard_map/ppermute | solution.py:949
  37.2 48.2 %collective-permute-start.10 = (bf16[512,512]{1,0:T(8,128)(2,1)S(1)}, bf16[512,512]{1,0:T(8,128)(2,1)}, u32[]{:S(2)}, u32[]{:S(2)}) collective-permute-start(bf16[512,512]{1,0:T(8,128)(2,1)S(1)} %copy-done.4), channel_id=1, source_target_pairs={{0,2},{1,3},{2,0},{3,1},{4,6},{5,7},{6,4},{7,5},{8,10},{9,11},{10,... | collective-permute-start | bytes 1572872 | tf_op jit(solution)/shard_map/ppermute | solution.py:949
  38.7 43.0 %collective-permute-start.6 = (bf16[128,512]{1,0:T(8,128)(2,1)S(1)}, bf16[128,512]{1,0:T(8,128)(2,1)S(1)}, u32[]{:S(2)}, u32[]{:S(2)}) collective-permute-start(bf16[128,512]{1,0:T(8,128)(2,1)S(1)} %copy-done.8), channel_id=1, source_target_pairs={{0,2},{1,3},{2,0},{3,1},{4,6},{5,7},{6,4},{7,5},{8,10},{9,11},{10,... | collective-permute-start | bytes 393224 | tf_op jit(solution)/shard_map/ppermute | solution.py:949
  39.2 3.1 copy-start.19
  39.2 0.7 copy-start.18
  40.6 5.2 %copy-start.14 = (s32[512]{0:T(512)}, s32[512]{0:T(512)S(1)}, u32[]{:S(2)}) copy-start(s32[512]{0:T(512)S(1)} %convert_add_fusion) | copy-start | bytes 6148
  40.6 5.2 %copy-start.21 = (s32[49]{0:T(128)}, s32[49]{0:T(128)S(1)}, u32[]{:S(2)}) copy-start(s32[49]{0:T(128)S(1)} %fusion.8) | copy-start | bytes 592
  45.8 32.5 %copy-start.2 = (bf16[8192,128]{1,0:T(8,128)(2,1)S(1)}, bf16[8192,128]{1,0:T(8,128)(2,1)}, u32[]{:S(2)}) copy-start(bf16[8192,128]{1,0:T(8,128)(2,1)} %param.22) | copy-start | bytes 6291460
  81.7 8.1 %collective-permute-start.2 = (bf16[1024,128]{1,0:T(8,128)(2,1)}, bf16[1024,128]{1,0:T(8,128)(2,1)}, u32[]{:S(2)}, u32[]{:S(2)}) collective-permute-start(bf16[1024,128]{1,0:T(8,128)(2,1)} %get-tuple-element.221), channel_id=1, source_target_pairs={{0,3},{1,2},{2,1},{3,0},{4,7},{5,6},{6,5},{7,4},{8,11},{9,10},{10,... | collective-permute-start | bytes 786440 | tf_op jit(solution)/shard_map/ppermute | solution.py:949
  82.3 50.1 %collective-permute-start.3 = (bf16[2048,128]{1,0:T(8,128)(2,1)}, bf16[2048,128]{1,0:T(8,128)(2,1)}, u32[]{:S(2)}, u32[]{:S(2)}) collective-permute-start(bf16[2048,128]{1,0:T(8,128)(2,1)} %get-tuple-element.219), channel_id=1, source_target_pairs={{0,1},{1,0},{2,3},{3,2},{4,5},{5,4},{6,7},{7,6},{8,9},{9,8},{10,11... | collective-permute-start | bytes 1572872 | tf_op jit(solution)/shard_map/ppermute | solution.py:949
  85.3 47.0 %collective-permute-start.4 = (bf16[2048,128]{1,0:T(8,128)(2,1)}, bf16[2048,128]{1,0:T(8,128)(2,1)}, u32[]{:S(2)}, u32[]{:S(2)}) collective-permute-start(bf16[2048,128]{1,0:T(8,128)(2,1)} %get-tuple-element.218), channel_id=1, source_target_pairs={{0,2},{1,3},{2,0},{3,1},{4,6},{5,7},{6,4},{7,5},{8,10},{9,11},{10,... | collective-permute-start | bytes 1572872 | tf_op jit(solution)/shard_map/ppermute | solution.py:949
  86.6 37.3 %collective-permute-start.7 = (bf16[2,128,512]{2,1,0:T(8,128)(2,1)S(1)}, bf16[2,128,512]{2,1,0:T(8,128)(2,1)S(1)}, u32[]{:S(2)}, u32[]{:S(2)}) collective-permute-start(bf16[2,128,512]{2,1,0:T(8,128)(2,1)S(1)} %pad_maximum_fusion.5), channel_id=1, source_target_pairs={{0,1},{1,0},{2,3},{3,2},{4,5},{5,4},{6,7},{7,6},{8,9},{9,8},{10,11... | collective-permute-start | bytes 786440 | tf_op jit(solution)/shard_map/ppermute | solution.py:949
  86.7 40.1 %collective-permute-start.9 = (bf16[2,512,512]{2,1,0:T(8,128)(2,1)S(1)}, bf16[2,512,512]{2,1,0:T(8,128)(2,1)S(1)}, u32[]{:S(2)}, u32[]{:S(2)}) collective-permute-start(bf16[2,512,512]{2,1,0:T(8,128)(2,1)S(1)} %pad_maximum_fusion.2), channel_id=1, source_target_pairs={{0,1},{1,0},{2,3},{3,2},{4,5},{5,4},{6,7},{7,6},{8,9},{9,8},{10,11... | collective-permute-start | bytes 3145736 | tf_op jit(solution)/shard_map/ppermute | solution.py:949
  89.8 39.8 %collective-permute-start.11 = (bf16[2,512,512]{2,1,0:T(8,128)(2,1)S(1)}, bf16[2,512,512]{2,1,0:T(8,128)(2,1)S(1)}, u32[]{:S(2)}, u32[]{:S(2)}) collective-permute-start(bf16[2,512,512]{2,1,0:T(8,128)(2,1)S(1)} %pad_maximum_fusion.3), channel_id=1, source_target_pairs={{0,1},{1,0},{2,3},{3,2},{4,5},{5,4},{6,7},{7,6},{8,9},{9,8},{10,11... | collective-permute-start | bytes 3145736 | tf_op jit(solution)/shard_map/ppermute | solution.py:949
  123.8 14.7 %collective-permute-start.5 = (bf16[2048,128]{1,0:T(8,128)(2,1)}, bf16[2048,128]{1,0:T(8,128)(2,1)}, u32[]{:S(2)}, u32[]{:S(2)}) collective-permute-start(bf16[2048,128]{1,0:T(8,128)(2,1)} %get-tuple-element.217), channel_id=1, source_target_pairs={{0,3},{1,2},{2,1},{3,0},{4,7},{5,6},{6,5},{7,4},{8,11},{9,10},{10,... | collective-permute-start | bytes 1572872 | tf_op jit(solution)/shard_map/ppermute | solution.py:949
  314.2 40.2 %copy-start.16 = (f32[8,512]{1,0:T(8,128)S(1)}, f32[8,512]{1,0:T(8,128)}, u32[]{:S(2)}) copy-start(f32[8,512]{1,0:T(8,128)} %get-tuple-element.147) | copy-start | bytes 49156
  314.2 42.5 %copy-start.7 = (f32[49,8,512]{2,1,0:T(8,128)S(1)}, f32[49,8,512]{2,1,0:T(8,128)}, u32[]{:S(2)}) copy-start(f32[49,8,512]{2,1,0:T(8,128)} %get-tuple-element.145) | copy-start | bytes 2408452
  314.2 43.9 %copy-start.15 = (s32[512]{0:T(512)S(1)}, s32[512]{0:T(512)}, u32[]{:S(2)}) copy-start(s32[512]{0:T(512)} %copy-done.14) | copy-start | bytes 6148
  314.2 43.9 %copy-start.22 = (s32[49]{0:T(128)S(1)}, s32[49]{0:T(128)}, u32[]{:S(2)}) copy-start(s32[49]{0:T(128)} %copy-done.21) | copy-start | bytes 592
  314.2 44.0 %copy-start.13 = (f32[9,8,512]{2,1,0:T(8,128)S(1)}, f32[9,8,512]{2,1,0:T(8,128)}, u32[]{:S(2)}) copy-start(f32[9,8,512]{2,1,0:T(8,128)} %get-tuple-element.143) | copy-start | bytes 442372
  314.3 51.6 %copy-start.1 = (f32[4,512,384]{2,1,0:T(8,128)S(1)}, f32[4,512,384]{2,1,0:T(8,128)}, u32[]{:S(2)}) copy-start(f32[4,512,384]{2,1,0:T(8,128)} %get-tuple-element.141) | copy-start | bytes 9437188
  354.4 6.1 %copy-start.20 = (pred[4]{0:T(512)(128)(4,1)S(1)}, pred[4]{0:T(512)(128)(4,1)}, u32[]{:S(2)}) copy-start(pred[4]{0:T(512)(128)(4,1)} %copy-done.19) | copy-start | bytes 16
  360.6 76.5 %collective-permute-start.15 = (bf16[1024,128]{1,0:T(8,128)(2,1)}, bf16[1024,128]{1,0:T(8,128)(2,1)S(1)}, u32[]{:S(2)}, u32[]{:S(2)}) collective-permute-start(bf16[1024,128]{1,0:T(8,128)(2,1)} %get-tuple-element.140), channel_id=1, source_target_pairs={{0,1},{1,0},{2,3},{3,2},{4,5},{5,4},{6,7},{7,6},{8,9},{9,8},{10,11... | collective-permute-start | bytes 786440 | tf_op jit(solution)/shard_map/ppermute | solution.py:949
  360.7 85.6 %collective-permute-start.16 = (bf16[1024,128]{1,0:T(8,128)(2,1)}, bf16[1024,128]{1,0:T(8,128)(2,1)}, u32[]{:S(2)}, u32[]{:S(2)}) collective-permute-start(bf16[1024,128]{1,0:T(8,128)(2,1)} %get-tuple-element.155), channel_id=1, source_target_pairs={{0,2},{1,3},{2,0},{3,1},{4,6},{5,7},{6,4},{7,5},{8,10},{9,11},{10,... | collective-permute-start | bytes 786440 | tf_op jit(solution)/shard_map/ppermute | solution.py:949
  364.0 88.1 %collective-permute-start.12 = (bf16[2048,128]{1,0:T(8,128)(2,1)}, bf16[2048,128]{1,0:T(8,128)(2,1)}, u32[]{:S(2)}, u32[]{:S(2)}) collective-permute-start(bf16[2048,128]{1,0:T(8,128)(2,1)} %get-tuple-element.127), channel_id=1, source_target_pairs={{0,1},{1,0},{2,3},{3,2},{4,5},{5,4},{6,7},{7,6},{8,9},{9,8},{10,11... | collective-permute-start | bytes 1572872 | tf_op jit(solution)/shard_map/ppermute | solution.py:949
  364.2 87.9 %collective-permute-start.13 = (bf16[2048,128]{1,0:T(8,128)(2,1)}, bf16[2048,128]{1,0:T(8,128)(2,1)}, u32[]{:S(2)}, u32[]{:S(2)}) collective-permute-start(bf16[2048,128]{1,0:T(8,128)(2,1)} %get-tuple-element.128), channel_id=1, source_target_pairs={{0,2},{1,3},{2,0},{3,1},{4,6},{5,7},{6,4},{7,5},{8,10},{9,11},{10,... | collective-permute-start | bytes 1572872 | tf_op jit(solution)/shard_map/ppermute | solution.py:949
  364.5 87.6 %collective-permute-start.14 = (bf16[2048,128]{1,0:T(8,128)(2,1)}, bf16[2048,128]{1,0:T(8,128)(2,1)}, u32[]{:S(2)}, u32[]{:S(2)}) collective-permute-start(bf16[2048,128]{1,0:T(8,128)(2,1)} %get-tuple-element.129), channel_id=1, source_target_pairs={{0,3},{1,2},{2,1},{3,0},{4,7},{5,6},{6,5},{7,4},{8,11},{9,10},{10,... | collective-permute-start | bytes 1572872 | tf_op jit(solution)/shard_map/ppermute | solution.py:949
  365.9 3.4 copy-start.17
  369.2 67.9 %copy-start.23 = (bf16[1024,128]{1,0:T(8,128)(2,1)S(1)}, bf16[1024,128]{1,0:T(8,128)(2,1)}, u32[]{:S(2)}) copy-start(bf16[1024,128]{1,0:T(8,128)(2,1)} %get-tuple-element.157) | copy-start | bytes 786436
  437.1 9.2 %copy-start.9 = (bf16[1024,128]{1,0:T(8,128)(2,1)}, bf16[1024,128]{1,0:T(8,128)(2,1)S(1)}, u32[]{:S(2)}) copy-start(bf16[1024,128]{1,0:T(8,128)(2,1)S(1)} %collective-permute-done.15.refs_2_) | copy-start | bytes 786436
  437.1 9.2 %collective-permute-start.17 = (bf16[1024,128]{1,0:T(8,128)(2,1)S(1)}, bf16[1024,128]{1,0:T(8,128)(2,1)S(1)}, u32[]{:S(2)}, u32[]{:S(2)}) collective-permute-start(bf16[1024,128]{1,0:T(8,128)(2,1)S(1)} %copy-done.23), channel_id=1, source_target_pairs={{0,3},{1,2},{2,1},{3,0},{4,7},{5,6},{6,5},{7,4},{8,11},{9,10},{10,... | collective-permute-start | bytes 786440 | tf_op jit(solution)/shard_map/ppermute | solution.py:949
  446.3 0.7 copy-start.10
  452.1 4.1 copy-start.11
  452.1 4.8 %copy-start.6 = (f32[512,512]{1,0:T(8,128)S(1)}, f32[512,512]{1,0:T(8,128)}, u32[]{:S(2)}) copy-start(f32[512,512]{1,0:T(8,128)} %get-tuple-element.281) | copy-start | bytes 3145732
  456.2 1.7 copy-start.5

commit v3 on v1

v3 whole, which is shorter than its diff:
```python
import jax
import jax.numpy as jnp
from jax import lax
from jax.experimental import pallas as pl
from jax.experimental.pallas import tpu as pltpu
from jax.sharding import PartitionSpec as P

D = 512
HEADS = 8
HEAD_DIM = 64
HIDDEN = 2048
SIDE = 16
PLACES = 256
LANES = 128
TILES = 4
REACH = (1, 2, 3, 3)
GAP = 3
GRID_ROWS = SIDE + 3 * GAP + 1
EPSILON = 1e-06
SCALE = HEAD_DIM ** (-0.5)
F32 = jnp.float32
BF16 = jnp.bfloat16


def dot(left, right, dims):
    return lax.dot_general(left, right, (dims, ((), ())), preferred_element_type=F32)


def nn(left, right):
    return dot(left, right, ((1,), (0,)))


def nt(left, right):
    return dot(left, right, ((1,), (1,)))


def tn(left, right):
    return dot(left, right, ((0,), (0,)))


def lane(tile):
    return pl.ds(LANES * tile, LANES)


def fill_masks(cut, col_cuts, mask_ref):
    col = lax.broadcasted_iota(jnp.int32, (SIDE, LANES), 0)
    for band in range(2):
        here = (col >= col_cuts[band]).astype(jnp.int32)
        for step in range(-3, 4):
            if step == 0:
                continue
            there = (col + step >= col_cuts[band]).astype(jnp.int32)
            good = (col + step >= 0) & (col + step < SIDE) & (here == there)
            mask_ref[band, step + 3] = jnp.where(good, 1.0, 0.0).astype(F32)


def place_ids(cut, col_cuts):
    place = lax.broadcasted_iota(jnp.int32, (PLACES, LANES), 0)
    row = lax.shift_right_logical(place, 4)
    col = lax.bitwise_and(place, 15)
    band = (row >= cut).astype(jnp.int32)
    col_cut = jnp.where(band > 0, col_cuts[1], col_cuts[0])
    side = (col >= col_cut).astype(jnp.int32)
    return band, side


def spread(read_row, reach, cut, mask_ref, grid_ref, plane):
    zero = jnp.zeros((GAP * SIDE, LANES), F32)
    for step in range(-reach, reach + 1):
        start = pl.multiple_of(SIDE * (GAP + cut), SIDE)
        grid_ref[plane + step, pl.ds(start, GAP * SIDE), :] = zero
    for row in range(SIDE):
        lower = (row >= cut).astype(jnp.int32)
        start = pl.multiple_of(SIDE * (row + GAP + GAP * lower), SIDE)
        values = read_row(row)
        for step in range(-reach, reach + 1):
            moved = values
            if step != 0:
                moved = pltpu.roll(values, (-step) % SIDE, 0) * mask_ref[lower, step + 3]
            grid_ref[plane + step, pl.ds(start, SIDE), :] = moved


def add_to(store, key, term):
    store[key] = term if key not in store else store[key] + term


def conv_tiles(items, reach, cut, grid_ref, taps_ref, tap_reach, out_ref):
    upper_pairs = (cut + 1) // 2
    pairs = upper_pairs + (SIDE - cut + 1) // 2
    width = 2 * tap_reach + 1
    chains = 3

    def body(index, carry):
        lower = (index >= upper_pairs).astype(jnp.int32)
        row = 2 * index + lower * (cut - 2 * upper_pairs)
        base = row + GAP * lower + (GAP - reach)
        for tile, plane in items:
            total = {}
            for step in range(-reach, reach + 1):
                taps = [
                    taps_ref[(dr + tap_reach) * width + step + tap_reach, :, lane(tile)]
                    for dr in range(-reach, reach + 1)
                ]
                for place in range(2 * reach + 2):
                    for half in range(2):
                        start = pl.multiple_of(SIDE * (base + place) + 8 * half, 8)
                        field = grid_ref[plane + step, pl.ds(start, 8), :]
                        for out in range(2):
                            tap = place - out
                            if 0 <= tap <= 2 * reach:
                                add_to(total, (out, half, step % chains), taps[tap] * field)
            for out in range(2):
                for half in range(2):
                    start = pl.multiple_of(SIDE * (row + out) + 8 * half, 8)
                    out_ref[pl.ds(start, 8), lane(tile)] = sum(
                        [total[out, half, chain] for chain in range(1, chains)], total[out, half, 0]
                    )
        return carry

    lax.fori_loop(0, pairs, body, 0)


def conv_back_tiles(items, reach, cut, grid_ref, taps_ref, tap_reach, other_ref, out_ref, sum_ref):
    upper_pairs = (cut + 1) // 2
    pairs = upper_pairs + (SIDE - cut + 1) // 2
    width = 2 * tap_reach + 1
    chains = 2

    def body(index, carry):
        lower = (index >= upper_pairs).astype(jnp.int32)
        row = 2 * index + lower * (cut - 2 * upper_pairs)
        base = row + GAP * lower + (GAP - reach)
        keep = jnp.where((lower == 0) & (row + 1 >= cut), 0.0, 1.0).astype(F32)
        for tile, plane in items:
            other = {}
            for out in range(2):
                for half in range(2):
                    start = pl.multiple_of(SIDE * (row + out) + 8 * half, 8)
                    value = other_ref[pl.ds(start, 8), lane(tile)]
                    other[out, half] = value * keep if out else value
            total = {}
            for step in range(-reach, reach + 1):
                sums = {}
                ids = [
                    (tap_reach - dr) * width + tap_reach - step for dr in range(-reach, reach + 1)
                ]
                taps = [taps_ref[item, :, lane(tile)] for item in ids]
                for place in range(2 * reach + 2):
                    for half in range(2):
                        start = pl.multiple_of(SIDE * (base + place) + 8 * half, 8)
                        field = grid_ref[plane + step, pl.ds(start, 8), :]
                        for out in range(2):
                            tap = place - out
                            if 0 <= tap <= 2 * reach:
                                add_to(total, (out, half, step % chains), taps[tap] * field)
                                add_to(sums, tap, other[out, half] * field)
                for tap in range(2 * reach + 1):
                    sum_ref[ids[tap], :, lane(tile)] += sums[tap]
            for out in range(2):
                for half in range(2):
                    start = pl.multiple_of(SIDE * (row + out) + 8 * half, 8)
                    out_ref[pl.ds(start, 8), lane(tile)] = sum(
                        [total[out, half, chain] for chain in range(1, chains)], total[out, half, 0]
                    )
        return carry

    lax.fori_loop(0, pairs, body, 0)


SMALL_ITEMS = tuple((tile, 3 * tile + 1) for tile in range(TILES))


def row_mean(values):
    return jnp.sum(values, axis=1, keepdims=True) * (1.0 / D)


def pick(ids, rows):
    out = rows[0]
    for crop in range(1, 4):
        out = jnp.where(ids >= crop, rows[crop], out)
    return out


def crop_reduce(ids, values, op, empty):
    return [op(jnp.where(ids == crop, values, empty), axis=0, keepdims=True) for crop in range(4)]


def head_block():
    row = lax.broadcasted_iota(jnp.int32, (2 * LANES, 2 * LANES), 0)
    col = lax.broadcasted_iota(jnp.int32, (2 * LANES, 2 * LANES), 1)
    same = lax.bitwise_and(row, HEAD_DIM) == lax.bitwise_and(col, HEAD_DIM)
    return jnp.where(same, 1.0, 0.0).astype(F32)


def both(values, masks):
    return jnp.concatenate([values * masks[0], values * masks[1]], axis=1)


def read_cuts(cuts_ref, base):
    step = pl.program_id(0) + base
    return cuts_ref[step, 0], (cuts_ref[step, 1], cuts_ref[step, 2])


def whole(shape):
    return pl.BlockSpec(shape, lambda *_: (0,) * len(shape))


def once(shape):
    return pl.BlockSpec(shape, lambda *_: (0,) * len(shape), pipeline_mode=pl.Buffered(1))


def rows_spec(width, base=0):
    return pl.BlockSpec((PLACES, width), lambda i, *_: (i + base, 0))


def context_spec(base):
    return pl.BlockSpec((1, TILES, 2 * LANES, 2 * LANES), lambda i, *_: (i + base, 0, 0, 0))


def like(shape, dtype):
    return jax.ShapeDtypeStruct(shape, dtype)


def params(**given):
    return pltpu.CompilerParams(vmem_limit_bytes=58 * 2**20, **given)


MESH = pl.DeviceIdType.MESH
PIECE_ROWS = 256
SMALL_ROWS = 128


def peer(move):
    return (lax.axis_index("dp"), lax.bitwise_xor(lax.axis_index("head"), move))


def meet(peers):
    barrier = pltpu.get_barrier_semaphore()
    for item in peers:
        pl.semaphore_signal(barrier, inc=1, device_id=item, device_id_type=MESH)
    pl.semaphore_wait(barrier, len(peers))


def remote(source, target, send, receive, device):
    return pltpu.make_async_remote_copy(
        src_ref=source, dst_ref=target, send_sem=send, recv_sem=receive,
        device_id=device, device_id_type=MESH,
    )


def plan_pieces(shapes, count):
    pieces = []
    for item, (rows, lanes) in enumerate(shapes):
        height = min(PIECE_ROWS, rows)
        for start in range(0, rows, height):
            pieces.append((item, start, height, padded_rows(height, count), lanes))
    return pieces


def padded_rows(height, count):
    unit = 16 * count
    return -(-height // unit) * unit


def place_on_dp():
    dp = lax.axis_index("dp")
    return dp, lax.rem(dp, 2), dp // 2


def low_peer():
    dp, low, _ = place_on_dp()
    return (dp + 1 - 2 * low, lax.axis_index("head"))


def high_peer(step, group):
    _, low, high = place_on_dp()
    return (lax.rem(high + step, group) * 2 + low, lax.axis_index("head"))


def aligned(index, size):
    return pl.ds(pl.multiple_of(index * size, size), size)


class HighSum:
    def __init__(self, count, mid, part, whole, got, send, receive, slot):
        self.group = count // 2
        self.got = got
        self.mid, self.part, self.whole = mid, part, whole
        self.send, self.receive, self.slot = send, receive, slot
        self.half = mid.shape[0]
        self.size = self.half // self.group

    def copy(self, source, target, slot, device):
        return remote(
            source, target, self.send.at[self.slot + slot], self.receive.at[self.slot + slot], device
        )

    def high(self, step):
        _, _, high = place_on_dp()
        other = lax.rem(high + step, self.group)
        return self.copy(
            self.mid.at[aligned(other, self.size)], self.part.at[step - 1], step - 1,
            high_peer(step, self.group),
        )

    def spot(self):
        dp, low, high = place_on_dp()
        return self.whole.at[aligned(low * self.group + high, self.size)]

    def share(self, step):
        spot = self.spot()
        return self.copy(spot, spot, self.group - 2 + step, high_peer(step, self.group))

    def last(self):
        _, low, _ = place_on_dp()
        here = self.whole.at[aligned(low, self.half)]
        return self.copy(here, self.got, 2 * self.group - 2, low_peer())

    def to_high(self):
        for step in range(1, self.group):
            self.high(step).start()

    def share_high(self):
        _, _, high = place_on_dp()
        total = self.mid[aligned(high, self.size), :].astype(F32)
        for step in range(1, self.group):
            self.high(step).wait()
            total += self.part[step - 1].astype(F32)
        self.spot()[...] = total.astype(BF16)
        for step in range(1, self.group):
            self.share(step).start()

    def share_low(self):
        for step in range(1, self.group):
            self.share(step).wait()
        self.last().start()

    def finish(self):
        _, low, _ = place_on_dp()
        self.last().wait()
        self.whole[aligned(1 - low, self.half), :] = self.got[...]


def high_slots(count):
    return count - 1


class FullSum:
    def __init__(self, count, grad, span, near, far, whole, mid, low, part, got, send, receive, slot):
        self.grad, self.span, self.near, self.far = grad, span, near, far
        self.whole, self.mid, self.low = whole, mid, low
        self.height = far.shape[0]
        self.send, self.receive, self.slot = send, receive, slot
        self.rest = HighSum(count, mid, part, whole, got, send, receive, slot + 4)

    def copy(self, source, target, slot, device):
        return remote(
            source, target, self.send.at[self.slot + slot], self.receive.at[self.slot + slot], device
        )

    def near_copy(self, item):
        return self.copy(
            self.grad.at[1 + 2 * item, self.span], self.near.at[item], item, peer(1)
        )

    def far_copy(self):
        return self.copy(self.whole.at[: self.height], self.far, 2, peer(2))

    def low_copy(self):
        _, low, _ = place_on_dp()
        return self.copy(self.whole.at[aligned(1 - low, self.mid.shape[0])], self.low, 3, low_peer())

    def to_core(self):
        self.near_copy(1).start()
        self.near_copy(0).start()

    def to_far(self):
        self.near_copy(1).wait()
        self.whole[: self.height, :] = (
            self.grad[2, self.span, :].astype(F32) + self.near[1].astype(F32)
        ).astype(BF16)
        self.far_copy().start()

    def to_low(self):
        self.near_copy(0).wait()
        self.far_copy().wait()
        self.whole[: self.height, :] = (
            self.grad[0, self.span, :].astype(F32) + self.near[0].astype(F32)
            + self.far[...].astype(F32)
        ).astype(BF16)
        rows = self.whole.shape[0]
        if rows > self.height:
            self.whole[self.height :, :] = jnp.zeros((rows - self.height, self.whole.shape[1]), BF16)
        self.low_copy().start()

    def to_high(self):
        _, low, _ = place_on_dp()
        self.low_copy().wait()
        half = self.mid.shape[0]
        self.mid[...] = (
            self.whole[aligned(low, half), :].astype(F32) + self.low[...].astype(F32)
        ).astype(BF16)
        self.rest.to_high()


def sum_scratch(pieces, count):
    scratch = []
    for _, _, height, padded, lanes in pieces:
        scratch += [
            pltpu.VMEM((2, height, lanes), BF16), pltpu.VMEM((height, lanes), BF16),
            pltpu.VMEM((padded, lanes), BF16), pltpu.VMEM((padded // 2, lanes), BF16),
            pltpu.VMEM((padded // 2, lanes), BF16),
            pltpu.VMEM((count // 2 - 1, padded // count, lanes), BF16),
            pltpu.VMEM((padded // 2, lanes), BF16),
        ]
    return scratch


def entry_kernel(
    rows, size, x_ref, qkv_ref, small_ref,
    x1_ref, x2_ref, x3_ref, all_qkv_ref, all_small_ref,
    send, receive, local,
):
    head = lax.axis_index("head")
    meet([peer(move) for move in (1, 2, 3)])
    copies = []
    far = remote(qkv_ref, all_qkv_ref.at[2], send.at[0], receive.at[0], peer(2))
    far.start()
    near = remote(qkv_ref, all_qkv_ref.at[1], send.at[1], receive.at[1], peer(1))
    near.start()
    for move in (1, 2, 3):
        copies.append(
            remote(small_ref, all_small_ref.at[move], send.at[1 + move], receive.at[1 + move], peer(move))
        )
        copies[-1].start()
    for move, target in ((2, x2_ref), (3, x3_ref), (1, x1_ref)):
        start = pl.multiple_of(lax.bitwise_xor(head, move) * rows, PLACES)
        copies.append(
            remote(x_ref.at[pl.ds(start, size)], target, send.at[4 + move], receive.at[4 + move], peer(move))
        )
        copies[-1].start()
    mine = pltpu.make_async_copy(qkv_ref, all_qkv_ref.at[0], local.at[0])
    mine.start()
    mine_small = pltpu.make_async_copy(small_ref, all_small_ref.at[0], local.at[1])
    mine_small.start()
    far.wait_recv()
    relay = remote(all_qkv_ref.at[2], all_qkv_ref.at[3], send.at[8], receive.at[8], peer(1))
    relay.start()
    far.wait_send()
    near.wait()
    for copy in copies:
        copy.wait()
    relay.wait()
    mine.wait()
    mine_small.wait()


def entry(block_in, size, qkv, small):
    rows = block_in.shape[0] // 4
    hbm = pl.BlockSpec(memory_space=pl.ANY)
    return pl.pallas_call(
        lambda *refs: entry_kernel(rows, size, *refs),
        in_specs=[hbm] * 3,
        out_specs=[hbm] * 5,
        out_shape=[like((size, LANES), BF16)] * 3 + [
            like((4,) + qkv.shape, BF16), like((4,) + small.shape, F32),
        ],
        scratch_shapes=[
            pltpu.SemaphoreType.DMA((9,)), pltpu.SemaphoreType.DMA((9,)),
            pltpu.SemaphoreType.DMA((2,)),
        ],
        compiler_params=params(collective_id=1, has_side_effects=True),
        name="entry",
    )(block_in, qkv, small)


def front_kernel(base, kept, *refs):
    (cuts_ref, me_ref, x0_ref, x1_ref, x2_ref, x3_ref, cpe_ref, vec_ref, qkv_ref, crpe_ref) = refs[:10]
    (first_ref, hidden_ref, query_ref, value_ref, soft_ref, context_ref, conv_ref, attended_ref,
     mask_ref, grid_ref, out_ref, x_ref) = refs[10 + kept :]
    cut, col_cuts = read_cuts(cuts_ref, base)
    me = me_ref[0]

    @pl.when(pl.program_id(0) == 0)
    def _():
        grid_ref[...] = jnp.zeros_like(grid_ref)

    for move, piece_ref in enumerate((x0_ref, x1_ref, x2_ref, x3_ref)):
        start = pl.multiple_of(LANES * lax.bitwise_xor(me, move), LANES)
        x_ref[:, pl.ds(start, LANES)] = piece_ref[...].astype(F32)
    fill_masks(cut, col_cuts, mask_ref)
    for tile, plane in SMALL_ITEMS:
        spread(
            lambda row: x_ref[SIDE * row : SIDE * row + SIDE, lane(tile)],
            1, cut, mask_ref, grid_ref, plane,
        )
    conv_tiles(SMALL_ITEMS, 1, cut, grid_ref, cpe_ref, 1, out_ref)
    first = x_ref[...] + out_ref[:PLACES, :] + vec_ref[0:1, :]
    first_ref[...] = first
    center = row_mean(first)
    square = row_mean(first * first)
    inverse = lax.rsqrt(square - center * center + EPSILON)
    hidden = ((first - center) * inverse * vec_ref[1:2, :] + vec_ref[2:3, :]).astype(BF16)
    hidden_ref[...] = hidden
    band, side = place_ids(cut, col_cuts)
    ids = 2 * band + side
    sides = [(side == item).astype(F32).astype(BF16) for item in range(2)]
    bands = [(band == item).astype(F32).astype(BF16) for item in range(2)]
    blocks = head_block()
    for tile in range(TILES):
        three = nn(hidden, qkv_ref[lax.bitwise_xor(me, tile)])
        query = (three[:, :LANES] + vec_ref[3:4, lane(tile)]).astype(BF16)
        keys = three[:, LANES : 2 * LANES].astype(BF16).astype(F32)
        value = (three[:, 2 * LANES :] + vec_ref[4:5, lane(tile)]).astype(BF16)
        query_ref[:, lane(tile)] = query
        value_ref[:, lane(tile)] = value
        highest = crop_reduce(ids, keys, jnp.max, -1e30)
        powers = jnp.exp(keys - pick(ids, highest))
        totals = crop_reduce(ids, powers, jnp.sum, 0.0)
        soft = (powers * pick(ids, [1.0 / item for item in totals])).astype(BF16)
        soft_ref[:, lane(tile)] = soft
        context = (tn(both(soft, sides), both(value, bands)) * blocks).astype(BF16)
        context_ref[0, tile] = context
        factor = nn(both(query, sides), context)
        x_ref[:, lane(tile)] = jnp.where(band > 0, factor[:, LANES:], factor[:, :LANES]) * SCALE
    for tile in range(TILES):
        spread(
            lambda row: value_ref[SIDE * row : SIDE * row + SIDE, lane(tile)].astype(F32),
            REACH[tile], cut, mask_ref, grid_ref, 3,
        )
        conv_tiles(((tile, 3),), REACH[tile], cut, grid_ref, crpe_ref, 3, out_ref)
    conv = out_ref[:PLACES, :]
    conv_ref[...] = conv.astype(BF16)
    attended_ref[...] = (x_ref[...] + query_ref[...].astype(F32) * conv).astype(BF16)


def front(cuts, me, x_parts, base, kept, cpe, vec, qkv, crpe):
    count = x_parts[0].shape[0] // PLACES
    total = cuts.shape[0]
    rows = total * PLACES
    wide = rows_spec(D, base)
    flops = 2 * count * PLACES * D * D * 4
    return pl.pallas_call(
        lambda *refs: front_kernel(base, len(kept), *refs),
        grid_spec=pltpu.PrefetchScalarGridSpec(
            num_scalar_prefetch=2,
            grid=(count,),
            in_specs=[rows_spec(LANES)] * 4
            + [whole(cpe.shape), whole(vec.shape), whole(qkv.shape), whole(crpe.shape)]
            + [pl.BlockSpec(memory_space=pl.ANY)] * len(kept),
            out_specs=[wide, wide, wide, wide, wide, context_spec(base), wide, wide],
            scratch_shapes=[
                pltpu.VMEM((2, 7, SIDE, LANES), F32),
                pltpu.VMEM((3 * TILES, GRID_ROWS * SIDE, LANES), F32),
                pltpu.VMEM((PLACES + SIDE, D), F32),
                pltpu.VMEM((PLACES, D), F32),
            ],
        ),
        out_shape=[
            like((rows, D), F32), like((rows, D), BF16), like((rows, D), BF16),
            like((rows, D), BF16), like((rows, D), BF16),
            like((total, TILES, 2 * LANES, 2 * LANES), BF16),
            like((rows, D), BF16), like((rows, D), BF16),
        ],
        input_output_aliases={10 + item: item for item in range(len(kept))},
        compiler_params=params(),
        cost_estimate=pl.CostEstimate(flops=flops * 6, bytes_accessed=count * 10**7, transcendentals=0),
        name="front",
    )(cuts, me, *x_parts, cpe, vec, qkv, crpe, *kept)


def gelu_both(pre):
    power = jnp.exp(pre * pre * -0.5)
    t = 1.0 / (1.0 + jnp.abs(pre) * (0.3275911 * 0.7071067811865476))
    poly = 0.5 * 1.061405429
    for item in (-1.453152027, 1.421413741, -0.284496736, 0.254829592):
        poly = poly * t + 0.5 * item
    tail = poly * t * power
    cdf = jnp.where(pre >= 0.0, 1.0 - tail, tail)
    return pre * cdf, cdf + pre * power * 0.3989422804014327


BLOCK = 512


def middle_kernel(
    count,
    attended_ref, first_ref, cot0_ref, cot1_ref, cot2_ref, cot3_ref, vec_ref, bias_ref,
    proj_ref, fc1_ref, fc2_ref,
    out0_ref, out1_ref, out2_ref, out3_ref, second_grad_ref, att_grad_ref, fc_mid_ref,
    proj_grad_ref, sum_ref, bias_grad_ref,
    cot_ref, hat_ref, inverse_ref, hidden_ref, total_ref, back_ref, active_ref, pre_grad_ref,
    grads_ref, near_ref, far_ref, own_ref, low_ref, send, receive,
):
    me = lax.axis_index("head")
    step = pl.program_id(0)
    rows = attended_ref.shape[0]
    blocks = rows // BLOCK
    _, low, _ = place_on_dp()
    half = low_ref.shape[1]

    def near(item, kind):
        return remote(
            grads_ref.at[2 * item, kind], near_ref.at[item, kind], send.at[2 * item + kind],
            receive.at[2 * item + kind], peer(1),
        )

    def far(kind):
        return remote(
            grads_ref.at[1, kind], far_ref.at[kind], send.at[4 + kind], receive.at[4 + kind], peer(2)
        )

    def to_low(kind):
        return remote(
            own_ref.at[kind, aligned(1 - low, half)], low_ref.at[kind], send.at[6 + kind],
            receive.at[6 + kind], low_peer(),
        )

    def part(index):
        return aligned(index, BLOCK)

    @pl.when(step == 0)
    def _():
        meet([peer(1), peer(2), low_peer()])
        own_ref[...] = jnp.zeros_like(own_ref)
        sum_ref[...] = jnp.zeros_like(sum_ref)
        for move, piece_ref in enumerate((cot0_ref, cot1_ref, cot2_ref, cot3_ref)):
            cot_ref[:, aligned(lax.bitwise_xor(me, move), LANES)] = piece_ref[...]

        def enter(index, carry):
            now = part(index)
            second = first_ref[now, :] + vec_ref[0:1, :]
            for tile in range(TILES):
                second += nn(attended_ref[now, lane(tile)], proj_ref[lax.bitwise_xor(me, tile)])
            center = row_mean(second)
            square = row_mean(second * second)
            inverse = lax.rsqrt(square - center * center + EPSILON)
            hat = (second - center) * inverse
            hidden_ref[now, :] = (hat * vec_ref[1:2, :] + vec_ref[2:3, :]).astype(BF16)
            hat_ref[now, :] = hat
            inverse_ref[now, :] = jnp.broadcast_to(inverse, (BLOCK, LANES))
            total_ref[now, :] = second + vec_ref[3:4, :]
            back_ref[now, :] = jnp.zeros((BLOCK, D), F32)
            sum_ref[0:1, :] += jnp.sum(cot_ref[now, :].astype(F32), axis=0, keepdims=True)
            return carry

        lax.fori_loop(0, blocks, enter, 0)

    bias_grad_ref[0] = jnp.zeros_like(bias_grad_ref[0])

    def chunk(index, carry):
        now = part(index)
        pre = nn(hidden_ref[now, :], fc1_ref[0]) + bias_ref[0]
        active, slope = gelu_both(pre)
        active = active.astype(BF16)
        active_ref[now, :] = active
        total_ref[now, :] += nn(active, fc2_ref[0])
        pre_grad_f = nt(cot_ref[now, :], fc2_ref[0]) * slope
        pre_grad = pre_grad_f.astype(BF16)
        pre_grad_ref[now, :] = pre_grad
        back_ref[now, :] += nt(pre_grad, fc1_ref[0])
        bias_grad_ref[0] += jnp.sum(pre_grad_f, axis=0, keepdims=True)
        return carry

    lax.fori_loop(0, blocks, chunk, 0)
    grads_ref[step, 0] = tn(hidden_ref[...], pre_grad_ref[...]).astype(BF16)
    grads_ref[step, 1] = tn(active_ref[...], cot_ref[...]).astype(BF16)

    @pl.when(step == 0)
    def _():
        for kind in range(2):
            near(0, kind).start()

    @pl.when(step == 1)
    def _():
        for kind in range(2):
            near(0, kind).wait()
            grads_ref[1, kind] = (
                grads_ref[1, kind].astype(F32) + near_ref[0, kind].astype(F32)
            ).astype(BF16)
            far(kind).start()

    @pl.when(step == 2)
    def _():
        for kind in range(2):
            near(1, kind).start()

    @pl.when(step == 3)
    def _():
        for kind in range(2):
            near(1, kind).wait()
            far(kind).wait()
            own_ref[kind, :D, :] = (
                grads_ref[3, kind].astype(F32) + near_ref[1, kind].astype(F32)
                + far_ref[kind].astype(F32)
            ).astype(BF16)
            to_low(kind).start()

        def leave(index, carry):
            now = part(index)
            for move, piece_ref in enumerate((out0_ref, out1_ref, out2_ref, out3_ref)):
                piece_ref[now, :] = total_ref[now, aligned(lax.bitwise_xor(me, move), LANES)].astype(BF16)
            hat = hat_ref[now, :]
            norm_grad = back_ref[now, :]
            weighted = norm_grad * vec_ref[1:2, :]
            second_grad = cot_ref[now, :].astype(F32) + inverse_ref[now, 0:1] * (
                weighted - row_mean(weighted) - hat * row_mean(weighted * hat)
            )
            second_grad_ref[now, :] = second_grad
            second_low = second_grad.astype(BF16)
            hidden_ref[now, :] = second_low
            for tile in range(TILES):
                att_grad_ref[now, lane(tile)] = nt(
                    second_low, proj_ref[lax.bitwise_xor(me, tile)]
                ).astype(BF16)
            sum_ref[1:2, :] += jnp.sum(norm_grad * hat, axis=0, keepdims=True)
            sum_ref[2:3, :] += jnp.sum(norm_grad, axis=0, keepdims=True)
            sum_ref[3:4, :] += jnp.sum(second_low.astype(F32), axis=0, keepdims=True)
            return carry

        lax.fori_loop(0, blocks, leave, 0)
        for tile in range(TILES):
            proj_grad_ref[lax.bitwise_xor(me, tile)] = tn(
                attended_ref[:, lane(tile)], hidden_ref[...]
            ).astype(BF16)
        for kind in range(2):
            to_low(kind).wait()
            fc_mid_ref[kind] = (
                own_ref[kind, aligned(low, half), :].astype(F32) + low_ref[kind].astype(F32)
            ).astype(BF16)


def middle(attended, first, cot_parts, vec, bias, proj, fc1, fc2):
    rows = attended.shape[0]
    count = lax.axis_size("dp")
    padded = padded_rows(D, count)
    shard = pl.BlockSpec((1, D, D), lambda i: (3 - i, 0, 0))
    piece = once((rows, LANES))
    wide = once((rows, D))
    line = pl.BlockSpec((1, 1, D), lambda i: (3 - i, 0, 0))
    return pl.pallas_call(
        lambda *refs: middle_kernel(count, *refs),
        grid=(4,),
        in_specs=[
            wide, wide, piece, piece, piece, piece, whole(vec.shape), line, once(proj.shape),
            shard, shard,
        ],
        out_specs=[
            piece, piece, piece, piece, wide, wide, once((2, padded // 2, D)), once(proj.shape),
            once((8, D)), line,
        ],
        out_shape=[like((rows, LANES), BF16)] * 4 + [
            like((rows, D), F32), like((rows, D), BF16), like((2, padded // 2, D), BF16),
            like(proj.shape, BF16), like((8, D), F32), like(bias.shape, F32),
        ],
        scratch_shapes=[
            pltpu.VMEM((rows, D), BF16), pltpu.VMEM((rows, D), F32),
            pltpu.VMEM((rows, LANES), F32),
            pltpu.VMEM((rows, D), BF16), pltpu.VMEM((rows, D), F32),
            pltpu.VMEM((rows, D), F32), pltpu.VMEM((rows, D), BF16),
            pltpu.VMEM((rows, D), BF16),
            pltpu.VMEM((4, 2, D, D), BF16), pltpu.VMEM((2, 2, D, D), BF16),
            pltpu.VMEM((2, D, D), BF16), pltpu.VMEM((2, padded, D), BF16),
            pltpu.VMEM((2, padded // 2, D), BF16),
            pltpu.SemaphoreType.DMA((8,)), pltpu.SemaphoreType.DMA((8,)),
        ],
        compiler_params=params(collective_id=2, has_side_effects=True),
        cost_estimate=pl.CostEstimate(flops=rows * D * D * 60, bytes_accessed=3 * 10**7, transcendentals=0),
        name="middle",
    )(attended, first, *cot_parts, vec, bias, proj, fc1, fc2)


def back_kernel(
    cuts_ref, me_ref, grad_ref, query_ref, value_ref, soft_ref, context_ref, conv_ref, hidden_ref,
    crpe_ref,
    three_ref, qkv_out_ref, crpe_sum_ref, sum_ref,
    mask_ref, grid_ref, out_ref, other_ref, value_part_ref, qkv_grad_ref,
):
    cut, col_cuts = read_cuts(cuts_ref, 0)
    me = me_ref[0]

    @pl.when(pl.program_id(0) == 0)
    def _():
        grid_ref[...] = jnp.zeros_like(grid_ref)
        other_ref[...] = jnp.zeros_like(other_ref)
        qkv_grad_ref[...] = jnp.zeros_like(qkv_grad_ref)
        crpe_sum_ref[...] = jnp.zeros_like(crpe_sum_ref)
        sum_ref[...] = jnp.zeros_like(sum_ref)

    fill_masks(cut, col_cuts, mask_ref)
    band, side = place_ids(cut, col_cuts)
    ids = 2 * band + side
    sides = [(side == item).astype(F32).astype(BF16) for item in range(2)]
    bands = [(band == item).astype(F32).astype(BF16) for item in range(2)]
    blocks = head_block() * SCALE
    for tile in range(TILES):
        grad = grad_ref[:, lane(tile)]
        query = query_ref[:, lane(tile)]
        value = value_ref[:, lane(tile)]
        soft = soft_ref[:, lane(tile)]
        context = context_ref[0, tile]
        grad_f = grad.astype(F32)
        grad_bands = both(grad, bands)
        context_grad = (tn(both(query, sides), grad_bands) * blocks).astype(BF16)
        part = nt(grad_bands, context)
        part = jnp.where(side > 0, part[:, LANES:], part[:, :LANES])
        query_grad = (
            part * SCALE + grad_f * conv_ref[:, lane(tile)].astype(F32)
        ).astype(BF16)
        soft_grad = nt(both(value, bands), context_grad)
        soft_grad = jnp.where(side > 0, soft_grad[:, LANES:], soft_grad[:, :LANES])
        soft_f = soft.astype(F32)
        inner = crop_reduce(ids, soft_f * soft_grad, jnp.sum, 0.0)
        keys_grad = (soft_f * (soft_grad - pick(ids, inner))).astype(BF16)
        value_part = nn(both(soft, sides), context_grad)
        value_part_ref[:, lane(tile)] = jnp.where(
            band > 0, value_part[:, LANES:], value_part[:, :LANES]
        )
        three_ref[tile, :, :LANES] = query_grad
        three_ref[tile, :, LANES : 2 * LANES] = keys_grad
        sum_ref[0:1, lane(tile)] += jnp.sum(query_grad.astype(F32), axis=0, keepdims=True)
    other_ref[:PLACES, :] = value_ref[...].astype(F32)
    for tile in range(TILES):

        def read_row(row):
            part = pl.ds(SIDE * row, SIDE)
            return grad_ref[part, lane(tile)].astype(F32) * query_ref[part, lane(tile)].astype(F32)

        spread(read_row, REACH[tile], cut, mask_ref, grid_ref, 3)
        conv_back_tiles(
            ((tile, 3),), REACH[tile], cut, grid_ref, crpe_ref, 3, other_ref, out_ref, crpe_sum_ref
        )
    hidden = hidden_ref[...]
    for tile in range(TILES):
        value_grad = (value_part_ref[:, lane(tile)] + out_ref[:PLACES, lane(tile)]).astype(BF16)
        three_ref[tile, :, 2 * LANES :] = value_grad
        sum_ref[1:2, lane(tile)] += jnp.sum(value_grad.astype(F32), axis=0, keepdims=True)
        qkv_grad_ref[lax.bitwise_xor(me, tile)] += tn(hidden, three_ref[tile])

    @pl.when(pl.program_id(0) == pl.num_programs(0) - 1)
    def _():
        qkv_out_ref[...] = qkv_grad_ref[...].astype(BF16)


def back(cuts, me, grad, query, value, soft, context, conv, hidden, crpe):
    rows = grad.shape[0]
    count = rows // PLACES
    wide = rows_spec(D)
    shards = (4, D, 3 * LANES)
    return pl.pallas_call(
        lambda *refs: back_kernel(*refs),
        grid_spec=pltpu.PrefetchScalarGridSpec(
            num_scalar_prefetch=2,
            grid=(count,),
            in_specs=[wide, wide, wide, wide, context_spec(0), wide, wide, whole(crpe.shape)],
            out_specs=[
                pl.BlockSpec((TILES, PLACES, 3 * LANES), lambda i, *_: (0, i, 0)),
                once(shards), whole((49, 8, D)), whole((8, D)),
            ],
            scratch_shapes=[
                pltpu.VMEM((2, 7, SIDE, LANES), F32),
                pltpu.VMEM((7, GRID_ROWS * SIDE, LANES), F32),
                pltpu.VMEM((PLACES + SIDE, D), F32),
                pltpu.VMEM((PLACES + SIDE, D), F32),
                pltpu.VMEM((PLACES, D), F32),
                pltpu.VMEM(shards, F32),
            ],
        ),
        out_shape=[
            like((TILES, rows, 3 * LANES), BF16), like(shards, BF16), like((49, 8, D), F32),
            like((8, D), F32),
        ],
        compiler_params=params(),
        cost_estimate=pl.CostEstimate(
            flops=rows * D * D * 64, bytes_accessed=count * 10**7, transcendentals=0
        ),
        name="back",
    )(cuts, me, grad, query, value, soft, context, conv, hidden, crpe)


def step_masks(cut, col_cuts):
    place = lax.broadcasted_iota(jnp.int32, (PLACES, LANES), 0)
    row = lax.shift_right_logical(place, 4)
    col = lax.bitwise_and(place, 15)
    col_cut = jnp.where(row >= cut, col_cuts[1], col_cuts[0])
    rows = {
        1: (row < SIDE - 1) & (row + 1 != cut),
        -1: (row > 0) & (row != cut),
    }
    cols = {
        1: (col < SIDE - 1) & (col + 1 != col_cut),
        -1: (col > 0) & (col != col_cut),
    }
    return [
        {key: jnp.where(mask, 1.0, 0.0).astype(F32) for key, mask in masks.items()}
        for masks in (rows, cols)
    ]


def shift_rows(values, step):
    if step == 0:
        return values
    zero = jnp.zeros((SIDE, values.shape[1]), values.dtype)
    if step > 0:
        return jnp.concatenate([values[SIDE:], zero], axis=0)
    return jnp.concatenate([zero, values[:-SIDE]], axis=0)


def shift_cols(values, masks, step):
    if step == 0:
        return values
    return pltpu.roll(values, (-step) % PLACES, 0) * masks[step]


LAST_ROWS = 16
STAGES = {"core": 0, "far": 1, "low": 3, "high": 4, "share": 5, "last": 6}
FC_STAGES = {"high": 0, "share": 2, "last": 4}


def tail_kernel(
    count, pieces,
    cuts_ref, x0_ref, x1_ref, x2_ref, x3_ref, three_ref, first_ref, second_grad_ref, vec_ref, qkv_ref,
    cpe_ref, fc_mid_in, qkv_grad_in, proj_grad_in, small_in,
    out0_ref, out1_ref, out2_ref, out3_ref, fc1_own_ref, fc2_own_ref, qkv_own_ref, proj_own_ref,
    small_own_ref, last_own_ref,
    x_ref, gone_ref, cpe_sum_ref, sum_ref, fc_part_ref, fc_whole_ref, fc_got_ref, mine_ref, first_got_ref,
    total_ref, second_got_ref, piece_send, piece_receive, send, receive, last_send, last_receive,
    fc_mid_ref, qkv_grad_ref, proj_grad_ref, small_ref, *buffers,
):
    me = lax.axis_index("head")
    dp = lax.axis_index("dp")
    step = pl.program_id(0)
    steps = pl.num_programs(0)
    slots = high_slots(count)
    fc_sums = [
        HighSum(
            count, fc_mid_ref.at[kind], fc_part_ref.at[kind], fc_whole_ref.at[kind],
            fc_got_ref.at[kind], send, receive, kind * slots,
        )
        for kind in range(2)
    ]
    sources = (qkv_grad_ref, proj_grad_ref, small_ref)
    targets = (qkv_own_ref, proj_own_ref, small_own_ref)
    sums = []
    for number, (item, start, height, padded, lanes) in enumerate(pieces):
        near, far, own, mid, low, part, got = buffers[7 * number : 7 * number + 7]
        sums.append(
            FullSum(
                count, sources[item], pl.ds(start, height), near, far, own, mid, low, part, got, send,
                receive, 2 * slots + number * (slots + 4),
            )
        )

    def piece_copy(index, move):
        target = (out1_ref, out2_ref, out3_ref)[move - 1]
        return remote(
            gone_ref.at[index, move - 1], target.at[aligned(index, PLACES)],
            piece_send.at[index, move - 1], piece_receive.at[index, move - 1], peer(move),
        )

    def first_copy(move):
        return remote(
            mine_ref.at[move], first_got_ref.at[move - 1], last_send.at[move - 1],
            last_receive.at[move - 1], peer(move),
        )

    def second_copy(hop):
        return remote(
            total_ref, second_got_ref.at[hop - 1], last_send.at[2 + hop], last_receive.at[2 + hop],
            (lax.rem(dp + hop, count), me),
        )

    @pl.when(step == 0)
    def _():
        meet(
            [peer(1), peer(2), peer(3)] + [(lax.rem(dp + hop, count), me) for hop in range(1, count)]
        )
        fc_mid_ref[...] = fc_mid_in[...]
        qkv_grad_ref[...] = qkv_grad_in[...]
        proj_grad_ref[...] = proj_grad_in[...]
        small_ref[...] = small_in[...]
        cpe_sum_ref[...] = jnp.zeros_like(cpe_sum_ref)
        sum_ref[...] = jnp.zeros_like(sum_ref)

    def at(when, action, items):
        @pl.when(step == when)
        def _():
            for item in items:
                action(item)

    at(STAGES["core"], lambda item: item.to_core(), sums)
    at(FC_STAGES["high"], lambda item: item.to_high(), fc_sums)
    at(STAGES["far"], lambda item: item.to_far(), sums)
    at(FC_STAGES["share"], lambda item: item.share_high(), fc_sums)
    at(STAGES["low"], lambda item: item.to_low(), sums)
    at(STAGES["high"], lambda item: item.to_high(), sums)
    at(FC_STAGES["last"], lambda item: item.share_low(), fc_sums)
    at(STAGES["share"], lambda item: item.rest.share_high(), sums)
    at(STAGES["last"], lambda item: item.rest.share_low(), sums)

    norm_grad = nt(three_ref[0], qkv_ref[lax.bitwise_xor(me, 0)])
    for tile in range(1, TILES):
        norm_grad += nt(three_ref[tile], qkv_ref[lax.bitwise_xor(me, tile)])
    first = first_ref[...]
    center = row_mean(first)
    square = row_mean(first * first)
    inverse = lax.rsqrt(square - center * center + EPSILON)
    hat = (first - center) * inverse
    weighted = norm_grad * vec_ref[1:2, :]
    first_grad = second_grad_ref[...] + inverse * (
        weighted - row_mean(weighted) - hat * row_mean(weighted * hat)
    )
    sum_ref[0:1, :] += jnp.sum(first_grad, axis=0, keepdims=True)
    sum_ref[1:2, :] += jnp.sum(norm_grad * hat, axis=0, keepdims=True)
    sum_ref[2:3, :] += jnp.sum(norm_grad, axis=0, keepdims=True)
    for move, piece_ref in enumerate((x0_ref, x1_ref, x2_ref, x3_ref)):
        x_ref[:, aligned(lax.bitwise_xor(me, move), LANES)] = piece_ref[...].astype(F32)
    rows, cols = step_masks(cuts_ref[step, 0], (cuts_ref[step, 1], cuts_ref[step, 2]))
    results = []
    for tile in range(TILES):
        field = first_grad[:, LANES * tile : LANES * (tile + 1)]
        other = x_ref[:, lane(tile)]
        others = {0: other, 1: shift_rows(other * rows[1], -1), -1: shift_rows(other * rows[-1], 1)}
        moved = [shift_cols(field, cols, col) for col in (-1, 0, 1)]
        result = field
        for row in (-1, 0, 1):
            line = None
            for col in (-1, 0, 1):
                tap = (1 - row) * 3 + 1 - col
                wide_tap = jnp.broadcast_to(cpe_ref[tap : tap + 1, lane(tile)], (PLACES, LANES))
                term = wide_tap * moved[col + 1]
                line = term if line is None else line + term
                product = others[row] * moved[col + 1]
                cpe_sum_ref[tap, :, lane(tile)] += jnp.sum(product.reshape(PLACES // 8, 8, LANES), axis=0)
            line = shift_rows(line, row)
            result = result + (line * rows[row] if row else line)
        results.append(result)
    result = jnp.concatenate(results, axis=1)
    x_ref[...] = result
    out0_ref[...] = x_ref[:, aligned(me, LANES)].astype(BF16)
    for move in (1, 2, 3):
        gone_ref[step, move - 1] = x_ref[:, aligned(lax.bitwise_xor(me, move), LANES)].astype(BF16)
    for move in (2, 3, 1):
        piece_copy(step, move).start()

    @pl.when(step == steps - 1)
    def _():
        sum_ref[3:12, :] = jnp.sum(cpe_sum_ref[...], axis=1)
        for move in range(4):
            mine_ref[move] = sum_ref[:, aligned(lax.bitwise_xor(me, move), LANES)]
        for move in (1, 2, 3):
            first_copy(move).start()
        for item in fc_sums:
            item.finish()
        fc1_own_ref[...] = fc_whole_ref[0, :D, :].astype(F32)
        fc2_own_ref[...] = fc_whole_ref[1, :D, :].astype(F32)
        total = mine_ref[0]
        for move in (1, 2, 3):
            first_copy(move).wait()
            total += first_got_ref[move - 1]
        total_ref[...] = total
        for hop in range(1, count):
            second_copy(hop).start()
        for piece, item in zip(pieces, sums):
            item.rest.finish()
            targets[piece[0]][piece[1] : piece[1] + piece[2], :] = item.whole[: piece[2], :].astype(F32)
        for hop in range(1, count):
            second_copy(hop).wait()
            total += second_got_ref[hop - 1]
        last_own_ref[...] = total

        def settle(index, carry):
            for move in (1, 2, 3):
                piece_copy(index, move).wait()
            return carry

        lax.fori_loop(0, steps, settle, 0)


def tail(cuts, x_parts, three, first, second_grad, vec, qkv, cpe, fc_mid, qkv_grad, proj_grad, small):
    rows = first.shape[0]
    canvases = rows // PLACES
    count = lax.axis_size("dp")
    segments = [qkv_grad, proj_grad, small]
    pieces = plan_pieces([item.shape[1:] for item in segments], count)
    slots = high_slots(count)
    wide = rows_spec(D)
    piece = rows_spec(LANES)
    hbm = pl.BlockSpec(memory_space=pl.ANY)
    half = fc_mid.shape[1]
    group = count // 2
    total_slots = 2 * slots + len(pieces) * (slots + 4)
    last = (LAST_ROWS, LANES)
    return pl.pallas_call(
        lambda *refs: tail_kernel(count, pieces, *refs),
        grid=(canvases,),
        in_specs=[pl.BlockSpec(memory_space=pltpu.SMEM)] + [piece] * 4 + [
            pl.BlockSpec((TILES, PLACES, 3 * LANES), lambda i: (0, i, 0)), wide, wide,
            once(vec.shape), once(qkv.shape), once(cpe.shape), once(fc_mid.shape),
        ] + [once(item.shape) for item in segments],
        out_specs=[piece, hbm, hbm, hbm, once((D, D)), once((D, D))]
        + [once(item.shape[1:]) for item in segments] + [once(last)],
        out_shape=[like((rows, LANES), BF16)] * 4 + [like((D, D), F32)] * 2
        + [like(item.shape[1:], F32) for item in segments] + [like(last, F32)],
        scratch_shapes=[
            pltpu.VMEM((PLACES, D), F32), pltpu.VMEM((canvases, 3, PLACES, LANES), BF16),
            pltpu.VMEM((9, 8, D), F32), pltpu.VMEM((LAST_ROWS, D), F32),
            pltpu.VMEM((2, group - 1, half // group, D), BF16), pltpu.VMEM((2, 2 * half, D), BF16),
            pltpu.VMEM((2, half, D), BF16),
            pltpu.VMEM((4,) + last, F32), pltpu.VMEM((3,) + last, F32), pltpu.VMEM(last, F32),
            pltpu.VMEM((count - 1,) + last, F32),
            pltpu.SemaphoreType.DMA((canvases, 3)), pltpu.SemaphoreType.DMA((canvases, 3)),
            pltpu.SemaphoreType.DMA((total_slots,)), pltpu.SemaphoreType.DMA((total_slots,)),
            pltpu.SemaphoreType.DMA((2 + count,)), pltpu.SemaphoreType.DMA((2 + count,)),
        ] + [pltpu.VMEM(item.shape, BF16) for item in [fc_mid] + segments]
        + sum_scratch(pieces, count),
        compiler_params=params(collective_id=3, has_side_effects=True),
        cost_estimate=pl.CostEstimate(
            flops=rows * D * D * 12, bytes_accessed=canvases * 3 * 10**6, transcendentals=0
        ),
        name="tail",
    )(cuts, *x_parts, three, first, second_grad, vec, qkv, cpe, fc_mid, *segments)


def collect_kernel(me_ref, *refs):
    out_ref = refs[-1]
    for item, piece_ref in enumerate(refs[:-1]):

        @pl.when(pl.program_id(0) == item)
        def _():
            out_ref[...] = piece_ref[...].astype(F32)


def collect(me, pieces):
    parts = len(pieces[0])
    rows = pieces[0][0].shape[0]
    return pl.pallas_call(
        collect_kernel,
        grid_spec=pltpu.PrefetchScalarGridSpec(
            num_scalar_prefetch=1,
            grid=(4 * parts,),
            in_specs=[once((rows, LANES))] * (4 * parts),
            out_specs=pl.BlockSpec(
                (rows, LANES),
                lambda i, me: (lax.bitwise_xor(me[0], i // parts) * parts + i % parts, 0),
            ),
        ),
        out_shape=like((4 * parts * rows, LANES), F32),
        compiler_params=params(),
        name="collect",
    )(me, *[piece for move in pieces for piece in move])


HALVES = 2


def find_cuts(crop_ids):
    cut = jnp.sum((crop_ids[:, :, 0] < 2).astype(jnp.int32), axis=1)
    upper = jnp.sum((crop_ids[:, 0, :] == 0).astype(jnp.int32), axis=1)
    lower = jnp.sum((crop_ids[:, SIDE - 1, :] == 2).astype(jnp.int32), axis=1)
    return jnp.stack([cut, upper, lower], axis=1)


def reach_mask():
    head = jnp.arange(D, dtype=jnp.int32) // HEAD_DIM
    reach = 1 + (head >= 2).astype(jnp.int32) + (head >= 5).astype(jnp.int32)
    taps = jnp.arange(49, dtype=jnp.int32)
    ring = jnp.maximum(jnp.abs(taps // 7 - 3), jnp.abs(taps % 7 - 3))
    return (ring[:, None] <= reach[None, :]).astype(F32)


def forward_parts(me, cuts, x_halves, small, qkv):
    zero = jnp.zeros((D,), F32)
    vec = jnp.stack([small[58], small[59], small[60], small[61], small[62], zero, zero, zero])
    crpe = jnp.broadcast_to((small[9:58] * reach_mask())[:, None, :], (49, 8, D))
    cpe = jnp.broadcast_to(small[:9][:, None, :], (9, 8, D))
    kept = ()
    base = 0
    for x_parts in x_halves:
        kept = front(cuts, me, x_parts, base, kept, cpe, vec, qkv, crpe)
        base += x_parts[0].shape[0] // PLACES
    return kept, vec, crpe, cpe


def middle_parts(kept, cot_parts, small, bias, proj, fc1, fc2):
    zero = jnp.zeros((D,), F32)
    vec = jnp.stack([small[63], small[64], small[65], small[66], zero, zero, zero, zero])
    return middle(kept[7], kept[0], cot_parts, vec, bias, proj, fc1, fc2)


def body(
    block_in, crop_ids, cotangent, cpe_kernel, cpe_bias, norm1_gain, norm1_shift, qkv_weight,
    qv_bias, crpe_kernel, proj_weight, proj_bias, norm2_gain, norm2_shift, fc1_weight, fc1_bias,
    fc2_weight, fc2_bias,
):
    head = lax.axis_index("head")
    me = head.reshape(1).astype(jnp.int32)
    canvases = crop_ids.shape[0] // 4
    rows = canvases * PLACES
    cuts = find_cuts(lax.dynamic_slice_in_dim(crop_ids, head * canvases, canvases, 0))

    def swap(values, move):
        return lax.ppermute(values, "head", [(item, item ^ move) for item in range(4)])

    def take(values, move, part, parts):
        size = rows // parts
        start = lax.bitwise_xor(head, move) * rows + part * size
        return lax.dynamic_slice_in_dim(values, start, size, 0)

    def bring(values, part, parts):
        pieces = [take(values, move, part, parts) for move in range(4)]
        return [pieces[0]] + [swap(pieces[move], move) for move in (1, 2, 3)]

    def gather(shard):
        far = swap(shard, 2)
        near = swap(jnp.stack([shard, far]), 1)
        return jnp.stack([shard, near[0], far, near[1]])

    packed = jnp.concatenate([
        cpe_kernel, crpe_kernel, cpe_bias[None], norm1_gain[None], norm1_shift[None], qv_bias,
        proj_bias[None], norm2_gain[None], norm2_shift[None], fc2_bias[None],
        fc1_bias.reshape(4, LANES), jnp.zeros((1, LANES), BF16),
    ]).astype(F32)
    part_rows = rows // HALVES
    order = lax.bitwise_xor(head, jnp.arange(4, dtype=jnp.int32))
    x1, x2, x3, qkv, small_all = entry(
        block_in, part_rows, qkv_weight.reshape(D, 3 * LANES), packed
    )
    x_halves = [[take(block_in, 0, 0, HALVES), x1, x2, x3]]
    block_in, proj_weight, cotangent, fc1_weight, fc2_weight, x_halves = lax.optimization_barrier(
        (block_in, proj_weight, cotangent, fc1_weight, fc2_weight, x_halves)
    )
    x_halves += [bring(block_in, part, HALVES) for part in range(1, HALVES)]
    cot_parts = bring(cotangent, 0, 1)
    proj = gather(proj_weight)
    fc1 = gather(fc1_weight)
    fc2 = gather(fc2_weight)
    small = jnp.take(small_all[:, :67], order, axis=0).transpose(1, 0, 2).reshape(67, D)
    bias = small_all[:, 67:71].reshape(4, 1, D)

    kept, vec, crpe, cpe = forward_parts(me, cuts, x_halves, small, qkv)
    first, hidden, query, value, soft, context, conv, attended = kept
    results = middle_parts(kept, cot_parts, small, bias, proj, fc1, fc2)
    second_grad, att_grad, fc_mid, proj_grad, sums2, bias_grad = results[4:]
    out_parts = [[results[0]]] + [[swap(results[move], move)] for move in (1, 2, 3)]
    three, qkv_grad, crpe_sum, sums1 = back(
        cuts, me, att_grad, query, value, soft, context, conv, hidden, crpe
    )
    small_grad = jnp.concatenate([
        jnp.sum(crpe_sum, axis=1) * reach_mask(), sums1[0:2], sums2[3:4], sums2[1:3], sums2[0:1],
    ])
    small_rows = small_grad.shape[0]
    small_grad = jnp.concatenate([
        jnp.take(small_grad.reshape(-1, 4, LANES).transpose(1, 0, 2), order, axis=0),
        bias_grad.reshape(4, 4, LANES), jnp.zeros((4, SMALL_ROWS - small_rows - 4, LANES), F32),
    ], axis=1).astype(BF16)
    x_parts = [jnp.concatenate([item[move] for item in x_halves]) for move in range(4)]
    results = tail(
        cuts, x_parts, three, first, second_grad, vec, qkv, small[:9], fc_mid, qkv_grad, proj_grad,
        small_grad,
    )
    fc1_own, fc2_own, qkv_own, proj_own, small_own, last_own = results[4:]
    return (
        collect(me, out_parts), collect(me, [[item] for item in results[:4]]),
        last_own[3:12], last_own[0], last_own[1], last_own[2],
        qkv_own.reshape(D, 3, LANES), small_own[49:51], small_own[:49],
        proj_own, small_own[51], small_own[52], small_own[53],
        fc1_own, small_own[55:59].reshape(D), fc2_own, small_own[54],
    )


def solution(mesh):
    return jax.shard_map(
        body,
        mesh=mesh,
        in_specs=(
            P("dp", "head"), P("dp", None, None), P("dp", "head"), P(None, "head"), P("head"),
            P("head"), P("head"), P(None, None, "head"), P(None, "head"), P(None, "head"),
            P("head", None), P("head"), P("head"), P("head"), P(None, "head"), P("head"),
            P("head", None), P("head"),
        ),
        out_specs=(
            P("dp", "head"), P("dp", "head"), P(None, "head"), P("head"), P("head"), P("head"),
            P(None, None, "head"), P(None, "head"), P(None, "head"), P("head", None), P("head"),
            P("head"), P("head"), P(None, "head"), P("head"), P("head", None), P("head"),
        ),
        check_vma=False,
    )
```

time: 540 us -> 361 us (0.67)
  waiting for transfers between devices: 178 us -> 7.54 us
  Pallas kernels: 225 us -> 279 us
  blocking collectives: 20.7 us -> 0 us
  other arithmetic: 38.2 us -> 23.5 us
  between operations: 14.9 us -> 1.17 us
  starting transfers between devices: 22.5 us -> 10.2 us
    psum x2 -> x0, waiting for transfers between devices: 94.5 us -> none  [the longest x1 77.6 us: body(): early = lax.psum(reduce_head(early).astype(BF16), 'dp')]
    ppermute x32 -> x15, waiting for transfers between devices: 83.8 us -> 7.54 us  [swap(): lax.ppermute(values, 'head', [(item, item ^ move) for item in range(4)])]
    pallas_call x3 -> x4, Pallas kernels: 150 us -> 219 us  [the longest x1 71.6 us: tail(): pl.pallas_call(lambda *refs: tail_kernel(count, pieces, *refs), grid=(can...]
    all_gather x1 -> x0, blocking collectives: 20.7 us -> none  [body(): small = lax.all_gather(packed, 'head', axis=1, tiled=True)]
    pallas_call x2, Pallas kernels: 65.9 us -> 51.6 us  [front(): pl.pallas_call(lambda *refs: front_kernel(base, len(kept), *refs), grid_s...]
    ppermute x32 -> x15, starting transfers between devices: 22.5 us -> 10.2 us  [swap(): lax.ppermute(values, 'head', [(item, item ^ move) for item in range(4)])]
    convert_element_type x6 -> x0, other arithmetic: 10.6 us -> none  [the longest x1 3.85 us: body(): early = lax.psum(reduce_head(early).astype(BF16), 'dp')]
    concatenate x0 -> x5, other arithmetic: none -> 6.97 us  [the longest x4 6.23 us: body(): jnp.concatenate([item[move] for item in x_halves])]
  transfers between devices with their start and end apart: 34 -> 15, of which waited for: 11 -> 1; matrix products, arithmetic and copies ran while one was open for 10% -> 12% of each run, Pallas kernels for 29% -> 35%
where the time goes in v3:
time: 361 us; the launch traced here: 360 us
  Pallas kernels  279 us (77%)
  local copies, waits for them, and re-layouts  38.8 us (11%)
  other arithmetic  23.5 us (7%)
  starting transfers between devices  10.2 us (3%)
  waiting for transfers between devices  7.54 us (2%)
    pallas_call x1, Pallas kernels, tail(): pl.pallas_call(lambda *refs: tail_kernel(count, pieces, *refs), grid=(can...  71.6 us
    pallas_call x1, Pallas kernels, middle(): pl.pallas_call(lambda *refs: middle_kernel(count, *refs), grid=(4,), in_s...  68.1 us
    pallas_call x1, Pallas kernels, back(): pl.pallas_call(lambda *refs: back_kernel(*refs), grid_spec=pltpu.Prefetch...  53.4 us
    pallas_call x2, Pallas kernels, front(): pl.pallas_call(lambda *refs: front_kernel(base, len(kept), *refs), grid_s...  51.6 us
    pallas_call x1, Pallas kernels, entry(): pl.pallas_call(lambda *refs: entry_kernel(rows, size, *refs), in_specs=[h...  25.9 us
    ppermute x15, starting transfers between devices, swap(): lax.ppermute(values, 'head', [(item, item ^ move) for item in range(4)])  10.2 us
    pallas_call x2, Pallas kernels, collect(): pl.pallas_call(collect_kernel, grid_spec=pltpu.PrefetchScalarGridSpec(num...  8.02 us
    unnamed x65, local copies, waits for them, and re-layouts  7.98 us
  transfers between devices with their start and end apart: 15, of which 1 were waited for; matrix products, arithmetic and copies ran while one was open for 12% of the time, Pallas kernels for 35%

profile of v3, /device:TPU:0, one launch (start us, length us, event | category | flops | bytes accessed | tf_op | source)
XLA Modules:
  0.0 359.8 jit_solution(9139914966077022123)
XLA Ops:
  0.7 1.2 copy.61
  1.9 0.9 copy.62.refs_1_
  2.8 3.0 concatenate.22
  6.4 1.7 constant_dynamic-slice_fusion.8.refs_2_
  8.0 25.9 %entry.1 = (bf16[1024,128]{1,0:T(8,128)(2,1)}, bf16[1024,128]{1,0:T(8,128)(2,1)}, bf16[1024,128]{1,0:T(8,128)(2,1)}, bf16[4,512,384]{2,1,0:T(8,128)(2,1)}, f32[4,72,128]{2,1,0:T(8,128)}) custom-call(bf16[8192,128]{1,0:T(8,128)(2,1)} %refs_0_.1, bf16[512,384]{1,0:T(8,128)(2,1)} %copy.62.refs_1_, f32[72,128]{1,0:T(8,128)} %convert_element_type.41.refs_2_), custom_call_target="tpu_custom_call" | custom-call | tf_op jit(solution)/shard_map/entry/pallas_call | solution.py:461
  34.0 0.9 constant_dynamic-slice_fusion.4
  35.0 1.6 collective-permute-start.1
  36.8 1.4 collective-permute-start.8
  38.1 0.7 collective-permute-start.6
  39.9 1.6 gather_fusion
  41.5 0.7 select_bitcast_fusion
  42.2 0.6 slice_bitcast_fusion
  44.0 1.3 slice.168
  45.3 1.5 fusion
  46.8 1.3 convert_reduce_fusion.2
  48.1 1.3 copy.59
  49.4 1.3 copy.60
  50.7 1.3 copy.58
  52.1 0.7 copy.69
  53.4 1.4 pad_add_fusion.refs_0_
  54.8 1.0 compare_select_fusion.1
  55.8 1.4 constant_dynamic-slice_fusion
  57.2 1.3 stack.73.refs_6_
  58.5 1.3 stack.71.refs_7_.refs_8_
  59.9 1.0 broadcast_in_dim.77.refs_9_
  60.9 0.7 broadcast_in_dim.76.refs_6_
  61.5 25.9 %front.2 = (f32[2048,512]{1,0:T(8,128)}, bf16[2048,512]{1,0:T(8,128)(2,1)}, bf16[2048,512]{1,0:T(8,128)(2,1)}, bf16[2048,512]{1,0:T(8,128)(2,1)}, bf16[2048,512]...) custom-call(s32[8,3]{1,0:T(8,128)} %pad_add_fusion.refs_0_, ...), custom_call_target="tpu_custom_call" | custom-call | flops 12884901888 | bytes 40000000 | tf_op jit(solution)/shard_map/front/pallas_call | solution.py:543
  87.5 0.8 pad_maximum_fusion.5.refs_1_
  88.3 1.0 collective-permute-start.10
  89.4 1.0 pad_maximum_fusion.9
  90.5 1.0 collective-permute-start.4
  91.7 25.6 %front.3 = (f32[2048,512]{1,0:T(8,128)}, bf16[2048,512]{1,0:T(8,128)(2,1)}, bf16[2048,512]{1,0:T(8,128)(2,1)}, bf16[2048,512]{1,0:T(8,128)(2,1)}, bf16[2048,512]...) custom-call(s32[8,3]{1,0:T(8,128)} %pad_add_fusion.refs_0_, ...), custom_call_target="tpu_custom_call", output_to_operand_aliasing={{0}: (10, {}), {1}: (11, {}), {2}: (12, {}), {3}: (13, {}),... | custom-call | flops 12884901888 | bytes 40000000 | tf_op jit(solution)/shard_map/front/pallas_call | solution.py:543
  118.3 1.8 pad_maximum_fusion.6.refs_2_
  120.1 1.8 pad_maximum_fusion.7.refs_3_
  122.5 1.8 pad_maximum_fusion.8.refs_4_
  124.3 1.2 collective-permute-start.5
  125.5 1.8 pad_maximum_fusion.4.refs_8_
  127.4 1.6 pad_maximum_fusion.refs_9_
  129.0 1.6 pad_maximum_fusion.1.refs_10_
  130.7 7.5 %collective-permute-done.5.refs_5_ = bf16[2048,128]{1,0:T(8,128)(2,1)S(1)} collective-permute-done((bf16[2048,128]{1,0:T(8,128)(2,1)S(1)}, bf16[2048,128]{1,0:T(8,128)(2,1)S(1)}, u32[]{:S(2)}, u32[]{:S(2)}) %collective-permute-start.5) | collective-permute-done | bytes 524320 | tf_op jit(solution)/shard_map/ppermute | solution.py:1203
  138.2 0.8 copy-done.27
  139.0 68.1 %middle.1 = (bf16[2048,128]{1,0:T(8,128)(2,1)}, bf16[2048,128]{1,0:T(8,128)(2,1)}, bf16[2048,128]{1,0:T(8,128)(2,1)}, bf16[2048,128]{1,0:T(8,128)(2,1)}, f32[204...) custom-call(bf16[2048,512]{1,0:T(8,128)(2,1)} %get-tuple-element.89., ...), custom_call_target="tpu_custom_call" | custom-call | flops 32212254720 | bytes 30000000 | tf_op jit(solution)/shard_map/middle/pallas_call | solution.py:741
  207.1 0.8 fusion.15
  207.9 0.7 slice.177
  208.7 53.4 %back.1 = (bf16[4,2048,384]{2,1,0:T(8,128)(2,1)}, bf16[4,512,384]{2,1,0:T(8,128)(2,1)}, f32[49,8,512]{2,1,0:T(8,128)}, f32[8,512]{1,0:T(8,128)}) custom-call(s32[8,3]{1,0:T(8,128)} %pad_add_fusion.refs_0_, s32[1]{0:T(128)} %bitcast.refs_1_.me_ref, bf16[2048,512]{1,0:T(8,128)(2,1)} %get-tuple-element.99.refs_2_, ...), custom_call_target="tpu_custom_call" | custom-call | flops 34359738368 | bytes 80000000 | tf_op jit(solution)/shard_map/back/pallas_call | solution.py:850
  262.1 1.3 reduce_sum.39
  263.6 0.7 slice.175
  264.4 0.7 gather_fusion.1
  265.3 1.1 collective-permute-start.13
  266.4 0.8 collective-permute-start.14
  267.2 0.7 maximum_maximum_fusion.refs_14_
  267.9 71.6 %tail.1 = (bf16[2048,128]{1,0:T(8,128)(2,1)}, bf16[2048,128]{1,0:T(8,128)(2,1)}, bf16[2048,128]{1,0:T(8,128)(2,1)}, bf16[2048,128]{1,0:T(8,128)(2,1)}, f32[512,5...) custom-call(s32[8,3]{1,0:T(8,128)} %pad_add_fusion.refs_0_, ...), custom_call_target="tpu_custom_call" | custom-call | flops 6442450944 | bytes 24000000 | tf_op jit(solution)/shard_map/tail/pallas_call | solution.py:1094
  339.5 1.4 slice.184
  340.9 1.2 slice.183
  342.2 1.4 copy.66
  343.6 1.1 copy.67
  345.3 4.0 %collect.3 = f32[8192,128]{1,0:T(8,128)} custom-call(s32[1]{0:T(128)} %bitcast.refs_1_.me_ref, bf16[2048,128]{1,0:T(8,128)(2,1)} %get-tuple-element.115.refs_0_, bf16[2048,128]{1,0:T(8,128)(2,1)} %get-tuple-element.116.refs_1_, bf16[2048,128]{1,0:T(8,128)(2,1)} %get-tuple-element.117.refs_2_, bf16[2048,128]{1,0:T(8,128)(2,1)} %get-tuple-element.118.refs_3_), custom_call_target="tpu_custom_call" | custom-call | tf_op jit(solution)/shard_map/collect/pallas_call | solution.py:1137
  349.3 1.3 slice_bitcast_fusion.9
  350.5 1.4 slice_bitcast_fusion.10
  352.0 0.7 copy-done.8
  353.0 4.1 %collect.2 = f32[8192,128]{1,0:T(8,128)} custom-call(s32[1]{0:T(128)} %bitcast.refs_1_.me_ref, bf16[2048,128]{1,0:T(8,128)(2,1)} %get-tuple-element.95.refs_0_, bf16[2048,128]{1,0:T(8,128)(2,1)} %copy-done.8, bf16[2048,128]{1,0:T(8,128)(2,1)} %copy-done.9, bf16[2048,128]{1,0:T(8,128)(2,1)} %copy-done.10), custom_call_target="tpu_custom_call" | custom-call | tf_op jit(solution)/shard_map/collect/pallas_call | solution.py:1137
  357.1 0.7 copy.83
  357.8 1.0 copy.84
  358.8 1.0 copy.85
  (107 shorter events, 7.1 us)
Async XLA Ops:
  1.8 32.1 %copy-start = (bf16[8192,128]{1,0:T(8,128)(2,1)S(1)}, bf16[8192,128]{1,0:T(8,128)(2,1)}, u32[]{:S(2)}) copy-start(bf16[8192,128]{1,0:T(8,128)(2,1)} %refs_0_.1) | copy-start | bytes 6291460
  8.0 28.7 %copy-start.2 = (bf16[512,512]{1,0:T(8,128)(2,1)S(1)}, bf16[512,512]{1,0:T(8,128)(2,1)}, u32[]{:S(2)}) copy-start(bf16[512,512]{1,0:T(8,128)(2,1)} %param.32) | copy-start | bytes 1572868
  34.9 52.6 %copy-start.6 = (bf16[1024,128]{1,0:T(8,128)(2,1)}, bf16[1024,128]{1,0:T(8,128)(2,1)S(1)}, u32[]{:S(2)}) copy-start(bf16[1024,128]{1,0:T(8,128)(2,1)S(1)} %get-tuple-element.185.refs_2_) | copy-start | bytes 786436
  34.9 20.9 %copy-start.1 = (bf16[8192,128]{1,0:T(8,128)(2,1)S(1)}, bf16[8192,128]{1,0:T(8,128)(2,1)}, u32[]{:S(2)}) copy-start(bf16[8192,128]{1,0:T(8,128)(2,1)} %param.20) | copy-start | bytes 6291460
  34.9 55.5 %collective-permute-start = (bf16[1024,128]{1,0:T(8,128)(2,1)}, bf16[1024,128]{1,0:T(8,128)(2,1)}, u32[]{:S(2)}, u32[]{:S(2)}) collective-permute-start(bf16[1024,128]{1,0:T(8,128)(2,1)} %get-tuple-element.184), channel_id=1, source_target_pairs={{0,1},{1,0},{2,3},{3,2},{4,5},{5,4},{6,7},{7,6},{8,9},{9,8},{10,11... | collective-permute-start | bytes 786440 | tf_op jit(solution)/shard_map/ppermute | solution.py:1203
  35.0 55.5 %collective-permute-start.1 = (bf16[1024,128]{1,0:T(8,128)(2,1)}, bf16[1024,128]{1,0:T(8,128)(2,1)}, u32[]{:S(2)}, u32[]{:S(2)}) collective-permute-start(bf16[1024,128]{1,0:T(8,128)(2,1)} %get-tuple-element.183), channel_id=1, source_target_pairs={{0,2},{1,3},{2,0},{3,1},{4,6},{5,7},{6,4},{7,5},{8,10},{9,11},{10,... | collective-permute-start | bytes 786440 | tf_op jit(solution)/shard_map/ppermute | solution.py:1203
  36.6 55.0 %collective-permute-start.2 = (bf16[1024,128]{1,0:T(8,128)(2,1)}, bf16[1024,128]{1,0:T(8,128)(2,1)}, u32[]{:S(2)}, u32[]{:S(2)}) collective-permute-start(bf16[1024,128]{1,0:T(8,128)(2,1)} %get-tuple-element.182), channel_id=1, source_target_pairs={{0,3},{1,2},{2,1},{3,0},{4,7},{5,6},{6,5},{7,4},{8,11},{9,10},{10,... | collective-permute-start | bytes 786440 | tf_op jit(solution)/shard_map/ppermute | solution.py:1203
  36.8 80.6 %collective-permute-start.8 = (bf16[512,512]{1,0:T(8,128)(2,1)S(1)}, bf16[512,512]{1,0:T(8,128)(2,1)S(1)}, u32[]{:S(2)}, u32[]{:S(2)}) collective-permute-start(bf16[512,512]{1,0:T(8,128)(2,1)S(1)} %copy-done.2), channel_id=1, source_target_pairs={{0,2},{1,3},{2,0},{3,1},{4,6},{5,7},{6,4},{7,5},{8,10},{9,11},{10,... | collective-permute-start | bytes 1572872 | tf_op jit(solution)/shard_map/ppermute | solution.py:1203
  38.1 50.2 %collective-permute-start.6 = (bf16[128,512]{1,0:T(8,128)(2,1)}, bf16[128,512]{1,0:T(8,128)(2,1)}, u32[]{:S(2)}, u32[]{:S(2)}) collective-permute-start(bf16[128,512]{1,0:T(8,128)(2,1)} %param.28), channel_id=1, source_target_pairs={{0,2},{1,3},{2,0},{3,1},{4,6},{5,7},{6,4},{7,5},{8,10},{9,11},{10,... | collective-permute-start | bytes 393224 | tf_op jit(solution)/shard_map/ppermute | solution.py:1203
  52.8 8.1 %copy-start.16 = (f32[2,8,4,128]{3,1,2,0:T(8,128)}, f32[2,8,4,128]{3,1,2,0:T(8,128)S(1)}, u32[]{:S(2)}) copy-start(f32[2,8,4,128]{3,1,2,0:T(8,128)S(1)} %copy.68) | copy-start | bytes 98308
  61.5 26.0 %copy-start.7 = (bf16[1024,128]{1,0:T(8,128)(2,1)S(1)}, bf16[1024,128]{1,0:T(8,128)(2,1)}, u32[]{:S(2)}) copy-start(bf16[1024,128]{1,0:T(8,128)(2,1)} %constant_dynamic-slice_fusion.8.refs_2_) | copy-start | bytes 786436
  61.5 26.8 %copy-start.3 = (bf16[512,512]{1,0:T(8,128)(2,1)S(1)}, bf16[512,512]{1,0:T(8,128)(2,1)}, u32[]{:S(2)}) copy-start(bf16[512,512]{1,0:T(8,128)(2,1)} %param.34) | copy-start | bytes 1572868
  88.3 33.6 %collective-permute-start.10 = (bf16[512,512]{1,0:T(8,128)(2,1)S(1)}, bf16[512,512]{1,0:T(8,128)(2,1)S(1)}, u32[]{:S(2)}, u32[]{:S(2)}) collective-permute-start(bf16[512,512]{1,0:T(8,128)(2,1)S(1)} %copy-done.3), channel_id=1, source_target_pairs={{0,2},{1,3},{2,0},{3,1},{4,6},{5,7},{6,4},{7,5},{8,10},{9,11},{10,... | collective-permute-start | bytes 1572872 | tf_op jit(solution)/shard_map/ppermute | solution.py:1203
  90.4 40.3 %collective-permute-start.3 = (bf16[2048,128]{1,0:T(8,128)(2,1)}, bf16[2048,128]{1,0:T(8,128)(2,1)S(1)}, u32[]{:S(2)}, u32[]{:S(2)}) collective-permute-start(bf16[2048,128]{1,0:T(8,128)(2,1)} %get-tuple-element.180), channel_id=1, source_target_pairs={{0,1},{1,0},{2,3},{3,2},{4,5},{5,4},{6,7},{7,6},{8,9},{9,8},{10,11... | collective-permute-start | bytes 1572872 | tf_op jit(solution)/shard_map/ppermute | solution.py:1203
  90.5 40.2 %collective-permute-start.4 = (bf16[2048,128]{1,0:T(8,128)(2,1)}, bf16[2048,128]{1,0:T(8,128)(2,1)S(1)}, u32[]{:S(2)}, u32[]{:S(2)}) collective-permute-start(bf16[2048,128]{1,0:T(8,128)(2,1)} %get-tuple-element.179), channel_id=1, source_target_pairs={{0,2},{1,3},{2,0},{3,1},{4,6},{5,7},{6,4},{7,5},{8,10},{9,11},{10,... | collective-permute-start | bytes 1572872 | tf_op jit(solution)/shard_map/ppermute | solution.py:1203
  91.5 32.7 %collective-permute-start.7 = (bf16[2,128,512]{2,1,0:T(8,128)(2,1)S(1)}, bf16[2,128,512]{2,1,0:T(8,128)(2,1)S(1)}, u32[]{:S(2)}, u32[]{:S(2)}) collective-permute-start(bf16[2,128,512]{2,1,0:T(8,128)(2,1)S(1)} %pad_maximum_fusion.9), channel_id=1, source_target_pairs={{0,1},{1,0},{2,3},{3,2},{4,5},{5,4},{6,7},{7,6},{8,9},{9,8},{10,11... | collective-permute-start | bytes 786440 | tf_op jit(solution)/shard_map/ppermute | solution.py:1203
  117.3 1.0 copy-start.15
  117.3 2.7 copy-start.14
  117.5 5.0 %copy-start.13 = (bf16[1024,128]{1,0:T(8,128)(2,1)S(1)}, bf16[1024,128]{1,0:T(8,128)(2,1)}, u32[]{:S(2)}) copy-start(bf16[1024,128]{1,0:T(8,128)(2,1)} %get-tuple-element.80.refs_5_) | copy-start | bytes 786436
  117.5 9.8 %collective-permute-start.9 = (bf16[2,512,512]{2,1,0:T(8,128)(2,1)S(1)}, bf16[2,512,512]{2,1,0:T(8,128)(2,1)S(1)}, u32[]{:S(2)}, u32[]{:S(2)}) collective-permute-start(bf16[2,512,512]{2,1,0:T(8,128)(2,1)S(1)} %pad_maximum_fusion.2), channel_id=1, source_target_pairs={{0,1},{1,0},{2,3},{3,2},{4,5},{5,4},{6,7},{7,6},{8,9},{9,8},{10,11... | collective-permute-start | bytes 3145736 | tf_op jit(solution)/shard_map/ppermute | solution.py:1203
  120.1 4.2 %copy-start.11 = (bf16[2048,128]{1,0:T(8,128)(2,1)S(1)}, bf16[2048,128]{1,0:T(8,128)(2,1)}, u32[]{:S(2)}) copy-start(bf16[2048,128]{1,0:T(8,128)(2,1)} %get-tuple-element.178) | copy-start | bytes 1572868
  122.0 7.0 %collective-permute-start.11 = (bf16[2,512,512]{2,1,0:T(8,128)(2,1)S(1)}, bf16[2,512,512]{2,1,0:T(8,128)(2,1)S(1)}, u32[]{:S(2)}, u32[]{:S(2)}) collective-permute-start(bf16[2,512,512]{2,1,0:T(8,128)(2,1)S(1)} %pad_maximum_fusion.3), channel_id=1, source_target_pairs={{0,1},{1,0},{2,3},{3,2},{4,5},{5,4},{6,7},{7,6},{8,9},{9,8},{10,11... | collective-permute-start | bytes 3145736 | tf_op jit(solution)/shard_map/ppermute | solution.py:1203
  124.3 13.9 %collective-permute-start.5 = (bf16[2048,128]{1,0:T(8,128)(2,1)S(1)}, bf16[2048,128]{1,0:T(8,128)(2,1)S(1)}, u32[]{:S(2)}, u32[]{:S(2)}) collective-permute-start(bf16[2048,128]{1,0:T(8,128)(2,1)S(1)} %copy-done.11), channel_id=1, source_target_pairs={{0,3},{1,2},{2,1},{3,0},{4,7},{5,6},{6,5},{7,4},{8,11},{9,10},{10,... | collective-permute-start | bytes 1572872 | tf_op jit(solution)/shard_map/ppermute | solution.py:1203
  130.7 7.5 %copy-start.25 = (bf16[2048,128]{1,0:T(8,128)(2,1)}, bf16[2048,128]{1,0:T(8,128)(2,1)S(1)}, u32[]{:S(2)}) copy-start(bf16[2048,128]{1,0:T(8,128)(2,1)S(1)} %collective-permute-done.3.refs_3_) | copy-start | bytes 1572868
  130.7 7.5 %copy-start.26 = (bf16[2048,128]{1,0:T(8,128)(2,1)}, bf16[2048,128]{1,0:T(8,128)(2,1)S(1)}, u32[]{:S(2)}) copy-start(bf16[2048,128]{1,0:T(8,128)(2,1)S(1)} %collective-permute-done.4.refs_4_) | copy-start | bytes 1572868
  138.2 0.8 copy-start.27
  208.6 54.8 %copy-start.17 = (s32[512]{0:T(512)S(1)}, s32[512]{0:T(512)}, u32[]{:S(2)}) copy-start(s32[512]{0:T(512)} %convert_add_fusion) | copy-start | bytes 6148
  208.7 54.8 %copy-start.21 = (s32[49]{0:T(128)S(1)}, s32[49]{0:T(128)}, u32[]{:S(2)}) copy-start(s32[49]{0:T(128)} %fusion.8) | copy-start | bytes 592
  208.7 56.4 %copy-start.20 = (pred[4]{0:T(512)(128)(4,1)S(1)}, pred[4]{0:T(512)(128)(4,1)}, u32[]{:S(2)}) copy-start(pred[4]{0:T(512)(128)(4,1)} %compare_and_fusion) | copy-start | bytes 16
  208.7 56.5 %copy-start.19 = (f32[4,1,512]{2,1,0:T(1,128)S(1)}, f32[4,1,512]{2,1,0:T(1,128)}, u32[]{:S(2)}) copy-start(f32[4,1,512]{2,1,0:T(1,128)} %get-tuple-element.114) | copy-start | bytes 24580
  208.7 56.6 %copy-start.24 = (bf16[2048,128]{1,0:T(8,128)(2,1)S(1)}, bf16[2048,128]{1,0:T(8,128)(2,1)}, u32[]{:S(2)}) copy-start(bf16[2048,128]{1,0:T(8,128)(2,1)} %get-tuple-element.97) | copy-start | bytes 1572868
  208.7 57.7 %copy-start.23 = (bf16[2048,128]{1,0:T(8,128)(2,1)S(1)}, bf16[2048,128]{1,0:T(8,128)(2,1)}, u32[]{:S(2)}) copy-start(bf16[2048,128]{1,0:T(8,128)(2,1)} %get-tuple-element.98) | copy-start | bytes 1572868
  208.7 58.5 %copy-start.22 = (bf16[128]{0:T(256)(128)(2,1)S(1)}, bf16[128]{0:T(256)(128)(2,1)}, u32[]{:S(2)}) copy-start(bf16[128]{0:T(256)(128)(2,1)} %pad.2.clone) | copy-start | bytes 772
  265.2 86.7 %collective-permute-start.12 = (bf16[2048,128]{1,0:T(8,128)(2,1)}, bf16[2048,128]{1,0:T(8,128)(2,1)S(1)}, u32[]{:S(2)}, u32[]{:S(2)}) collective-permute-start(bf16[2048,128]{1,0:T(8,128)(2,1)} %get-tuple-element.96), channel_id=1, source_target_pairs={{0,1},{1,0},{2,3},{3,2},{4,5},{5,4},{6,7},{7,6},{8,9},{9,8},{10,11... | collective-permute-start | bytes 1572872 | tf_op jit(solution)/shard_map/ppermute | solution.py:1203
  265.3 86.6 %collective-permute-start.13 = (bf16[2048,128]{1,0:T(8,128)(2,1)S(1)}, bf16[2048,128]{1,0:T(8,128)(2,1)S(1)}, u32[]{:S(2)}, u32[]{:S(2)}) collective-permute-start(bf16[2048,128]{1,0:T(8,128)(2,1)S(1)} %copy-done.24), channel_id=1, source_target_pairs={{0,2},{1,3},{2,0},{3,1},{4,6},{5,7},{6,4},{7,5},{8,10},{9,11},{10,... | collective-permute-start | bytes 1572872 | tf_op jit(solution)/shard_map/ppermute | solution.py:1203
  266.4 85.6 %collective-permute-start.14 = (bf16[2048,128]{1,0:T(8,128)(2,1)S(1)}, bf16[2048,128]{1,0:T(8,128)(2,1)S(1)}, u32[]{:S(2)}, u32[]{:S(2)}) collective-permute-start(bf16[2048,128]{1,0:T(8,128)(2,1)S(1)} %copy-done.23), channel_id=1, source_target_pairs={{0,3},{1,2},{2,1},{3,0},{4,7},{5,6},{6,5},{7,4},{8,11},{9,10},{10,... | collective-permute-start | bytes 1572872 | tf_op jit(solution)/shard_map/ppermute | solution.py:1203
  339.5 5.2 %copy-start.18 = (f32[16,128]{1,0:T(8,128)S(1)}, f32[16,128]{1,0:T(8,128)}, u32[]{:S(2)}) copy-start(f32[16,128]{1,0:T(8,128)} %get-tuple-element.119) | copy-start | bytes 24580
  351.9 0.8 copy-start.8
  351.9 0.9 copy-start.9
  352.0 1.1 copy-start.10
  353.0 4.1 %copy-start.12 = (f32[128,512]{1,0:T(8,128)S(1)}, f32[128,512]{1,0:T(8,128)}, u32[]{:S(2)}) copy-start(f32[128,512]{1,0:T(8,128)} %get-tuple-element.239) | copy-start | bytes 786436
  353.0 4.8 %copy-start.5 = (f32[512,512]{1,0:T(8,128)S(1)}, f32[512,512]{1,0:T(8,128)}, u32[]{:S(2)}) copy-start(f32[512,512]{1,0:T(8,128)} %get-tuple-element.243) | copy-start | bytes 3145732
  357.1 1.7 copy-start.4

commit v4 on v3

--- a/solution.py
+++ b/solution.py
@@ -196,9 +196,46 @@
     return jnp.concatenate([values * masks[0], values * masks[1]], axis=1)
 
 
-def read_cuts(cuts_ref, base):
-    step = pl.program_id(0) + base
-    return cuts_ref[step, 0], (cuts_ref[step, 1], cuts_ref[step, 2])
+def read_cuts(ids_ref, canvases):
+    canvas = lax.axis_index("head") * canvases + pl.program_id(0)
+
+    def count(places, bound):
+        return sum(jnp.where(ids_ref[canvas, place] < bound, 1, 0) for place in places)
+
+    cut = count(range(0, PLACES, SIDE), 2)
+    upper = count(range(SIDE), 1)
+    lower = count(range(PLACES - SIDE, PLACES), 3)
+    return cut, (upper, lower)
+
+
+SMALL_SIZE = 72
+(CPE, CRPE, CPE_BIAS, GAIN1, SHIFT1, QUERY_BIAS, VALUE_BIAS, PROJ_BIAS, GAIN2, SHIFT2, FC2_BIAS, FC1_BIAS) = (
+    0, 9, 58, 59, 60, 61, 62, 63, 64, 65, 66, 67,
+)
+
+
+def spread_small(small_in, small_ref):
+    me = lax.axis_index("head")
+    for tile in range(TILES):
+        small_ref[:, lane(tile)] = small_in[lax.bitwise_xor(me, tile)]
+
+
+def outer_taps(tap):
+    return max(abs(tap // 7 - 3), abs(tap % 7 - 3)) > 2
+
+
+def keep_head(tap, tile, values):
+    if tile != 2 or not outer_taps(tap):
+        return values
+    col = lax.broadcasted_iota(jnp.int32, values.shape, len(values.shape) - 1)
+    return jnp.where(col < HEAD_DIM, 0.0, values)
+
+
+def spread_taps(small_ref, row, count, masked, taps_ref):
+    for tap in range(count):
+        for tile in range(TILES):
+            values = jnp.broadcast_to(small_ref[row + tap : row + tap + 1, lane(tile)], (8, LANES))
+            taps_ref[tap, :, lane(tile)] = keep_head(tap, tile, values) if masked else values
 
 
 def whole(shape):
@@ -417,77 +454,74 @@
 
 
 def entry_kernel(
-    rows, size, x_ref, qkv_ref, small_ref,
-    x1_ref, x2_ref, x3_ref, all_qkv_ref, all_small_ref,
+    rows, x_ref, qkv_ref, small_ref,
+    x0_ref, x1_ref, x2_ref, x3_ref, all_qkv_ref, all_small_ref,
     send, receive, local,
 ):
     head = lax.axis_index("head")
     meet([peer(move) for move in (1, 2, 3)])
-    copies = []
     far = remote(qkv_ref, all_qkv_ref.at[2], send.at[0], receive.at[0], peer(2))
-    far.start()
     near = remote(qkv_ref, all_qkv_ref.at[1], send.at[1], receive.at[1], peer(1))
-    near.start()
+    copies = [near]
     for move in (1, 2, 3):
         copies.append(
             remote(small_ref, all_small_ref.at[move], send.at[1 + move], receive.at[1 + move], peer(move))
         )
-        copies[-1].start()
     for move, target in ((2, x2_ref), (3, x3_ref), (1, x1_ref)):
-        start = pl.multiple_of(lax.bitwise_xor(head, move) * rows, PLACES)
-        copies.append(
-            remote(x_ref.at[pl.ds(start, size)], target, send.at[4 + move], receive.at[4 + move], peer(move))
-        )
-        copies[-1].start()
-    mine = pltpu.make_async_copy(qkv_ref, all_qkv_ref.at[0], local.at[0])
-    mine.start()
-    mine_small = pltpu.make_async_copy(small_ref, all_small_ref.at[0], local.at[1])
-    mine_small.start()
-    far.wait_recv()
+        source = x_ref.at[aligned(lax.bitwise_xor(head, move), rows)]
+        copies.append(remote(source, target, send.at[4 + move], receive.at[4 + move], peer(move)))
+    mine = [
+        pltpu.make_async_copy(qkv_ref, all_qkv_ref.at[0], local.at[0]),
+        pltpu.make_async_copy(small_ref, all_small_ref.at[0], local.at[1]),
+        pltpu.make_async_copy(x_ref.at[aligned(head, rows)], x0_ref, local.at[2]),
+    ]
+    far.start()
+    for copy in copies + mine:
+        copy.start()
+    far.wait()
     relay = remote(all_qkv_ref.at[2], all_qkv_ref.at[3], send.at[8], receive.at[8], peer(1))
     relay.start()
-    far.wait_send()
-    near.wait()
-    for copy in copies:
+    for copy in copies + mine:
         copy.wait()
     relay.wait()
-    mine.wait()
-    mine_small.wait()
-
-
-def entry(block_in, size, qkv, small):
+
+
+def entry(block_in, qkv, small):
     rows = block_in.shape[0] // 4
     hbm = pl.BlockSpec(memory_space=pl.ANY)
     return pl.pallas_call(
-        lambda *refs: entry_kernel(rows, size, *refs),
+        lambda *refs: entry_kernel(rows, *refs),
         in_specs=[hbm] * 3,
-        out_specs=[hbm] * 5,
-        out_shape=[like((size, LANES), BF16)] * 3 + [
+        out_specs=[hbm] * 6,
+        out_shape=[like((rows, LANES), BF16)] * 4 + [
             like((4,) + qkv.shape, BF16), like((4,) + small.shape, F32),
         ],
         scratch_shapes=[
             pltpu.SemaphoreType.DMA((9,)), pltpu.SemaphoreType.DMA((9,)),
-            pltpu.SemaphoreType.DMA((2,)),
+            pltpu.SemaphoreType.DMA((3,)),
         ],
         compiler_params=params(collective_id=1, has_side_effects=True),
         name="entry",
     )(block_in, qkv, small)
 
 
-def front_kernel(base, kept, *refs):
-    (cuts_ref, me_ref, x0_ref, x1_ref, x2_ref, x3_ref, cpe_ref, vec_ref, qkv_ref, crpe_ref) = refs[:10]
-    (first_ref, hidden_ref, query_ref, value_ref, soft_ref, context_ref, conv_ref, attended_ref,
-     mask_ref, grid_ref, out_ref, x_ref) = refs[10 + kept :]
-    cut, col_cuts = read_cuts(cuts_ref, base)
-    me = me_ref[0]
+def front_kernel(
+    canvases, ids_ref, x0_ref, x1_ref, x2_ref, x3_ref, small_in, qkv_ref,
+    first_ref, hidden_ref, query_ref, value_ref, soft_ref, context_ref, conv_ref, attended_ref,
+    mask_ref, grid_ref, out_ref, x_ref, small_ref, cpe_ref, crpe_ref,
+):
+    cut, col_cuts = read_cuts(ids_ref, canvases)
+    me = lax.axis_index("head")
 
     @pl.when(pl.program_id(0) == 0)
     def _():
         grid_ref[...] = jnp.zeros_like(grid_ref)
+        spread_small(small_in, small_ref)
+        spread_taps(small_ref, CPE, 9, False, cpe_ref)
+        spread_taps(small_ref, CRPE, 49, True, crpe_ref)
 
     for move, piece_ref in enumerate((x0_ref, x1_ref, x2_ref, x3_ref)):
-        start = pl.multiple_of(LANES * lax.bitwise_xor(me, move), LANES)
-        x_ref[:, pl.ds(start, LANES)] = piece_ref[...].astype(F32)
+        x_ref[:, aligned(lax.bitwise_xor(me, move), LANES)] = piece_ref[...].astype(F32)
     fill_masks(cut, col_cuts, mask_ref)
     for tile, plane in SMALL_ITEMS:
         spread(
@@ -495,12 +529,14 @@
             1, cut, mask_ref, grid_ref, plane,
         )
     conv_tiles(SMALL_ITEMS, 1, cut, grid_ref, cpe_ref, 1, out_ref)
-    first = x_ref[...] + out_ref[:PLACES, :] + vec_ref[0:1, :]
+    first = x_ref[...] + out_ref[:PLACES, :] + small_ref[CPE_BIAS : CPE_BIAS + 1, :]
     first_ref[...] = first
     center = row_mean(first)
     square = row_mean(first * first)
     inverse = lax.rsqrt(square - center * center + EPSILON)
-    hidden = ((first - center) * inverse * vec_ref[1:2, :] + vec_ref[2:3, :]).astype(BF16)
+    hidden = (
+        (first - center) * inverse * small_ref[GAIN1 : GAIN1 + 1, :] + small_ref[SHIFT1 : SHIFT1 + 1, :]
+    ).astype(BF16)
     hidden_ref[...] = hidden
     band, side = place_ids(cut, col_cuts)
     ids = 2 * band + side
@@ -509,9 +545,11 @@
     blocks = head_block()
     for tile in range(TILES):
         three = nn(hidden, qkv_ref[lax.bitwise_xor(me, tile)])
-        query = (three[:, :LANES] + vec_ref[3:4, lane(tile)]).astype(BF16)
+        query = (three[:, :LANES] + small_ref[QUERY_BIAS : QUERY_BIAS + 1, lane(tile)]).astype(BF16)
         keys = three[:, LANES : 2 * LANES].astype(BF16).astype(F32)
-        value = (three[:, 2 * LANES :] + vec_ref[4:5, lane(tile)]).astype(BF16)
+        value = (
+            three[:, 2 * LANES :] + small_ref[VALUE_BIAS : VALUE_BIAS + 1, lane(tile)]
+        ).astype(BF16)
         query_ref[:, lane(tile)] = query
         value_ref[:, lane(tile)] = value
         highest = crop_reduce(ids, keys, jnp.max, -1e30)
@@ -534,39 +572,39 @@
     attended_ref[...] = (x_ref[...] + query_ref[...].astype(F32) * conv).astype(BF16)
 
 
-def front(cuts, me, x_parts, base, kept, cpe, vec, qkv, crpe):
-    count = x_parts[0].shape[0] // PLACES
-    total = cuts.shape[0]
-    rows = total * PLACES
-    wide = rows_spec(D, base)
-    flops = 2 * count * PLACES * D * D * 4
+def front(ids, x_parts, small, qkv):
+    rows = x_parts[0].shape[0]
+    count = rows // PLACES
+    wide = rows_spec(D)
     return pl.pallas_call(
-        lambda *refs: front_kernel(base, len(kept), *refs),
+        lambda *refs: front_kernel(count, *refs),
         grid_spec=pltpu.PrefetchScalarGridSpec(
-            num_scalar_prefetch=2,
+            num_scalar_prefetch=1,
             grid=(count,),
-            in_specs=[rows_spec(LANES)] * 4
-            + [whole(cpe.shape), whole(vec.shape), whole(qkv.shape), whole(crpe.shape)]
-            + [pl.BlockSpec(memory_space=pl.ANY)] * len(kept),
-            out_specs=[wide, wide, wide, wide, wide, context_spec(base), wide, wide],
+            in_specs=[rows_spec(LANES)] * 4 + [once(small.shape), once(qkv.shape)],
+            out_specs=[wide, wide, wide, wide, wide, context_spec(0), wide, wide],
             scratch_shapes=[
                 pltpu.VMEM((2, 7, SIDE, LANES), F32),
                 pltpu.VMEM((3 * TILES, GRID_ROWS * SIDE, LANES), F32),
                 pltpu.VMEM((PLACES + SIDE, D), F32),
                 pltpu.VMEM((PLACES, D), F32),
+                pltpu.VMEM((SMALL_SIZE, D), F32),
+                pltpu.VMEM((9, 8, D), F32),
+                pltpu.VMEM((49, 8, D), F32),
             ],
         ),
         out_shape=[
             like((rows, D), F32), like((rows, D), BF16), like((rows, D), BF16),
             like((rows, D), BF16), like((rows, D), BF16),
-            like((total, TILES, 2 * LANES, 2 * LANES), BF16),
+            like((count, TILES, 2 * LANES, 2 * LANES), BF16),
             like((rows, D), BF16), like((rows, D), BF16),
         ],
-        input_output_aliases={10 + item: item for item in range(len(kept))},
         compiler_params=params(),
-        cost_estimate=pl.CostEstimate(flops=flops * 6, bytes_accessed=count * 10**7, transcendentals=0),
+        cost_estimate=pl.CostEstimate(
+            flops=rows * D * D * 60, bytes_accessed=count * 10**7, transcendentals=0
+        ),
         name="front",
-    )(cuts, me, *x_parts, cpe, vec, qkv, crpe, *kept)
+    )(ids, *x_parts, small, qkv)
 
 
 def gelu_both(pre):
@@ -585,12 +623,12 @@
 
 def middle_kernel(
     count,
-    attended_ref, first_ref, cot0_ref, cot1_ref, cot2_ref, cot3_ref, vec_ref, bias_ref,
-    proj_ref, fc1_ref, fc2_ref,
+    attended_ref, first_ref, cot0_ref, cot1_ref, cot2_ref, cot3_ref, small_in, own_weights,
+    far_weights,
     out0_ref, out1_ref, out2_ref, out3_ref, second_grad_ref, att_grad_ref, fc_mid_ref,
     proj_grad_ref, sum_ref, bias_grad_ref,
     cot_ref, hat_ref, inverse_ref, hidden_ref, total_ref, back_ref, active_ref, pre_grad_ref,
-    grads_ref, near_ref, far_ref, own_ref, low_ref, send, receive,
+    grads_ref, near_ref, far_ref, own_ref, low_ref, small_ref, weights_ref, send, receive, fetch,
 ):
     me = lax.axis_index("head")
     step = pl.program_id(0)
@@ -619,46 +657,83 @@
     def part(index):
         return aligned(index, BLOCK)
 
+    shard = 3 - step
+    fc1 = weights_ref.at[shard, :D]
+    fc2 = weights_ref.at[shard, D : 2 * D]
+
+    def proj(tile):
+        return weights_ref[lax.bitwise_xor(me, tile), 2 * D :, :]
+
+    def relay(number, source, target, part):
+        return remote(
+            source.at[part], weights_ref.at[target, part], send.at[8 + number], receive.at[8 + number],
+            peer(1),
+        )
+
+    narrow, broad = pl.ds(2 * D, LANES), pl.ds(0, 2 * D)
+    relays = [
+        relay(0, own_weights, 1, narrow), relay(1, far_weights, 3, narrow),
+        relay(2, far_weights, 3, broad), relay(3, own_weights, 1, broad),
+    ]
+
     @pl.when(step == 0)
     def _():
+        loads = [
+            pltpu.make_async_copy(own_weights, weights_ref.at[0], fetch.at[0]),
+            pltpu.make_async_copy(far_weights, weights_ref.at[2], fetch.at[1]),
+        ]
+        for load in loads:
+            load.start()
         meet([peer(1), peer(2), low_peer()])
+        for item in relays:
+            item.start()
+        spread_small(small_in, small_ref)
         own_ref[...] = jnp.zeros_like(own_ref)
         sum_ref[...] = jnp.zeros_like(sum_ref)
         for move, piece_ref in enumerate((cot0_ref, cot1_ref, cot2_ref, cot3_ref)):
             cot_ref[:, aligned(lax.bitwise_xor(me, move), LANES)] = piece_ref[...]
+        for item in loads + relays[:2]:
+            item.wait()
 
         def enter(index, carry):
             now = part(index)
-            second = first_ref[now, :] + vec_ref[0:1, :]
+            second = first_ref[now, :] + small_ref[PROJ_BIAS : PROJ_BIAS + 1, :]
             for tile in range(TILES):
-                second += nn(attended_ref[now, lane(tile)], proj_ref[lax.bitwise_xor(me, tile)])
+                second += nn(attended_ref[now, lane(tile)], proj(tile))
             center = row_mean(second)
             square = row_mean(second * second)
             inverse = lax.rsqrt(square - center * center + EPSILON)
             hat = (second - center) * inverse
-            hidden_ref[now, :] = (hat * vec_ref[1:2, :] + vec_ref[2:3, :]).astype(BF16)
+            hidden_ref[now, :] = (
+                hat * small_ref[GAIN2 : GAIN2 + 1, :] + small_ref[SHIFT2 : SHIFT2 + 1, :]
+            ).astype(BF16)
             hat_ref[now, :] = hat
             inverse_ref[now, :] = jnp.broadcast_to(inverse, (BLOCK, LANES))
-            total_ref[now, :] = second + vec_ref[3:4, :]
+            total_ref[now, :] = second + small_ref[FC2_BIAS : FC2_BIAS + 1, :]
             back_ref[now, :] = jnp.zeros((BLOCK, D), F32)
-            sum_ref[0:1, :] += jnp.sum(cot_ref[now, :].astype(F32), axis=0, keepdims=True)
+            sum_ref[3:4, :] += jnp.sum(cot_ref[now, :].astype(F32), axis=0, keepdims=True)
             return carry
 
         lax.fori_loop(0, blocks, enter, 0)
+        for item in relays[2:]:
+            item.wait()
 
     bias_grad_ref[0] = jnp.zeros_like(bias_grad_ref[0])
 
     def chunk(index, carry):
         now = part(index)
-        pre = nn(hidden_ref[now, :], fc1_ref[0]) + bias_ref[0]
+        bias = jnp.concatenate(
+            [small_in[shard, FC1_BIAS + tile : FC1_BIAS + tile + 1, :] for tile in range(TILES)], axis=1
+        )
+        pre = nn(hidden_ref[now, :], fc1[...]) + bias
         active, slope = gelu_both(pre)
         active = active.astype(BF16)
         active_ref[now, :] = active
-        total_ref[now, :] += nn(active, fc2_ref[0])
-        pre_grad_f = nt(cot_ref[now, :], fc2_ref[0]) * slope
+        total_ref[now, :] += nn(active, fc2[...])
+        pre_grad_f = nt(cot_ref[now, :], fc2[...]) * slope
         pre_grad = pre_grad_f.astype(BF16)
         pre_grad_ref[now, :] = pre_grad
-        back_ref[now, :] += nt(pre_grad, fc1_ref[0])
+        back_ref[now, :] += nt(pre_grad, fc1[...])
         bias_grad_ref[0] += jnp.sum(pre_grad_f, axis=0, keepdims=True)
         return carry
 
@@ -702,7 +777,7 @@
                 piece_ref[now, :] = total_ref[now, aligned(lax.bitwise_xor(me, move), LANES)].astype(BF16)
             hat = hat_ref[now, :]
             norm_grad = back_ref[now, :]
-            weighted = norm_grad * vec_ref[1:2, :]
+            weighted = norm_grad * small_ref[GAIN2 : GAIN2 + 1, :]
             second_grad = cot_ref[now, :].astype(F32) + inverse_ref[now, 0:1] * (
                 weighted - row_mean(weighted) - hat * row_mean(weighted * hat)
             )
@@ -711,11 +786,11 @@
             hidden_ref[now, :] = second_low
             for tile in range(TILES):
                 att_grad_ref[now, lane(tile)] = nt(
-                    second_low, proj_ref[lax.bitwise_xor(me, tile)]
+                    second_low, proj(tile)
                 ).astype(BF16)
             sum_ref[1:2, :] += jnp.sum(norm_grad * hat, axis=0, keepdims=True)
             sum_ref[2:3, :] += jnp.sum(norm_grad, axis=0, keepdims=True)
-            sum_ref[3:4, :] += jnp.sum(second_low.astype(F32), axis=0, keepdims=True)
+            sum_ref[0:1, :] += jnp.sum(second_low.astype(F32), axis=0, keepdims=True)
             return carry
 
         lax.fori_loop(0, blocks, leave, 0)
@@ -730,11 +805,12 @@
             ).astype(BF16)
 
 
-def middle(attended, first, cot_parts, vec, bias, proj, fc1, fc2):
+def middle(attended, first, cot_parts, small, own_weights, far_weights):
     rows = attended.shape[0]
     count = lax.axis_size("dp")
     padded = padded_rows(D, count)
-    shard = pl.BlockSpec((1, D, D), lambda i: (3 - i, 0, 0))
+    hbm = pl.BlockSpec(memory_space=pl.ANY)
+    proj_shape = (4, LANES, D)
     piece = once((rows, LANES))
     wide = once((rows, D))
     line = pl.BlockSpec((1, 1, D), lambda i: (3 - i, 0, 0))
@@ -742,16 +818,15 @@
         lambda *refs: middle_kernel(count, *refs),
         grid=(4,),
         in_specs=[
-            wide, wide, piece, piece, piece, piece, whole(vec.shape), line, once(proj.shape),
-            shard, shard,
+            wide, wide, piece, piece, piece, piece, once(small.shape), hbm, hbm,
         ],
         out_specs=[
-            piece, piece, piece, piece, wide, wide, once((2, padded // 2, D)), once(proj.shape),
+            piece, piece, piece, piece, wide, wide, once((2, padded // 2, D)), once(proj_shape),
             once((8, D)), line,
         ],
         out_shape=[like((rows, LANES), BF16)] * 4 + [
             like((rows, D), F32), like((rows, D), BF16), like((2, padded // 2, D), BF16),
-            like(proj.shape, BF16), like((8, D), F32), like(bias.shape, F32),
+            like(proj_shape, BF16), like((8, D), F32), like((4, 1, D), F32),
         ],
         scratch_shapes=[
             pltpu.VMEM((rows, D), BF16), pltpu.VMEM((rows, D), F32),
@@ -762,22 +837,25 @@
             pltpu.VMEM((4, 2, D, D), BF16), pltpu.VMEM((2, 2, D, D), BF16),
             pltpu.VMEM((2, D, D), BF16), pltpu.VMEM((2, padded, D), BF16),
             pltpu.VMEM((2, padded // 2, D), BF16),
-            pltpu.SemaphoreType.DMA((8,)), pltpu.SemaphoreType.DMA((8,)),
+            pltpu.VMEM((SMALL_SIZE, D), F32), pltpu.VMEM((4,) + own_weights.shape, BF16),
+            pltpu.SemaphoreType.DMA((12,)), pltpu.SemaphoreType.DMA((12,)),
+            pltpu.SemaphoreType.DMA((2,)),
         ],
         compiler_params=params(collective_id=2, has_side_effects=True),
         cost_estimate=pl.CostEstimate(flops=rows * D * D * 60, bytes_accessed=3 * 10**7, transcendentals=0),
         name="middle",
-    )(attended, first, *cot_parts, vec, bias, proj, fc1, fc2)
+    )(attended, first, *cot_parts, small, own_weights, far_weights)
 
 
 def back_kernel(
-    cuts_ref, me_ref, grad_ref, query_ref, value_ref, soft_ref, context_ref, conv_ref, hidden_ref,
-    crpe_ref,
-    three_ref, qkv_out_ref, crpe_sum_ref, sum_ref,
-    mask_ref, grid_ref, out_ref, other_ref, value_part_ref, qkv_grad_ref,
+    canvases, ids_ref, grad_ref, query_ref, value_ref, soft_ref, context_ref, conv_ref, hidden_ref,
+    small_in, middle_sum_ref, bias_grad_ref,
+    three_ref, qkv_out_ref, small_out_ref,
+    mask_ref, grid_ref, out_ref, other_ref, value_part_ref, qkv_grad_ref, small_ref, crpe_ref,
+    crpe_sum_ref, sum_ref, late_ref,
 ):
-    cut, col_cuts = read_cuts(cuts_ref, 0)
-    me = me_ref[0]
+    cut, col_cuts = read_cuts(ids_ref, canvases)
+    me = lax.axis_index("head")
 
     @pl.when(pl.program_id(0) == 0)
     def _():
@@ -786,6 +864,8 @@
         qkv_grad_ref[...] = jnp.zeros_like(qkv_grad_ref)
         crpe_sum_ref[...] = jnp.zeros_like(crpe_sum_ref)
         sum_ref[...] = jnp.zeros_like(sum_ref)
+        spread_small(small_in, small_ref)
+        spread_taps(small_ref, CRPE, 49, True, crpe_ref)
 
     fill_masks(cut, col_cuts, mask_ref)
     band, side = place_ids(cut, col_cuts)
@@ -840,22 +920,42 @@
     @pl.when(pl.program_id(0) == pl.num_programs(0) - 1)
     def _():
         qkv_out_ref[...] = qkv_grad_ref[...].astype(BF16)
-
-
-def back(cuts, me, grad, query, value, soft, context, conv, hidden, crpe):
+        late_ref[...] = jnp.zeros_like(late_ref)
+        for tap in range(49):
+            for tile in range(TILES):
+                late_ref[tap : tap + 1, lane(tile)] = keep_head(
+                    tap, tile, jnp.sum(crpe_sum_ref[tap, :, lane(tile)], axis=0, keepdims=True)
+                )
+        late_ref[49:51, :] = sum_ref[0:2, :]
+        late_ref[51:55, :] = middle_sum_ref[0:4, :]
+        for move in range(4):
+            late = late_ref[:, aligned(lax.bitwise_xor(me, move), LANES)]
+            small_out_ref[move] = late.astype(BF16)
+            small_out_ref[move, 64:80, :] = jnp.concatenate(
+                [bias_grad_ref[move, :, lane(tile)] for tile in range(TILES)]
+                + [jnp.zeros((12, LANES), F32)],
+                axis=0,
+            ).astype(BF16)
+
+
+def back(ids, grad, query, value, soft, context, conv, hidden, small, middle_sum, bias_grad):
     rows = grad.shape[0]
     count = rows // PLACES
     wide = rows_spec(D)
     shards = (4, D, 3 * LANES)
+    late = (4, SMALL_ROWS, LANES)
     return pl.pallas_call(
-        lambda *refs: back_kernel(*refs),
+        lambda *refs: back_kernel(count, *refs),
         grid_spec=pltpu.PrefetchScalarGridSpec(
-            num_scalar_prefetch=2,
+            num_scalar_prefetch=1,
             grid=(count,),
-            in_specs=[wide, wide, wide, wide, context_spec(0), wide, wide, whole(crpe.shape)],
+            in_specs=[
+                wide, wide, wide, wide, context_spec(0), wide, wide, once(small.shape),
+                once(middle_sum.shape), once(bias_grad.shape),
+            ],
             out_specs=[
                 pl.BlockSpec((TILES, PLACES, 3 * LANES), lambda i, *_: (0, i, 0)),
-                once(shards), whole((49, 8, D)), whole((8, D)),
+                once(shards), once(late),
             ],
             scratch_shapes=[
                 pltpu.VMEM((2, 7, SIDE, LANES), F32),
@@ -864,18 +964,22 @@
                 pltpu.VMEM((PLACES + SIDE, D), F32),
                 pltpu.VMEM((PLACES, D), F32),
                 pltpu.VMEM(shards, F32),
+                pltpu.VMEM((SMALL_SIZE, D), F32),
+                pltpu.VMEM((49, 8, D), F32),
+                pltpu.VMEM((49, 8, D), F32),
+                pltpu.VMEM((8, D), F32),
+                pltpu.VMEM((SMALL_ROWS, D), F32),
             ],
         ),
         out_shape=[
-            like((TILES, rows, 3 * LANES), BF16), like(shards, BF16), like((49, 8, D), F32),
-            like((8, D), F32),
+            like((TILES, rows, 3 * LANES), BF16), like(shards, BF16), like(late, BF16),
         ],
         compiler_params=params(),
         cost_estimate=pl.CostEstimate(
             flops=rows * D * D * 64, bytes_accessed=count * 10**7, transcendentals=0
         ),
         name="back",
-    )(cuts, me, grad, query, value, soft, context, conv, hidden, crpe)
+    )(ids, grad, query, value, soft, context, conv, hidden, small, middle_sum, bias_grad)
 
 
 def step_masks(cut, col_cuts):
@@ -919,13 +1023,13 @@
 
 def tail_kernel(
     count, pieces,
-    cuts_ref, x0_ref, x1_ref, x2_ref, x3_ref, three_ref, first_ref, second_grad_ref, vec_ref, qkv_ref,
-    cpe_ref, fc_mid_in, qkv_grad_in, proj_grad_in, small_in,
+    canvases, ids_ref, x0_ref, x1_ref, x2_ref, x3_ref, three_ref, first_ref, second_grad_ref, small_params,
+    qkv_ref, fc_mid_in, qkv_grad_in, proj_grad_in, small_in,
     out0_ref, out1_ref, out2_ref, out3_ref, fc1_own_ref, fc2_own_ref, qkv_own_ref, proj_own_ref,
     small_own_ref, last_own_ref,
     x_ref, gone_ref, cpe_sum_ref, sum_ref, fc_part_ref, fc_whole_ref, fc_got_ref, mine_ref, first_got_ref,
     total_ref, second_got_ref, piece_send, piece_receive, send, receive, last_send, last_receive,
-    fc_mid_ref, qkv_grad_ref, proj_grad_ref, small_ref, *buffers,
+    cpe_ref, fc_mid_ref, qkv_grad_ref, proj_grad_ref, small_ref, *buffers,
 ):
     me = lax.axis_index("head")
     dp = lax.axis_index("dp")
@@ -975,6 +1079,7 @@
         meet(
             [peer(1), peer(2), peer(3)] + [(lax.rem(dp + hop, count), me) for hop in range(1, count)]
         )
+        spread_small(small_params, cpe_ref)
         fc_mid_ref[...] = fc_mid_in[...]
         qkv_grad_ref[...] = qkv_grad_in[...]
         proj_grad_ref[...] = proj_grad_in[...]
@@ -1006,7 +1111,7 @@
     square = row_mean(first * first)
     inverse = lax.rsqrt(square - center * center + EPSILON)
     hat = (first - center) * inverse
-    weighted = norm_grad * vec_ref[1:2, :]
+    weighted = norm_grad * cpe_ref[GAIN1 : GAIN1 + 1, :]
     first_grad = second_grad_ref[...] + inverse * (
         weighted - row_mean(weighted) - hat * row_mean(weighted * hat)
     )
@@ -1015,7 +1120,7 @@
     sum_ref[2:3, :] += jnp.sum(norm_grad, axis=0, keepdims=True)
     for move, piece_ref in enumerate((x0_ref, x1_ref, x2_ref, x3_ref)):
         x_ref[:, aligned(lax.bitwise_xor(me, move), LANES)] = piece_ref[...].astype(F32)
-    rows, cols = step_masks(cuts_ref[step, 0], (cuts_ref[step, 1], cuts_ref[step, 2]))
+    rows, cols = step_masks(*read_cuts(ids_ref, canvases))
     results = []
     for tile in range(TILES):
         field = first_grad[:, LANES * tile : LANES * (tile + 1)]
@@ -1052,8 +1157,8 @@
             first_copy(move).start()
         for item in fc_sums:
             item.finish()
-        fc1_own_ref[...] = fc_whole_ref[0, :D, :].astype(F32)
-        fc2_own_ref[...] = fc_whole_ref[1, :D, :].astype(F32)
+        fc1_own_ref[...] = fc_whole_ref[0, :D, :]
+        fc2_own_ref[...] = fc_whole_ref[1, :D, :]
         total = mine_ref[0]
         for move in (1, 2, 3):
             first_copy(move).wait()
@@ -1063,7 +1168,7 @@
             second_copy(hop).start()
         for piece, item in zip(pieces, sums):
             item.rest.finish()
-            targets[piece[0]][piece[1] : piece[1] + piece[2], :] = item.whole[: piece[2], :].astype(F32)
+            targets[piece[0]][piece[1] : piece[1] + piece[2], :] = item.whole[: piece[2], :]
         for hop in range(1, count):
             second_copy(hop).wait()
             total += second_got_ref[hop - 1]
@@ -1077,7 +1182,7 @@
         lax.fori_loop(0, steps, settle, 0)
 
 
-def tail(cuts, x_parts, three, first, second_grad, vec, qkv, cpe, fc_mid, qkv_grad, proj_grad, small):
+def tail(ids, x_parts, three, first, second_grad, params_small, qkv, fc_mid, qkv_grad, proj_grad, small):
     rows = first.shape[0]
     canvases = rows // PLACES
     count = lax.axis_size("dp")
@@ -1092,16 +1197,16 @@
     total_slots = 2 * slots + len(pieces) * (slots + 4)
     last = (LAST_ROWS, LANES)
     return pl.pallas_call(
-        lambda *refs: tail_kernel(count, pieces, *refs),
+        lambda *refs: tail_kernel(count, pieces, canvases, *refs),
         grid=(canvases,),
         in_specs=[pl.BlockSpec(memory_space=pltpu.SMEM)] + [piece] * 4 + [
             pl.BlockSpec((TILES, PLACES, 3 * LANES), lambda i: (0, i, 0)), wide, wide,
-            once(vec.shape), once(qkv.shape), once(cpe.shape), once(fc_mid.shape),
+            once(params_small.shape), once(qkv.shape), once(fc_mid.shape),
         ] + [once(item.shape) for item in segments],
         out_specs=[piece, hbm, hbm, hbm, once((D, D)), once((D, D))]
         + [once(item.shape[1:]) for item in segments] + [once(last)],
-        out_shape=[like((rows, LANES), BF16)] * 4 + [like((D, D), F32)] * 2
-        + [like(item.shape[1:], F32) for item in segments] + [like(last, F32)],
+        out_shape=[like((rows, LANES), BF16)] * 4 + [like((D, D), BF16)] * 2
+        + [like(item.shape[1:], BF16) for item in segments] + [like(last, F32)],
         scratch_shapes=[
             pltpu.VMEM((PLACES, D), F32), pltpu.VMEM((canvases, 3, PLACES, LANES), BF16),
             pltpu.VMEM((9, 8, D), F32), pltpu.VMEM((LAST_ROWS, D), F32),
@@ -1112,14 +1217,15 @@
             pltpu.SemaphoreType.DMA((canvases, 3)), pltpu.SemaphoreType.DMA((canvases, 3)),
             pltpu.SemaphoreType.DMA((total_slots,)), pltpu.SemaphoreType.DMA((total_slots,)),
             pltpu.SemaphoreType.DMA((2 + count,)), pltpu.SemaphoreType.DMA((2 + count,)),
-        ] + [pltpu.VMEM(item.shape, BF16) for item in [fc_mid] + segments]
+        ] + [pltpu.VMEM((SMALL_SIZE, D), F32)]
+        + [pltpu.VMEM(item.shape, BF16) for item in [fc_mid] + segments]
         + sum_scratch(pieces, count),
         compiler_params=params(collective_id=3, has_side_effects=True),
         cost_estimate=pl.CostEstimate(
             flops=rows * D * D * 12, bytes_accessed=canvases * 3 * 10**6, transcendentals=0
         ),
         name="tail",
-    )(cuts, *x_parts, three, first, second_grad, vec, qkv, cpe, fc_mid, *segments)
+    )(ids, *x_parts, three, first, second_grad, params_small, qkv, fc_mid, *segments)
 
 
 def collect_kernel(me_ref, *refs):
@@ -1132,60 +1238,69 @@
 
 
 def collect(me, pieces):
-    parts = len(pieces[0])
-    rows = pieces[0][0].shape[0]
+    rows = pieces[0].shape[0]
     return pl.pallas_call(
         collect_kernel,
         grid_spec=pltpu.PrefetchScalarGridSpec(
             num_scalar_prefetch=1,
-            grid=(4 * parts,),
-            in_specs=[once((rows, LANES))] * (4 * parts),
-            out_specs=pl.BlockSpec(
-                (rows, LANES),
-                lambda i, me: (lax.bitwise_xor(me[0], i // parts) * parts + i % parts, 0),
-            ),
+            grid=(4,),
+            in_specs=[once((rows, LANES))] * 4,
+            out_specs=pl.BlockSpec((rows, LANES), lambda i, me: (lax.bitwise_xor(me[0], i), 0)),
         ),
-        out_shape=like((4 * parts * rows, LANES), F32),
+        out_shape=like((4 * rows, LANES), F32),
         compiler_params=params(),
         name="collect",
-    )(me, *[piece for move in pieces for piece in move])
-
-
-HALVES = 2
-
-
-def find_cuts(crop_ids):
-    cut = jnp.sum((crop_ids[:, :, 0] < 2).astype(jnp.int32), axis=1)
-    upper = jnp.sum((crop_ids[:, 0, :] == 0).astype(jnp.int32), axis=1)
-    lower = jnp.sum((crop_ids[:, SIDE - 1, :] == 2).astype(jnp.int32), axis=1)
-    return jnp.stack([cut, upper, lower], axis=1)
-
-
-def reach_mask():
-    head = jnp.arange(D, dtype=jnp.int32) // HEAD_DIM
-    reach = 1 + (head >= 2).astype(jnp.int32) + (head >= 5).astype(jnp.int32)
-    taps = jnp.arange(49, dtype=jnp.int32)
-    ring = jnp.maximum(jnp.abs(taps // 7 - 3), jnp.abs(taps % 7 - 3))
-    return (ring[:, None] <= reach[None, :]).astype(F32)
-
-
-def forward_parts(me, cuts, x_halves, small, qkv):
-    zero = jnp.zeros((D,), F32)
-    vec = jnp.stack([small[58], small[59], small[60], small[61], small[62], zero, zero, zero])
-    crpe = jnp.broadcast_to((small[9:58] * reach_mask())[:, None, :], (49, 8, D))
-    cpe = jnp.broadcast_to(small[:9][:, None, :], (9, 8, D))
-    kept = ()
-    base = 0
-    for x_parts in x_halves:
-        kept = front(cuts, me, x_parts, base, kept, cpe, vec, qkv, crpe)
-        base += x_parts[0].shape[0] // PLACES
-    return kept, vec, crpe, cpe
-
-
-def middle_parts(kept, cot_parts, small, bias, proj, fc1, fc2):
-    zero = jnp.zeros((D,), F32)
-    vec = jnp.stack([small[63], small[64], small[65], small[66], zero, zero, zero, zero])
-    return middle(kept[7], kept[0], cot_parts, vec, bias, proj, fc1, fc2)
+    )(me, *pieces)
+
+
+def finish_kernel(
+    me_ref, p0_ref, p1_ref, p2_ref, p3_ref, fc1_ref, fc2_ref, qkv_ref, proj_ref, small_ref, last_ref,
+    grad_ref, cpe_ref, vectors_ref, qkv_out_ref, qv_ref, crpe_ref, proj_out_ref, fc1_out_ref,
+    bias_ref, fc2_out_ref,
+):
+    for item, piece_ref in enumerate((p0_ref, p1_ref, p2_ref, p3_ref)):
+
+        @pl.when(pl.program_id(0) == item)
+        def _():
+            grad_ref[...] = piece_ref[...].astype(F32)
+
+    @pl.when(pl.program_id(0) == 0)
+    def _():
+        cpe_ref[...] = last_ref[3:12, :]
+        small = small_ref[...].astype(F32)
+        vectors_ref[...] = jnp.concatenate(
+            [last_ref[0:3, :], small[51:55, :], jnp.zeros((1, LANES), F32)], axis=0
+        )
+        qkv_out_ref[...] = qkv_ref[...].astype(F32)
+        qv_ref[...] = small[49:51, :]
+        crpe_ref[...] = small[:49, :]
+        proj_out_ref[...] = proj_ref[...].astype(F32)
+        fc1_out_ref[...] = fc1_ref[...].astype(F32)
+        bias_ref[...] = small[64:68, :]
+        fc2_out_ref[...] = fc2_ref[...].astype(F32)
+
+
+def finish(me, pieces, fc1, fc2, qkv, proj, small, last):
+    rows = pieces[0].shape[0]
+    shapes = [
+        (9, LANES), (8, LANES), qkv.shape, (2, LANES), (49, LANES), proj.shape, fc1.shape,
+        (4, LANES), fc2.shape,
+    ]
+    return pl.pallas_call(
+        finish_kernel,
+        grid_spec=pltpu.PrefetchScalarGridSpec(
+            num_scalar_prefetch=1,
+            grid=(4,),
+            in_specs=[once((rows, LANES))] * 4
+            + [once(item.shape) for item in (fc1, fc2, qkv, proj, small, last)],
+            out_specs=[
+                pl.BlockSpec((rows, LANES), lambda i, me: (lax.bitwise_xor(me[0], i), 0)),
+            ] + [once(shape) for shape in shapes],
+        ),
+        out_shape=[like((4 * rows, LANES), F32)] + [like(shape, F32) for shape in shapes],
+        compiler_params=params(),
+        name="finish",
+    )(me, *pieces, fc1, fc2, qkv, proj, small, last)
 
 
 def body(
@@ -1195,77 +1310,45 @@
 ):
     head = lax.axis_index("head")
     me = head.reshape(1).astype(jnp.int32)
-    canvases = crop_ids.shape[0] // 4
-    rows = canvases * PLACES
-    cuts = find_cuts(lax.dynamic_slice_in_dim(crop_ids, head * canvases, canvases, 0))
+    rows = block_in.shape[0] // 4
+    ids = crop_ids.reshape(crop_ids.shape[0], PLACES)
 
     def swap(values, move):
         return lax.ppermute(values, "head", [(item, item ^ move) for item in range(4)])
-
-    def take(values, move, part, parts):
-        size = rows // parts
-        start = lax.bitwise_xor(head, move) * rows + part * size
-        return lax.dynamic_slice_in_dim(values, start, size, 0)
-
-    def bring(values, part, parts):
-        pieces = [take(values, move, part, parts) for move in range(4)]
-        return [pieces[0]] + [swap(pieces[move], move) for move in (1, 2, 3)]
-
-    def gather(shard):
-        far = swap(shard, 2)
-        near = swap(jnp.stack([shard, far]), 1)
-        return jnp.stack([shard, near[0], far, near[1]])
 
     packed = jnp.concatenate([
         cpe_kernel, crpe_kernel, cpe_bias[None], norm1_gain[None], norm1_shift[None], qv_bias,
         proj_bias[None], norm2_gain[None], norm2_shift[None], fc2_bias[None],
         fc1_bias.reshape(4, LANES), jnp.zeros((1, LANES), BF16),
     ]).astype(F32)
-    part_rows = rows // HALVES
-    order = lax.bitwise_xor(head, jnp.arange(4, dtype=jnp.int32))
-    x1, x2, x3, qkv, small_all = entry(
-        block_in, part_rows, qkv_weight.reshape(D, 3 * LANES), packed
+    own_weights = jnp.concatenate([fc1_weight, fc2_weight, proj_weight])
+    *x_parts, qkv, small = entry(block_in, qkv_weight.reshape(D, 3 * LANES), packed)
+    own_weights, cotangent, x_parts = lax.optimization_barrier((own_weights, cotangent, x_parts))
+    far_weights = swap(own_weights, 2)
+    cot_pieces = [
+        lax.dynamic_slice_in_dim(cotangent, lax.bitwise_xor(head, move) * rows, rows, 0)
+        for move in range(4)
+    ]
+    cot_parts = [cot_pieces[0]] + [swap(cot_pieces[move], move) for move in (1, 2, 3)]
+
+    first, hidden, query, value, soft, context, conv, attended = front(ids, x_parts, small, qkv)
+    results = middle(attended, first, cot_parts, small, own_weights, far_weights)
+    second_grad, att_grad, fc_mid, proj_grad, middle_sum, bias_grad = results[4:]
+    out_parts = [results[0]] + [swap(results[move], move) for move in (1, 2, 3)]
+    three, qkv_grad, small_grad = back(
+        ids, att_grad, query, value, soft, context, conv, hidden, small, middle_sum, bias_grad
     )
-    x_halves = [[take(block_in, 0, 0, HALVES), x1, x2, x3]]
-    block_in, proj_weight, cotangent, fc1_weight, fc2_weight, x_halves = lax.optimization_barrier(
-        (block_in, proj_weight, cotangent, fc1_weight, fc2_weight, x_halves)
+    three, out_parts = lax.optimization_barrier((three, out_parts))
+    results = tail(
+        ids, x_parts, three, first, second_grad, small, qkv, fc_mid, qkv_grad, proj_grad, small_grad
     )
-    x_halves += [bring(block_in, part, HALVES) for part in range(1, HALVES)]
-    cot_parts = bring(cotangent, 0, 1)
-    proj = gather(proj_weight)
-    fc1 = gather(fc1_weight)
-    fc2 = gather(fc2_weight)
-    small = jnp.take(small_all[:, :67], order, axis=0).transpose(1, 0, 2).reshape(67, D)
-    bias = small_all[:, 67:71].reshape(4, 1, D)
-
-    kept, vec, crpe, cpe = forward_parts(me, cuts, x_halves, small, qkv)
-    first, hidden, query, value, soft, context, conv, attended = kept
-    results = middle_parts(kept, cot_parts, small, bias, proj, fc1, fc2)
-    second_grad, att_grad, fc_mid, proj_grad, sums2, bias_grad = results[4:]
-    out_parts = [[results[0]]] + [[swap(results[move], move)] for move in (1, 2, 3)]
-    three, qkv_grad, crpe_sum, sums1 = back(
-        cuts, me, att_grad, query, value, soft, context, conv, hidden, crpe
+    (input_grad, cpe_g, vectors, qkv_g, qv_g, crpe_g, proj_g, fc1_g, bias_g, fc2_g) = finish(
+        me, results[:4], *results[4:]
     )
-    small_grad = jnp.concatenate([
-        jnp.sum(crpe_sum, axis=1) * reach_mask(), sums1[0:2], sums2[3:4], sums2[1:3], sums2[0:1],
-    ])
-    small_rows = small_grad.shape[0]
-    small_grad = jnp.concatenate([
-        jnp.take(small_grad.reshape(-1, 4, LANES).transpose(1, 0, 2), order, axis=0),
-        bias_grad.reshape(4, 4, LANES), jnp.zeros((4, SMALL_ROWS - small_rows - 4, LANES), F32),
-    ], axis=1).astype(BF16)
-    x_parts = [jnp.concatenate([item[move] for item in x_halves]) for move in range(4)]
-    results = tail(
-        cuts, x_parts, three, first, second_grad, vec, qkv, small[:9], fc_mid, qkv_grad, proj_grad,
-        small_grad,
-    )
-    fc1_own, fc2_own, qkv_own, proj_own, small_own, last_own = results[4:]
     return (
-        collect(me, out_parts), collect(me, [[item] for item in results[:4]]),
-        last_own[3:12], last_own[0], last_own[1], last_own[2],
-        qkv_own.reshape(D, 3, LANES), small_own[49:51], small_own[:49],
-        proj_own, small_own[51], small_own[52], small_own[53],
-        fc1_own, small_own[55:59].reshape(D), fc2_own, small_own[54],
+        collect(me, out_parts), input_grad, cpe_g, vectors[0], vectors[1], vectors[2],
+        qkv_g.reshape(D, 3, LANES), qv_g, crpe_g, proj_g, vectors[3], vectors[4], vectors[5],
+        fc1_g, bias_g.reshape(D), fc2_g, vectors[6],
     )
 
 

time: 361 us -> 305 us (0.84)
  local copies, waits for them, and re-layouts: 38.8 us -> 12.3 us
  other arithmetic: 23.5 us -> 2.11 us
  waiting for transfers between devices: 7.54 us -> 0.02 us
  starting transfers between devices: 10.2 us -> 5.26 us
  Pallas kernels: 279 us -> 283 us
    pallas_call x5, Pallas kernels: 202 us -> 211 us  [the longest x1 61.3 us: tail(): pl.pallas_call(lambda *refs: tail_kernel(count, pieces, canvases, *refs),...]
    another operation x9 -> x0, other arithmetic: 7.77 us -> none  [the longest x3 5.08 us: gather(): return jnp.stack([shard, near[0], far, near[1]])]
    slice x15 -> x0, local copies, waits for them, and re-layouts: 7.61 us -> none  [the longest x1 1.36 us: body(): small_own[:49]]
    ppermute x15 -> x7, waiting for transfers between devices: 7.54 us -> 0.02 us  [swap(): lax.ppermute(values, 'head', [(item, item ^ move) for item in range(4)])]
    another operation x8 -> x0, local copies, waits for them, and re-layouts: 6.63 us -> none  [the longest x3 3.96 us: find_cuts(): return jnp.stack([cut, upper, lower], axis=1)]
    concatenate x5 -> x1, other arithmetic: 6.97 us -> 1.49 us  [body(): own_weights = jnp.concatenate([fc1_weight, fc2_weight, proj_weight])]
    ppermute x15 -> x7, starting transfers between devices: 10.2 us -> 5.26 us  [swap(): lax.ppermute(values, 'head', [(item, item ^ move) for item in range(4)])]
    unnamed x65 -> x20, local copies, waits for them, and re-layouts: 7.98 us -> 3.42 us
  transfers between devices with their start and end apart: 15 -> 7, of which waited for: 1 -> 0; matrix products, arithmetic and copies ran while one was open for 12% -> 1% of each run, Pallas kernels for 35% -> 35%
where the time goes in v4:
time: 305 us; the launch traced here: 303 us
  Pallas kernels  283 us (93%)
  local copies, waits for them, and re-layouts  12.3 us (4%)
  starting transfers between devices  5.26 us (2%)
    pallas_call x1, Pallas kernels, middle(): pl.pallas_call(lambda *refs: middle_kernel(count, *refs), grid=(4,), in_s...  67.8 us
    pallas_call x1, Pallas kernels, tail(): pl.pallas_call(lambda *refs: tail_kernel(count, pieces, canvases, *refs),...  61.3 us
    pallas_call x1, Pallas kernels, back(): pl.pallas_call(lambda *refs: back_kernel(count, *refs), grid_spec=pltpu.P...  58.4 us
    pallas_call x1, Pallas kernels, front(): pl.pallas_call(lambda *refs: front_kernel(count, *refs), grid_spec=pltpu....  48.5 us
    pallas_call x1, Pallas kernels, entry(): pl.pallas_call(lambda *refs: entry_kernel(rows, *refs), in_specs=[hbm] *...  37.1 us
  transfers between devices with their start and end apart: 7, of which 0 were waited for; matrix products, arithmetic and copies ran while one was open for 1% of the time, Pallas kernels for 35%

profile of v4, /device:TPU:0, one launch (start us, length us, event | category | flops | bytes accessed | tf_op | source)
XLA Modules:
  0.0 303.4 jit_solution(11776328442533688352)
XLA Ops:
  0.7 3.0 concatenate.7
  3.7 0.6 convert_element_type.3.refs_2_
  4.3 1.2 copy.38
  5.5 0.9 copy.39.refs_1_
  6.4 0.0 copy-start
  6.4 1.5 pad_maximum_fusion.refs_7_
  7.9 0.0 copy-start.1
  7.9 37.1 %entry.1 = (bf16[2048,128]{1,0:T(8,128)(2,1)}, bf16[2048,128]{1,0:T(8,128)(2,1)}, bf16[2048,128]{1,0:T(8,128)(2,1)}, bf16[2048,128]{1,0:T(8,128)(2,1)}, bf16[4,5...) custom-call(bf16[8192,128]{1,0:T(8,128)(2,1)} %refs_0_.1, bf16[512,384]{1,0:T(8,128)(2,1)} %copy.39.refs_1_, ...), custom_call_target="tpu_custom_call" | custom-call | tf_op jit(solution)/shard_map/entry/pallas_call | solution.py:492
  45.0 1.5 collective-permute-start.3
  46.5 0.0 copy-done
  46.5 0.0 copy-start.5
  46.5 1.4 constant_dynamic-slice_fusion
  47.9 0.0 copy-done.1
  47.9 0.1 collective-permute-start.2
  48.0 1.6 collective-permute-start.1
  49.6 0.2 collective-permute-start
  49.8 0.0 copy-done.5
  49.8 0.7 copy.41.refs_0_
  50.5 48.5 %front.1 = (f32[2048,512]{1,0:T(8,128)}, bf16[2048,512]{1,0:T(8,128)(2,1)}, bf16[2048,512]{1,0:T(8,128)(2,1)}, bf16[2048,512]{1,0:T(8,128)(2,1)}, bf16[2048,512]...) custom-call(s32[32,256]{1,0:T(8,128)} %copy.41.refs_0_, ...), custom_call_target="tpu_custom_call" | custom-call | flops 32212254720 | bytes 80000000 | tf_op jit(solution)/shard_map/front/pallas_call | solution.py:579
  98.9 0.0 collective-permute-done.2.refs_5_
  98.9 0.0 copy-start.6
  99.0 0.0 collective-permute-done.1.refs_4_
  99.0 0.0 copy-start.7
  99.0 0.0 collective-permute-done.refs_3_
  99.0 0.0 copy-start.8
  99.0 0.0 collective-permute-done.3.refs_8_
  99.0 0.8 copy-done.6
  99.8 0.1 copy-done.7
  99.9 0.2 copy-done.8
  100.1 67.8 %middle.1 = (bf16[2048,128]{1,0:T(8,128)(2,1)}, bf16[2048,128]{1,0:T(8,128)(2,1)}, bf16[2048,128]{1,0:T(8,128)(2,1)}, bf16[2048,128]{1,0:T(8,128)(2,1)}, f32[204...) custom-call(bf16[2048,512]{1,0:T(8,128)(2,1)} %get-tuple-element.85., ...), custom_call_target="tpu_custom_call" | custom-call | flops 32212254720 | bytes 30000000 | tf_op jit(solution)/shard_map/middle/pallas_call | solution.py:817
  167.9 0.1 collective-permute-start.4
  168.0 1.6 collective-permute-start.5
  169.6 0.3 collective-permute-start.6
  169.8 58.4 %back.1 = (bf16[4,2048,384]{2,1,0:T(8,128)(2,1)}, bf16[4,512,384]{2,1,0:T(8,128)(2,1)}, bf16[4,128,128]{2,1,0:T(8,128)(2,1)}) custom-call(s32[32,256]{1,0:T(8,128)} %copy.41.refs_0_, bf16[2048,512]{1,0:T(8,128)(2,1)} %get-tuple-element.89.refs_1_, bf16[2048,512]{1,0:T(8,128)(2,1)} %get-tuple-element.90.refs_2_, bf16[2048,512]{1,0:T(8,128)(2,1)} %get-tuple-element.91.refs_3_, ...), custom_call_target="tpu_custom_call" | custom-call | flops 34359738368 | bytes 80000000 | tf_op jit(solution)/shard_map/back/pallas_call | solution.py:947
  228.3 0.0 collective-permute-done.4.refs_1_
  228.3 0.0 copy-start.2
  228.3 0.0 collective-permute-done.5.refs_2_
  228.3 0.0 copy-start.3
  228.3 0.0 collective-permute-done.6.refs_3_
  228.3 0.0 copy-start.4
  228.3 61.3 %tail.1 = (bf16[2048,128]{1,0:T(8,128)(2,1)}, bf16[2048,128]{1,0:T(8,128)(2,1)}, bf16[2048,128]{1,0:T(8,128)(2,1)}, bf16[2048,128]{1,0:T(8,128)(2,1)}, bf16[512,...) custom-call(s32[32,256]{1,0:T(8,128)} %copy.41.refs_0_, ...), custom_call_target="tpu_custom_call" | custom-call | flops 6442450944 | bytes 24000000 | tf_op jit(solution)/shard_map/tail/pallas_call | solution.py:1199
  289.7 0.0 copy-done.2
  289.7 0.0 copy-done.3
  289.7 0.0 copy-done.4
  289.7 5.7 %finish.1 = (f32[8192,128]{1,0:T(8,128)}, f32[9,128]{1,0:T(8,128)}, f32[8,128]{1,0:T(8,128)}, f32[512,384]{1,0:T(8,128)}, f32[2,128]{1,0:T(2,128)}, /*index=5*/f...) custom-call(s32[1]{0:T(128)} %bitcast.me_ref, ...), custom_call_target="tpu_custom_call" | custom-call | tf_op jit(solution)/shard_map/finish/pallas_call | solution.py:1289
  295.5 1.5 slice_bitcast_fusion
  296.9 1.4 copy.43
  298.3 1.1 copy.44
  299.5 4.0 %collect.1 = f32[8192,128]{1,0:T(8,128)} custom-call(s32[1]{0:T(128)} %bitcast.me_ref, bf16[2048,128]{1,0:T(8,128)(2,1)} %get-tuple-element.103.refs_0_, bf16[2048,128]{1,0:T(8,128)(2,1)} %copy-done.2, bf16[2048,128]{1,0:T(8,128)(2,1)} %copy-done.3, bf16[2048,128]{1,0:T(8,128)(2,1)} %copy-done.4), custom_call_target="tpu_custom_call" | custom-call | tf_op jit(solution)/shard_map/collect/pallas_call | solution.py:1242
  (1 shorter events, 0.0 us)
Async XLA Ops:
  6.4 40.1 %copy-start = (bf16[8192,128]{1,0:T(8,128)(2,1)S(1)}, bf16[8192,128]{1,0:T(8,128)(2,1)}, u32[]{:S(2)}) copy-start(bf16[8192,128]{1,0:T(8,128)(2,1)} %param.20) | copy-start | bytes 6291460
  7.9 40.0 %copy-start.1 = (bf16[1152,512]{1,0:T(8,128)(2,1)}, bf16[1152,512]{1,0:T(8,128)(2,1)S(1)}, u32[]{:S(2)}) copy-start(bf16[1152,512]{1,0:T(8,128)(2,1)S(1)} %pad_maximum_fusion.refs_7_) | copy-start | bytes 3538948
  45.0 54.0 %collective-permute-start.3 = (bf16[1152,512]{1,0:T(8,128)(2,1)S(1)}, bf16[1152,512]{1,0:T(8,128)(2,1)}, u32[]{:S(2)}, u32[]{:S(2)}) collective-permute-start(bf16[1152,512]{1,0:T(8,128)(2,1)S(1)} %pad_maximum_fusion.refs_7_), channel_id=1, source_target_pairs={{0,2},{1,3},{2,0},{3,1},{4,6},{5,7},{6,4},{7,5},{8,10},{9,11},{10,... | collective-permute-start | bytes 3538952 | tf_op jit(solution)/shard_map/ppermute | solution.py:1317
  46.5 3.3 %copy-start.5 = (s32[32,16,16]{0,2,1:T(8,128)S(1)}, s32[32,16,16]{0,2,1:T(8,128)}, u32[]{:S(2)}) copy-start(s32[32,16,16]{0,2,1:T(8,128)} %param.19) | copy-start | bytes 98308
  47.9 51.0 %collective-permute-start.2 = (bf16[2048,128]{1,0:T(8,128)(2,1)}, bf16[2048,128]{1,0:T(8,128)(2,1)S(1)}, u32[]{:S(2)}, u32[]{:S(2)}) collective-permute-start(bf16[2048,128]{1,0:T(8,128)(2,1)} %get-tuple-element.167), channel_id=1, source_target_pairs={{0,3},{1,2},{2,1},{3,0},{4,7},{5,6},{6,5},{7,4},{8,11},{9,10},{10,... | collective-permute-start | bytes 1572872 | tf_op jit(solution)/shard_map/ppermute | solution.py:1317
  48.0 51.0 %collective-permute-start.1 = (bf16[2048,128]{1,0:T(8,128)(2,1)}, bf16[2048,128]{1,0:T(8,128)(2,1)S(1)}, u32[]{:S(2)}, u32[]{:S(2)}) collective-permute-start(bf16[2048,128]{1,0:T(8,128)(2,1)} %get-tuple-element.168), channel_id=1, source_target_pairs={{0,2},{1,3},{2,0},{3,1},{4,6},{5,7},{6,4},{7,5},{8,10},{9,11},{10,... | collective-permute-start | bytes 1572872 | tf_op jit(solution)/shard_map/ppermute | solution.py:1317
  49.6 49.4 %collective-permute-start = (bf16[2048,128]{1,0:T(8,128)(2,1)}, bf16[2048,128]{1,0:T(8,128)(2,1)S(1)}, u32[]{:S(2)}, u32[]{:S(2)}) collective-permute-start(bf16[2048,128]{1,0:T(8,128)(2,1)} %get-tuple-element.169), channel_id=1, source_target_pairs={{0,1},{1,0},{2,3},{3,2},{4,5},{5,4},{6,7},{7,6},{8,9},{9,8},{10,11... | collective-permute-start | bytes 1572872 | tf_op jit(solution)/shard_map/ppermute | solution.py:1317
  98.9 0.9 copy-start.6
  99.0 0.9 copy-start.7
  99.0 1.1 copy-start.8
  167.9 60.4 %collective-permute-start.4 = (bf16[2048,128]{1,0:T(8,128)(2,1)}, bf16[2048,128]{1,0:T(8,128)(2,1)S(1)}, u32[]{:S(2)}, u32[]{:S(2)}) collective-permute-start(bf16[2048,128]{1,0:T(8,128)(2,1)} %get-tuple-element.100), channel_id=1, source_target_pairs={{0,1},{1,0},{2,3},{3,2},{4,5},{5,4},{6,7},{7,6},{8,9},{9,8},{10,11... | collective-permute-start | bytes 1572872 | tf_op jit(solution)/shard_map/ppermute | solution.py:1317
  168.0 60.3 %collective-permute-start.5 = (bf16[2048,128]{1,0:T(8,128)(2,1)}, bf16[2048,128]{1,0:T(8,128)(2,1)S(1)}, u32[]{:S(2)}, u32[]{:S(2)}) collective-permute-start(bf16[2048,128]{1,0:T(8,128)(2,1)} %get-tuple-element.101), channel_id=1, source_target_pairs={{0,2},{1,3},{2,0},{3,1},{4,6},{5,7},{6,4},{7,5},{8,10},{9,11},{10,... | collective-permute-start | bytes 1572872 | tf_op jit(solution)/shard_map/ppermute | solution.py:1317
  169.6 58.7 %collective-permute-start.6 = (bf16[2048,128]{1,0:T(8,128)(2,1)}, bf16[2048,128]{1,0:T(8,128)(2,1)S(1)}, u32[]{:S(2)}, u32[]{:S(2)}) collective-permute-start(bf16[2048,128]{1,0:T(8,128)(2,1)} %get-tuple-element.102), channel_id=1, source_target_pairs={{0,3},{1,2},{2,1},{3,0},{4,7},{5,6},{6,5},{7,4},{8,11},{9,10},{10,... | collective-permute-start | bytes 1572872 | tf_op jit(solution)/shard_map/ppermute | solution.py:1317
  228.3 61.4 %copy-start.2 = (bf16[2048,128]{1,0:T(8,128)(2,1)}, bf16[2048,128]{1,0:T(8,128)(2,1)S(1)}, u32[]{:S(2)}) copy-start(bf16[2048,128]{1,0:T(8,128)(2,1)S(1)} %collective-permute-done.4.refs_1_) | copy-start | bytes 1572868
  228.3 61.4 %copy-start.3 = (bf16[2048,128]{1,0:T(8,128)(2,1)}, bf16[2048,128]{1,0:T(8,128)(2,1)S(1)}, u32[]{:S(2)}) copy-start(bf16[2048,128]{1,0:T(8,128)(2,1)S(1)} %collective-permute-done.5.refs_2_) | copy-start | bytes 1572868
  228.3 61.4 %copy-start.4 = (bf16[2048,128]{1,0:T(8,128)(2,1)}, bf16[2048,128]{1,0:T(8,128)(2,1)S(1)}, u32[]{:S(2)}) copy-start(bf16[2048,128]{1,0:T(8,128)(2,1)S(1)} %collective-permute-done.6.refs_3_) | copy-start | bytes 1572868

commit v5 on v4

--- a/solution.py
+++ b/solution.py
@@ -84,16 +84,32 @@
     store[key] = term if key not in store else store[key] + term
 
 
+def over_bands(reach, cut, body):
+    every = range(2 * reach + 2)
+    for lower in range(2):
+        first = cut if lower else 0
+        height = SIDE - cut if lower else cut
+        pairs = (height + 1) // 2
+        shift = GAP * lower + GAP - reach
+
+        def pair(index, places):
+            row = first + 2 * index
+            body(row, row + shift, first + height - 1, places)
+
+        def inner(index, carry):
+            pair(index, every)
+            return carry
+
+        pair(0, every[reach:])
+        lax.fori_loop(1, pairs - 1, inner, 0)
+        pair(pairs - 1, every[: reach + 2])
+
+
 def conv_tiles(items, reach, cut, grid_ref, taps_ref, tap_reach, out_ref):
-    upper_pairs = (cut + 1) // 2
-    pairs = upper_pairs + (SIDE - cut + 1) // 2
     width = 2 * tap_reach + 1
     chains = 3
 
-    def body(index, carry):
-        lower = (index >= upper_pairs).astype(jnp.int32)
-        row = 2 * index + lower * (cut - 2 * upper_pairs)
-        base = row + GAP * lower + (GAP - reach)
+    def body(row, base, last, places):
         for tile, plane in items:
             total = {}
             for step in range(-reach, reach + 1):
@@ -101,7 +117,7 @@
                     taps_ref[(dr + tap_reach) * width + step + tap_reach, :, lane(tile)]
                     for dr in range(-reach, reach + 1)
                 ]
-                for place in range(2 * reach + 2):
+                for place in places:
                     for half in range(2):
                         start = pl.multiple_of(SIDE * (base + place) + 8 * half, 8)
                         field = grid_ref[plane + step, pl.ds(start, 8), :]
@@ -115,22 +131,16 @@
                     out_ref[pl.ds(start, 8), lane(tile)] = sum(
                         [total[out, half, chain] for chain in range(1, chains)], total[out, half, 0]
                     )
-        return carry
-
-    lax.fori_loop(0, pairs, body, 0)
+
+    over_bands(reach, cut, body)
 
 
 def conv_back_tiles(items, reach, cut, grid_ref, taps_ref, tap_reach, other_ref, out_ref, sum_ref):
-    upper_pairs = (cut + 1) // 2
-    pairs = upper_pairs + (SIDE - cut + 1) // 2
     width = 2 * tap_reach + 1
     chains = 2
 
-    def body(index, carry):
-        lower = (index >= upper_pairs).astype(jnp.int32)
-        row = 2 * index + lower * (cut - 2 * upper_pairs)
-        base = row + GAP * lower + (GAP - reach)
-        keep = jnp.where((lower == 0) & (row + 1 >= cut), 0.0, 1.0).astype(F32)
+    def body(row, base, last, places):
+        keep = jnp.where(row + 1 > last, 0.0, 1.0).astype(F32)
         for tile, plane in items:
             other = {}
             for out in range(2):
@@ -145,7 +155,7 @@
                     (tap_reach - dr) * width + tap_reach - step for dr in range(-reach, reach + 1)
                 ]
                 taps = [taps_ref[item, :, lane(tile)] for item in ids]
-                for place in range(2 * reach + 2):
+                for place in places:
                     for half in range(2):
                         start = pl.multiple_of(SIDE * (base + place) + 8 * half, 8)
                         field = grid_ref[plane + step, pl.ds(start, 8), :]
@@ -154,20 +164,16 @@
                             if 0 <= tap <= 2 * reach:
                                 add_to(total, (out, half, step % chains), taps[tap] * field)
                                 add_to(sums, tap, other[out, half] * field)
-                for tap in range(2 * reach + 1):
-                    sum_ref[ids[tap], :, lane(tile)] += sums[tap]
+                for tap, part in sums.items():
+                    sum_ref[ids[tap], :, lane(tile)] += part
             for out in range(2):
                 for half in range(2):
                     start = pl.multiple_of(SIDE * (row + out) + 8 * half, 8)
                     out_ref[pl.ds(start, 8), lane(tile)] = sum(
                         [total[out, half, chain] for chain in range(1, chains)], total[out, half, 0]
                     )
-        return carry
-
-    lax.fori_loop(0, pairs, body, 0)
-
-
-SMALL_ITEMS = tuple((tile, 3 * tile + 1) for tile in range(TILES))
+
+    over_bands(reach, cut, body)
 
 
 def row_mean(values):
@@ -453,84 +459,149 @@
     return scratch
 
 
-def entry_kernel(
-    rows, x_ref, qkv_ref, small_ref,
-    x0_ref, x1_ref, x2_ref, x3_ref, all_qkv_ref, all_small_ref,
-    send, receive, local,
+def step_masks(cut, col_cuts):
+    place = lax.broadcasted_iota(jnp.int32, (PLACES, LANES), 0)
+    row = lax.shift_right_logical(place, 4)
+    col = lax.bitwise_and(place, 15)
+    col_cut = jnp.where(row >= cut, col_cuts[1], col_cuts[0])
+    rows = {
+        1: (row < SIDE - 1) & (row + 1 != cut),
+        -1: (row > 0) & (row != cut),
+    }
+    cols = {
+        1: (col < SIDE - 1) & (col + 1 != col_cut),
+        -1: (col > 0) & (col != col_cut),
+    }
+    return [
+        {key: jnp.where(mask, 1.0, 0.0).astype(F32) for key, mask in masks.items()}
+        for masks in (rows, cols)
+    ]
+
+
+def shift_rows(values, step):
+    if step == 0:
+        return values
+    zero = jnp.zeros((SIDE, values.shape[1]), values.dtype)
+    if step > 0:
+        return jnp.concatenate([values[SIDE:], zero], axis=0)
+    return jnp.concatenate([zero, values[:-SIDE]], axis=0)
+
+
+def shift_cols(values, masks, step):
+    if step == 0:
+        return values
+    return pltpu.roll(values, (-step) % PLACES, 0) * masks[step]
+
+
+def head_kernel(
+    canvases, count, ids_ref, small_own, qkv_own, x_in, qkv_in, share_in,
+    first_ref, hidden_ref, query_ref, key_ref, value_ref, x_out, qkv_ref, small_out, far_out,
+    x_ref, landing_ref, mine_ref, small_ref, qkv_all, small_got, send, receive, weight_send, weight_receive,
+    share_send, share_receive, local,
 ):
-    head = lax.axis_index("head")
-    meet([peer(move) for move in (1, 2, 3)])
-    far = remote(qkv_ref, all_qkv_ref.at[2], send.at[0], receive.at[0], peer(2))
-    near = remote(qkv_ref, all_qkv_ref.at[1], send.at[1], receive.at[1], peer(1))
-    copies = [near]
+    me = lax.axis_index("head")
+    step = pl.program_id(0)
+    rows = canvases * PLACES
+
+    def piece(index, move):
+        start = pl.multiple_of(lax.bitwise_xor(me, move) * rows + index * PLACES, PLACES)
+        return remote(
+            x_in.at[pl.ds(start, PLACES)], landing_ref.at[index, move - 1], send.at[index, move - 1],
+            receive.at[index, move - 1], peer(move),
+        )
+
+    def weight(number, source, target, move):
+        return remote(source, target, weight_send.at[number], weight_receive.at[number], peer(move))
+
+    far = weight(0, qkv_in, qkv_all.at[1], 2)
+    near = weight(1, qkv_in, qkv_all.at[0], 1)
+    relay = weight(2, qkv_all.at[1], qkv_all.at[2], 1)
+    smalls = [weight(2 + move, small_got.at[0], small_got.at[move], move) for move in (1, 2, 3)]
+    mine = pltpu.make_async_copy(x_in.at[aligned(me, rows)], mine_ref, local.at[0])
+    dp = lax.axis_index("dp")
+    spot = aligned(dp, share_in.shape[0] // count)
+    share = remote(share_in.at[spot], far_out.at[spot], share_send.at[0], share_receive.at[0], peer(2))
+    group = count // 2
+    _, low, high = place_on_dp()
+    spread_high = [
+        remote(
+            far_out.at[spot], far_out.at[spot], share_send.at[hop], share_receive.at[hop],
+            high_peer(hop, group),
+        )
+        for hop in range(1, group)
+    ]
+    spread_low = []
+    for hop in range(group):
+        source = lax.rem(high - hop + group, group) * 2 + low
+        there = aligned(source, share_in.shape[0] // count)
+        spread_low.append(
+            remote(
+                far_out.at[there], far_out.at[there], share_send.at[group + hop],
+                share_receive.at[group + hop], low_peer(),
+            )
+        )
+
+    @pl.when(step == 0)
+    def _():
+        mine.start()
+        small_got[0] = small_own[...]
+        meet(
+            [peer(move) for move in (1, 2, 3)] + [low_peer()]
+            + [high_peer(hop, group) for hop in range(1, group)]
+        )
+        for item in smalls:
+            item.start()
+        share.start()
+        for move in (2, 3, 1):
+            piece(0, move).start()
+        far.start()
+        near.start()
+
+        def send_piece(index, carry):
+            for move in (2, 3, 1):
+                piece(index, move).start()
+            return carry
+
+        lax.fori_loop(1, canvases, send_piece, 0)
+        for item in smalls:
+            item.wait()
+        for move in range(4):
+            small_ref[:, aligned(lax.bitwise_xor(me, move), LANES)] = small_got[move]
+            small_out[move] = small_got[move]
+        mine.wait()
+
+    for hop in range(1, group):
+
+        @pl.when(step == min(1 + hop, canvases - 1))
+        def _():
+            spread_high[hop - 1].wait()
+            spread_low[hop].start()
+
+    @pl.when(step == canvases - 1)
+    def _():
+        for item in spread_low:
+            item.wait()
+
+    x_ref[:, aligned(me, LANES)] = mine_ref[aligned(step, PLACES), :].astype(F32)
     for move in (1, 2, 3):
-        copies.append(
-            remote(small_ref, all_small_ref.at[move], send.at[1 + move], receive.at[1 + move], peer(move))
-        )
-    for move, target in ((2, x2_ref), (3, x3_ref), (1, x1_ref)):
-        source = x_ref.at[aligned(lax.bitwise_xor(head, move), rows)]
-        copies.append(remote(source, target, send.at[4 + move], receive.at[4 + move], peer(move)))
-    mine = [
-        pltpu.make_async_copy(qkv_ref, all_qkv_ref.at[0], local.at[0]),
-        pltpu.make_async_copy(small_ref, all_small_ref.at[0], local.at[1]),
-        pltpu.make_async_copy(x_ref.at[aligned(head, rows)], x0_ref, local.at[2]),
-    ]
-    far.start()
-    for copy in copies + mine:
-        copy.start()
-    far.wait()
-    relay = remote(all_qkv_ref.at[2], all_qkv_ref.at[3], send.at[8], receive.at[8], peer(1))
-    relay.start()
-    for copy in copies + mine:
-        copy.wait()
-    relay.wait()
-
-
-def entry(block_in, qkv, small):
-    rows = block_in.shape[0] // 4
-    hbm = pl.BlockSpec(memory_space=pl.ANY)
-    return pl.pallas_call(
-        lambda *refs: entry_kernel(rows, *refs),
-        in_specs=[hbm] * 3,
-        out_specs=[hbm] * 6,
-        out_shape=[like((rows, LANES), BF16)] * 4 + [
-            like((4,) + qkv.shape, BF16), like((4,) + small.shape, F32),
-        ],
-        scratch_shapes=[
-            pltpu.SemaphoreType.DMA((9,)), pltpu.SemaphoreType.DMA((9,)),
-            pltpu.SemaphoreType.DMA((3,)),
-        ],
-        compiler_params=params(collective_id=1, has_side_effects=True),
-        name="entry",
-    )(block_in, qkv, small)
-
-
-def front_kernel(
-    canvases, ids_ref, x0_ref, x1_ref, x2_ref, x3_ref, small_in, qkv_ref,
-    first_ref, hidden_ref, query_ref, value_ref, soft_ref, context_ref, conv_ref, attended_ref,
-    mask_ref, grid_ref, out_ref, x_ref, small_ref, cpe_ref, crpe_ref,
-):
-    cut, col_cuts = read_cuts(ids_ref, canvases)
-    me = lax.axis_index("head")
-
-    @pl.when(pl.program_id(0) == 0)
-    def _():
-        grid_ref[...] = jnp.zeros_like(grid_ref)
-        spread_small(small_in, small_ref)
-        spread_taps(small_ref, CPE, 9, False, cpe_ref)
-        spread_taps(small_ref, CRPE, 49, True, crpe_ref)
-
-    for move, piece_ref in enumerate((x0_ref, x1_ref, x2_ref, x3_ref)):
-        x_ref[:, aligned(lax.bitwise_xor(me, move), LANES)] = piece_ref[...].astype(F32)
-    fill_masks(cut, col_cuts, mask_ref)
-    for tile, plane in SMALL_ITEMS:
-        spread(
-            lambda row: x_ref[SIDE * row : SIDE * row + SIDE, lane(tile)],
-            1, cut, mask_ref, grid_ref, plane,
-        )
-    conv_tiles(SMALL_ITEMS, 1, cut, grid_ref, cpe_ref, 1, out_ref)
-    first = x_ref[...] + out_ref[:PLACES, :] + small_ref[CPE_BIAS : CPE_BIAS + 1, :]
-    first_ref[...] = first
+        piece(step, move).wait()
+        x_ref[:, aligned(lax.bitwise_xor(me, move), LANES)] = landing_ref[step, move - 1].astype(F32)
+    rows_mask, cols_mask = step_masks(*read_cuts(ids_ref, canvases))
+    for tile in range(TILES):
+        field = x_ref[:, lane(tile)]
+        moved = [shift_cols(field, cols_mask, col) for col in (-1, 0, 1)]
+        result = field + small_ref[CPE_BIAS : CPE_BIAS + 1, lane(tile)]
+        for row in (-1, 0, 1):
+            line = None
+            for col in (-1, 0, 1):
+                tap = CPE + (row + 1) * 3 + col + 1
+                term = jnp.broadcast_to(small_ref[tap : tap + 1, lane(tile)], (PLACES, LANES)) * moved[col + 1]
+                line = term if line is None else line + term
+            line = shift_rows(line, row)
+            result = result + (line * rows_mask[row] if row else line)
+        first_ref[:, lane(tile)] = result
+    x_out[...] = x_ref[...].astype(BF16)
+    first = first_ref[...]
     center = row_mean(first)
     square = row_mean(first * first)
     inverse = lax.rsqrt(square - center * center + EPSILON)
@@ -538,20 +609,84 @@
         (first - center) * inverse * small_ref[GAIN1 : GAIN1 + 1, :] + small_ref[SHIFT1 : SHIFT1 + 1, :]
     ).astype(BF16)
     hidden_ref[...] = hidden
+
+    @pl.when(step == 0)
+    def _():
+        share.wait()
+        for item in spread_high + spread_low[:1]:
+            item.start()
+        far.wait()
+        relay.start()
+        near.wait()
+        relay.wait()
+        qkv_ref[0] = qkv_own[...]
+        for move in (1, 2, 3):
+            qkv_ref[move] = qkv_all[move - 1]
+
+    for tile in range(TILES):
+        three = nn(hidden, qkv_ref[lax.bitwise_xor(me, tile)])
+        query_ref[:, lane(tile)] = (
+            three[:, :LANES] + small_ref[QUERY_BIAS : QUERY_BIAS + 1, lane(tile)]
+        ).astype(BF16)
+        key_ref[:, lane(tile)] = three[:, LANES : 2 * LANES].astype(BF16)
+        value_ref[:, lane(tile)] = (
+            three[:, 2 * LANES :] + small_ref[VALUE_BIAS : VALUE_BIAS + 1, lane(tile)]
+        ).astype(BF16)
+
+
+def head_part(ids, small, qkv, block_in, share):
+    count = lax.axis_size("dp")
+    rows = block_in.shape[0] // 4
+    canvases = rows // PLACES
+    wide = rows_spec(D)
+    hbm = pl.BlockSpec(memory_space=pl.ANY)
+    return pl.pallas_call(
+        lambda *refs: head_kernel(canvases, count, *refs),
+        grid=(canvases,),
+        in_specs=[
+            pl.BlockSpec(memory_space=pltpu.SMEM), once(small.shape), once(qkv.shape), hbm, hbm, hbm,
+        ],
+        out_specs=[wide] * 6 + [once((4,) + qkv.shape), once((4,) + small.shape), hbm],
+        out_shape=[like((rows, D), F32)] + [like((rows, D), BF16)] * 5 + [
+            like((4,) + qkv.shape, BF16), like((4,) + small.shape, F32), like(share.shape, BF16),
+        ],
+        scratch_shapes=[
+            pltpu.VMEM((PLACES, D), F32), pltpu.VMEM((canvases, 3, PLACES, LANES), BF16),
+            pltpu.VMEM((rows, LANES), BF16), pltpu.VMEM((SMALL_SIZE, D), F32),
+            pltpu.VMEM((3,) + qkv.shape, BF16), pltpu.VMEM((4,) + small.shape, F32),
+            pltpu.SemaphoreType.DMA((canvases, 3)), pltpu.SemaphoreType.DMA((canvases, 3)),
+            pltpu.SemaphoreType.DMA((6,)), pltpu.SemaphoreType.DMA((6,)),
+            pltpu.SemaphoreType.DMA((count,)), pltpu.SemaphoreType.DMA((count,)),
+            pltpu.SemaphoreType.DMA((1,)),
+        ],
+        compiler_params=params(collective_id=1, has_side_effects=True),
+        name="head",
+    )(ids, small, qkv, block_in, qkv, share)
+
+
+def front_kernel(
+    canvases, ids_ref, query_ref, key_ref, value_ref, small_in,
+    soft_ref, context_ref, conv_ref, attended_ref,
+    mask_ref, grid_ref, out_ref, x_ref, small_ref, crpe_ref,
+):
+    cut, col_cuts = read_cuts(ids_ref, canvases)
+
+    @pl.when(pl.program_id(0) == 0)
+    def _():
+        grid_ref[...] = jnp.zeros_like(grid_ref)
+        spread_small(small_in, small_ref)
+        spread_taps(small_ref, CRPE, 49, True, crpe_ref)
+
+    fill_masks(cut, col_cuts, mask_ref)
     band, side = place_ids(cut, col_cuts)
     ids = 2 * band + side
     sides = [(side == item).astype(F32).astype(BF16) for item in range(2)]
     bands = [(band == item).astype(F32).astype(BF16) for item in range(2)]
     blocks = head_block()
     for tile in range(TILES):
-        three = nn(hidden, qkv_ref[lax.bitwise_xor(me, tile)])
-        query = (three[:, :LANES] + small_ref[QUERY_BIAS : QUERY_BIAS + 1, lane(tile)]).astype(BF16)
-        keys = three[:, LANES : 2 * LANES].astype(BF16).astype(F32)
-        value = (
-            three[:, 2 * LANES :] + small_ref[VALUE_BIAS : VALUE_BIAS + 1, lane(tile)]
-        ).astype(BF16)
-        query_ref[:, lane(tile)] = query
-        value_ref[:, lane(tile)] = value
+        query = query_ref[:, lane(tile)]
+        keys = key_ref[:, lane(tile)].astype(F32)
+        value = value_ref[:, lane(tile)]
         highest = crop_reduce(ids, keys, jnp.max, -1e30)
         powers = jnp.exp(keys - pick(ids, highest))
         totals = crop_reduce(ids, powers, jnp.sum, 0.0)
@@ -572,8 +707,8 @@
     attended_ref[...] = (x_ref[...] + query_ref[...].astype(F32) * conv).astype(BF16)
 
 
-def front(ids, x_parts, small, qkv):
-    rows = x_parts[0].shape[0]
+def front(ids, query, key, value, small):
+    rows = query.shape[0]
     count = rows // PLACES
     wide = rows_spec(D)
     return pl.pallas_call(
@@ -581,30 +716,27 @@
         grid_spec=pltpu.PrefetchScalarGridSpec(
             num_scalar_prefetch=1,
             grid=(count,),
-            in_specs=[rows_spec(LANES)] * 4 + [once(small.shape), once(qkv.shape)],
-            out_specs=[wide, wide, wide, wide, wide, context_spec(0), wide, wide],
+            in_specs=[wide, wide, wide, once(small.shape)],
+            out_specs=[wide, context_spec(0), wide, wide],
             scratch_shapes=[
                 pltpu.VMEM((2, 7, SIDE, LANES), F32),
-                pltpu.VMEM((3 * TILES, GRID_ROWS * SIDE, LANES), F32),
+                pltpu.VMEM((7, GRID_ROWS * SIDE, LANES), F32),
                 pltpu.VMEM((PLACES + SIDE, D), F32),
                 pltpu.VMEM((PLACES, D), F32),
                 pltpu.VMEM((SMALL_SIZE, D), F32),
-                pltpu.VMEM((9, 8, D), F32),
                 pltpu.VMEM((49, 8, D), F32),
             ],
         ),
         out_shape=[
-            like((rows, D), F32), like((rows, D), BF16), like((rows, D), BF16),
-            like((rows, D), BF16), like((rows, D), BF16),
-            like((count, TILES, 2 * LANES, 2 * LANES), BF16),
+            like((rows, D), BF16), like((count, TILES, 2 * LANES, 2 * LANES), BF16),
             like((rows, D), BF16), like((rows, D), BF16),
         ],
         compiler_params=params(),
         cost_estimate=pl.CostEstimate(
-            flops=rows * D * D * 60, bytes_accessed=count * 10**7, transcendentals=0
+            flops=rows * D * D * 40, bytes_accessed=count * 10**7, transcendentals=0
         ),
         name="front",
-    )(ids, *x_parts, small, qkv)
+    )(ids, query, key, value, small)
 
 
 def gelu_both(pre):
@@ -618,7 +750,7 @@
     return pre * cdf, cdf + pre * power * 0.3989422804014327
 
 
-BLOCK = 512
+BLOCK = 1024
 
 
 def middle_kernel(
@@ -662,7 +794,7 @@
     fc2 = weights_ref.at[shard, D : 2 * D]
 
     def proj(tile):
-        return weights_ref[lax.bitwise_xor(me, tile), 2 * D :, :]
+        return weights_ref[lax.bitwise_xor(me, tile), 2 * D : 2 * D + LANES, :]
 
     def relay(number, source, target, part):
         return remote(
@@ -679,9 +811,12 @@
     @pl.when(step == 0)
     def _():
         loads = [
-            pltpu.make_async_copy(own_weights, weights_ref.at[0], fetch.at[0]),
-            pltpu.make_async_copy(far_weights, weights_ref.at[2], fetch.at[1]),
+            pltpu.make_async_copy(own_weights.at[pl.ds(0, 2 * D + LANES)], weights_ref.at[0], fetch.at[0]),
+            pltpu.make_async_copy(far_weights.at[pl.ds(0, 2 * D + LANES)], weights_ref.at[2], fetch.at[1]),
         ]
+        for move, piece_ref in enumerate((cot0_ref, cot1_ref, cot2_ref, cot3_ref)):
+            spot = cot_ref.at[:, aligned(lax.bitwise_xor(me, move), LANES)]
+            loads.append(pltpu.make_async_copy(piece_ref, spot, fetch.at[2 + move]))
         for load in loads:
             load.start()
         meet([peer(1), peer(2), low_peer()])
@@ -690,8 +825,6 @@
         spread_small(small_in, small_ref)
         own_ref[...] = jnp.zeros_like(own_ref)
         sum_ref[...] = jnp.zeros_like(sum_ref)
-        for move, piece_ref in enumerate((cot0_ref, cot1_ref, cot2_ref, cot3_ref)):
-            cot_ref[:, aligned(lax.bitwise_xor(me, move), LANES)] = piece_ref[...]
         for item in loads + relays[:2]:
             item.wait()
 
@@ -818,7 +951,7 @@
         lambda *refs: middle_kernel(count, *refs),
         grid=(4,),
         in_specs=[
-            wide, wide, piece, piece, piece, piece, once(small.shape), hbm, hbm,
+            wide, wide, hbm, hbm, hbm, hbm, once(small.shape), hbm, hbm,
         ],
         out_specs=[
             piece, piece, piece, piece, wide, wide, once((2, padded // 2, D)), once(proj_shape),
@@ -837,9 +970,9 @@
             pltpu.VMEM((4, 2, D, D), BF16), pltpu.VMEM((2, 2, D, D), BF16),
             pltpu.VMEM((2, D, D), BF16), pltpu.VMEM((2, padded, D), BF16),
             pltpu.VMEM((2, padded // 2, D), BF16),
-            pltpu.VMEM((SMALL_SIZE, D), F32), pltpu.VMEM((4,) + own_weights.shape, BF16),
+            pltpu.VMEM((SMALL_SIZE, D), F32), pltpu.VMEM((4, 2 * D + LANES, D), BF16),
             pltpu.SemaphoreType.DMA((12,)), pltpu.SemaphoreType.DMA((12,)),
-            pltpu.SemaphoreType.DMA((2,)),
+            pltpu.SemaphoreType.DMA((6,)),
         ],
         compiler_params=params(collective_id=2, has_side_effects=True),
         cost_estimate=pl.CostEstimate(flops=rows * D * D * 60, bytes_accessed=3 * 10**7, transcendentals=0),
@@ -982,54 +1115,20 @@
     )(ids, grad, query, value, soft, context, conv, hidden, small, middle_sum, bias_grad)
 
 
-def step_masks(cut, col_cuts):
-    place = lax.broadcasted_iota(jnp.int32, (PLACES, LANES), 0)
-    row = lax.shift_right_logical(place, 4)
-    col = lax.bitwise_and(place, 15)
-    col_cut = jnp.where(row >= cut, col_cuts[1], col_cuts[0])
-    rows = {
-        1: (row < SIDE - 1) & (row + 1 != cut),
-        -1: (row > 0) & (row != cut),
-    }
-    cols = {
-        1: (col < SIDE - 1) & (col + 1 != col_cut),
-        -1: (col > 0) & (col != col_cut),
-    }
-    return [
-        {key: jnp.where(mask, 1.0, 0.0).astype(F32) for key, mask in masks.items()}
-        for masks in (rows, cols)
-    ]
-
-
-def shift_rows(values, step):
-    if step == 0:
-        return values
-    zero = jnp.zeros((SIDE, values.shape[1]), values.dtype)
-    if step > 0:
-        return jnp.concatenate([values[SIDE:], zero], axis=0)
-    return jnp.concatenate([zero, values[:-SIDE]], axis=0)
-
-
-def shift_cols(values, masks, step):
-    if step == 0:
-        return values
-    return pltpu.roll(values, (-step) % PLACES, 0) * masks[step]
-
-
 LAST_ROWS = 16
-STAGES = {"core": 0, "far": 1, "low": 3, "high": 4, "share": 5, "last": 6}
-FC_STAGES = {"high": 0, "share": 2, "last": 4}
+STAGES = ((0, 1, 2, 3, 4, 5), (0, 1, 3, 4, 5, 6), (0, 1, 4, 6, 7, 8), (0, 1, 5, 7, 8, 9))
+FC_STAGES = ((0, 2, 4), (1, 4, 6))
 
 
 def tail_kernel(
     count, pieces,
-    canvases, ids_ref, x0_ref, x1_ref, x2_ref, x3_ref, three_ref, first_ref, second_grad_ref, small_params,
-    qkv_ref, fc_mid_in, qkv_grad_in, proj_grad_in, small_in,
-    out0_ref, out1_ref, out2_ref, out3_ref, fc1_own_ref, fc2_own_ref, qkv_own_ref, proj_own_ref,
-    small_own_ref, last_own_ref,
+    canvases, ids_ref, x_in, three_ref, first_ref, second_grad_ref, small_params,
+    qkv_ref, fc_mid_in, small_in, proj_grad_in, qkv_grad_in,
+    out0_ref, out1_ref, out2_ref, out3_ref, fc1_own_ref, fc2_own_ref, small_own_ref, proj_own_ref,
+    qkv_own_ref, last_own_ref,
     x_ref, gone_ref, cpe_sum_ref, sum_ref, fc_part_ref, fc_whole_ref, fc_got_ref, mine_ref, first_got_ref,
     total_ref, second_got_ref, piece_send, piece_receive, send, receive, last_send, last_receive,
-    cpe_ref, fc_mid_ref, qkv_grad_ref, proj_grad_ref, small_ref, *buffers,
+    cpe_ref, fc_mid_ref, small_ref, proj_grad_ref, qkv_grad_ref, *buffers,
 ):
     me = lax.axis_index("head")
     dp = lax.axis_index("dp")
@@ -1043,8 +1142,8 @@
         )
         for kind in range(2)
     ]
-    sources = (qkv_grad_ref, proj_grad_ref, small_ref)
-    targets = (qkv_own_ref, proj_own_ref, small_own_ref)
+    sources = (small_ref, proj_grad_ref, qkv_grad_ref)
+    targets = (small_own_ref, proj_own_ref, qkv_own_ref)
     sums = []
     for number, (item, start, height, padded, lanes) in enumerate(pieces):
         near, far, own, mid, low, part, got = buffers[7 * number : 7 * number + 7]
@@ -1087,21 +1186,22 @@
         cpe_sum_ref[...] = jnp.zeros_like(cpe_sum_ref)
         sum_ref[...] = jnp.zeros_like(sum_ref)
 
-    def at(when, action, items):
-        @pl.when(step == when)
-        def _():
-            for item in items:
-                action(item)
-
-    at(STAGES["core"], lambda item: item.to_core(), sums)
-    at(FC_STAGES["high"], lambda item: item.to_high(), fc_sums)
-    at(STAGES["far"], lambda item: item.to_far(), sums)
-    at(FC_STAGES["share"], lambda item: item.share_high(), fc_sums)
-    at(STAGES["low"], lambda item: item.to_low(), sums)
-    at(STAGES["high"], lambda item: item.to_high(), sums)
-    at(FC_STAGES["last"], lambda item: item.share_low(), fc_sums)
-    at(STAGES["share"], lambda item: item.rest.share_high(), sums)
-    at(STAGES["last"], lambda item: item.rest.share_low(), sums)
+    events = []
+    for item, slots_of in zip(sums, STAGES):
+        actions = (
+            item.to_core, item.to_far, item.to_low, item.to_high, item.rest.share_high, item.rest.share_low,
+        )
+        events += list(zip(slots_of, actions))
+    for item, slots_of in zip(fc_sums, FC_STAGES):
+        events += list(zip(slots_of, (item.to_high, item.share_high, item.share_low)))
+
+    def run(when):
+        for slot, action in events:
+            if slot == when:
+                action()
+
+    for when in range(canvases):
+        pl.when(step == when)(lambda: run(when))
 
     norm_grad = nt(three_ref[0], qkv_ref[lax.bitwise_xor(me, 0)])
     for tile in range(1, TILES):
@@ -1118,8 +1218,7 @@
     sum_ref[0:1, :] += jnp.sum(first_grad, axis=0, keepdims=True)
     sum_ref[1:2, :] += jnp.sum(norm_grad * hat, axis=0, keepdims=True)
     sum_ref[2:3, :] += jnp.sum(norm_grad, axis=0, keepdims=True)
-    for move, piece_ref in enumerate((x0_ref, x1_ref, x2_ref, x3_ref)):
-        x_ref[:, aligned(lax.bitwise_xor(me, move), LANES)] = piece_ref[...].astype(F32)
+    x_ref[...] = x_in[...].astype(F32)
     rows, cols = step_masks(*read_cuts(ids_ref, canvases))
     results = []
     for tile in range(TILES):
@@ -1145,8 +1244,13 @@
     out0_ref[...] = x_ref[:, aligned(me, LANES)].astype(BF16)
     for move in (1, 2, 3):
         gone_ref[step, move - 1] = x_ref[:, aligned(lax.bitwise_xor(me, move), LANES)].astype(BF16)
-    for move in (2, 3, 1):
-        piece_copy(step, move).start()
+    late = canvases // 2
+
+    @pl.when(step >= late)
+    def _():
+        for item in range(2):
+            for move in (2, 3, 1):
+                piece_copy(2 * (step - late) + item, move).start()
 
     @pl.when(step == steps - 1)
     def _():
@@ -1155,10 +1259,7 @@
             mine_ref[move] = sum_ref[:, aligned(lax.bitwise_xor(me, move), LANES)]
         for move in (1, 2, 3):
             first_copy(move).start()
-        for item in fc_sums:
-            item.finish()
-        fc1_own_ref[...] = fc_whole_ref[0, :D, :]
-        fc2_own_ref[...] = fc_whole_ref[1, :D, :]
+        run(canvases)
         total = mine_ref[0]
         for move in (1, 2, 3):
             first_copy(move).wait()
@@ -1166,13 +1267,18 @@
         total_ref[...] = total
         for hop in range(1, count):
             second_copy(hop).start()
-        for piece, item in zip(pieces, sums):
-            item.rest.finish()
-            targets[piece[0]][piece[1] : piece[1] + piece[2], :] = item.whole[: piece[2], :]
+        run(canvases + 1)
+        for item in fc_sums:
+            item.finish()
+        fc1_own_ref[...] = fc_whole_ref[0, :D, :]
+        fc2_own_ref[...] = fc_whole_ref[1, :D, :]
         for hop in range(1, count):
             second_copy(hop).wait()
             total += second_got_ref[hop - 1]
         last_own_ref[...] = total
+        for piece, item in zip(pieces, sums):
+            item.rest.finish()
+            targets[piece[0]][piece[1] : piece[1] + piece[2], :] = item.whole[: piece[2], :]
 
         def settle(index, carry):
             for move in (1, 2, 3):
@@ -1182,11 +1288,11 @@
         lax.fori_loop(0, steps, settle, 0)
 
 
-def tail(ids, x_parts, three, first, second_grad, params_small, qkv, fc_mid, qkv_grad, proj_grad, small):
+def tail(ids, x, three, first, second_grad, params_small, qkv, fc_mid, qkv_grad, proj_grad, small):
     rows = first.shape[0]
     canvases = rows // PLACES
     count = lax.axis_size("dp")
-    segments = [qkv_grad, proj_grad, small]
+    segments = [small, proj_grad, qkv_grad]
     pieces = plan_pieces([item.shape[1:] for item in segments], count)
     slots = high_slots(count)
     wide = rows_spec(D)
@@ -1199,7 +1305,7 @@
     return pl.pallas_call(
         lambda *refs: tail_kernel(count, pieces, canvases, *refs),
         grid=(canvases,),
-        in_specs=[pl.BlockSpec(memory_space=pltpu.SMEM)] + [piece] * 4 + [
+        in_specs=[pl.BlockSpec(memory_space=pltpu.SMEM), wide] + [
             pl.BlockSpec((TILES, PLACES, 3 * LANES), lambda i: (0, i, 0)), wide, wide,
             once(params_small.shape), once(qkv.shape), once(fc_mid.shape),
         ] + [once(item.shape) for item in segments],
@@ -1225,7 +1331,7 @@
             flops=rows * D * D * 12, bytes_accessed=canvases * 3 * 10**6, transcendentals=0
         ),
         name="tail",
-    )(ids, *x_parts, three, first, second_grad, params_small, qkv, fc_mid, *segments)
+    )(ids, x, three, first, second_grad, params_small, qkv, fc_mid, *segments)
 
 
 def collect_kernel(me_ref, *refs):
@@ -1254,7 +1360,7 @@
 
 
 def finish_kernel(
-    me_ref, p0_ref, p1_ref, p2_ref, p3_ref, fc1_ref, fc2_ref, qkv_ref, proj_ref, small_ref, last_ref,
+    me_ref, p0_ref, p1_ref, p2_ref, p3_ref, fc1_ref, fc2_ref, small_ref, proj_ref, qkv_ref, last_ref,
     grad_ref, cpe_ref, vectors_ref, qkv_out_ref, qv_ref, crpe_ref, proj_out_ref, fc1_out_ref,
     bias_ref, fc2_out_ref,
 ):
@@ -1280,7 +1386,7 @@
         fc2_out_ref[...] = fc2_ref[...].astype(F32)
 
 
-def finish(me, pieces, fc1, fc2, qkv, proj, small, last):
+def finish(me, pieces, fc1, fc2, small, proj, qkv, last):
     rows = pieces[0].shape[0]
     shapes = [
         (9, LANES), (8, LANES), qkv.shape, (2, LANES), (49, LANES), proj.shape, fc1.shape,
@@ -1292,7 +1398,7 @@
             num_scalar_prefetch=1,
             grid=(4,),
             in_specs=[once((rows, LANES))] * 4
-            + [once(item.shape) for item in (fc1, fc2, qkv, proj, small, last)],
+            + [once(item.shape) for item in (fc1, fc2, small, proj, qkv, last)],
             out_specs=[
                 pl.BlockSpec((rows, LANES), lambda i, me: (lax.bitwise_xor(me[0], i), 0)),
             ] + [once(shape) for shape in shapes],
@@ -1300,7 +1406,7 @@
         out_shape=[like((4 * rows, LANES), F32)] + [like(shape, F32) for shape in shapes],
         compiler_params=params(),
         name="finish",
-    )(me, *pieces, fc1, fc2, qkv, proj, small, last)
+    )(me, *pieces, fc1, fc2, small, proj, qkv, last)
 
 
 def body(
@@ -1322,16 +1428,20 @@
         fc1_bias.reshape(4, LANES), jnp.zeros((1, LANES), BF16),
     ]).astype(F32)
     own_weights = jnp.concatenate([fc1_weight, fc2_weight, proj_weight])
-    *x_parts, qkv, small = entry(block_in, qkv_weight.reshape(D, 3 * LANES), packed)
-    own_weights, cotangent, x_parts = lax.optimization_barrier((own_weights, cotangent, x_parts))
-    far_weights = swap(own_weights, 2)
+    extra = padded_rows(own_weights.shape[0], lax.axis_size("dp")) - own_weights.shape[0]
+    if extra:
+        own_weights = jnp.pad(own_weights, ((0, extra), (0, 0)))
+    first, hidden, query, key, value, x, qkv, small, far_weights = head_part(
+        ids, packed, qkv_weight.reshape(D, 3 * LANES), block_in, own_weights
+    )
+    cotangent, query = lax.optimization_barrier((cotangent, query))
     cot_pieces = [
         lax.dynamic_slice_in_dim(cotangent, lax.bitwise_xor(head, move) * rows, rows, 0)
         for move in range(4)
     ]
     cot_parts = [cot_pieces[0]] + [swap(cot_pieces[move], move) for move in (1, 2, 3)]
 
-    first, hidden, query, value, soft, context, conv, attended = front(ids, x_parts, small, qkv)
+    soft, context, conv, attended = front(ids, query, key, value, small)
     results = middle(attended, first, cot_parts, small, own_weights, far_weights)
     second_grad, att_grad, fc_mid, proj_grad, middle_sum, bias_grad = results[4:]
     out_parts = [results[0]] + [swap(results[move], move) for move in (1, 2, 3)]
@@ -1340,7 +1450,7 @@
     )
     three, out_parts = lax.optimization_barrier((three, out_parts))
     results = tail(
-        ids, x_parts, three, first, second_grad, small, qkv, fc_mid, qkv_grad, proj_grad, small_grad
+        ids, x, three, first, second_grad, small, qkv, fc_mid, qkv_grad, proj_grad, small_grad
     )
     (input_grad, cpe_g, vectors, qkv_g, qv_g, crpe_g, proj_g, fc1_g, bias_g, fc2_g) = finish(
         me, results[:4], *results[4:]

time: 305 us -> 284 us (0.931)
  Pallas kernels: 283 us -> 264 us
    pallas_call x1, Pallas kernels: 48.5 us -> 29.8 us  [front(): pl.pallas_call(lambda *refs: front_kernel(count, *refs), grid_spec=pltpu....]
    pallas_call x1, Pallas kernels: 37.1 us -> 46.7 us  [head_part(): pl.pallas_call(lambda *refs: head_kernel(canvases, count, *refs), grid=(c...]
    pallas_call x1, Pallas kernels: 58.4 us -> 50.4 us  [back(): pl.pallas_call(lambda *refs: back_kernel(count, *refs), grid_spec=pltpu.P...]
  transfers between devices with their start and end apart: 7 -> 6, of which waited for: 0 -> 0; matrix products, arithmetic and copies ran while one was open for 1% -> 0% of each run, Pallas kernels for 35% -> 28%
where the time goes in v5:
time: 284 us
  Pallas kernels  264 us (93%)
  local copies, waits for them, and re-layouts  14 us (5%)
  starting transfers between devices  4.41 us (2%)
    pallas_call x1, Pallas kernels, middle(): pl.pallas_call(lambda *refs: middle_kernel(count, *refs), grid=(4,), in_s...  65.5 us
    pallas_call x1, Pallas kernels, tail(): pl.pallas_call(lambda *refs: tail_kernel(count, pieces, canvases, *refs),...  61.7 us
    pallas_call x1, Pallas kernels, back(): pl.pallas_call(lambda *refs: back_kernel(count, *refs), grid_spec=pltpu.P...  50.4 us
    pallas_call x1, Pallas kernels, head_part(): pl.pallas_call(lambda *refs: head_kernel(canvases, count, *refs), grid=(c...  46.7 us
    pallas_call x1, Pallas kernels, front(): pl.pallas_call(lambda *refs: front_kernel(count, *refs), grid_spec=pltpu....  29.8 us
    pallas_call x1, Pallas kernels, finish(): pl.pallas_call(finish_kernel, grid_spec=pltpu.PrefetchScalarGridSpec(num_...  5.78 us
  transfers between devices with their start and end apart: 6, of which 0 were waited for; matrix products, arithmetic and copies ran while one was open for 0% of the time, Pallas kernels for 28%

profile of v5, /device:TPU:0, one launch (start us, length us, event | category | flops | bytes accessed | tf_op | source)
XLA Modules:
  0.0 283.6 jit_solution(4923295353466548628)
XLA Ops:
  0.7 0.0 copy-start.5
  0.7 0.0 copy-start.6
  0.7 0.0 copy-start.7
  0.7 3.1 %concatenate.6 = bf16[72,128]{1,0:T(8,128)(2,1)S(1)} concatenate(bf16[9,128]{1,0:T(8,128)(2,1)} %param.21, bf16[49,128]{1,0:T(8,128)(2,1)} %param.27, bf16[1,128]{1,0:T(2,128)(2,1)} %bitcast.31, bf16[1,128]{1,0:T(2,128)(2,1)} %bitcast.32, bf16[1,128]{1,0:T(2,128)(2,1)} %bitcast.33, bf16[2,128]{1,0:T(2,128)(2,1)} %param.26, bf16[1,128]{1,0:T(2,128)(2,1)} %bitcast.34, ...), dimensions={0} | concatenate | bytes 36864 | tf_op jit(solution)/shard_map/concatenate | solution.py:1425
  3.8 0.6 convert_element_type.3.refs_1_
  4.4 1.6 copy.43.refs_0_
  6.0 1.2 copy.38
  7.2 0.9 copy.40.refs_2_.refs_4_
  8.1 0.0 copy-done.5
  8.1 0.0 copy-done.6
  8.2 0.0 copy-done.7
  8.2 0.0 copy-start
  8.2 1.0 copy-done
  9.3 0.0 copy-start.1
  9.3 46.7 %head.1 = (f32[2048,512]{1,0:T(8,128)}, bf16[2048,512]{1,0:T(8,128)(2,1)}, bf16[2048,512]{1,0:T(8,128)(2,1)}, bf16[2048,512]{1,0:T(8,128)(2,1)}, bf16[2048,512]{...) custom-call(s32[32,256]{1,0:T(8,128)} %copy.43.refs_0_, ...), custom_call_target="tpu_custom_call" | custom-call | tf_op jit(solution)/shard_map/head/pallas_call | solution.py:643
  56.0 0.0 copy-done.1
  56.0 0.9 constant_dynamic-slice_fusion
  56.9 1.0 collective-permute-start.2
  57.9 1.5 collective-permute-start.1
  59.4 0.0 collective-permute-start
  59.4 29.8 %front.1 = (bf16[2048,512]{1,0:T(8,128)(2,1)}, bf16[8,4,256,256]{3,2,1,0:T(8,128)(2,1)}, bf16[2048,512]{1,0:T(8,128)(2,1)}, bf16[2048,512]{1,0:T(8,128)(2,1)}) custom-call(s32[32,256]{1,0:T(8,128)} %copy.43.refs_0_, bf16[2048,512]{1,0:T(8,128)(2,1)} %get-tuple-element.71.refs_1_.refs_2_, bf16[2048,512]{1,0:T(8,128)(2,1)} %get-tuple-element.72.refs_2_, ...), custom_call_target="tpu_custom_call" | custom-call | flops 21474836480 | bytes 80000000 | tf_op jit(solution)/shard_map/front/pallas_call | solution.py:714
  89.1 0.0 collective-permute-done.2.refs_5_
  89.1 0.0 copy-start.8
  89.2 0.0 collective-permute-done.1.refs_4_
  89.2 0.0 copy-start.9
  89.2 0.0 collective-permute-done.refs_3_
  89.2 0.0 copy-start.10
  89.2 0.8 copy-done.8
  90.0 0.2 copy-done.9
  90.1 0.2 copy-done.10
  90.3 65.5 %middle.1 = (bf16[2048,128]{1,0:T(8,128)(2,1)}, bf16[2048,128]{1,0:T(8,128)(2,1)}, bf16[2048,128]{1,0:T(8,128)(2,1)}, bf16[2048,128]{1,0:T(8,128)(2,1)}, f32[204...) custom-call(bf16[2048,512]{1,0:T(8,128)(2,1)} %get-tuple-element.75., ...), custom_call_target="tpu_custom_call" | custom-call | flops 32212254720 | bytes 30000000 | tf_op jit(solution)/shard_map/middle/pallas_call | solution.py:950
  155.8 0.1 collective-permute-start.3
  155.8 1.6 collective-permute-start.4
  157.4 0.3 collective-permute-start.5
  157.7 50.4 %back.1 = (bf16[4,2048,384]{2,1,0:T(8,128)(2,1)}, bf16[4,512,384]{2,1,0:T(8,128)(2,1)}, bf16[4,128,128]{2,1,0:T(8,128)(2,1)}) custom-call(s32[32,256]{1,0:T(8,128)} %copy.43.refs_0_, bf16[2048,512]{1,0:T(8,128)(2,1)} %get-tuple-element.79.refs_1_, bf16[2048,512]{1,0:T(8,128)(2,1)} %get-tuple-element.71.refs_1_.refs_2_, ...), custom_call_target="tpu_custom_call" | custom-call | flops 34359738368 | bytes 80000000 | tf_op jit(solution)/shard_map/back/pallas_call | solution.py:1080
  208.1 0.0 collective-permute-done.3.refs_1_
  208.1 0.0 copy-start.2
  208.1 0.0 collective-permute-done.4.refs_2_
  208.1 0.0 copy-start.3
  208.1 0.0 collective-permute-done.5.refs_3_
  208.2 0.0 copy-start.4
  208.2 61.7 %tail.1 = (bf16[2048,128]{1,0:T(8,128)(2,1)}, bf16[2048,128]{1,0:T(8,128)(2,1)}, bf16[2048,128]{1,0:T(8,128)(2,1)}, bf16[2048,128]{1,0:T(8,128)(2,1)}, bf16[512,...) custom-call(s32[32,256]{1,0:T(8,128)} %copy.43.refs_0_, ...), custom_call_target="tpu_custom_call" | custom-call | flops 6442450944 | bytes 24000000 | tf_op jit(solution)/shard_map/tail/pallas_call | solution.py:1305
  269.8 0.0 copy-done.2
  269.8 0.0 copy-done.3
  269.8 0.0 copy-done.4
  269.9 5.8 %finish.1 = (f32[8192,128]{1,0:T(8,128)}, f32[9,128]{1,0:T(8,128)}, f32[8,128]{1,0:T(8,128)}, f32[512,384]{1,0:T(8,128)}, f32[2,128]{1,0:T(2,128)}, /*index=5*/f...) custom-call(s32[1]{0:T(128)} %bitcast.me_ref, ...), custom_call_target="tpu_custom_call" | custom-call | tf_op jit(solution)/shard_map/finish/pallas_call | solution.py:1395
  275.6 1.5 slice_bitcast_fusion
  277.1 1.4 copy.45
  278.5 1.1 copy.46
  279.7 4.0 %collect.1 = f32[8192,128]{1,0:T(8,128)} custom-call(s32[1]{0:T(128)} %bitcast.me_ref, bf16[2048,128]{1,0:T(8,128)(2,1)} %get-tuple-element.91.refs_0_, bf16[2048,128]{1,0:T(8,128)(2,1)} %copy-done.2, bf16[2048,128]{1,0:T(8,128)(2,1)} %copy-done.3, bf16[2048,128]{1,0:T(8,128)(2,1)} %copy-done.4), custom_call_target="tpu_custom_call" | custom-call | tf_op jit(solution)/shard_map/collect/pallas_call | solution.py:1348
  (4 shorter events, 0.1 us)
Async XLA Ops:
  0.7 7.4 %copy-start.5 = (bf16[512,512]{1,0:T(8,128)(2,1)S(1)}, bf16[512,512]{1,0:T(8,128)(2,1)}, u32[]{:S(2)}) copy-start(bf16[512,512]{1,0:T(8,128)(2,1)} %param.32) | copy-start | bytes 1572868
  0.7 7.5 %copy-start.6 = (bf16[512,512]{1,0:T(8,128)(2,1)S(1)}, bf16[512,512]{1,0:T(8,128)(2,1)}, u32[]{:S(2)}) copy-start(bf16[512,512]{1,0:T(8,128)(2,1)} %param.34) | copy-start | bytes 1572868
  0.7 7.5 %copy-start.7 = (bf16[128,512]{1,0:T(8,128)(2,1)S(1)}, bf16[128,512]{1,0:T(8,128)(2,1)}, u32[]{:S(2)}) copy-start(bf16[128,512]{1,0:T(8,128)(2,1)} %param.28) | copy-start | bytes 393220
  8.2 1.1 copy-start
  9.3 46.7 %copy-start.1 = (bf16[8192,128]{1,0:T(8,128)(2,1)S(1)}, bf16[8192,128]{1,0:T(8,128)(2,1)}, u32[]{:S(2)}) copy-start(bf16[8192,128]{1,0:T(8,128)(2,1)} %param.20) | copy-start | bytes 6291460
  56.9 32.2 %collective-permute-start.2 = (bf16[2048,128]{1,0:T(8,128)(2,1)S(1)}, bf16[2048,128]{1,0:T(8,128)(2,1)S(1)}, u32[]{:S(2)}, u32[]{:S(2)}) collective-permute-start(bf16[2048,128]{1,0:T(8,128)(2,1)S(1)} %get-tuple-element.157), channel_id=1, source_target_pairs={{0,3},{1,2},{2,1},{3,0},{4,7},{5,6},{6,5},{7,4},{8,11},{9,10},{10,... | collective-permute-start | bytes 1572872 | tf_op jit(solution)/shard_map/ppermute | solution.py:1423
  57.9 31.3 %collective-permute-start.1 = (bf16[2048,128]{1,0:T(8,128)(2,1)S(1)}, bf16[2048,128]{1,0:T(8,128)(2,1)S(1)}, u32[]{:S(2)}, u32[]{:S(2)}) collective-permute-start(bf16[2048,128]{1,0:T(8,128)(2,1)S(1)} %get-tuple-element.158), channel_id=1, source_target_pairs={{0,2},{1,3},{2,0},{3,1},{4,6},{5,7},{6,4},{7,5},{8,10},{9,11},{10,... | collective-permute-start | bytes 1572872 | tf_op jit(solution)/shard_map/ppermute | solution.py:1423
  59.4 29.8 %collective-permute-start = (bf16[2048,128]{1,0:T(8,128)(2,1)S(1)}, bf16[2048,128]{1,0:T(8,128)(2,1)S(1)}, u32[]{:S(2)}, u32[]{:S(2)}) collective-permute-start(bf16[2048,128]{1,0:T(8,128)(2,1)S(1)} %get-tuple-element.159), channel_id=1, source_target_pairs={{0,1},{1,0},{2,3},{3,2},{4,5},{5,4},{6,7},{7,6},{8,9},{9,8},{10,11... | collective-permute-start | bytes 1572872 | tf_op jit(solution)/shard_map/ppermute | solution.py:1423
  89.1 0.8 copy-start.8
  89.2 0.9 copy-start.9
  89.2 1.1 copy-start.10
  155.8 52.3 %collective-permute-start.3 = (bf16[2048,128]{1,0:T(8,128)(2,1)}, bf16[2048,128]{1,0:T(8,128)(2,1)S(1)}, u32[]{:S(2)}, u32[]{:S(2)}) collective-permute-start(bf16[2048,128]{1,0:T(8,128)(2,1)} %get-tuple-element.88), channel_id=1, source_target_pairs={{0,1},{1,0},{2,3},{3,2},{4,5},{5,4},{6,7},{7,6},{8,9},{9,8},{10,11... | collective-permute-start | bytes 1572872 | tf_op jit(solution)/shard_map/ppermute | solution.py:1423
  155.8 52.3 %collective-permute-start.4 = (bf16[2048,128]{1,0:T(8,128)(2,1)}, bf16[2048,128]{1,0:T(8,128)(2,1)S(1)}, u32[]{:S(2)}, u32[]{:S(2)}) collective-permute-start(bf16[2048,128]{1,0:T(8,128)(2,1)} %get-tuple-element.89), channel_id=1, source_target_pairs={{0,2},{1,3},{2,0},{3,1},{4,6},{5,7},{6,4},{7,5},{8,10},{9,11},{10,... | collective-permute-start | bytes 1572872 | tf_op jit(solution)/shard_map/ppermute | solution.py:1423
  157.4 50.7 %collective-permute-start.5 = (bf16[2048,128]{1,0:T(8,128)(2,1)}, bf16[2048,128]{1,0:T(8,128)(2,1)S(1)}, u32[]{:S(2)}, u32[]{:S(2)}) collective-permute-start(bf16[2048,128]{1,0:T(8,128)(2,1)} %get-tuple-element.90), channel_id=1, source_target_pairs={{0,3},{1,2},{2,1},{3,0},{4,7},{5,6},{6,5},{7,4},{8,11},{9,10},{10,... | collective-permute-start | bytes 1572872 | tf_op jit(solution)/shard_map/ppermute | solution.py:1423
  208.1 61.7 %copy-start.2 = (bf16[2048,128]{1,0:T(8,128)(2,1)}, bf16[2048,128]{1,0:T(8,128)(2,1)S(1)}, u32[]{:S(2)}) copy-start(bf16[2048,128]{1,0:T(8,128)(2,1)S(1)} %collective-permute-done.3.refs_1_) | copy-start | bytes 1572868
  208.1 61.7 %copy-start.3 = (bf16[2048,128]{1,0:T(8,128)(2,1)}, bf16[2048,128]{1,0:T(8,128)(2,1)S(1)}, u32[]{:S(2)}) copy-start(bf16[2048,128]{1,0:T(8,128)(2,1)S(1)} %collective-permute-done.4.refs_2_) | copy-start | bytes 1572868
  208.2 61.7 %copy-start.4 = (bf16[2048,128]{1,0:T(8,128)(2,1)}, bf16[2048,128]{1,0:T(8,128)(2,1)S(1)}, u32[]{:S(2)}) copy-start(bf16[2048,128]{1,0:T(8,128)(2,1)S(1)} %collective-permute-done.5.refs_3_) | copy-start | bytes 1572868

commit v6 on v5

--- a/solution.py
+++ b/solution.py
@@ -1117,7 +1117,7 @@
 
 LAST_ROWS = 16
 STAGES = ((0, 1, 2, 3, 4, 5), (0, 1, 3, 4, 5, 6), (0, 1, 4, 6, 7, 8), (0, 1, 5, 7, 8, 9))
-FC_STAGES = ((0, 2, 4), (1, 4, 6))
+FC_STAGES = ((0, 3, 6), (2, 5, 8))
 
 
 def tail_kernel(
@@ -1244,13 +1244,8 @@
     out0_ref[...] = x_ref[:, aligned(me, LANES)].astype(BF16)
     for move in (1, 2, 3):
         gone_ref[step, move - 1] = x_ref[:, aligned(lax.bitwise_xor(me, move), LANES)].astype(BF16)
-    late = canvases // 2
-
-    @pl.when(step >= late)
-    def _():
-        for item in range(2):
-            for move in (2, 3, 1):
-                piece_copy(2 * (step - late) + item, move).start()
+    for move in (2, 3, 1):
+        piece_copy(step, move).start()
 
     @pl.when(step == steps - 1)
     def _():

time: 284 us -> 279 us (0.982)
  Pallas kernels: 264 us -> 257 us
    pallas_call x1, Pallas kernels: 61.7 us -> 55.8 us  [tail(): pl.pallas_call(lambda *refs: tail_kernel(count, pieces, canvases, *refs),...]
where the time goes in v6:
time: 279 us; the launch traced here: 277 us
  Pallas kernels  257 us (92%)
  local copies, waits for them, and re-layouts  14 us (5%)
  starting transfers between devices  4.41 us (2%)
    pallas_call x1, Pallas kernels, middle(): pl.pallas_call(lambda *refs: middle_kernel(count, *refs), grid=(4,), in_s...  66.1 us
    pallas_call x1, Pallas kernels, tail(): pl.pallas_call(lambda *refs: tail_kernel(count, pieces, canvases, *refs),...  55.8 us
    pallas_call x1, Pallas kernels, back(): pl.pallas_call(lambda *refs: back_kernel(count, *refs), grid_spec=pltpu.P...  49.6 us
    pallas_call x1, Pallas kernels, head_part(): pl.pallas_call(lambda *refs: head_kernel(canvases, count, *refs), grid=(c...  46.7 us
    pallas_call x1, Pallas kernels, front(): pl.pallas_call(lambda *refs: front_kernel(count, *refs), grid_spec=pltpu....  29.4 us
    pallas_call x1, Pallas kernels, finish(): pl.pallas_call(finish_kernel, grid_spec=pltpu.PrefetchScalarGridSpec(num_...  5.78 us
  transfers between devices with their start and end apart: 6, of which 0 were waited for; matrix products, arithmetic and copies ran while one was open for 0% of the time, Pallas kernels for 28%

profile of v6, /device:TPU:0, one launch (start us, length us, event | category | flops | bytes accessed | tf_op | source)
XLA Modules:
  0.0 277.2 jit_solution(8979877278698386595)
XLA Ops:
  0.7 0.0 copy-start.5
  0.7 0.0 copy-start.6
  0.7 0.0 copy-start.7
  0.7 3.1 %concatenate.6 = bf16[72,128]{1,0:T(8,128)(2,1)S(1)} concatenate(bf16[9,128]{1,0:T(8,128)(2,1)} %param.21, bf16[49,128]{1,0:T(8,128)(2,1)} %param.27, bf16[1,128]{1,0:T(2,128)(2,1)} %bitcast.31, bf16[1,128]{1,0:T(2,128)(2,1)} %bitcast.32, bf16[1,128]{1,0:T(2,128)(2,1)} %bitcast.33, bf16[2,128]{1,0:T(2,128)(2,1)} %param.26, bf16[1,128]{1,0:T(2,128)(2,1)} %bitcast.34, ...), dimensions={0} | concatenate | bytes 36864 | tf_op jit(solution)/shard_map/concatenate | solution.py:1420
  3.8 0.6 convert_element_type.3.refs_1_
  4.4 1.6 copy.43.refs_0_
  6.0 1.2 copy.38
  7.2 0.9 copy.40.refs_2_.refs_4_
  8.1 0.0 copy-done.5
  8.1 0.0 copy-done.6
  8.2 0.0 copy-done.7
  8.2 0.0 copy-start
  8.2 1.0 copy-done
  9.3 0.0 copy-start.1
  9.3 46.7 %head.1 = (f32[2048,512]{1,0:T(8,128)}, bf16[2048,512]{1,0:T(8,128)(2,1)}, bf16[2048,512]{1,0:T(8,128)(2,1)}, bf16[2048,512]{1,0:T(8,128)(2,1)}, bf16[2048,512]{...) custom-call(s32[32,256]{1,0:T(8,128)} %copy.43.refs_0_, ...), custom_call_target="tpu_custom_call" | custom-call | tf_op jit(solution)/shard_map/head/pallas_call | solution.py:643
  56.0 0.0 copy-done.1
  56.0 0.9 constant_dynamic-slice_fusion
  56.9 1.0 collective-permute-start.2
  57.9 1.5 collective-permute-start.1
  59.4 0.0 collective-permute-start
  59.4 29.4 %front.1 = (bf16[2048,512]{1,0:T(8,128)(2,1)}, bf16[8,4,256,256]{3,2,1,0:T(8,128)(2,1)}, bf16[2048,512]{1,0:T(8,128)(2,1)}, bf16[2048,512]{1,0:T(8,128)(2,1)}) custom-call(s32[32,256]{1,0:T(8,128)} %copy.43.refs_0_, bf16[2048,512]{1,0:T(8,128)(2,1)} %get-tuple-element.71.refs_1_.refs_2_, bf16[2048,512]{1,0:T(8,128)(2,1)} %get-tuple-element.72.refs_2_, ...), custom_call_target="tpu_custom_call" | custom-call | flops 21474836480 | bytes 80000000 | tf_op jit(solution)/shard_map/front/pallas_call | solution.py:714
  88.8 0.0 collective-permute-done.2.refs_5_
  88.8 0.0 copy-start.8
  88.8 0.0 collective-permute-done.1.refs_4_
  88.8 0.0 copy-start.9
  88.8 0.0 collective-permute-done.refs_3_
  88.8 0.0 copy-start.10
  88.9 0.8 copy-done.8
  89.6 0.2 copy-done.9
  89.8 0.2 copy-done.10
  89.9 66.1 %middle.1 = (bf16[2048,128]{1,0:T(8,128)(2,1)}, bf16[2048,128]{1,0:T(8,128)(2,1)}, bf16[2048,128]{1,0:T(8,128)(2,1)}, bf16[2048,128]{1,0:T(8,128)(2,1)}, f32[204...) custom-call(bf16[2048,512]{1,0:T(8,128)(2,1)} %get-tuple-element.75., ...), custom_call_target="tpu_custom_call" | custom-call | flops 32212254720 | bytes 30000000 | tf_op jit(solution)/shard_map/middle/pallas_call | solution.py:950
  156.1 0.1 collective-permute-start.3
  156.2 1.6 collective-permute-start.4
  157.8 0.3 collective-permute-start.5
  158.0 49.6 %back.1 = (bf16[4,2048,384]{2,1,0:T(8,128)(2,1)}, bf16[4,512,384]{2,1,0:T(8,128)(2,1)}, bf16[4,128,128]{2,1,0:T(8,128)(2,1)}) custom-call(s32[32,256]{1,0:T(8,128)} %copy.43.refs_0_, bf16[2048,512]{1,0:T(8,128)(2,1)} %get-tuple-element.79.refs_1_, bf16[2048,512]{1,0:T(8,128)(2,1)} %get-tuple-element.71.refs_1_.refs_2_, ...), custom_call_target="tpu_custom_call" | custom-call | flops 34359738368 | bytes 80000000 | tf_op jit(solution)/shard_map/back/pallas_call | solution.py:1080
  207.6 0.0 collective-permute-done.3.refs_1_
  207.6 0.0 copy-start.2
  207.6 0.0 collective-permute-done.4.refs_2_
  207.6 0.0 copy-start.3
  207.6 0.0 collective-permute-done.5.refs_3_
  207.6 0.0 copy-start.4
  207.7 55.8 %tail.1 = (bf16[2048,128]{1,0:T(8,128)(2,1)}, bf16[2048,128]{1,0:T(8,128)(2,1)}, bf16[2048,128]{1,0:T(8,128)(2,1)}, bf16[2048,128]{1,0:T(8,128)(2,1)}, bf16[512,...) custom-call(s32[32,256]{1,0:T(8,128)} %copy.43.refs_0_, ...), custom_call_target="tpu_custom_call" | custom-call | flops 6442450944 | bytes 24000000 | tf_op jit(solution)/shard_map/tail/pallas_call | solution.py:1300
  263.4 0.0 copy-done.2
  263.4 0.0 copy-done.3
  263.4 0.0 copy-done.4
  263.5 5.8 %finish.1 = (f32[8192,128]{1,0:T(8,128)}, f32[9,128]{1,0:T(8,128)}, f32[8,128]{1,0:T(8,128)}, f32[512,384]{1,0:T(8,128)}, f32[2,128]{1,0:T(2,128)}, /*index=5*/f...) custom-call(s32[1]{0:T(128)} %bitcast.me_ref, ...), custom_call_target="tpu_custom_call" | custom-call | tf_op jit(solution)/shard_map/finish/pallas_call | solution.py:1390
  269.2 1.5 slice_bitcast_fusion
  270.7 1.4 copy.45
  272.1 1.1 copy.46
  273.3 4.0 %collect.1 = f32[8192,128]{1,0:T(8,128)} custom-call(s32[1]{0:T(128)} %bitcast.me_ref, bf16[2048,128]{1,0:T(8,128)(2,1)} %get-tuple-element.91.refs_0_, bf16[2048,128]{1,0:T(8,128)(2,1)} %copy-done.2, bf16[2048,128]{1,0:T(8,128)(2,1)} %copy-done.3, bf16[2048,128]{1,0:T(8,128)(2,1)} %copy-done.4), custom_call_target="tpu_custom_call" | custom-call | tf_op jit(solution)/shard_map/collect/pallas_call | solution.py:1343
  (4 shorter events, 0.1 us)
Async XLA Ops:
  0.7 7.4 %copy-start.5 = (bf16[512,512]{1,0:T(8,128)(2,1)S(1)}, bf16[512,512]{1,0:T(8,128)(2,1)}, u32[]{:S(2)}) copy-start(bf16[512,512]{1,0:T(8,128)(2,1)} %param.32) | copy-start | bytes 1572868
  0.7 7.5 %copy-start.6 = (bf16[512,512]{1,0:T(8,128)(2,1)S(1)}, bf16[512,512]{1,0:T(8,128)(2,1)}, u32[]{:S(2)}) copy-start(bf16[512,512]{1,0:T(8,128)(2,1)} %param.34) | copy-start | bytes 1572868
  0.7 7.5 %copy-start.7 = (bf16[128,512]{1,0:T(8,128)(2,1)S(1)}, bf16[128,512]{1,0:T(8,128)(2,1)}, u32[]{:S(2)}) copy-start(bf16[128,512]{1,0:T(8,128)(2,1)} %param.28) | copy-start | bytes 393220
  8.2 1.1 copy-start
  9.3 46.7 %copy-start.1 = (bf16[8192,128]{1,0:T(8,128)(2,1)S(1)}, bf16[8192,128]{1,0:T(8,128)(2,1)}, u32[]{:S(2)}) copy-start(bf16[8192,128]{1,0:T(8,128)(2,1)} %param.20) | copy-start | bytes 6291460
  56.9 31.9 %collective-permute-start.2 = (bf16[2048,128]{1,0:T(8,128)(2,1)S(1)}, bf16[2048,128]{1,0:T(8,128)(2,1)S(1)}, u32[]{:S(2)}, u32[]{:S(2)}) collective-permute-start(bf16[2048,128]{1,0:T(8,128)(2,1)S(1)} %get-tuple-element.157), channel_id=1, source_target_pairs={{0,3},{1,2},{2,1},{3,0},{4,7},{5,6},{6,5},{7,4},{8,11},{9,10},{10,... | collective-permute-start | bytes 1572872 | tf_op jit(solution)/shard_map/ppermute | solution.py:1418
  57.9 31.0 %collective-permute-start.1 = (bf16[2048,128]{1,0:T(8,128)(2,1)S(1)}, bf16[2048,128]{1,0:T(8,128)(2,1)S(1)}, u32[]{:S(2)}, u32[]{:S(2)}) collective-permute-start(bf16[2048,128]{1,0:T(8,128)(2,1)S(1)} %get-tuple-element.158), channel_id=1, source_target_pairs={{0,2},{1,3},{2,0},{3,1},{4,6},{5,7},{6,4},{7,5},{8,10},{9,11},{10,... | collective-permute-start | bytes 1572872 | tf_op jit(solution)/shard_map/ppermute | solution.py:1418
  59.4 29.5 %collective-permute-start = (bf16[2048,128]{1,0:T(8,128)(2,1)S(1)}, bf16[2048,128]{1,0:T(8,128)(2,1)S(1)}, u32[]{:S(2)}, u32[]{:S(2)}) collective-permute-start(bf16[2048,128]{1,0:T(8,128)(2,1)S(1)} %get-tuple-element.159), channel_id=1, source_target_pairs={{0,1},{1,0},{2,3},{3,2},{4,5},{5,4},{6,7},{7,6},{8,9},{9,8},{10,11... | collective-permute-start | bytes 1572872 | tf_op jit(solution)/shard_map/ppermute | solution.py:1418
  88.8 0.8 copy-start.8
  88.8 0.9 copy-start.9
  88.8 1.1 copy-start.10
  156.1 51.5 %collective-permute-start.3 = (bf16[2048,128]{1,0:T(8,128)(2,1)}, bf16[2048,128]{1,0:T(8,128)(2,1)S(1)}, u32[]{:S(2)}, u32[]{:S(2)}) collective-permute-start(bf16[2048,128]{1,0:T(8,128)(2,1)} %get-tuple-element.88), channel_id=1, source_target_pairs={{0,1},{1,0},{2,3},{3,2},{4,5},{5,4},{6,7},{7,6},{8,9},{9,8},{10,11... | collective-permute-start | bytes 1572872 | tf_op jit(solution)/shard_map/ppermute | solution.py:1418
  156.2 51.4 %collective-permute-start.4 = (bf16[2048,128]{1,0:T(8,128)(2,1)}, bf16[2048,128]{1,0:T(8,128)(2,1)S(1)}, u32[]{:S(2)}, u32[]{:S(2)}) collective-permute-start(bf16[2048,128]{1,0:T(8,128)(2,1)} %get-tuple-element.89), channel_id=1, source_target_pairs={{0,2},{1,3},{2,0},{3,1},{4,6},{5,7},{6,4},{7,5},{8,10},{9,11},{10,... | collective-permute-start | bytes 1572872 | tf_op jit(solution)/shard_map/ppermute | solution.py:1418
  157.8 49.9 %collective-permute-start.5 = (bf16[2048,128]{1,0:T(8,128)(2,1)}, bf16[2048,128]{1,0:T(8,128)(2,1)S(1)}, u32[]{:S(2)}, u32[]{:S(2)}) collective-permute-start(bf16[2048,128]{1,0:T(8,128)(2,1)} %get-tuple-element.90), channel_id=1, source_target_pairs={{0,3},{1,2},{2,1},{3,0},{4,7},{5,6},{6,5},{7,4},{8,11},{9,10},{10,... | collective-permute-start | bytes 1572872 | tf_op jit(solution)/shard_map/ppermute | solution.py:1418
  207.6 55.8 %copy-start.2 = (bf16[2048,128]{1,0:T(8,128)(2,1)}, bf16[2048,128]{1,0:T(8,128)(2,1)S(1)}, u32[]{:S(2)}) copy-start(bf16[2048,128]{1,0:T(8,128)(2,1)S(1)} %collective-permute-done.3.refs_1_) | copy-start | bytes 1572868
  207.6 55.8 %copy-start.3 = (bf16[2048,128]{1,0:T(8,128)(2,1)}, bf16[2048,128]{1,0:T(8,128)(2,1)S(1)}, u32[]{:S(2)}) copy-start(bf16[2048,128]{1,0:T(8,128)(2,1)S(1)} %collective-permute-done.4.refs_2_) | copy-start | bytes 1572868
  207.6 55.8 %copy-start.4 = (bf16[2048,128]{1,0:T(8,128)(2,1)}, bf16[2048,128]{1,0:T(8,128)(2,1)S(1)}, u32[]{:S(2)}) copy-start(bf16[2048,128]{1,0:T(8,128)(2,1)S(1)} %collective-permute-done.5.refs_3_) | copy-start | bytes 1572868

commit v7 on v6

--- a/solution.py
+++ b/solution.py
@@ -1117,7 +1117,7 @@
 
 LAST_ROWS = 16
 STAGES = ((0, 1, 2, 3, 4, 5), (0, 1, 3, 4, 5, 6), (0, 1, 4, 6, 7, 8), (0, 1, 5, 7, 8, 9))
-FC_STAGES = ((0, 3, 6), (2, 5, 8))
+FC_STAGES = ((0, 2, 4), (1, 4, 6))
 
 
 def tail_kernel(

time: 279 us -> 280 us (level)
  transfers between devices with their start and end apart: 6 -> 6, of which waited for: 0 -> 0; matrix products, arithmetic and copies ran while one was open for 0% -> 0% of each run, Pallas kernels for 28% -> 29%
where the time goes in v7:
time: 280 us; the launch traced here: 279 us
  Pallas kernels  259 us (92%)
  local copies, waits for them, and re-layouts  14 us (5%)
  starting transfers between devices  4.41 us (2%)
    pallas_call x1, Pallas kernels, middle(): pl.pallas_call(lambda *refs: middle_kernel(count, *refs), grid=(4,), in_s...  66.2 us
    pallas_call x1, Pallas kernels, tail(): pl.pallas_call(lambda *refs: tail_kernel(count, pieces, canvases, *refs),...  57.2 us
    pallas_call x1, Pallas kernels, back(): pl.pallas_call(lambda *refs: back_kernel(count, *refs), grid_spec=pltpu.P...  50.1 us
    pallas_call x1, Pallas kernels, head_part(): pl.pallas_call(lambda *refs: head_kernel(canvases, count, *refs), grid=(c...  46.7 us
    pallas_call x1, Pallas kernels, front(): pl.pallas_call(lambda *refs: front_kernel(count, *refs), grid_spec=pltpu....  29.6 us
    pallas_call x1, Pallas kernels, finish(): pl.pallas_call(finish_kernel, grid_spec=pltpu.PrefetchScalarGridSpec(num_...  5.78 us
  transfers between devices with their start and end apart: 6, of which 0 were waited for; matrix products, arithmetic and copies ran while one was open for 0% of the time, Pallas kernels for 29%

profile of v7, /device:TPU:0, one launch (start us, length us, event | category | flops | bytes accessed | tf_op | source)
XLA Modules:
  0.0 279.4 jit_solution(17338648381097919787)
XLA Ops:
  0.7 0.0 copy-start.5
  0.7 0.0 copy-start.6
  0.7 0.0 copy-start.7
  0.7 3.1 %concatenate.6 = bf16[72,128]{1,0:T(8,128)(2,1)S(1)} concatenate(bf16[9,128]{1,0:T(8,128)(2,1)} %param.21, bf16[49,128]{1,0:T(8,128)(2,1)} %param.27, bf16[1,128]{1,0:T(2,128)(2,1)} %bitcast.31, bf16[1,128]{1,0:T(2,128)(2,1)} %bitcast.32, bf16[1,128]{1,0:T(2,128)(2,1)} %bitcast.33, bf16[2,128]{1,0:T(2,128)(2,1)} %param.26, bf16[1,128]{1,0:T(2,128)(2,1)} %bitcast.34, ...), dimensions={0} | concatenate | bytes 36864 | tf_op jit(solution)/shard_map/concatenate | solution.py:1420
  3.8 0.6 convert_element_type.3.refs_1_
  4.4 1.6 copy.43.refs_0_
  6.0 1.2 copy.38
  7.2 0.9 copy.40.refs_2_.refs_4_
  8.1 0.0 copy-done.5
  8.1 0.0 copy-done.6
  8.2 0.0 copy-done.7
  8.2 0.0 copy-start
  8.2 1.0 copy-done
  9.3 0.0 copy-start.1
  9.3 46.7 %head.1 = (f32[2048,512]{1,0:T(8,128)}, bf16[2048,512]{1,0:T(8,128)(2,1)}, bf16[2048,512]{1,0:T(8,128)(2,1)}, bf16[2048,512]{1,0:T(8,128)(2,1)}, bf16[2048,512]{...) custom-call(s32[32,256]{1,0:T(8,128)} %copy.43.refs_0_, ...), custom_call_target="tpu_custom_call" | custom-call | tf_op jit(solution)/shard_map/head/pallas_call | solution.py:643
  56.0 0.0 copy-done.1
  56.0 0.9 constant_dynamic-slice_fusion
  56.9 1.0 collective-permute-start.2
  57.9 1.5 collective-permute-start.1
  59.4 0.0 collective-permute-start
  59.4 29.6 %front.1 = (bf16[2048,512]{1,0:T(8,128)(2,1)}, bf16[8,4,256,256]{3,2,1,0:T(8,128)(2,1)}, bf16[2048,512]{1,0:T(8,128)(2,1)}, bf16[2048,512]{1,0:T(8,128)(2,1)}) custom-call(s32[32,256]{1,0:T(8,128)} %copy.43.refs_0_, bf16[2048,512]{1,0:T(8,128)(2,1)} %get-tuple-element.71.refs_1_.refs_2_, bf16[2048,512]{1,0:T(8,128)(2,1)} %get-tuple-element.72.refs_2_, ...), custom_call_target="tpu_custom_call" | custom-call | flops 21474836480 | bytes 80000000 | tf_op jit(solution)/shard_map/front/pallas_call | solution.py:714
  89.0 0.0 collective-permute-done.2.refs_5_
  89.0 0.0 copy-start.8
  89.1 0.0 collective-permute-done.1.refs_4_
  89.1 0.0 copy-start.9
  89.1 0.0 collective-permute-done.refs_3_
  89.1 0.0 copy-start.10
  89.1 0.8 copy-done.8
  89.8 0.2 copy-done.9
  90.0 0.2 copy-done.10
  90.2 66.2 %middle.1 = (bf16[2048,128]{1,0:T(8,128)(2,1)}, bf16[2048,128]{1,0:T(8,128)(2,1)}, bf16[2048,128]{1,0:T(8,128)(2,1)}, bf16[2048,128]{1,0:T(8,128)(2,1)}, f32[204...) custom-call(bf16[2048,512]{1,0:T(8,128)(2,1)} %get-tuple-element.75., ...), custom_call_target="tpu_custom_call" | custom-call | flops 32212254720 | bytes 30000000 | tf_op jit(solution)/shard_map/middle/pallas_call | solution.py:950
  156.3 0.1 collective-permute-start.3
  156.4 1.1 collective-permute-start.4
  157.5 0.8 collective-permute-start.5
  158.3 50.1 %back.1 = (bf16[4,2048,384]{2,1,0:T(8,128)(2,1)}, bf16[4,512,384]{2,1,0:T(8,128)(2,1)}, bf16[4,128,128]{2,1,0:T(8,128)(2,1)}) custom-call(s32[32,256]{1,0:T(8,128)} %copy.43.refs_0_, bf16[2048,512]{1,0:T(8,128)(2,1)} %get-tuple-element.79.refs_1_, bf16[2048,512]{1,0:T(8,128)(2,1)} %get-tuple-element.71.refs_1_.refs_2_, ...), custom_call_target="tpu_custom_call" | custom-call | flops 34359738368 | bytes 80000000 | tf_op jit(solution)/shard_map/back/pallas_call | solution.py:1080
  208.4 0.0 collective-permute-done.3.refs_1_
  208.4 0.0 copy-start.2
  208.4 0.0 collective-permute-done.4.refs_2_
  208.4 0.0 copy-start.3
  208.4 0.0 collective-permute-done.5.refs_3_
  208.4 0.0 copy-start.4
  208.4 57.2 %tail.1 = (bf16[2048,128]{1,0:T(8,128)(2,1)}, bf16[2048,128]{1,0:T(8,128)(2,1)}, bf16[2048,128]{1,0:T(8,128)(2,1)}, bf16[2048,128]{1,0:T(8,128)(2,1)}, bf16[512,...) custom-call(s32[32,256]{1,0:T(8,128)} %copy.43.refs_0_, ...), custom_call_target="tpu_custom_call" | custom-call | flops 6442450944 | bytes 24000000 | tf_op jit(solution)/shard_map/tail/pallas_call | solution.py:1300
  265.6 0.0 copy-done.2
  265.6 0.0 copy-done.3
  265.6 0.0 copy-done.4
  265.7 5.8 %finish.1 = (f32[8192,128]{1,0:T(8,128)}, f32[9,128]{1,0:T(8,128)}, f32[8,128]{1,0:T(8,128)}, f32[512,384]{1,0:T(8,128)}, f32[2,128]{1,0:T(2,128)}, /*index=5*/f...) custom-call(s32[1]{0:T(128)} %bitcast.me_ref, ...), custom_call_target="tpu_custom_call" | custom-call | tf_op jit(solution)/shard_map/finish/pallas_call | solution.py:1390
  271.4 1.5 slice_bitcast_fusion
  272.9 1.4 copy.45
  274.3 1.1 copy.46
  275.5 4.0 %collect.1 = f32[8192,128]{1,0:T(8,128)} custom-call(s32[1]{0:T(128)} %bitcast.me_ref, bf16[2048,128]{1,0:T(8,128)(2,1)} %get-tuple-element.91.refs_0_, bf16[2048,128]{1,0:T(8,128)(2,1)} %copy-done.2, bf16[2048,128]{1,0:T(8,128)(2,1)} %copy-done.3, bf16[2048,128]{1,0:T(8,128)(2,1)} %copy-done.4), custom_call_target="tpu_custom_call" | custom-call | tf_op jit(solution)/shard_map/collect/pallas_call | solution.py:1343
  (4 shorter events, 0.1 us)
Async XLA Ops:
  0.7 7.4 %copy-start.5 = (bf16[512,512]{1,0:T(8,128)(2,1)S(1)}, bf16[512,512]{1,0:T(8,128)(2,1)}, u32[]{:S(2)}) copy-start(bf16[512,512]{1,0:T(8,128)(2,1)} %param.32) | copy-start | bytes 1572868
  0.7 7.5 %copy-start.6 = (bf16[512,512]{1,0:T(8,128)(2,1)S(1)}, bf16[512,512]{1,0:T(8,128)(2,1)}, u32[]{:S(2)}) copy-start(bf16[512,512]{1,0:T(8,128)(2,1)} %param.34) | copy-start | bytes 1572868
  0.7 7.5 %copy-start.7 = (bf16[128,512]{1,0:T(8,128)(2,1)S(1)}, bf16[128,512]{1,0:T(8,128)(2,1)}, u32[]{:S(2)}) copy-start(bf16[128,512]{1,0:T(8,128)(2,1)} %param.28) | copy-start | bytes 393220
  8.2 1.1 copy-start
  9.3 46.7 %copy-start.1 = (bf16[8192,128]{1,0:T(8,128)(2,1)S(1)}, bf16[8192,128]{1,0:T(8,128)(2,1)}, u32[]{:S(2)}) copy-start(bf16[8192,128]{1,0:T(8,128)(2,1)} %param.20) | copy-start | bytes 6291460
  56.9 32.1 %collective-permute-start.2 = (bf16[2048,128]{1,0:T(8,128)(2,1)S(1)}, bf16[2048,128]{1,0:T(8,128)(2,1)S(1)}, u32[]{:S(2)}, u32[]{:S(2)}) collective-permute-start(bf16[2048,128]{1,0:T(8,128)(2,1)S(1)} %get-tuple-element.157), channel_id=1, source_target_pairs={{0,3},{1,2},{2,1},{3,0},{4,7},{5,6},{6,5},{7,4},{8,11},{9,10},{10,... | collective-permute-start | bytes 1572872 | tf_op jit(solution)/shard_map/ppermute | solution.py:1418
  57.9 31.2 %collective-permute-start.1 = (bf16[2048,128]{1,0:T(8,128)(2,1)S(1)}, bf16[2048,128]{1,0:T(8,128)(2,1)S(1)}, u32[]{:S(2)}, u32[]{:S(2)}) collective-permute-start(bf16[2048,128]{1,0:T(8,128)(2,1)S(1)} %get-tuple-element.158), channel_id=1, source_target_pairs={{0,2},{1,3},{2,0},{3,1},{4,6},{5,7},{6,4},{7,5},{8,10},{9,11},{10,... | collective-permute-start | bytes 1572872 | tf_op jit(solution)/shard_map/ppermute | solution.py:1418
  59.4 29.7 %collective-permute-start = (bf16[2048,128]{1,0:T(8,128)(2,1)S(1)}, bf16[2048,128]{1,0:T(8,128)(2,1)S(1)}, u32[]{:S(2)}, u32[]{:S(2)}) collective-permute-start(bf16[2048,128]{1,0:T(8,128)(2,1)S(1)} %get-tuple-element.159), channel_id=1, source_target_pairs={{0,1},{1,0},{2,3},{3,2},{4,5},{5,4},{6,7},{7,6},{8,9},{9,8},{10,11... | collective-permute-start | bytes 1572872 | tf_op jit(solution)/shard_map/ppermute | solution.py:1418
  89.0 0.8 copy-start.8
  89.1 0.9 copy-start.9
  89.1 1.1 copy-start.10
  156.3 52.0 %collective-permute-start.3 = (bf16[2048,128]{1,0:T(8,128)(2,1)}, bf16[2048,128]{1,0:T(8,128)(2,1)S(1)}, u32[]{:S(2)}, u32[]{:S(2)}) collective-permute-start(bf16[2048,128]{1,0:T(8,128)(2,1)} %get-tuple-element.88), channel_id=1, source_target_pairs={{0,1},{1,0},{2,3},{3,2},{4,5},{5,4},{6,7},{7,6},{8,9},{9,8},{10,11... | collective-permute-start | bytes 1572872 | tf_op jit(solution)/shard_map/ppermute | solution.py:1418
  156.4 52.0 %collective-permute-start.4 = (bf16[2048,128]{1,0:T(8,128)(2,1)}, bf16[2048,128]{1,0:T(8,128)(2,1)S(1)}, u32[]{:S(2)}, u32[]{:S(2)}) collective-permute-start(bf16[2048,128]{1,0:T(8,128)(2,1)} %get-tuple-element.89), channel_id=1, source_target_pairs={{0,2},{1,3},{2,0},{3,1},{4,6},{5,7},{6,4},{7,5},{8,10},{9,11},{10,... | collective-permute-start | bytes 1572872 | tf_op jit(solution)/shard_map/ppermute | solution.py:1418
  157.5 50.9 %collective-permute-start.5 = (bf16[2048,128]{1,0:T(8,128)(2,1)}, bf16[2048,128]{1,0:T(8,128)(2,1)S(1)}, u32[]{:S(2)}, u32[]{:S(2)}) collective-permute-start(bf16[2048,128]{1,0:T(8,128)(2,1)} %get-tuple-element.90), channel_id=1, source_target_pairs={{0,3},{1,2},{2,1},{3,0},{4,7},{5,6},{6,5},{7,4},{8,11},{9,10},{10,... | collective-permute-start | bytes 1572872 | tf_op jit(solution)/shard_map/ppermute | solution.py:1418
  208.4 57.2 %copy-start.2 = (bf16[2048,128]{1,0:T(8,128)(2,1)}, bf16[2048,128]{1,0:T(8,128)(2,1)S(1)}, u32[]{:S(2)}) copy-start(bf16[2048,128]{1,0:T(8,128)(2,1)S(1)} %collective-permute-done.3.refs_1_) | copy-start | bytes 1572868
  208.4 57.2 %copy-start.3 = (bf16[2048,128]{1,0:T(8,128)(2,1)}, bf16[2048,128]{1,0:T(8,128)(2,1)S(1)}, u32[]{:S(2)}) copy-start(bf16[2048,128]{1,0:T(8,128)(2,1)S(1)} %collective-permute-done.4.refs_2_) | copy-start | bytes 1572868
  208.4 57.2 %copy-start.4 = (bf16[2048,128]{1,0:T(8,128)(2,1)}, bf16[2048,128]{1,0:T(8,128)(2,1)S(1)}, u32[]{:S(2)}) copy-start(bf16[2048,128]{1,0:T(8,128)(2,1)S(1)} %collective-permute-done.5.refs_3_) | copy-start | bytes 1572868

commit v8 on v7

--- a/solution.py
+++ b/solution.py
@@ -1116,7 +1116,7 @@
 
 
 LAST_ROWS = 16
-STAGES = ((0, 1, 2, 3, 4, 5), (0, 1, 3, 4, 5, 6), (0, 1, 4, 6, 7, 8), (0, 1, 5, 7, 8, 9))
+STAGES = ((0, 1, 2, 3, 4, 5), (0, 1, 3, 4, 5, 6), (0, 1, 3, 5, 6, 7), (0, 1, 4, 6, 7, 8))
 FC_STAGES = ((0, 2, 4), (1, 4, 6))
 
 
@@ -1329,41 +1329,18 @@
     )(ids, x, three, first, second_grad, params_small, qkv, fc_mid, *segments)
 
 
-def collect_kernel(me_ref, *refs):
-    out_ref = refs[-1]
-    for item, piece_ref in enumerate(refs[:-1]):
-
-        @pl.when(pl.program_id(0) == item)
-        def _():
-            out_ref[...] = piece_ref[...].astype(F32)
-
-
-def collect(me, pieces):
-    rows = pieces[0].shape[0]
-    return pl.pallas_call(
-        collect_kernel,
-        grid_spec=pltpu.PrefetchScalarGridSpec(
-            num_scalar_prefetch=1,
-            grid=(4,),
-            in_specs=[once((rows, LANES))] * 4,
-            out_specs=pl.BlockSpec((rows, LANES), lambda i, me: (lax.bitwise_xor(me[0], i), 0)),
-        ),
-        out_shape=like((4 * rows, LANES), F32),
-        compiler_params=params(),
-        name="collect",
-    )(me, *pieces)
-
-
 def finish_kernel(
-    me_ref, p0_ref, p1_ref, p2_ref, p3_ref, fc1_ref, fc2_ref, small_ref, proj_ref, qkv_ref, last_ref,
-    grad_ref, cpe_ref, vectors_ref, qkv_out_ref, qv_ref, crpe_ref, proj_out_ref, fc1_out_ref,
+    me_ref, p0_ref, p1_ref, p2_ref, p3_ref, q0_ref, q1_ref, q2_ref, q3_ref, fc1_ref, fc2_ref, small_ref, proj_ref, qkv_ref, last_ref,
+    grad_ref, block_out_ref, cpe_ref, vectors_ref, qkv_out_ref, qv_ref, crpe_ref, proj_out_ref, fc1_out_ref,
     bias_ref, fc2_out_ref,
 ):
-    for item, piece_ref in enumerate((p0_ref, p1_ref, p2_ref, p3_ref)):
+    pairs = ((p0_ref, q0_ref), (p1_ref, q1_ref), (p2_ref, q2_ref), (p3_ref, q3_ref))
+    for item, (piece_ref, out_piece_ref) in enumerate(pairs):
 
         @pl.when(pl.program_id(0) == item)
         def _():
             grad_ref[...] = piece_ref[...].astype(F32)
+            block_out_ref[...] = out_piece_ref[...].astype(F32)
 
     @pl.when(pl.program_id(0) == 0)
     def _():
@@ -1381,7 +1358,7 @@
         fc2_out_ref[...] = fc2_ref[...].astype(F32)
 
 
-def finish(me, pieces, fc1, fc2, small, proj, qkv, last):
+def finish(me, pieces, out_pieces, fc1, fc2, small, proj, qkv, last):
     rows = pieces[0].shape[0]
     shapes = [
         (9, LANES), (8, LANES), qkv.shape, (2, LANES), (49, LANES), proj.shape, fc1.shape,
@@ -1392,16 +1369,16 @@
         grid_spec=pltpu.PrefetchScalarGridSpec(
             num_scalar_prefetch=1,
             grid=(4,),
-            in_specs=[once((rows, LANES))] * 4
+            in_specs=[once((rows, LANES))] * 8
             + [once(item.shape) for item in (fc1, fc2, small, proj, qkv, last)],
             out_specs=[
                 pl.BlockSpec((rows, LANES), lambda i, me: (lax.bitwise_xor(me[0], i), 0)),
-            ] + [once(shape) for shape in shapes],
+            ] * 2 + [once(shape) for shape in shapes],
         ),
-        out_shape=[like((4 * rows, LANES), F32)] + [like(shape, F32) for shape in shapes],
+        out_shape=[like((4 * rows, LANES), F32)] * 2 + [like(shape, F32) for shape in shapes],
         compiler_params=params(),
         name="finish",
-    )(me, *pieces, fc1, fc2, small, proj, qkv, last)
+    )(me, *pieces, *out_pieces, fc1, fc2, small, proj, qkv, last)
 
 
 def body(
@@ -1447,11 +1424,11 @@
     results = tail(
         ids, x, three, first, second_grad, small, qkv, fc_mid, qkv_grad, proj_grad, small_grad
     )
-    (input_grad, cpe_g, vectors, qkv_g, qv_g, crpe_g, proj_g, fc1_g, bias_g, fc2_g) = finish(
-        me, results[:4], *results[4:]
+    (input_grad, block_out, cpe_g, vectors, qkv_g, qv_g, crpe_g, proj_g, fc1_g, bias_g, fc2_g) = finish(
+        me, results[:4], out_parts, *results[4:]
     )
     return (
-        collect(me, out_parts), input_grad, cpe_g, vectors[0], vectors[1], vectors[2],
+        block_out, input_grad, cpe_g, vectors[0], vectors[1], vectors[2],
         qkv_g.reshape(D, 3, LANES), qv_g, crpe_g, proj_g, vectors[3], vectors[4], vectors[5],
         fc1_g, bias_g.reshape(D), fc2_g, vectors[6],
     )

time: 280 us -> 278 us (level)
  Pallas kernels: 259 us -> 256 us
    pallas_call x1 -> x0, Pallas kernels: 3.96 us -> none  [collect(): pl.pallas_call(collect_kernel, grid_spec=pltpu.PrefetchScalarGridSpec(num...]
where the time goes in v8:
time: 278 us; the launch traced here: 276 us
  Pallas kernels  256 us (92%)
  local copies, waits for them, and re-layouts  14 us (5%)
  starting transfers between devices  4.41 us (2%)
    pallas_call x1, Pallas kernels, middle(): pl.pallas_call(lambda *refs: middle_kernel(count, *refs), grid=(4,), in_s...  65.6 us
    pallas_call x1, Pallas kernels, tail(): pl.pallas_call(lambda *refs: tail_kernel(count, pieces, canvases, *refs),...  55.7 us
    pallas_call x1, Pallas kernels, back(): pl.pallas_call(lambda *refs: back_kernel(count, *refs), grid_spec=pltpu.P...  50.7 us
    pallas_call x1, Pallas kernels, head_part(): pl.pallas_call(lambda *refs: head_kernel(canvases, count, *refs), grid=(c...  46.7 us
    pallas_call x1, Pallas kernels, front(): pl.pallas_call(lambda *refs: front_kernel(count, *refs), grid_spec=pltpu....  29.9 us
    pallas_call x1, Pallas kernels, finish(): pl.pallas_call(finish_kernel, grid_spec=pltpu.PrefetchScalarGridSpec(num_...  7.49 us
  transfers between devices with their start and end apart: 6, of which 0 were waited for; matrix products, arithmetic and copies ran while one was open for 0% of the time, Pallas kernels for 29%

profile of v8, /device:TPU:0, one launch (start us, length us, event | category | flops | bytes accessed | tf_op | source)
XLA Modules:
  0.0 276.1 jit_solution(15789549394369913622)
XLA Ops:
  0.7 0.0 copy-start.5
  0.7 0.0 copy-start.6
  0.7 0.0 copy-start.7
  0.7 3.1 %concatenate.6 = bf16[72,128]{1,0:T(8,128)(2,1)S(1)} concatenate(bf16[9,128]{1,0:T(8,128)(2,1)} %param.21, bf16[49,128]{1,0:T(8,128)(2,1)} %param.27, bf16[1,128]{1,0:T(2,128)(2,1)} %bitcast.31, bf16[1,128]{1,0:T(2,128)(2,1)} %bitcast.32, bf16[1,128]{1,0:T(2,128)(2,1)} %bitcast.33, bf16[2,128]{1,0:T(2,128)(2,1)} %param.26, bf16[1,128]{1,0:T(2,128)(2,1)} %bitcast.34, ...), dimensions={0} | concatenate | bytes 36864 | tf_op jit(solution)/shard_map/concatenate | solution.py:1397
  3.8 0.6 convert_element_type.3.refs_1_
  4.4 1.6 copy.44.refs_0_
  6.0 1.2 copy.38
  7.2 0.9 copy.40.refs_2_.refs_4_
  8.1 0.0 copy-done.5
  8.1 0.0 copy-done.6
  8.2 0.0 copy-done.7
  8.2 0.0 copy-start
  8.2 1.0 copy-done
  9.3 0.0 copy-start.1
  9.3 46.7 %head.1 = (f32[2048,512]{1,0:T(8,128)}, bf16[2048,512]{1,0:T(8,128)(2,1)}, bf16[2048,512]{1,0:T(8,128)(2,1)}, bf16[2048,512]{1,0:T(8,128)(2,1)}, bf16[2048,512]{...) custom-call(s32[32,256]{1,0:T(8,128)} %copy.44.refs_0_, ...), custom_call_target="tpu_custom_call" | custom-call | tf_op jit(solution)/shard_map/head/pallas_call | solution.py:643
  56.0 0.0 copy-done.1
  56.0 0.9 constant_dynamic-slice_fusion
  56.9 1.0 collective-permute-start.2
  57.9 1.5 collective-permute-start.1
  59.4 0.0 collective-permute-start
  59.4 29.9 %front.1 = (bf16[2048,512]{1,0:T(8,128)(2,1)}, bf16[8,4,256,256]{3,2,1,0:T(8,128)(2,1)}, bf16[2048,512]{1,0:T(8,128)(2,1)}, bf16[2048,512]{1,0:T(8,128)(2,1)}) custom-call(s32[32,256]{1,0:T(8,128)} %copy.44.refs_0_, bf16[2048,512]{1,0:T(8,128)(2,1)} %get-tuple-element.73.refs_1_.refs_2_, bf16[2048,512]{1,0:T(8,128)(2,1)} %get-tuple-element.74.refs_2_, ...), custom_call_target="tpu_custom_call" | custom-call | flops 21474836480 | bytes 80000000 | tf_op jit(solution)/shard_map/front/pallas_call | solution.py:714
  89.3 0.0 collective-permute-done.2.refs_5_
  89.3 0.0 copy-start.8
  89.3 0.0 collective-permute-done.1.refs_4_
  89.3 0.0 copy-start.9
  89.4 0.0 collective-permute-done.refs_3_
  89.4 0.0 copy-start.10
  89.4 0.8 copy-done.8
  90.1 0.2 copy-done.9
  90.3 0.2 copy-done.10
  90.5 65.6 %middle.1 = (bf16[2048,128]{1,0:T(8,128)(2,1)}, bf16[2048,128]{1,0:T(8,128)(2,1)}, bf16[2048,128]{1,0:T(8,128)(2,1)}, bf16[2048,128]{1,0:T(8,128)(2,1)}, f32[204...) custom-call(bf16[2048,512]{1,0:T(8,128)(2,1)} %get-tuple-element.77., ...), custom_call_target="tpu_custom_call" | custom-call | flops 32212254720 | bytes 30000000 | tf_op jit(solution)/shard_map/middle/pallas_call | solution.py:950
  156.1 0.1 collective-permute-start.3
  156.2 1.3 collective-permute-start.4
  157.4 0.6 collective-permute-start.5
  158.0 50.7 %back.1 = (bf16[4,2048,384]{2,1,0:T(8,128)(2,1)}, bf16[4,512,384]{2,1,0:T(8,128)(2,1)}, bf16[4,128,128]{2,1,0:T(8,128)(2,1)}) custom-call(s32[32,256]{1,0:T(8,128)} %copy.44.refs_0_, bf16[2048,512]{1,0:T(8,128)(2,1)} %get-tuple-element.81.refs_1_, bf16[2048,512]{1,0:T(8,128)(2,1)} %get-tuple-element.73.refs_1_.refs_2_, ...), custom_call_target="tpu_custom_call" | custom-call | flops 34359738368 | bytes 80000000 | tf_op jit(solution)/shard_map/back/pallas_call | solution.py:1080
  208.8 0.0 collective-permute-done.3.q1_ref
  208.8 0.0 copy-start.2
  208.8 0.0 collective-permute-done.4.q2_ref
  208.8 0.0 copy-start.3
  208.8 0.0 collective-permute-done.5.q3_ref
  208.8 0.0 copy-start.4
  208.8 55.7 %tail.1 = (bf16[2048,128]{1,0:T(8,128)(2,1)}, bf16[2048,128]{1,0:T(8,128)(2,1)}, bf16[2048,128]{1,0:T(8,128)(2,1)}, bf16[2048,128]{1,0:T(8,128)(2,1)}, bf16[512,...) custom-call(s32[32,256]{1,0:T(8,128)} %copy.44.refs_0_, ...), custom_call_target="tpu_custom_call" | custom-call | flops 6442450944 | bytes 24000000 | tf_op jit(solution)/shard_map/tail/pallas_call | solution.py:1300
  264.6 0.0 copy-done.2
  264.6 0.0 copy-done.3
  264.6 0.0 copy-done.4
  264.6 7.5 %finish.1 = (f32[8192,128]{1,0:T(8,128)}, f32[8192,128]{1,0:T(8,128)}, f32[9,128]{1,0:T(8,128)}, f32[8,128]{1,0:T(8,128)}, f32[512,384]{1,0:T(8,128)}, /*index=5...) custom-call(s32[1]{0:T(128)} %bitcast.me_ref, ...), custom_call_target="tpu_custom_call" | custom-call | tf_op jit(solution)/shard_map/finish/pallas_call | solution.py:1367
  272.1 1.5 slice_bitcast_fusion
  273.6 1.4 copy.45
  275.0 1.1 copy.46
  (4 shorter events, 0.1 us)
Async XLA Ops:
  0.7 7.4 %copy-start.5 = (bf16[512,512]{1,0:T(8,128)(2,1)S(1)}, bf16[512,512]{1,0:T(8,128)(2,1)}, u32[]{:S(2)}) copy-start(bf16[512,512]{1,0:T(8,128)(2,1)} %param.32) | copy-start | bytes 1572868
  0.7 7.5 %copy-start.6 = (bf16[512,512]{1,0:T(8,128)(2,1)S(1)}, bf16[512,512]{1,0:T(8,128)(2,1)}, u32[]{:S(2)}) copy-start(bf16[512,512]{1,0:T(8,128)(2,1)} %param.34) | copy-start | bytes 1572868
  0.7 7.5 %copy-start.7 = (bf16[128,512]{1,0:T(8,128)(2,1)S(1)}, bf16[128,512]{1,0:T(8,128)(2,1)}, u32[]{:S(2)}) copy-start(bf16[128,512]{1,0:T(8,128)(2,1)} %param.28) | copy-start | bytes 393220
  8.2 1.1 copy-start
  9.3 46.7 %copy-start.1 = (bf16[8192,128]{1,0:T(8,128)(2,1)S(1)}, bf16[8192,128]{1,0:T(8,128)(2,1)}, u32[]{:S(2)}) copy-start(bf16[8192,128]{1,0:T(8,128)(2,1)} %param.20) | copy-start | bytes 6291460
  56.9 32.4 %collective-permute-start.2 = (bf16[2048,128]{1,0:T(8,128)(2,1)S(1)}, bf16[2048,128]{1,0:T(8,128)(2,1)S(1)}, u32[]{:S(2)}, u32[]{:S(2)}) collective-permute-start(bf16[2048,128]{1,0:T(8,128)(2,1)S(1)} %get-tuple-element.159), channel_id=1, source_target_pairs={{0,3},{1,2},{2,1},{3,0},{4,7},{5,6},{6,5},{7,4},{8,11},{9,10},{10,... | collective-permute-start | bytes 1572872 | tf_op jit(solution)/shard_map/ppermute | solution.py:1395
  57.9 31.5 %collective-permute-start.1 = (bf16[2048,128]{1,0:T(8,128)(2,1)S(1)}, bf16[2048,128]{1,0:T(8,128)(2,1)S(1)}, u32[]{:S(2)}, u32[]{:S(2)}) collective-permute-start(bf16[2048,128]{1,0:T(8,128)(2,1)S(1)} %get-tuple-element.160), channel_id=1, source_target_pairs={{0,2},{1,3},{2,0},{3,1},{4,6},{5,7},{6,4},{7,5},{8,10},{9,11},{10,... | collective-permute-start | bytes 1572872 | tf_op jit(solution)/shard_map/ppermute | solution.py:1395
  59.4 30.0 %collective-permute-start = (bf16[2048,128]{1,0:T(8,128)(2,1)S(1)}, bf16[2048,128]{1,0:T(8,128)(2,1)S(1)}, u32[]{:S(2)}, u32[]{:S(2)}) collective-permute-start(bf16[2048,128]{1,0:T(8,128)(2,1)S(1)} %get-tuple-element.161), channel_id=1, source_target_pairs={{0,1},{1,0},{2,3},{3,2},{4,5},{5,4},{6,7},{7,6},{8,9},{9,8},{10,11... | collective-permute-start | bytes 1572872 | tf_op jit(solution)/shard_map/ppermute | solution.py:1395
  89.3 0.8 copy-start.8
  89.3 0.9 copy-start.9
  89.4 1.1 copy-start.10
  156.1 52.7 %collective-permute-start.3 = (bf16[2048,128]{1,0:T(8,128)(2,1)}, bf16[2048,128]{1,0:T(8,128)(2,1)S(1)}, u32[]{:S(2)}, u32[]{:S(2)}) collective-permute-start(bf16[2048,128]{1,0:T(8,128)(2,1)} %get-tuple-element.90), channel_id=1, source_target_pairs={{0,1},{1,0},{2,3},{3,2},{4,5},{5,4},{6,7},{7,6},{8,9},{9,8},{10,11... | collective-permute-start | bytes 1572872 | tf_op jit(solution)/shard_map/ppermute | solution.py:1395
  156.2 52.6 %collective-permute-start.4 = (bf16[2048,128]{1,0:T(8,128)(2,1)}, bf16[2048,128]{1,0:T(8,128)(2,1)S(1)}, u32[]{:S(2)}, u32[]{:S(2)}) collective-permute-start(bf16[2048,128]{1,0:T(8,128)(2,1)} %get-tuple-element.91), channel_id=1, source_target_pairs={{0,2},{1,3},{2,0},{3,1},{4,6},{5,7},{6,4},{7,5},{8,10},{9,11},{10,... | collective-permute-start | bytes 1572872 | tf_op jit(solution)/shard_map/ppermute | solution.py:1395
  157.4 51.4 %collective-permute-start.5 = (bf16[2048,128]{1,0:T(8,128)(2,1)}, bf16[2048,128]{1,0:T(8,128)(2,1)S(1)}, u32[]{:S(2)}, u32[]{:S(2)}) collective-permute-start(bf16[2048,128]{1,0:T(8,128)(2,1)} %get-tuple-element.92), channel_id=1, source_target_pairs={{0,3},{1,2},{2,1},{3,0},{4,7},{5,6},{6,5},{7,4},{8,11},{9,10},{10,... | collective-permute-start | bytes 1572872 | tf_op jit(solution)/shard_map/ppermute | solution.py:1395
  208.8 55.8 %copy-start.2 = (bf16[2048,128]{1,0:T(8,128)(2,1)}, bf16[2048,128]{1,0:T(8,128)(2,1)S(1)}, u32[]{:S(2)}) copy-start(bf16[2048,128]{1,0:T(8,128)(2,1)S(1)} %collective-permute-done.3.q1_ref) | copy-start | bytes 1572868
  208.8 55.8 %copy-start.3 = (bf16[2048,128]{1,0:T(8,128)(2,1)}, bf16[2048,128]{1,0:T(8,128)(2,1)S(1)}, u32[]{:S(2)}) copy-start(bf16[2048,128]{1,0:T(8,128)(2,1)S(1)} %collective-permute-done.4.q2_ref) | copy-start | bytes 1572868
  208.8 55.8 %copy-start.4 = (bf16[2048,128]{1,0:T(8,128)(2,1)}, bf16[2048,128]{1,0:T(8,128)(2,1)S(1)}, u32[]{:S(2)}) copy-start(bf16[2048,128]{1,0:T(8,128)(2,1)S(1)} %collective-permute-done.5.q3_ref) | copy-start | bytes 1572868
